TPU v7x, 32 devices: a whole 2x2x4 slice. The times are simulated.
32 devices in a mesh: seq: 8 (over y, x, core), exp: 4 (over z).
Axes of the slice: x: 2, y: 2, z: 4, core: 2. Of those that a mesh axis runs over, the one named last changes fastest.
Arguments:
- tokens: bfloat16 [4, 1024, 1152], P('exp', 'seq'), may hold values from -6 to 6
- segment_ids: int32 [4, 1024], P('exp', 'seq'), may hold values from 0 to 1, as said below
- routes: int32 [4, 1024, 1], P('exp', 'seq'), may hold values from 0 to 3; in each aligned block of 128 rows (0 to 127, 128 to 255, ..., all dimensions but the last counted through in order) at most 64 rows name the same one
- cotangent: bfloat16 [4, 1024, 1152], P('exp', 'seq'), may hold values from -6 to 6
- norm_gain: bfloat16 [1152], P('exp'), may hold values from 0.5 to 1.5
- in_proj: bfloat16 [1152, 4608], P('exp'), may hold values from -0.1875 to 0.1875
- conv_weight: bfloat16 [4, 2304], P(None, 'exp'), may hold values from -3 to 3
- conv_bias: bfloat16 [2304], P('exp'), may hold values from -3 to 3
- x_proj: bfloat16 [2304, 104], P('exp'), may hold values from -0.125 to 0.125
- dt_proj: bfloat16 [72, 2304], P(None, 'exp'), may hold values from -0.75 to 0.75
- dt_bias: bfloat16 [2304], P('exp'), may hold values from -12 to -1
- a_log: bfloat16 [16, 2304], P(None, 'exp'), may hold values from -1 to 1.5
- d_skip: bfloat16 [2304], P('exp'), may hold values from 0.5 to 1.5
- out_proj: bfloat16 [2304, 1152], P('exp'), may hold values from -0.5 to 0.5
- moe_gain: bfloat16 [1152], P('exp'), may hold values from 0.5 to 1.5
- router: bfloat16 [1152, 4], P('exp'), may hold values from -0.09375 to 0.09375
- up_proj: bfloat16 [4, 1152, 3072], P('exp'), may hold values from -0.1875 to 0.1875
- down_proj: bfloat16 [4, 3072, 1152], P('exp'), may hold values from -0.875 to 0.875
Outputs:
- output: bfloat16 [4, 1024, 1152], P('exp', 'seq')
- grad_tokens: float32 [4, 1024, 1152], P('exp', 'seq')
- grad_norm_gain: float32 [1152], P('exp')
- grad_in_proj: float32 [1152, 4608], P('exp')
- grad_conv_weight: float32 [4, 2304], P(None, 'exp')
- grad_conv_bias: float32 [2304], P('exp')
- grad_x_proj: float32 [2304, 104], P('exp')
- grad_dt_proj: float32 [72, 2304], P(None, 'exp')
- grad_dt_bias: float32 [2304], P('exp')
- grad_a_log: float32 [16, 2304], P(None, 'exp')
- grad_d_skip: float32 [2304], P('exp')
- grad_out_proj: float32 [2304, 1152], P('exp')
- grad_moe_gain: float32 [1152], P('exp')
- grad_router: float32 [1152, 4], P('exp')
- grad_up_proj: float32 [4, 1152, 3072], P('exp', 'seq')
- grad_down_proj: float32 [4, 3072, 1152], P('exp', 'seq')
Inputs may be any that keep to these rules, and one draw needn't show every extreme that they name: `segment_ids`: along each row the ids start at 0 and rise by 0 or 1 from one position to the next. `routes`: at most 64 tokens of one device go to one expert, and some expert takes exactly 64 tokens of some device.
All inputs are finite; a program needn't handle non-finite values.
Results may differ from a plain program's by a relative error of at most 0.015.
Values may be sent and summed in bfloat16 or wider, within the bound.
A program may use at most 640 MiB of HBM per device.

v0:
```python
import math

import jax
import jax.numpy as jnp
from jax import lax
from jax.sharding import PartitionSpec as P

EPSILON = 1e-05
TOP_PRECISION = lax.Precision.HIGHEST


def from_behind(block, axis, distance):
    devices = range(lax.axis_size(axis))
    route = [(i - distance, i) for i in devices if i - distance in devices]
    return lax.ppermute(block, axis, route)


def carried_in(array, axis, combine, identity):
    count, index = (lax.axis_size(axis), lax.axis_index(axis))
    everything = jax.tree.map(
        lambda part, kind: lax.all_gather(part.astype(kind), axis),
        array,
        jax.tree.map(lambda a: jnp.bfloat16 if a.dtype == jnp.float32 else a.dtype, array),
    )
    start = jax.tree.map(
        lambda part, zero: jnp.broadcast_to(jnp.asarray(zero, part.dtype), part.shape),
        array,
        identity,
    )

    def carried_turn(k, before):
        reached = k < index
        new = combine(
            before, jax.tree.map(lambda part, own: part[k].astype(own.dtype), everything, array)
        )
        return jax.tree.map(lambda a, b: jnp.where(reached, a, b), new, before)

    return lax.fori_loop(0, count, carried_turn, start)


def entering(array, axis, combine, identity):
    count, index = (lax.axis_size(axis), lax.axis_index(axis))
    everything = jax.tree.map(
        lambda part, kind: lax.all_gather(part.astype(kind), axis),
        array,
        (jnp.bfloat16, jnp.bfloat16),
    )
    start = jax.tree.map(
        lambda part, zero: jnp.broadcast_to(jnp.asarray(zero, part.dtype), part.shape),
        array,
        identity,
    )

    def entering_turn(k, before):
        at = count - 1 - k
        reached = at > index
        new = combine(
            before, jax.tree.map(lambda part, own: part[at].astype(own.dtype), everything, array)
        )
        return jax.tree.map(lambda a, b: jnp.where(reached, a, b), new, before)

    return lax.fori_loop(0, count, entering_turn, start)


def compose(earlier, later):
    return (earlier[0] * later[0], later[0] * earlier[1] + later[1])


def rms_apply(residual, gain_vec):
    return (
        residual
        * lax.rsqrt(jnp.mean(residual * residual, axis=-1, keepdims=True) + EPSILON)
        * gain_vec
    )


def gelu_exact(values):
    return jax.nn.gelu(values, approximate=False)


def contract_rows(first_op, second_op, precision=None):
    return lax.dot_general(
        first_op,
        second_op,
        (((0,), (0,)), ((), ())),
        precision=precision,
        preferred_element_type=jnp.float32,
    )


def contract_cols(first_op, second_op, precision=None):
    return lax.dot_general(
        first_op,
        second_op,
        (((1,), (1,)), ((), ())),
        precision=precision,
        preferred_element_type=jnp.float32,
    )


def blocked(array_in, block_rows):
    return array_in.reshape((array_in.shape[0] // block_rows, block_rows) + array_in.shape[1:])


def block_terms(step_size, in_coef, signal, carry_on, rates):
    decays = jnp.exp(step_size[:, None, :] * rates[None]) * carry_on[:, None, None]
    drives = (step_size * signal)[:, None, :] * in_coef[:, :, None]
    return (decays, drives)


def carry_summary(step_size, in_coef, signal, carry_on, rates):
    length = step_size.shape[0]
    places = jnp.arange(length)
    later_rows = (places[None, :] > places[:, None]).astype(jnp.float32)
    suffix = jnp.dot(
        later_rows, step_size, precision=TOP_PRECISION, preferred_element_type=jnp.float32
    )
    breaks = jnp.dot(
        later_rows, 1.0 - carry_on, precision=TOP_PRECISION, preferred_element_type=jnp.float32
    )
    open_rows = (breaks < 0.5).astype(jnp.float32)
    summands = (
        jnp.exp(rates[None] * suffix[:, None, :])
        * (open_rows[:, None] * in_coef)[:, :, None]
        * (step_size * signal)[:, None, :]
    )
    overall = jnp.exp(rates * jnp.sum(step_size, axis=0)[None, :]) * jnp.min(carry_on)
    return (overall, jnp.sum(summands, axis=0))


def flow_summary(step_size, out_coef, carry_on, y_grad, rates):
    length = step_size.shape[0]
    places = jnp.arange(length)
    upto_rows = (places[None, :] <= places[:, None]).astype(jnp.float32)
    prefix = jnp.dot(
        upto_rows, step_size, precision=TOP_PRECISION, preferred_element_type=jnp.float32
    )
    breaks = jnp.dot(
        upto_rows, 1.0 - carry_on, precision=TOP_PRECISION, preferred_element_type=jnp.float32
    )
    open_rows = (breaks < 0.5).astype(jnp.float32)
    summands = (
        jnp.exp(rates[None] * prefix[:, None, :])
        * (open_rows[:, None] * out_coef)[:, :, None]
        * y_grad[:, None, :]
    )
    return jnp.sum(summands, axis=0)


def forward_pass(incoming, step_size, in_coef, out_coef, signal, carry_on, rates, block_rows):

    def advance(hidden, inputs):
        part_step, part_in, part_out, part_signal, part_carry = inputs
        decays, drives = block_terms(part_step, part_in, part_signal, part_carry, rates)
        lead_prod, local_state = lax.associative_scan(compose, (decays, drives), axis=0)
        states = local_state + lead_prod * hidden[None]
        return (states[-1], (hidden, jnp.sum(part_out[:, :, None] * states, axis=1)))

    sectioned = tuple(
        (
            blocked(array_in, block_rows)
            for array_in in (step_size, in_coef, out_coef, signal, carry_on)
        )
    )
    _, (starts, outputs) = lax.scan(advance, incoming, sectioned)
    return (starts, outputs.reshape(step_size.shape))


def grad_pass(
    flow_in, starts, step_size, in_coef, out_coef, signal, carry_on, y_grad, rates, block_rows
):

    def retreat(carried, inputs):
        flow_now, rate_total = carried
        start_state, part_step, part_in, part_out, part_signal, part_carry, part_grad = inputs
        decays, drives = block_terms(part_step, part_in, part_signal, part_carry, rates)
        lead_prod, local_state = lax.associative_scan(compose, (decays, drives), axis=0)
        states = local_state + lead_prod * start_state[None]
        before = jnp.concatenate([start_state[None], states[:-1]], axis=0)
        emitted = part_out[:, :, None] * part_grad[:, None, :]
        factors = jnp.concatenate([decays[1:], jnp.ones_like(decays[:1])], axis=0)
        tail_prod, local_grad = lax.associative_scan(
            compose, (factors, emitted), reverse=True, axis=0
        )
        gradient = local_grad + tail_prod * flow_now[None]
        rate_term = gradient * before * decays
        drive_grad = jnp.sum(gradient * part_in[:, :, None], axis=1)
        step_grad = jnp.sum(rate_term * rates[None], axis=1) + drive_grad * part_signal
        signal_grad = drive_grad * part_step
        in_grad = jnp.sum(gradient * (part_step * part_signal)[:, None, :], axis=2)
        out_grad = jnp.sum(states * part_grad[:, None, :], axis=2)
        rate_total = rate_total + jnp.sum(rate_term * part_step[:, None, :], axis=0)
        return ((decays[0] * gradient[0], rate_total), (step_grad, signal_grad, in_grad, out_grad))

    sectioned = (starts,) + tuple(
        (
            blocked(array_in, block_rows)
            for array_in in (step_size, in_coef, out_coef, signal, carry_on, y_grad)
        )
    )
    (_, rate_total), (step_grad, signal_grad, in_grad, out_grad) = lax.scan(
        retreat, (flow_in, jnp.zeros_like(rates)), sectioned, reverse=True
    )
    length = step_size.shape[0]
    return (
        step_grad.reshape(length, -1),
        signal_grad.reshape(length, -1),
        in_grad.reshape(length, -1),
        out_grad.reshape(length, -1),
        rate_total,
    )


def stack_parts(gradients, axes_list, groups):
    return jnp.concatenate(
        [
            jnp.moveaxis(gradient, axis_at, 0).reshape(groups, -1)
            for gradient, axis_at in zip(gradients, axes_list)
        ],
        axis=1,
    )


def unstack_parts(flattened, gradients, axes_list, groups):
    pieces = []
    cursor = 0
    for gradient, axis_at in zip(gradients, axes_list):
        reordered = jnp.moveaxis(gradient, axis_at, 0)
        piece_shape = (reordered.shape[0] // groups,) + reordered.shape[1:]
        amount = math.prod(piece_shape)
        pieces.append(
            jnp.moveaxis(flattened[cursor : cursor + amount].reshape(piece_shape), 0, axis_at)
        )
        cursor = cursor + amount
    return pieces


def on_device(
    tokens,
    segment_ids,
    routes,
    cotangent,
    norm_gain,
    in_proj,
    conv_weight,
    conv_bias,
    x_proj,
    dt_proj,
    dt_bias,
    a_log,
    d_skip,
    out_proj,
    moe_gain,
    router,
    up_proj,
    down_proj,
):
    exp_count = lax.axis_size("exp")
    seq_count = lax.axis_size("seq")
    gathered = (
        lax.all_gather(norm_gain, "exp", axis=0, tiled=True),
        lax.all_gather(in_proj, "exp", axis=0, tiled=True),
        lax.all_gather(conv_weight, "exp", axis=1, tiled=True),
        lax.all_gather(conv_bias, "exp", axis=0, tiled=True),
        lax.all_gather(x_proj, "exp", axis=0, tiled=True),
        lax.all_gather(dt_proj, "exp", axis=1, tiled=True),
        lax.all_gather(dt_bias, "exp", axis=0, tiled=True),
        lax.all_gather(a_log, "exp", axis=1, tiled=True),
        lax.all_gather(d_skip, "exp", axis=0, tiled=True),
        lax.all_gather(out_proj, "exp", axis=0, tiled=True),
        lax.all_gather(moe_gain, "exp", axis=0, tiled=True),
        lax.all_gather(router, "exp", axis=0, tiled=True),
    )
    gain_one = gathered[0].astype(jnp.float32)
    proj_in = gathered[1]
    conv_taps = gathered[2].astype(jnp.float32)
    conv_shift = gathered[3].astype(jnp.float32)
    proj_x = gathered[4]
    proj_dt = gathered[5]
    dt_shift = gathered[6].astype(jnp.float32)
    log_rates = gathered[7].astype(jnp.float32)
    skip_gain = gathered[8].astype(jnp.float32)
    proj_out = gathered[9]
    gain_two = gathered[10].astype(jnp.float32)
    router_w = gathered[11]
    row_count = tokens.shape[1]
    model_width = tokens.shape[2]
    inner_width = proj_dt.shape[1]
    dt_rank = proj_dt.shape[0]
    state_count = log_rates.shape[0]
    tap_count = conv_taps.shape[0]
    experts = router_w.shape[1]
    capacity = 2 * row_count // exp_count
    block_rows = 32
    resid_in = tokens[0].astype(jnp.float32)
    seg_float = segment_ids[0].astype(jnp.float32)
    route_row = routes[0, :, 0]
    normed = rms_apply(resid_in, gain_one).astype(jnp.bfloat16)
    projected = jnp.dot(normed, proj_in, preferred_element_type=jnp.float32)
    conv_in = projected[:, :inner_width]
    gate_in = projected[:, inner_width:]
    edge_rows, edge_seg = from_behind(
        (conv_in[row_count - tap_count + 1 :], seg_float[row_count - tap_count + 1 :]), "seq", 1
    )
    padded = jnp.concatenate([edge_rows, conv_in], axis=0)
    padded_seg = jnp.concatenate([edge_seg, seg_float], axis=0)
    valid = [
        (padded_seg[offset : offset + row_count] == seg_float).astype(jnp.float32)[:, None]
        for offset in range(tap_count)
    ]
    conv_out = conv_shift[None, :] + sum(
        (
            conv_taps[offset][None, :] * padded[offset : offset + row_count] * valid[offset]
            for offset in range(tap_count)
        )
    )
    signal = jax.nn.silu(conv_out).astype(jnp.bfloat16)
    signal_up = signal.astype(jnp.float32)
    mixed_proj = jnp.dot(signal, proj_x, preferred_element_type=jnp.float32)
    dt_low = mixed_proj[:, :dt_rank].astype(jnp.bfloat16)
    in_coef = mixed_proj[:, dt_rank : dt_rank + state_count]
    out_coef = mixed_proj[:, dt_rank + state_count :]
    dt_pre = jnp.dot(dt_low, proj_dt, preferred_element_type=jnp.float32) + dt_shift
    step_size = jax.nn.softplus(dt_pre)
    carry_on = (padded_seg[tap_count - 2 : tap_count - 2 + row_count] == seg_float).astype(
        jnp.float32
    )
    rates = -jnp.exp(log_rates)
    local_summary = carry_summary(step_size, in_coef, signal_up, carry_on, rates)
    identity = (jnp.ones_like(rates), jnp.zeros_like(rates))
    incoming = carried_in(local_summary, "seq", compose, identity)[1]
    starts, scanned = forward_pass(
        incoming, step_size, in_coef, out_coef, signal_up, carry_on, rates, block_rows
    )
    y_full = scanned + skip_gain * signal_up
    gate_act = jax.nn.silu(gate_in)
    gated = (y_full * gate_act).astype(jnp.bfloat16)
    resid_mid = resid_in + jnp.dot(gated, proj_out, preferred_element_type=jnp.float32)
    moe_in = rms_apply(resid_mid, gain_two).astype(jnp.bfloat16)
    chances = jax.nn.softmax(jnp.dot(moe_in, router_w, preferred_element_type=jnp.float32), axis=-1)
    choose = route_row[:, None] == jnp.arange(experts)[None, :]
    choose_float = choose.astype(jnp.float32)
    choose_int = choose.astype(jnp.int32)
    gating = jnp.sum(chances * choose_float, axis=-1)
    slot_rank = jnp.sum(jnp.cumsum(choose_int, axis=0) * choose_int, axis=-1) - 1
    slot_ids = route_row * capacity + slot_rank
    dispatch_table = (jnp.arange(experts * capacity)[:, None] == slot_ids[None, :]).astype(
        jnp.bfloat16
    )
    outbound = (
        jnp.dot(dispatch_table, moe_in, preferred_element_type=jnp.float32)
        .astype(jnp.bfloat16)
        .reshape(experts, capacity, model_width)
    )
    up_weight = up_proj[0]
    down_weight = down_proj[0]
    arrived = lax.all_to_all(outbound, "exp", split_axis=0, concat_axis=0, tiled=True)
    flattened = arrived.reshape(-1, model_width)
    expert_pre = jnp.dot(flattened, up_weight, preferred_element_type=jnp.float32)
    hidden = gelu_exact(expert_pre).astype(jnp.bfloat16)
    result = jnp.dot(hidden, down_weight, preferred_element_type=jnp.float32).astype(jnp.bfloat16)
    returned = lax.all_to_all(
        result.reshape(arrived.shape), "exp", split_axis=0, concat_axis=0, tiled=True
    )
    returned, expert_pre, arrived = (
        returned,
        expert_pre.reshape(arrived.shape[0], arrived.shape[1], -1),
        arrived,
    )
    expert_out = contract_rows(dispatch_table, returned.reshape(-1, model_width))
    output = resid_mid + gating[:, None] * expert_out
    out_grad = cotangent[0].astype(jnp.float32)
    gate_grad = jnp.sum(out_grad * expert_out, axis=-1)
    token_slots = (gating[:, None] * out_grad).astype(jnp.bfloat16)
    slot_grad = (
        jnp.dot(dispatch_table, token_slots, preferred_element_type=jnp.float32)
        .astype(jnp.bfloat16)
        .reshape(experts, capacity, model_width)
    )
    result_grad = lax.all_to_all(slot_grad, "exp", split_axis=0, concat_axis=0, tiled=True).reshape(
        -1, model_width
    )
    pre_flat = expert_pre.reshape(-1, expert_pre.shape[-1])
    hidden_float, gelu_pull = jax.vjp(gelu_exact, pre_flat)
    hidden = hidden_float.astype(jnp.bfloat16)
    hidden_grad = contract_cols(result_grad, down_weight)
    pre_grad = gelu_pull(hidden_grad)[0].astype(jnp.bfloat16)
    down_grad = contract_rows(hidden, result_grad)
    up_grad = contract_rows(arrived.reshape(-1, model_width), pre_grad)
    arrived_grad = (
        contract_cols(pre_grad, up_weight)
        .astype(jnp.bfloat16)
        .reshape(experts, capacity, model_width)
    )
    back_slots = lax.all_to_all(arrived_grad, "exp", split_axis=0, concat_axis=0, tiled=True)
    moe_in_grad = contract_rows(dispatch_table, back_slots.reshape(-1, model_width))
    up_part, down_part = (
        lax.psum_scatter(
            up_grad[None].astype(jnp.bfloat16), "seq", scatter_dimension=1, tiled=True
        ).astype(jnp.float32),
        lax.psum_scatter(
            down_grad[None].astype(jnp.bfloat16), "seq", scatter_dimension=1, tiled=True
        ).astype(jnp.float32),
    )
    chance_grad = gate_grad[:, None] * choose_float
    logit_grad = chances * (chance_grad - jnp.sum(chances * chance_grad, axis=-1, keepdims=True))
    router_grad = contract_rows(moe_in.astype(jnp.float32), logit_grad, TOP_PRECISION)
    moe_in_grad = moe_in_grad + contract_cols(
        logit_grad, router_w.astype(jnp.float32), TOP_PRECISION
    )
    _, norm_two_pull = jax.vjp(rms_apply, resid_mid, gain_two)
    resid_two_grad, gain_two_grad = norm_two_pull(moe_in_grad)
    mid_grad = out_grad + resid_two_grad
    branch_grad = mid_grad.astype(jnp.bfloat16)
    out_proj_grad = contract_rows(gated, branch_grad)
    gated_grad = contract_cols(branch_grad, proj_out)
    y_grad = gated_grad * gate_act
    _, silu_gate_pull = jax.vjp(jax.nn.silu, gate_in)
    gate_in_grad = silu_gate_pull(gated_grad * y_full)[0]
    skip_grad = jnp.sum(y_grad * signal_up, axis=0)
    flow_local = flow_summary(step_size, out_coef, carry_on, y_grad, rates)
    flow_in = entering((local_summary[0], flow_local), "seq", compose, identity)[1]
    step_grad, signal_grad, in_grad, out_coef_grad, rate_total = grad_pass(
        flow_in,
        starts,
        step_size,
        in_coef,
        out_coef,
        signal_up,
        carry_on,
        y_grad,
        rates,
        block_rows,
    )
    log_rate_grad = rate_total * rates
    dt_pre_grad = step_grad * jax.nn.sigmoid(dt_pre)
    dt_shift_grad = jnp.sum(dt_pre_grad, axis=0)
    dt_pre_low = dt_pre_grad.astype(jnp.bfloat16)
    dt_proj_grad = contract_rows(dt_low, dt_pre_low)
    dt_low_grad = contract_cols(dt_pre_low, proj_dt)
    mixed_grad = jnp.concatenate([dt_low_grad, in_grad, out_coef_grad], axis=1).astype(jnp.bfloat16)
    x_proj_grad = contract_rows(signal, mixed_grad)
    signal_grad = signal_grad + y_grad * skip_gain + contract_cols(mixed_grad, proj_x)
    _, silu_conv_pull = jax.vjp(jax.nn.silu, conv_out)
    conv_grad = silu_conv_pull(signal_grad)[0]
    taps_grad = jnp.stack(
        [
            jnp.sum(conv_grad * padded[offset : offset + row_count] * valid[offset], axis=0)
            for offset in range(tap_count)
        ]
    )
    shift_grad = jnp.sum(conv_grad, axis=0)
    padded_grad = sum(
        (
            jnp.pad(
                conv_taps[offset][None, :] * conv_grad * valid[offset],
                ((offset, tap_count - 1 - offset), (0, 0)),
            )
            for offset in range(tap_count)
        )
    )
    edge_grad = from_behind(padded_grad[: tap_count - 1], "seq", -1)
    conv_in_grad = padded_grad[tap_count - 1 :] + jnp.pad(
        edge_grad, ((row_count - tap_count + 1, 0), (0, 0))
    )
    proj_grad = jnp.concatenate([conv_in_grad, gate_in_grad], axis=1).astype(jnp.bfloat16)
    in_proj_grad = contract_rows(normed, proj_grad)
    normed_grad = contract_cols(proj_grad, proj_in)
    _, norm_one_pull = jax.vjp(rms_apply, resid_in, gain_one)
    resid_one_grad, gain_one_grad = norm_one_pull(normed_grad)
    token_grad = mid_grad + resid_one_grad
    gradients = (
        gain_one_grad,
        in_proj_grad,
        taps_grad,
        shift_grad,
        x_proj_grad,
        dt_proj_grad,
        dt_shift_grad,
        log_rate_grad,
        skip_grad,
        out_proj_grad,
        gain_two_grad,
        router_grad,
    )
    axes_list = (0, 0, 1, 0, 0, 1, 0, 1, 0, 0, 0, 0)
    flattened = stack_parts(gradients, axes_list, exp_count)
    reordered = (
        flattened.reshape(exp_count, seq_count, -1)
        .transpose(1, 0, 2)
        .reshape(seq_count * exp_count, -1)
    )
    partial_value = lax.psum_scatter(reordered, ("seq", "exp"), scatter_dimension=0, tiled=True)
    summed = (
        lax.all_gather(partial_value.astype(jnp.bfloat16), "seq", axis=0, tiled=True)
        .astype(partial_value.dtype)
        .reshape(-1)
    )
    shards = unstack_parts(summed, gradients, axes_list, exp_count)
    return (
        output.astype(jnp.bfloat16)[None],
        token_grad[None],
        shards[0],
        shards[1],
        shards[2],
        shards[3],
        shards[4],
        shards[5],
        shards[6],
        shards[7],
        shards[8],
        shards[9],
        shards[10],
        shards[11],
        up_part,
        down_part,
    )


def solution(mesh):
    in_specs = (
        P("exp", "seq", None),
        P("exp", "seq"),
        P("exp", "seq", None),
        P("exp", "seq", None),
        P("exp"),
        P("exp", None),
        P(None, "exp"),
        P("exp"),
        P("exp", None),
        P(None, "exp"),
        P("exp"),
        P(None, "exp"),
        P("exp"),
        P("exp", None),
        P("exp"),
        P("exp", None),
        P("exp", None, None),
        P("exp", None, None),
    )
    out_specs = (
        P("exp", "seq", None),
        P("exp", "seq", None),
        P("exp"),
        P("exp", None),
        P(None, "exp"),
        P("exp"),
        P("exp", None),
        P(None, "exp"),
        P("exp"),
        P(None, "exp"),
        P("exp"),
        P("exp", None),
        P("exp"),
        P("exp", None),
        P("exp", "seq", None),
        P("exp", "seq", None),
    )
    return jax.shard_map(
        on_device, mesh=mesh, in_specs=in_specs, out_specs=out_specs, check_vma=False
    )
```

profile of v0, /device:TPU:23, one launch (start us, length us, event | category | flops | bytes accessed | tf_op | source)
XLA Modules:
  0.0 3912.3 jit_solution(14248144054675732995)
XLA Ops:
  12.8 16.8 all-reduce.73
  29.8 15.0 all-gather.4
  45.1 22.7 all-gather.5
  68.5 18.9 all-gather.6
  88.0 15.1 all-gather.3
  107.2 104.2 %all-gather.13.cloned.1.call-done = bf16[1152,4608]{1,0:T(8,128)(2,1)} async-done(((bf16[288,4608]{1,0:T(8,128)(2,1)}), bf16[1152,4608]{1,0:T(8,128)(2,1)}) %all-gather.13.cloned.1.call-update) | async-done | bytes 10616848 | tf_op jit(solution)/shard_map/all_gather | solution.py:262
  233.2 12.6 all-gather.1
  256.5 11.9 while.70
  272.3 620.5 %while.69 = (s32[]{:T(128)}, f32[16,2304]{1,0:T(8,128)}, f32[4,16,2304]{2,1,0:T(8,128)}, f32[4,32,2304]{2,1,0:T(8,128)}, f32[4,32,2304]{2,1,0:T(8,128)}, /*index...) while((s32[]{:T(128)}, f32[16,2304]{1,0:T(8,128)}, ...), condition=%wide.region_8.9_spmd, body=%wide.region_6.8_spmd.sunk | while | flops 23261184 | bytes 276649984 | solution.py:165
  345.7 11.8 pad.925
  379.3 11.6 pad.923
  500.8 11.8 pad.925
  534.4 11.6 pad.923
  655.8 11.8 pad.925
  689.4 11.6 pad.923
  810.8 11.8 pad.925
  844.5 11.6 pad.923
  899.4 18.0 all_to_all.20
  936.8 16.5 all-gather.7
  955.2 18.2 all_to_all.21
  1015.2 11.9 all-gather.2
  1038.7 1288.5 %while.72 = (s32[]{:T(128)}, f32[16,2304]{1,0:T(8,128)S(1)}, f32[16,2304]{1,0:T(8,128)}, f32[4,32,2304]{2,1,0:T(8,128)}, f32[4,32,2304]{2,1,0:T(8,128)}, /*index...) while((s32[]{:T(128)}, f32[16,2304]{1,0:T(8,128)S(1)}, ...), condition=%wide.region_27.28_spmd.clone, body=%wide.region_21.27_spmd.clone.sunk | while | flops 56769536 | bytes 726283264 | solution.py:201
  1118.1 11.7 pad.981
  1151.6 11.7 pad.979
  1271.4 11.7 pad.997
  1440.1 11.7 pad.981
  1473.6 11.7 pad.979
  1593.4 11.7 pad.997
  1762.1 11.7 pad.981
  1795.6 11.7 pad.979
  1915.4 11.7 pad.997
  2084.1 11.7 pad.981
  2117.6 11.7 pad.979
  2237.4 11.7 pad.997
  2362.4 13.1 reshape.369
  2386.2 30.9 reshape.361
  2427.3 109.4 %dynamic-update-slice.6 = f32[4,2107008]{1,0:T(4,128)} dynamic-update-slice(f32[4,2107008]{1,0:T(4,128)} %dynamic-update-slice.5, f32[4,1327104]{1,0:T(4,128)} %reshape.361, s32[]{} %constant.465, s32[]{} %constant.466) | dynamic-update-slice | bytes 42467332
  2556.2 55.3 %dynamic-update-slice.14 = f32[4,2107008]{1,0:T(4,128)} dynamic-update-slice(f32[4,2107008]{1,0:T(4,128)} %dynamic-update-slice.13, f32[4,663552]{1,0:T(4,128)} %reshape.369, s32[]{} %constant.465, s32[]{} %constant.474) | dynamic-update-slice | bytes 21233668
  2613.8 94.8 %reshape.456 = f32[8428032]{0:T(1024)} reshape(f32[4,2107008]{1,0:T(4,128)} %constant_dynamic-update-slice_fusion) | data formatting | bytes 67424256
  2708.6 42.1 %reshape.372 = f32[4,8,263376]{2,1,0:T(8,128)} reshape(f32[8428032]{0:T(1024)} %reshape.456) | data formatting | bytes 67424256 | tf_op jit(solution)/shard_map/reshape | solution.py:489
  2750.6 25.6 copy.187
  2776.2 38.5 reshape.373
  2814.7 556.3 %all-reduce.75 = bf16[32,263376]{1,0:T(8,128)(2,1)} all-reduce(f32[32,263376]{1,0:T(8,128)} %reshape.373), channel_id=5, replica_groups=mesh['seq'=8,'exp'=4] {'seq','exp'}, use_global_device_ids=true, to_apply=%region_38.39.clone | all-reduce | flops 8428032 | bytes 50568192
  3389.9 43.5 %all-gather.17.cloned.1.call-done = bf16[8,1,263376]{2,1,0:T(2,128)(2,1)} async-done(((bf16[1,1,263376]{2,1,0:T(2,128)(2,1)}), bf16[8,1,263376]{2,1,0:T(2,128)(2,1)}) %all-gather.17.cloned.1.call-update) | async-done | bytes 4214032 | tf_op jit(solution)/shard_map/all_gather | solution.py:495
  3433.4 91.6 %convert_reduce_fusion = f32[8,263376]{1,0:T(8,128)} fusion(bf16[8,1,263376]{2,1,0:T(2,128)(2,1)} %all-gather.17.cloned.1.call-done), kind=kLoop, calls=%fused_computation.171 | loop fusion | flops 2107008 | bytes 12642048 | tf_op jit(solution)/shard_map/convert_element_type | solution.py:496
  3536.7 282.2 %slice.1136 = f32[526752,4]{1,0:T(8,128)} reshape(f32[2107008]{0:T(1024)} %reshape.374) | data formatting | bytes 16856064 | tf_op jit(solution)/shard_map/slice | solution.py:232
  3818.9 37.9 slice.1143
  3856.8 17.3 slice.1140
  (1662 shorter events, 1957.7 us)
Async XLA Ops:
  7.3 37.8 copy-start.103
  7.3 204.1 %all-gather.13.cloned.1.call-start = ((), (), s32[]{:S(2)}) async-start(), calls=%async_computation.6 | async-start | bytes 13271040 | tf_op jit(solution)/shard_map/all_gather | solution.py:262
  8.0 887.1 %all-gather.15.cloned.1.call-start = ((), (), s32[]{:S(2)}) async-start(), calls=%async_computation.7 | async-start | bytes 6635520 | tf_op jit(solution)/shard_map/all_gather | solution.py:270
  8.2 60.4 %copy-start.108 = (bf16[72,576]{1,0:T(8,128)(2,1)S(1)}, bf16[72,576]{1,0:T(8,128)(2,1)}, u32[]{:S(2)}) copy-start(bf16[72,576]{1,0:T(8,128)(2,1)} %param.35) | copy-start | bytes 248836
  8.2 98.0 %collective-permute-start.1 = (f32[3]{0:T(128)S(1)}, f32[3]{0:T(128)S(1)}, u32[]{:S(2)}, u32[]{:S(2)}) collective-permute-start(f32[3]{0:T(128)S(1)} %slice_bitcast_fusion.4), channel_id=1, source_target_pairs={{0,4},{4,8},{8,12},{12,16},{16,20},{20,24},{24,28},{1,5},{5,9},{9,... | collective-permute-start | bytes 44 | tf_op jit(solution)/shard_map/ppermute | solution.py:15
  29.6 181.8 %copy-start.98 = (f32[1152]{0:T(1024)}, f32[1152]{0:T(1024)S(1)}, u32[]{:S(2)}) copy-start(f32[1152]{0:T(1024)S(1)} %convert_element_type.246) | copy-start | bytes 13828
  29.8 181.6 %copy-start.125 = (f32[128]{0:T(128)}, f32[128]{0:T(128)S(1)}, u32[]{:S(2)}) copy-start(f32[128]{0:T(128)S(1)} %fusion.123) | copy-start | bytes 1540
  45.0 43.0 %copy-start.124 = (bf16[16,576]{1,0:T(8,128)(2,1)S(1)}, bf16[16,576]{1,0:T(8,128)(2,1)}, u32[]{:S(2)}) copy-start(bf16[16,576]{1,0:T(8,128)(2,1)} %param.37) | copy-start | bytes 55300
  45.1 175.4 %copy-start.112 = (f32[2304]{0:T(1024)}, f32[2304]{0:T(1024)S(1)}, u32[]{:S(2)}) copy-start(f32[2304]{0:T(1024)S(1)} %get-tuple-element.931) | copy-start | bytes 27652
  45.1 175.4 %copy-start.114 = (f32[2304]{0:T(1024)}, f32[2304]{0:T(1024)S(1)}, u32[]{:S(2)}) copy-start(f32[2304]{0:T(1024)S(1)} %get-tuple-element.932) | copy-start | bytes 27652
  45.1 175.4 %copy-start.116 = (f32[2304]{0:T(1024)}, f32[2304]{0:T(1024)S(1)}, u32[]{:S(2)}) copy-start(f32[2304]{0:T(1024)S(1)} %get-tuple-element.933) | copy-start | bytes 27652
  45.1 175.4 %copy-start.117 = (f32[2304]{0:T(1024)}, f32[2304]{0:T(1024)S(1)}, u32[]{:S(2)}) copy-start(f32[2304]{0:T(1024)S(1)} %get-tuple-element.934) | copy-start | bytes 27652
  67.9 37.4 copy-start.128
  68.5 154.0 %copy-start.90 = (bf16[2304,104]{0,1:T(8,128)(2,1)}, bf16[2304,104]{0,1:T(8,128)(2,1)S(1)}, u32[]{:S(2)}) copy-start(bf16[2304,104]{0,1:T(8,128)(2,1)S(1)} %reshape.407) | copy-start | bytes 1437700
  87.9 134.9 %copy-start.84 = (bf16[2304,72]{0,1:T(8,128)(2,1)}, bf16[2304,72]{0,1:T(8,128)(2,1)S(1)}, u32[]{:S(2)}) copy-start(bf16[2304,72]{0,1:T(8,128)(2,1)S(1)} %reshape.409) | copy-start | bytes 995332
  106.9 113.6 %copy-start.140 = (f32[128]{0:T(128)}, f32[128]{0:T(128)S(1)}, u32[]{:S(2)}) copy-start(f32[128]{0:T(128)S(1)} %get-tuple-element.1025) | copy-start | bytes 1540
  107.0 113.5 %copy-start.141 = (f32[128]{0:T(128)}, f32[128]{0:T(128)S(1)}, u32[]{:S(2)}) copy-start(f32[128]{0:T(128)S(1)} %get-tuple-element.1126) | copy-start | bytes 1540
  107.0 113.5 %copy-start.142 = (f32[128]{0:T(128)}, f32[128]{0:T(128)S(1)}, u32[]{:S(2)}) copy-start(f32[128]{0:T(128)S(1)} %get-tuple-element.1127) | copy-start | bytes 1540
  107.0 113.5 %copy-start.143 = (f32[128]{0:T(128)}, f32[128]{0:T(128)S(1)}, u32[]{:S(2)}) copy-start(f32[128]{0:T(128)S(1)} %get-tuple-element.1129) | copy-start | bytes 1540
  217.2 3.2 collective-permute-start
  222.5 47.5 %copy-start.52 = (bf16[128,2304]{1,0:T(8,128)(2,1)}, bf16[128,2304]{1,0:T(8,128)(2,1)S(1)}, u32[]{:S(2)}) copy-start(bf16[128,2304]{1,0:T(8,128)(2,1)S(1)} %get-tuple-element.1026) | copy-start | bytes 1769476
  279.8 44.2 %copy-start.12 = (f32[16,16,2304]{2,1,0:T(8,128)}, f32[16,16,2304]{2,1,0:T(8,128)S(1)}, u32[]{:S(2)}) copy-start(f32[16,16,2304]{2,1,0:T(8,128)S(1)} %get-tuple-element.1426) | copy-start | bytes 7077892 | tf_op jit(solution)/shard_map/while
  434.8 44.2 %copy-start.12 = (f32[16,16,2304]{2,1,0:T(8,128)}, f32[16,16,2304]{2,1,0:T(8,128)S(1)}, u32[]{:S(2)}) copy-start(f32[16,16,2304]{2,1,0:T(8,128)S(1)} %get-tuple-element.1426) | copy-start | bytes 7077892 | tf_op jit(solution)/shard_map/while
  589.9 44.2 %copy-start.12 = (f32[16,16,2304]{2,1,0:T(8,128)}, f32[16,16,2304]{2,1,0:T(8,128)S(1)}, u32[]{:S(2)}) copy-start(f32[16,16,2304]{2,1,0:T(8,128)S(1)} %get-tuple-element.1426) | copy-start | bytes 7077892 | tf_op jit(solution)/shard_map/while
  744.9 44.2 %copy-start.12 = (f32[16,16,2304]{2,1,0:T(8,128)}, f32[16,16,2304]{2,1,0:T(8,128)S(1)}, u32[]{:S(2)}) copy-start(f32[16,16,2304]{2,1,0:T(8,128)S(1)} %get-tuple-element.1426) | copy-start | bytes 7077892 | tf_op jit(solution)/shard_map/while
  899.4 28.3 slice-start.11
  927.7 26.0 copy-start.86
  930.7 24.1 copy-start.129
  930.7 22.9 all-to-all-start.1
  954.8 26.4 slice-start.13
  984.4 17.3 all-to-all-start.3
  989.7 2443.7 %all-gather.17.cloned.1.call-start = ((), (), s32[]{:S(2)}) async-start(), calls=%async_computation.10 | async-start | bytes 9483264 | tf_op jit(solution)/shard_map/all_gather | solution.py:495
  1052.1 44.2 %copy-start.13 = (f32[16,16,2304]{2,1,0:T(8,128)}, f32[16,16,2304]{2,1,0:T(8,128)S(1)}, u32[]{:S(2)}) copy-start(f32[16,16,2304]{2,1,0:T(8,128)S(1)} %get-tuple-element.1478) | copy-start | bytes 7077892 | tf_op jit(solution)/shard_map/while
  1205.4 44.1 %copy-start.11 = (f32[16,16,2304]{2,1,0:T(8,128)}, f32[16,16,2304]{2,1,0:T(8,128)S(1)}, u32[]{:S(2)}) copy-start(f32[16,16,2304]{2,1,0:T(8,128)S(1)} %get-tuple-element.1507) | copy-start | bytes 7077892 | tf_op jit(solution)/shard_map/while
  1374.1 44.2 %copy-start.13 = (f32[16,16,2304]{2,1,0:T(8,128)}, f32[16,16,2304]{2,1,0:T(8,128)S(1)}, u32[]{:S(2)}) copy-start(f32[16,16,2304]{2,1,0:T(8,128)S(1)} %get-tuple-element.1478) | copy-start | bytes 7077892 | tf_op jit(solution)/shard_map/while
  1527.4 44.1 %copy-start.11 = (f32[16,16,2304]{2,1,0:T(8,128)}, f32[16,16,2304]{2,1,0:T(8,128)S(1)}, u32[]{:S(2)}) copy-start(f32[16,16,2304]{2,1,0:T(8,128)S(1)} %get-tuple-element.1507) | copy-start | bytes 7077892 | tf_op jit(solution)/shard_map/while
  1696.1 44.2 %copy-start.13 = (f32[16,16,2304]{2,1,0:T(8,128)}, f32[16,16,2304]{2,1,0:T(8,128)S(1)}, u32[]{:S(2)}) copy-start(f32[16,16,2304]{2,1,0:T(8,128)S(1)} %get-tuple-element.1478) | copy-start | bytes 7077892 | tf_op jit(solution)/shard_map/while
  1849.4 44.1 %copy-start.11 = (f32[16,16,2304]{2,1,0:T(8,128)}, f32[16,16,2304]{2,1,0:T(8,128)S(1)}, u32[]{:S(2)}) copy-start(f32[16,16,2304]{2,1,0:T(8,128)S(1)} %get-tuple-element.1507) | copy-start | bytes 7077892 | tf_op jit(solution)/shard_map/while
  2018.1 44.2 %copy-start.13 = (f32[16,16,2304]{2,1,0:T(8,128)}, f32[16,16,2304]{2,1,0:T(8,128)S(1)}, u32[]{:S(2)}) copy-start(f32[16,16,2304]{2,1,0:T(8,128)S(1)} %get-tuple-element.1478) | copy-start | bytes 7077892 | tf_op jit(solution)/shard_map/while
  2171.3 44.1 %copy-start.11 = (f32[16,16,2304]{2,1,0:T(8,128)}, f32[16,16,2304]{2,1,0:T(8,128)S(1)}, u32[]{:S(2)}) copy-start(f32[16,16,2304]{2,1,0:T(8,128)S(1)} %get-tuple-element.1507) | copy-start | bytes 7077892 | tf_op jit(solution)/shard_map/while
  2345.9 29.6 collective-permute-start.2
  2386.2 30.9 copy-start.126
  2427.3 109.4 %copy-start.102 = (f32[4,2304]{1,0:T(4,128)S(1)}, f32[4,2304]{1,0:T(4,128)}, u32[]{:S(2)}) copy-start(f32[4,2304]{1,0:T(4,128)} %reshape.362) | copy-start | bytes 110596
  2427.3 111.1 %copy-start.120 = (f32[4,576]{1,0:T(4,128)S(1)}, f32[4,576]{1,0:T(4,128)}, u32[]{:S(2)}) copy-start(f32[4,576]{1,0:T(4,128)} %reshape.363) | copy-start | bytes 27652
  2427.3 112.7 %copy-start.78 = (f32[4,59904]{1,0:T(4,128)S(1)}, f32[4,59904]{1,0:T(4,128)}, u32[]{:S(2)}) copy-start(f32[4,59904]{1,0:T(4,128)} %reshape.364) | copy-start | bytes 2875396
  2556.2 57.0 %copy-start.109 = (f32[4,1152]{1,0:T(4,128)S(1)}, f32[4,1152]{1,0:T(4,128)}, u32[]{:S(2)}) copy-start(f32[4,1152]{1,0:T(4,128)} %reshape.371) | copy-start | bytes 55300
  3375.6 524.8 %reduce-scatter.5.cloned.1.call-start = ((), (), s32[]{:S(2)}) async-start(), calls=%async_computation.9 | async-start | bytes 7962624 | tf_op jit(solution)/shard_map/reduce_scatter | solution.py:401
  3381.0 522.0 %reduce-scatter.3.cloned.1.call-start = ((), (), s32[]{:S(2)}) async-start(), calls=%async_computation.8 | async-start | bytes 7962624 | tf_op jit(solution)/shard_map/reduce_scatter | solution.py:398
  (349 other events, 1779.8 us)
Sparse Core Ops, SparseCore 0:
  9.7 201.6 all-gather.12
  213.0 97.4 all-gather.14
  3375.8 57.6 all-gather.16
  3436.8 65.0 reduce-scatter.4
  3505.7 65.4 reduce-scatter.2
where the time goes:
time: 3950 us; the launch traced here: 3910 us
  local copies, waits for them, and re-layouts  2070 us (52%)
  other arithmetic  825 us (21%)
  blocking collectives  731 us (19%)
  waiting for transfers between devices  158 us (4%)
  matrix products  91 us (2%)
    unnamed x2, blocking collectives  573 us
    slice x10, local copies, waits for them, and re-layouts, unstack_parts(): flattened[cursor:cursor + amount].reshape(piece_shape)  349 us
    pad x64, local copies, waits for them, and re-layouts, retreat(): lax.associative_scan(compose, (decays, drives), axis=0)  348 us
    pad x64, local copies, waits for them, and re-layouts, advance(): lax.associative_scan(compose, (decays, drives), axis=0)  348 us
    pad x64, local copies, waits for them, and re-layouts, retreat(): lax.associative_scan(compose, (factors, emitted), reverse=True, axis=0)  331 us
    unnamed x220, local copies, waits for them, and re-layouts  299 us
    add x96, other arithmetic, compose(): return (earlier[0] * later[0], later[0] * earlier[1] + later[1])  150 us
    all_gather x1, waiting for transfers between devices, on_device(): lax.all_gather(in_proj, 'exp', axis=0, tiled=True)  104 us
  transfers between devices with their start and end apart: 10, of which 4 were waited for; matrix products, arithmetic and copies ran while one was open for 30% of the time, Pallas kernels for 0%

commit v1 on v0

v1 whole, which is shorter than its diff:
```python
import functools
import math

import jax
import jax.numpy as jnp
from jax import lax
from jax.experimental import pallas as pl
from jax.experimental.pallas import tpu as pltpu
from jax.sharding import PartitionSpec as P

EPSILON = 1e-05
LOG2E = math.log2(math.e)
LN2 = math.log(2.0)
CLOSED = 1e30
LANES = 128
SUB = 8
F32 = jnp.float32
BF16 = jnp.bfloat16
VMEM_LIMIT = 56 * 1024 * 1024


def mm(a, b):
    return lax.dot_general(a, b, (((1,), (0,)), ((), ())), preferred_element_type=F32)


def mm_nt(a, b):
    return lax.dot_general(a, b, (((1,), (1,)), ((), ())), preferred_element_type=F32)


def mm_tn(a, b):
    return lax.dot_general(a, b, (((0,), (0,)), ((), ())), preferred_element_type=F32)


def split_hi_lo(value):
    high = value.astype(BF16)
    return high, (value - high.astype(F32)).astype(BF16)


def sigmoid(v):
    return 1.0 / (1.0 + jnp.exp(-v))


def softplus(v):
    e = jnp.exp(-jnp.abs(v))
    small = e * (1.0 - e * (0.5 - e * (1.0 / 3.0 - e * 0.25)))
    return jnp.maximum(v, 0.0) + jnp.where(e < 0.01, small, jnp.log(1.0 + e))


def rms_scale(v):
    return lax.rsqrt(jnp.mean(v * v, axis=-1, keepdims=True) + EPSILON)


def rms_back(resid, gain, grad):
    s = rms_scale(resid)
    v = gain * grad
    out = s * v - resid * (s * s * s) * jnp.mean(resid * v, axis=-1, keepdims=True)
    return out, jnp.sum(grad * resid * s, axis=0, keepdims=True)


def block(shape, index):
    return pl.BlockSpec(shape, index)


def whole(shape):
    zeros = (0,) * len(shape)
    return pl.BlockSpec(shape, lambda *_: zeros)


def call(body, name, grid, ins, in_specs, outs, out_specs, scratch, cost=None):
    return pl.pallas_call(
        body,
        name=name,
        grid=grid,
        in_specs=in_specs,
        out_specs=out_specs,
        out_shape=outs,
        scratch_shapes=scratch,
        cost_estimate=cost,
        compiler_params=pltpu.CompilerParams(vmem_limit_bytes=VMEM_LIMIT),
    )(*ins)


def sds(shape, dtype):
    return jax.ShapeDtypeStruct(shape, dtype)


def pick(total, options):
    for o in options:
        if total % o == 0:
            return o
    return total


CONV_W, CONV_B, DT_B, SKIP, A_LOG = 0, 4, 5, 6, 8


class Sizes:
    def __init__(self, tokens, in_proj, dt_proj, x_proj, a_log, up_proj, exp_count):
        self.T = tokens.shape[1]
        self.D = tokens.shape[2]
        self.DI = in_proj.shape[1] // 2
        self.N = a_log.shape[0]
        self.R = dt_proj.shape[0]
        self.XW = x_proj.shape[1]
        self.FF = up_proj.shape[2]
        self.E = exp_count
        self.CAP = 2 * self.T // exp_count
        self.J = self.T // SUB
        self.DT0 = A_LOG + self.N
        self.X0 = self.DT0 + self.R
        self.SMALL = self.X0 + self.XW


def front(z, tokens, halo, masks, gpack, w_conv, w_gate, small):
    T, D, DI, J = z.T, z.D, z.DI, z.J
    H = halo.shape[0]
    cb = pick(DI, (384, 256, 128))
    steps = DI // cb

    def body(tok, hal, msk, gp, wc, wg, sm, normed_o, conv_o, hconv_o, gate_o, sig_o, mixed_o, nrm):
        i = pl.program_id(0)

        @pl.when(i == 0)
        def _():
            gain = gp[0:1, :]
            t = tok[...].astype(F32)
            nt = (t * rms_scale(t) * gain).astype(BF16)
            h = hal[...].astype(F32)
            nrm[0:T, :] = nt
            nrm[T : T + H, :] = (h * rms_scale(h) * gain).astype(BF16)
            normed_o[...] = nt
            mixed_o[...] = jnp.zeros_like(mixed_o)

        conv = mm(nrm[...], wc[...])
        gate_o[...] = mm(nrm[0:T, :], wg[...])
        main, edge = conv[:T], conv[T:]
        conv_o[...] = main
        hconv_o[...] = edge
        xpad = padded_rows(main, edge, J, cb)
        out = jnp.broadcast_to(sm[CONV_B : CONV_B + 1, :], (T, cb))
        for o in range(4):
            m = jnp.broadcast_to(msk[:, o : o + 1], (T, cb))
            out = out + sm[CONV_W + o : CONV_W + o + 1, :] * xpad[o : o + J].reshape(T, cb) * m
        sig = (out * sigmoid(out)).astype(BF16)
        sig_o[...] = sig
        mixed_o[...] += mm_nt(sig, sm[z.X0 : z.X0 + z.XW, :].astype(BF16))

    col = lambda r: block((r, cb), lambda i: (0, i))
    return call(
        body,
        "front",
        (steps,),
        (tokens, halo, masks, gpack, w_conv, w_gate, small),
        [
            whole(tokens.shape),
            whole(halo.shape),
            whole(masks.shape),
            whole(gpack.shape),
            col(D),
            col(D),
            col(z.SMALL),
        ],
        [
            sds((T, D), BF16),
            sds((T, DI), F32),
            sds((H, DI), F32),
            sds((T, DI), F32),
            sds((T, DI), BF16),
            sds((T, z.XW), F32),
        ],
        [whole((T, D)), col(T), col(H), col(T), col(T), whole((T, z.XW))],
        [pltpu.VMEM((T + H, D), BF16)],
    )


def expand_columns(z, src, col0, dst):
    def one(j, carry):
        rows = src[pl.ds(pl.multiple_of(j * SUB, SUB), SUB), :]
        for n in range(z.N):
            at = pl.multiple_of((j * z.N + n) * SUB, SUB)
            dst[pl.ds(at, SUB), :] = jnp.broadcast_to(
                rows[:, col0 + n : col0 + n + 1], (SUB, LANES)
            )
        return carry

    lax.fori_loop(0, z.J, one, 0)


def expand_closed(z, masks, dst):
    dst[...] = jnp.broadcast_to((1.0 - masks[:, 2:3]) * CLOSED, (z.T, LANES))


def tile_groups(cb):
    return 2 if cb % (2 * LANES) == 0 else 1


def lane_at(p, tg, k):
    return pl.ds(pl.multiple_of(p * tg * LANES, LANES) + k * LANES, LANES)


def row8(j):
    return pl.ds(pl.multiple_of(j * SUB, SUB), SUB)


def shift_down(v, d):
    rows = lax.broadcasted_iota(jnp.int32, v.shape, 0)
    return jnp.where(rows >= d, pltpu.roll(v, d, 0), 0.0)


def shift_up(v, d):
    rows = lax.broadcasted_iota(jnp.int32, v.shape, 0)
    return jnp.where(rows < SUB - d, pltpu.roll(v, SUB - d, 0), 0.0)


def summary(z, mixed, sig, masks, small):
    T, DI, N, J = z.T, z.DI, z.N, z.J
    cb = pick(DI, (768, 384, 256, 128))
    tg = tile_groups(cb)
    ng = 8

    def body(mix, sg, msk, sm, dt_o, pre_o, hdev_o, stot_o, dwin_o, bx, cl, u_s, hd, rates_s):
        i = pl.program_id(0)

        @pl.when(i == 0)
        def _():
            expand_columns(z, mix, z.R, bx)
            expand_closed(z, msk, cl)

        low = mix[:, 0 : z.R].astype(BF16)
        pre = mm(low, sm[z.DT0 : z.DT0 + z.R, :].astype(BF16)) + sm[DT_B : DT_B + 1, :]
        step = softplus(pre)
        dt_o[...] = step
        u_s[...] = step * sg[...].astype(F32)
        rates_s[...] = -jnp.exp(sm[A_LOG : A_LOG + N, :]) * LOG2E

        def pair(p, carry):
            totals = []
            for k in range(tg):
                tot = jnp.zeros((SUB, LANES), F32)
                for j in range(J):
                    tot = tot + (dt_o[j * SUB : j * SUB + SUB, lane_at(p, tg, k)] + cl[j * SUB : j * SUB + SUB, :])
                totals.append(tot)
            wins = []
            for k in range(tg):
                w1 = totals[k]
                w2 = w1 + shift_down(w1, 1)
                w4 = w2 + shift_down(w2, 2)
                w8 = w4 + shift_down(w4, 4)
                wins.append((w1, w2, w4))
                dwin_o[0:SUB, lane_at(p, tg, k)] = w1
                dwin_o[SUB : 2 * SUB, lane_at(p, tg, k)] = shift_down(w8, 1)
                stot_o[:, lane_at(p, tg, k)] = w8[SUB - 1 : SUB, :]
            for g in range(0, N, ng):
                rr = [
                    [
                        jnp.broadcast_to(rates_s[g + n : g + n + 1, lane_at(p, tg, k)], (SUB, LANES))
                        for k in range(tg)
                    ]
                    for n in range(ng)
                ]

                def step_j(j, hs):
                    dts = [dt_o[row8(j), lane_at(p, tg, k)] + cl[row8(j), :] for k in range(tg)]
                    us = [u_s[row8(j), lane_at(p, tg, k)] for k in range(tg)]
                    new = []
                    for n in range(ng):
                        b = bx[row8(j * N + g + n), :]
                        for k in range(tg):
                            new.append(
                                jnp.exp2(dts[k] * rr[n][k]) * hs[n * tg + k] + us[k] * b
                            )
                    return tuple(new)

                hs = lax.fori_loop(
                    0, J, step_j, tuple(jnp.zeros((SUB, LANES), F32) for _ in range(ng * tg)), unroll=2
                )
                for n in range(ng):
                    for k in range(tg):
                        h = hs[n * tg + k]
                        w1, w2, w4 = wins[k]
                        r = rr[n][k]
                        h = h + jnp.exp2(r * w1) * shift_down(h, 1)
                        h = h + jnp.exp2(r * w2) * shift_down(h, 2)
                        h = h + jnp.exp2(r * w4) * shift_down(h, 4)
                        at = (g + n) * SUB
                        pre_o[at : at + SUB, lane_at(p, tg, k)] = shift_down(h, 1)
                        hd[g + n : g + n + 1, lane_at(p, tg, k)] = h[SUB - 1 : SUB, :]
            return carry

        lax.fori_loop(0, cb // (tg * LANES), pair, 0)
        hdev_o[...] = hd[...].astype(BF16)

    col = lambda r: block((r, cb), lambda i: (0, i))
    return call(
        body,
        "summary",
        (DI // cb,),
        (mixed, sig, masks, small),
        [whole(mixed.shape), col(T), whole(masks.shape), col(z.SMALL)],
        [
            sds((T, DI), F32),
            sds((N * SUB, DI), F32),
            sds((N, DI), BF16),
            sds((1, DI), F32),
            sds((2 * SUB, DI), F32),
        ],
        [col(T), col(N * SUB), col(N), col(1), col(2 * SUB)],
        [
            pltpu.VMEM((J * N * SUB, LANES), F32),
            pltpu.VMEM((T, LANES), F32),
            pltpu.VMEM((T, cb), F32),
            pltpu.VMEM((N, cb), F32),
            pltpu.VMEM((N, cb), F32),
        ],
    )


def chain_states(count, mine, order, sums, heads, rates2):
    state = jnp.zeros_like(rates2)
    for k in range(count):
        at = order(k)
        new = jnp.exp2(rates2 * sums(at)) * state + heads(at).astype(F32)
        state = jnp.where(mine(at), new, state)
    return state


def scan_forward(z, where, mixed, dt, sig, gate, masks, small, pre, dwin, h_all, s_all, w_out,
                 tokens, gpack, router, table):
    T, D, DI, N, J, E = z.T, z.D, z.DI, z.N, z.J, z.E
    cb = pick(DI, (768, 384, 256, 128))
    tg = tile_groups(cb)
    ng = 8
    S = h_all.shape[0]
    slots = table.shape[1]
    steps = DI // cb

    def body(wh, mix, dt_r, sg, gt, msk, sm, pr, dw, ha, sa, wo, tok, gp, rt, tb,
             st_o, y_o, mid_o, moe_o, ch_o, out_o, bx, cx, cl, u_s, rates_s, hin, acc):
        i = pl.program_id(0)

        @pl.when(i == 0)
        def _():
            expand_columns(z, mix, z.R, bx)
            expand_columns(z, mix, z.R + N, cx)
            expand_closed(z, msk, cl)
            acc[...] = jnp.zeros_like(acc)

        me = wh[0]
        rates2 = -jnp.exp(sm[A_LOG : A_LOG + N, :]) * LOG2E
        rates_s[...] = rates2
        hin[...] = chain_states(
            S - 1, lambda k: k < me, lambda k: k, lambda k: sa[k], lambda k: ha[k], rates2
        )
        u_s[...] = dt_r[...] * sg[...].astype(F32)

        def pair(p, carry):
            lanes = [lane_at(p, tg, k) for k in range(tg)]
            for g in range(0, N, ng):
                rr = [
                    [jnp.broadcast_to(rates_s[g + n : g + n + 1, lanes[k]], (SUB, LANES)) for k in range(tg)]
                    for n in range(ng)
                ]
                init = []
                for n in range(ng):
                    for k in range(tg):
                        at = (g + n) * SUB
                        init.append(
                            pr[at : at + SUB, lanes[k]]
                            + jnp.exp2(rr[n][k] * dw[SUB : 2 * SUB, lanes[k]])
                            * jnp.broadcast_to(hin[g + n : g + n + 1, lanes[k]], (SUB, LANES))
                        )

                def keep(j, hs):
                    for n in range(0, ng, 2):
                        for k in range(tg):
                            two = jnp.concatenate([hs[n * tg + k], hs[(n + 1) * tg + k]], axis=0)
                            at = pl.multiple_of(j * N * SUB + (g + n) * SUB, 2 * SUB)
                            st_o[pl.ds(at, 2 * SUB), lanes[k]] = two.astype(BF16)

                keep(0, init)

                def step_j(j, hs):
                    dts = [dt_r[row8(j), lanes[k]] + cl[row8(j), :] for k in range(tg)]
                    us = [u_s[row8(j), lanes[k]] for k in range(tg)]
                    if g == 0:
                        ys = [jnp.zeros((SUB, LANES), F32) for k in range(tg)]
                    else:
                        ys = [y_o[row8(j), lanes[k]] for k in range(tg)]
                    new = []
                    for n in range(ng):
                        b = bx[row8(j * N + g + n), :]
                        c = cx[row8(j * N + g + n), :]
                        for k in range(tg):
                            h = jnp.exp2(dts[k] * rr[n][k]) * hs[n * tg + k] + us[k] * b
                            ys[k] = ys[k] + h * c
                            new.append(h)
                    for k in range(tg):
                        y_o[row8(j), lanes[k]] = ys[k]
                    keep(j + 1, new)
                    return tuple(new)

                lax.fori_loop(0, J, step_j, tuple(init), unroll=2)
            return carry

        lax.fori_loop(0, cb // (tg * LANES), pair, 0)
        y = y_o[...] + sm[SKIP : SKIP + 1, :] * sg[...].astype(F32)
        y_o[...] = y
        g_in = gt[...]
        gated = (y * (g_in * sigmoid(g_in))).astype(BF16)
        acc[...] += mm(gated, wo[...])

        @pl.when(i == steps - 1)
        def _():
            mid = tok[...].astype(F32) + acc[...]
            mid_o[...] = mid
            moe = (mid * rms_scale(mid) * gp[1:2, :]).astype(BF16)
            moe_o[...] = moe
            logits = mm_nt(moe, rt[...])
            ch_o[...] = router_softmax(logits, E)
            out_o[...] = mm_tn(tb[...], moe).astype(BF16)

    col = lambda r: block((r, cb), lambda i: (0, i))
    return call(
        body,
        "scan_forward",
        (steps,),
        (where, mixed, dt, sig, gate, masks, small, pre, dwin, h_all, s_all, w_out, tokens, gpack, router, table),
        [
            pl.BlockSpec(memory_space=pltpu.SMEM),
            whole(mixed.shape),
            col(T),
            col(T),
            col(T),
            whole(masks.shape),
            col(z.SMALL),
            col(N * SUB),
            col(2 * SUB),
            block((S, N, cb), lambda i: (0, 0, i)),
            block((S, 1, cb), lambda i: (0, 0, i)),
            block((cb, D), lambda i: (i, 0)),
            whole(tokens.shape),
            whole(gpack.shape),
            whole(router.shape),
            whole(table.shape),
        ],
        [
            sds(((J + 1) * N * SUB, DI), BF16),
            sds((T, DI), F32),
            sds((T, D), F32),
            sds((T, D), BF16),
            sds((T, LANES), F32),
            sds((slots, D), BF16),
        ],
        [
            col((J + 1) * N * SUB),
            col(T),
            whole((T, D)),
            whole((T, D)),
            whole((T, LANES)),
            whole((slots, D)),
        ],
        [
            pltpu.VMEM((J * N * SUB, LANES), F32),
            pltpu.VMEM((J * N * SUB, LANES), F32),
            pltpu.VMEM((T, LANES), F32),
            pltpu.VMEM((T, cb), F32),
            pltpu.VMEM((N, cb), F32),
            pltpu.VMEM((N, cb), F32),
            pltpu.VMEM((T, D), F32),
        ],
    )


def router_softmax(logits, experts):
    lane = lax.broadcasted_iota(jnp.int32, logits.shape, 1)
    logits = jnp.where(lane < experts, logits, -1e30)
    top = jnp.max(logits, axis=-1, keepdims=True)
    e = jnp.where(lane < experts, jnp.exp(logits - top), 0.0)
    return e / jnp.sum(e, axis=-1, keepdims=True)


def expert(z, where, x, cot, router, up, down):
    D, FF, E = z.D, z.FF, z.E
    M = x.shape[0]
    fb = pick(FF, (512, 256, 128))
    steps = FF // fb

    def body(wh, x_r, c_r, rt, up_r, dn_r, ret_o, gg_o, dwu_o, dwd_o, g_s, out_s, dx_s):
        i = pl.program_id(0)

        @pl.when(i == 0)
        def _():
            ch = router_softmax(mm_nt(x_r[...], rt[...]), E)
            lane = lax.broadcasted_iota(jnp.int32, ch.shape, 1)
            gating = jnp.sum(jnp.where(lane == wh[1], ch, 0.0), axis=-1, keepdims=True)
            g_s[...] = (gating * c_r[...].astype(F32)).astype(BF16)
            out_s[...] = jnp.zeros_like(out_s)
            dx_s[...] = jnp.zeros_like(dx_s)

        xv, gv = x_r[...], g_s[...]
        upv, dnv = up_r[...], dn_r[...]
        pre = mm(xv, upv)
        cdf = 0.5 * (1.0 + lax.erf(pre * (2.0 ** -0.5)))
        hidden = (pre * cdf).astype(BF16)
        slope = cdf + pre * jnp.exp(-0.5 * pre * pre) * (1.0 / math.sqrt(2.0 * math.pi))
        out_s[...] += mm(hidden, dnv)
        pg = (mm_nt(gv, dnv) * slope).astype(BF16)
        dx_s[...] += mm_nt(pg, upv)
        dwd_o[...] = mm_tn(hidden, gv).astype(BF16)
        dwu_o[...] = mm_tn(xv, pg).astype(BF16)

        @pl.when(i == steps - 1)
        def _():
            out = out_s[...].astype(BF16)
            ret_o[0] = out
            ret_o[1] = dx_s[...].astype(BF16)
            gg_o[...] = jnp.broadcast_to(
                jnp.sum(out.astype(F32) * c_r[...].astype(F32), axis=-1, keepdims=True), gg_o.shape
            )

    return call(
        body,
        "expert",
        (steps,),
        (where, x, cot, router, up, down),
        [
            pl.BlockSpec(memory_space=pltpu.SMEM),
            whole(x.shape),
            whole(cot.shape),
            whole(router.shape),
            block((D, fb), lambda i: (0, i)),
            block((fb, D), lambda i: (i, 0)),
        ],
        [
            sds((2, M, D), BF16),
            sds((M, LANES), F32),
            sds((D, FF), BF16),
            sds((FF, D), BF16),
        ],
        [
            whole((2, M, D)),
            whole((M, LANES)),
            block((D, fb), lambda i: (0, i)),
            block((fb, D), lambda i: (i, 0)),
        ],
        [pltpu.VMEM((M, D), BF16), pltpu.VMEM((M, D), F32), pltpu.VMEM((M, D), F32)],
    )


def middle(z, ret_out, ret_dx, table, choose, chances, mid, moe, cot, gpack, router, gate, y, sig,
           small, w_out, mixed, dt, masks, normed):
    T, D, DI, N, J, E = z.T, z.D, z.DI, z.N, z.J, z.E
    cb = pick(DI, (384, 256, 128))
    tg = 1 if cb % 256 else 2
    tg = 3 if cb == 384 else tg
    ng = 4
    steps = DI // cb
    G = gpack.shape[0]

    def body(ro, rd, tb, cho, chn, md, me_r, ct, gp, rt, gt, yr, sg, sm, wo, mix, dt_r, msk, nm,
             out_o, mg_o, gg_o, yg_o, gi_o, dwo_o, dwg_o, fdev_o, suf_o, skip_o,
             cx, cl, rates_s, br, fd):
        i = pl.program_id(0)

        @pl.when(i == 0)
        def _():
            expand_columns(z, mix, z.R + N, cx)
            expand_closed(z, msk, cl)
            tbv = tb[...]
            eo = mm(tbv, ro[...])
            grad = ct[...].astype(F32)
            ch = chn[...]
            pick_e = cho[...]
            gating = jnp.sum(ch * pick_e, axis=-1, keepdims=True)
            out_o[...] = (md[...] + gating * eo).astype(BF16)
            gate_grad = jnp.sum(grad * eo, axis=-1, keepdims=True)
            lg = ch * (gate_grad * pick_e - gate_grad * gating)
            hi, lo = split_hi_lo(lg)
            rtv = rt[...]
            mig = mm(tbv, rd[...]) + mm(hi, rtv) + mm(lo, rtv)
            mev = me_r[...]
            rg = mm_tn(hi, mev) + mm_tn(lo, mev)
            d, gain_g = rms_back(md[...], gp[1:2, :], mig)
            total = grad + d
            mg_o[...] = total
            br[...] = total.astype(BF16)
            gg_o[...] = jnp.zeros_like(gg_o)
            gg_o[1:2, :] = gain_g
            gg_o[2 : 2 + E, :] = rg[0:E, :]

        gg = mm_nt(br[...], wo[...])
        g_in = gt[...]
        s = sigmoid(g_in)
        act = g_in * s
        yv = yr[...]
        yg = gg * act
        yg_o[...] = yg
        gi = (gg * yv * (s * (1.0 + g_in * (1.0 - s)))).astype(BF16)
        gi_o[...] = gi
        gated = (yv * act).astype(BF16)
        dwo_o[...] = mm_tn(gated, br[...]).astype(BF16)
        dwg_o[...] = mm_tn(nm[...], gi).astype(BF16)
        skip_o[...] = jnp.sum(yg * sg[...].astype(F32), axis=0, keepdims=True)
        rates_s[...] = -jnp.exp(sm[A_LOG : A_LOG + N, :]) * LOG2E

        lanes = [slice(k * LANES, (k + 1) * LANES) for k in range(tg)]
        for p in range(cb // (tg * LANES)):
            wins = []
            for k in range(tg):
                tot = jnp.zeros((SUB, LANES), F32)
                for j in range(J):
                    tot = tot + (dt_r[j * SUB : j * SUB + SUB, lanes[k]] + cl[j * SUB : j * SUB + SUB, :])
                w1 = tot
                w2 = w1 + shift_up(w1, 1)
                w4 = w2 + shift_up(w2, 2)
                w8 = w4 + shift_up(w4, 4)
                wins.append((w1, w2, w4))
                suf_o[N * SUB : (N + 1) * SUB, lanes[k]] = shift_up(w8, 1)
            for g in range(0, N, ng):
                rr = [
                    [jnp.broadcast_to(rates_s[g + n : g + n + 1, lanes[k]], (SUB, LANES)) for k in range(tg)]
                    for n in range(ng)
                ]

                def step_j(jj, fs):
                    j = J - 1 - jj
                    dts = [dt_r[row8(j), lanes[k]] + cl[row8(j), :] for k in range(tg)]
                    ygs = [yg_o[row8(j), lanes[k]] for k in range(tg)]
                    new = []
                    for n in range(ng):
                        c = cx[row8(j * N + g + n), :]
                        for k in range(tg):
                            new.append(
                                jnp.exp2(dts[k] * rr[n][k]) * (fs[n * tg + k] + ygs[k] * c)
                            )
                    return tuple(new)

                fs = lax.fori_loop(
                    0, J, step_j, tuple(jnp.zeros((SUB, LANES), F32) for _ in range(ng * tg)), unroll=2
                )
                for n in range(ng):
                    for k in range(tg):
                        f = fs[n * tg + k]
                        w1, w2, w4 = wins[k]
                        r = rr[n][k]
                        f = f + jnp.exp2(r * w1) * shift_up(f, 1)
                        f = f + jnp.exp2(r * w2) * shift_up(f, 2)
                        f = f + jnp.exp2(r * w4) * shift_up(f, 4)
                        at = (g + n) * SUB
                        suf_o[at : at + SUB, lanes[k]] = shift_up(f, 1)
                        fd[g + n : g + n + 1, lanes[k]] = f[0:1, :]
        fdev_o[...] = fd[...].astype(BF16)

    assert cb == tg * LANES
    col = lambda r: block((r, cb), lambda i: (0, i))
    row = lambda c: block((cb, c), lambda i: (i, 0))
    return call(
        body,
        "middle",
        (steps,),
        (ret_out, ret_dx, table, choose, chances, mid, moe, cot, gpack, router, gate, y, sig, small,
         w_out, mixed, dt, masks, normed),
        [
            whole(ret_out.shape),
            whole(ret_dx.shape),
            whole(table.shape),
            whole(choose.shape),
            whole(chances.shape),
            whole(mid.shape),
            whole(moe.shape),
            whole(cot.shape),
            whole(gpack.shape),
            whole(router.shape),
            col(T),
            col(T),
            col(T),
            col(z.SMALL),
            row(D),
            whole(mixed.shape),
            col(T),
            whole(masks.shape),
            whole(normed.shape),
        ],
        [
            sds((T, D), BF16),
            sds((T, D), F32),
            sds((G, D), F32),
            sds((T, DI), F32),
            sds((T, DI), BF16),
            sds((DI, D), BF16),
            sds((D, DI), BF16),
            sds((N, DI), BF16),
            sds(((N + 1) * SUB, DI), F32),
            sds((1, DI), F32),
        ],
        [
            whole((T, D)),
            whole((T, D)),
            whole((G, D)),
            col(T),
            col(T),
            row(D),
            col(D),
            col(N),
            col((N + 1) * SUB),
            col(1),
        ],
        [
            pltpu.VMEM((J * N * SUB, LANES), F32),
            pltpu.VMEM((T, LANES), F32),
            pltpu.VMEM((N, cb), F32),
            pltpu.VMEM((T, D), BF16),
            pltpu.VMEM((N, cb), F32),
        ],
    )


def scan_backward(z, where, mixed, dt, sig, yg, masks, small, suf, f_all, s_all, states):
    T, DI, N, J = z.T, z.DI, z.N, z.J
    cb = pick(DI, (768, 384, 256, 128))
    tg = tile_groups(cb)
    ng = 4
    S = f_all.shape[0]
    steps = DI // cb

    def body(wh, mix, dt_r, sg, yr, msk, sm, sf, fa, sa, st, ssg_o, dpl_o, mg_o, gs_o,
             bx, cx, cl, u_s, rates_s, fin, dg_s, rs_s, ia, oa, rt_s, low_s):
        i = pl.program_id(0)

        @pl.when(i == 0)
        def _():
            expand_columns(z, mix, z.R, bx)
            expand_columns(z, mix, z.R + N, cx)
            expand_closed(z, msk, cl)
            ia[...] = jnp.zeros_like(ia)
            oa[...] = jnp.zeros_like(oa)
            low_s[...] = jnp.zeros_like(low_s)

        me = wh[0]
        rates2 = -jnp.exp(sm[A_LOG : A_LOG + N, :]) * LOG2E
        rates_s[...] = rates2
        fin[...] = chain_states(
            S - 1, lambda k: k > me, lambda k: S - 1 - k, lambda k: sa[k], lambda k: fa[k], rates2
        )
        sigf = sg[...].astype(F32)
        u_s[...] = dt_r[...] * sigf

        def pair(p, carry):
            lanes = [lane_at(p, tg, k) for k in range(tg)]
            for g in range(0, N, ng):
                rr = [
                    [jnp.broadcast_to(rates_s[g + n : g + n + 1, lanes[k]], (SUB, LANES)) for k in range(tg)]
                    for n in range(ng)
                ]
                flow = []
                for n in range(ng):
                    for k in range(tg):
                        at = (g + n) * SUB
                        flow.append(
                            sf[at : at + SUB, lanes[k]]
                            + jnp.exp2(rr[n][k] * sf[N * SUB : (N + 1) * SUB, lanes[k]])
                            * jnp.broadcast_to(fin[g + n : g + n + 1, lanes[k]], (SUB, LANES))
                        )

                def load(j):
                    got = [[None] * tg for _ in range(ng)]
                    for n in range(0, ng, 2):
                        for k in range(tg):
                            at = pl.multiple_of(j * N * SUB + (g + n) * SUB, 2 * SUB)
                            two = st[pl.ds(at, 2 * SUB), lanes[k]].astype(F32)
                            got[n][k] = two[0:SUB]
                            got[n + 1][k] = two[SUB : 2 * SUB]
                    return [got[n][k] for n in range(ng) for k in range(tg)]

                def step_j(jj, carry):
                    fs, hs, rts = carry
                    j = J - 1 - jj
                    dtp = [dt_r[row8(j), lanes[k]] for k in range(tg)]
                    dts = [dtp[k] + cl[row8(j), :] for k in range(tg)]
                    us = [u_s[row8(j), lanes[k]] for k in range(tg)]
                    ygs = [yr[row8(j), lanes[k]] for k in range(tg)]
                    before = load(j)
                    if g == 0:
                        dgs = [jnp.zeros((SUB, LANES), F32) for k in range(tg)]
                        rss = [jnp.zeros((SUB, LANES), F32) for k in range(tg)]
                    else:
                        dgs = [dg_s[row8(j), lanes[k]] for k in range(tg)]
                        rss = [rs_s[row8(j), lanes[k]] for k in range(tg)]
                    nf, nr = [], []
                    for n in range(ng):
                        at = row8(j * N + g + n)
                        b = bx[at, :]
                        c = cx[at, :]
                        ig = jnp.zeros((SUB, LANES), F32)
                        og = jnp.zeros((SUB, LANES), F32)
                        for k in range(tg):
                            q = n * tg + k
                            grad = ygs[k] * c + fs[q]
                            f = jnp.exp2(dts[k] * rr[n][k]) * grad
                            rt = f * before[q]
                            rss[k] = rss[k] + rt * rr[n][k]
                            dgs[k] = dgs[k] + grad * b
                            nr.append(rts[q] + rt * dtp[k])
                            ig = ig + grad * us[k]
                            og = og + hs[q] * ygs[k]
                            nf.append(f)
                        ia[at, :] += ig
                        oa[at, :] += og
                    for k in range(tg):
                        dg_s[row8(j), lanes[k]] = dgs[k]
                        rs_s[row8(j), lanes[k]] = rss[k]
                    return tuple(nf), tuple(before), tuple(nr)

                zero = tuple(jnp.zeros((SUB, LANES), F32) for _ in range(ng * tg))
                _, _, rts = lax.fori_loop(
                    0, J, step_j, (tuple(flow), tuple(load(J)), zero), unroll=2
                )
                for n in range(ng):
                    for k in range(tg):
                        rt_s[g + n : g + n + 1, lanes[k]] = jnp.sum(rts[n * tg + k], axis=0, keepdims=True)
            return carry

        lax.fori_loop(0, cb // (tg * LANES), pair, 0)
        dg = dg_s[...]
        ssg_o[...] = dg * dt_r[...] + yr[...] * sm[SKIP : SKIP + 1, :]
        step_grad = rs_s[...] * LN2 + dg * sigf
        low = mix[:, 0 : z.R].astype(BF16)
        dtw = sm[z.DT0 : z.DT0 + z.R, :].astype(BF16)
        pre = mm(low, dtw) + sm[DT_B : DT_B + 1, :]
        dpg = step_grad * sigmoid(pre)
        dpl = dpg.astype(BF16)
        dpl_o[...] = dpl
        gs_o[...] = jnp.zeros_like(gs_o)
        gs_o[DT_B : DT_B + 1, :] = jnp.sum(dpg, axis=0, keepdims=True)
        gs_o[A_LOG : A_LOG + N, :] = rt_s[...] * (rates2 * LN2)
        gs_o[z.DT0 : z.DT0 + z.R, :] = mm_tn(low, dpl)
        low_s[...] += mm_nt(dpl, dtw)

        @pl.when(i == steps - 1)
        def _():
            mg_o[:, 0 : z.R] = low_s[...].astype(BF16)
            lane = lax.broadcasted_iota(jnp.int32, (SUB, LANES), 1)

            def gather(j, carry):
                both = jnp.zeros((SUB, LANES), F32)
                for n in range(N):
                    at = row8(j * N + n)
                    both = jnp.where(lane == n, jnp.sum(ia[at, :], axis=1, keepdims=True), both)
                    both = jnp.where(lane == N + n, jnp.sum(oa[at, :], axis=1, keepdims=True), both)
                cl[row8(j), :] = both
                return carry

            lax.fori_loop(0, J, gather, 0)
            mg_o[:, z.R : z.R + 2 * N] = cl[:, 0 : 2 * N].astype(BF16)

    col = lambda r: block((r, cb), lambda i: (0, i))
    wide = lambda: pltpu.VMEM((J * N * SUB, LANES), F32)
    return call(
        body,
        "scan_backward",
        (steps,),
        (where, mixed, dt, sig, yg, masks, small, suf, f_all, s_all, states),
        [
            pl.BlockSpec(memory_space=pltpu.SMEM),
            whole(mixed.shape),
            col(T),
            col(T),
            col(T),
            whole(masks.shape),
            col(z.SMALL),
            col((N + 1) * SUB),
            block((S, N, cb), lambda i: (0, 0, i)),
            block((S, 1, cb), lambda i: (0, 0, i)),
            col((J + 1) * N * SUB),
        ],
        [sds((T, DI), F32), sds((T, DI), BF16), sds((T, z.XW), BF16), sds((z.X0, DI), F32)],
        [col(T), col(T), whole((T, z.XW)), col(z.X0)],
        [
            wide(),
            wide(),
            pltpu.VMEM((T, LANES), F32),
            pltpu.VMEM((T, cb), F32),
            pltpu.VMEM((N, cb), F32),
            pltpu.VMEM((N, cb), F32),
            pltpu.VMEM((T, cb), F32),
            pltpu.VMEM((T, cb), F32),
            wide(),
            wide(),
            pltpu.VMEM((N, cb), F32),
            pltpu.VMEM((T, z.R), F32),
        ],
    )


def padded_rows(main, edge, J, cb):
    H = edge.shape[0]
    m3 = main.reshape(J, SUB, cb)
    first = lax.broadcasted_iota(jnp.int32, (SUB, cb), 0) == 0
    tail = jnp.stack(
        [
            jnp.where(
                first,
                jnp.broadcast_to(edge[H - 3 + k : H - 2 + k, :], (SUB, cb)),
                pltpu.roll(m3[J - 3 + k], 1, 0),
            )
            for k in range(3)
        ]
    )
    return jnp.concatenate([tail, m3], axis=0)


def conv_backward(z, mixed_grad, sig, ssg, conv_in, hconv, masks, small, skip):
    T, DI, J = z.T, z.DI, z.J
    H = hconv.shape[0]
    cb = pick(DI, (384, 256, 128))
    steps = DI // cb

    def body(mg, sg, ss, ci, hc, msk, sm, sk, cig_o, edge_o, gt_o, gx_o):
        mgv = mg[...]
        sgv = sg[...]
        xw = sm[z.X0 : z.X0 + z.XW, :].astype(BF16)
        gx_o[...] = mm_tn(mgv, sgv)
        sgrad = ss[...] + mm(mgv, xw)
        xpad = padded_rows(ci[...], hc[...], J, cb)
        valid = [jnp.broadcast_to(msk[:, o : o + 1], (T, cb)) for o in range(4)]
        out = jnp.broadcast_to(sm[CONV_B : CONV_B + 1, :], (T, cb))
        for o in range(4):
            out = out + sm[CONV_W + o : CONV_W + o + 1, :] * xpad[o : o + J].reshape(T, cb) * valid[o]
        s = sigmoid(out)
        cg = sgrad * (s * (1.0 + out * (1.0 - s)))
        gt_o[CONV_B : CONV_B + 1, :] = jnp.sum(cg, axis=0, keepdims=True)
        gt_o[DT_B : DT_B + 1, :] = jnp.zeros((1, cb), F32)
        gt_o[SKIP : SKIP + 1, :] = sk[...]
        gt_o[SKIP + 1 : SKIP + 2, :] = jnp.zeros((1, cb), F32)
        total = jnp.zeros((J, SUB, cb), F32)
        last = lax.broadcasted_iota(jnp.int32, (SUB, cb), 0) == SUB - 1
        edges = [jnp.zeros((1, cb), F32) for _ in range(3)]
        for o in range(4):
            masked = cg * valid[o]
            gt_o[CONV_W + o : CONV_W + o + 1, :] = jnp.sum(
                masked * xpad[o : o + J].reshape(T, cb), axis=0, keepdims=True
            )
            c3 = (sm[CONV_W + o : CONV_W + o + 1, :] * masked).reshape(J, SUB, cb)
            k = 3 - o
            if k == 0:
                total = total + c3
            else:
                wrap = jnp.stack(
                    [jnp.where(last, 0.0, pltpu.roll(c3[t], SUB - 1, 0)) for t in range(k)]
                )
                total = total + jnp.concatenate([c3[k:], wrap], axis=0)
                for i in range(o, 3):
                    edges[i] = edges[i] + c3[i - o, 0:1, :]
        cig_o[...] = total.reshape(T, cb)
        edge_o[...] = jnp.zeros_like(edge_o)
        for i in range(3):
            edge_o[i : i + 1, :] = edges[i]

    col = lambda r: block((r, cb), lambda i: (0, i))
    return call(
        body,
        "conv_backward",
        (steps,),
        (mixed_grad, sig, ssg, conv_in, hconv, masks, small, skip),
        [
            whole(mixed_grad.shape),
            col(T),
            col(T),
            col(T),
            col(H),
            whole(masks.shape),
            col(z.SMALL),
            col(1),
        ],
        [sds((T, DI), F32), sds((SUB, DI), F32), sds((SUB, DI), F32), sds((z.XW, DI), F32)],
        [col(T), col(SUB), col(SUB), col(z.XW)],
        [],
    )


def last(z, cig, edge, gate_grad, normed, w_conv, w_gate, tokens, mid_grad, gpack, ggrad):
    T, D, DI, J = z.T, z.D, z.DI, z.J
    cb = pick(DI, (384, 256, 128))
    steps = DI // cb
    G = gpack.shape[0]

    def body(cg, eg, gg, nm, wc, wg, tok, mg, gp, gpre, dw_o, tg_o, gn_o, acc):
        i = pl.program_id(0)

        @pl.when(i == 0)
        def _():
            acc[...] = jnp.zeros_like(acc)

        c3 = cg[...].reshape(J, SUB, cb)
        is_last = lax.broadcasted_iota(jnp.int32, (SUB, cb), 0) == SUB - 1
        fixed = jnp.stack(
            [
                c3[J - 3 + k]
                + jnp.where(is_last, jnp.broadcast_to(eg[k : k + 1, :], (SUB, cb)), 0.0)
                for k in range(3)
            ]
        )
        pc = jnp.concatenate([c3[: J - 3], fixed], axis=0).reshape(T, cb).astype(BF16)
        dw_o[...] = mm_tn(nm[...], pc).astype(BF16)
        acc[...] += mm_nt(pc, wc[...]) + mm_nt(gg[...], wg[...])

        @pl.when(i == steps - 1)
        def _():
            d, gain_g = rms_back(tok[...].astype(F32), gp[0:1, :], acc[...])
            tg_o[...] = mg[...] + d
            gn_o[...] = gpre[...]
            gn_o[0:1, :] = gain_g

    col = lambda r: block((r, cb), lambda i: (0, i))
    return call(
        body,
        "last",
        (steps,),
        (cig, edge, gate_grad, normed, w_conv, w_gate, tokens, mid_grad, gpack, ggrad),
        [
            col(T),
            col(SUB),
            col(T),
            whole(normed.shape),
            col(D),
            col(D),
            whole(tokens.shape),
            whole(mid_grad.shape),
            whole(gpack.shape),
            whole(ggrad.shape),
        ],
        [sds((D, DI), BF16), sds((T, D), F32), sds((G, D), F32)],
        [col(D), whole((T, D)), whole((G, D))],
        [pltpu.VMEM((T, D), F32)],
    )


def to_chunks(a, J):
    return a.reshape((SUB, J) + a.shape[1:]).swapaxes(0, 1).reshape(a.shape)


def from_chunks(a, J):
    return a.reshape((J, SUB) + a.shape[1:]).swapaxes(0, 1).reshape(a.shape)


def from_behind(block_in, axis, distance):
    devices = range(lax.axis_size(axis))
    route = [(i - distance, i) for i in devices if i - distance in devices]
    return lax.ppermute(block_in, axis, route)


def on_device(
    tokens, segment_ids, routes, cotangent, norm_gain, in_proj, conv_weight, conv_bias, x_proj,
    dt_proj, dt_bias, a_log, d_skip, out_proj, moe_gain, router, up_proj, down_proj,
):
    E = lax.axis_size("exp")
    S = lax.axis_size("seq")
    z = Sizes(tokens, in_proj, dt_proj, x_proj, a_log, up_proj, E)
    T, D, DI, N, J, CAP = z.T, z.D, z.DI, z.N, z.J, z.CAP
    me_s, me_e = lax.axis_index("seq"), lax.axis_index("exp")
    where = jnp.stack([me_s, me_e]).astype(jnp.int32)
    halo = from_behind(tokens[0, T - J :], "seq", 1)
    seg = segment_ids[0]
    seg_tail = from_behind(seg[T - 3 :], "seq", 1)

    own = in_proj.shape[1] // 2
    cw = dt_proj.shape[1]
    zero = jnp.zeros((1, cw), BF16)
    small_own = jnp.concatenate(
        [conv_weight, conv_bias[None], dt_bias[None], d_skip[None], zero, a_log, dt_proj, x_proj.T], axis=0
    )
    gr = 8 * -(-(2 + E) // 8)
    g_own = jnp.concatenate(
        [norm_gain[None], moe_gain[None], router.T, jnp.zeros((gr - 2 - E, router.shape[0]), BF16)], axis=0
    )
    w_in = lax.all_gather(in_proj, "exp", axis=0, tiled=True)
    w_out = lax.all_gather(out_proj, "exp", axis=0, tiled=True)
    small = lax.all_gather(small_own, "exp", axis=1, tiled=True).astype(F32)
    gpack_low = lax.all_gather(g_own, "exp", axis=1, tiled=True)
    gpack = gpack_low.astype(F32)
    router_t = jnp.zeros((LANES, D), BF16).at[0:E].set(gpack_low[2 : 2 + E])
    w_conv, w_gate = w_in[:, :DI], w_in[:, DI:]

    padded_seg = jnp.concatenate([seg_tail, seg])
    masks = jnp.stack([(padded_seg[o : o + T] == seg).astype(F32) for o in range(4)] + [seg * 0.0] * 4, axis=1)
    masks = to_chunks(masks, J)
    tok = to_chunks(tokens[0], J)
    cot = to_chunks(cotangent[0], J)
    route = to_chunks(routes[0, :, 0], J)
    choose = route[:, None] == jnp.arange(E)[None, :]
    upto = (jnp.arange(T)[None, :] <= jnp.arange(T)[:, None]).astype(BF16)
    counts = jnp.dot(upto, choose.astype(BF16), preferred_element_type=F32)
    rank = jnp.sum(counts * choose, axis=-1).astype(jnp.int32) - 1
    table = ((route * CAP + rank)[:, None] == jnp.arange(E * CAP)[None, :]).astype(BF16)
    choose_wide = (route[:, None] == jnp.arange(LANES)[None, :]).astype(F32)
    cot_slots = lax.dot_general(table, cot, (((0,), (0,)), ((), ())), preferred_element_type=F32).astype(BF16)

    def trade(a):
        return lax.all_to_all(a.reshape(E, CAP, -1), "exp", split_axis=0, concat_axis=0, tiled=True).reshape(a.shape)

    cot_here = trade(cot_slots)

    normed, conv_in, hconv, gate, sig, mixed = front(z, tok, halo, masks, gpack, w_conv, w_gate, small)
    dt, pre, hdev, stot, dwin = summary(z, mixed, sig, masks, small)
    h_all = lax.all_gather(hdev, "seq")
    s_all = lax.all_gather(stot, "seq")
    states, y, mid, moe, chances, outbound = scan_forward(
        z, where, mixed, dt, sig, gate, masks, small, pre, dwin, h_all, s_all, w_out, tok, gpack, router_t, table
    )
    arrived = trade(outbound)
    ret, _, dwu, dwd = expert(z, where, arrived, cot_here, router_t, up_proj[0], down_proj[0])
    up_part = lax.psum_scatter(dwu, "seq", scatter_dimension=0, tiled=True).astype(F32)
    down_part = lax.psum_scatter(dwd, "seq", scatter_dimension=0, tiled=True).astype(F32)
    ret_dx = trade(ret[1])
    ret_out = trade(ret[0])
    output, mid_grad, ggrad, yg, gate_grad, dw_out, dw_gate, fdev, suf, skip = middle(
        z, ret_out, ret_dx, table, choose_wide, chances, mid, moe, cot, gpack, router_t, gate, y, sig, small,
        w_out, mixed, dt, masks, normed
    )
    f_all = lax.all_gather(fdev, "seq")
    ssg, dpl, mixed_grad, gs = scan_backward(
        z, where, mixed, dt, sig, yg, masks, small, suf, f_all, s_all, states
    )
    cig, edge, gtop, gx = conv_backward(z, mixed_grad, sig, ssg, conv_in, hconv, masks, small, skip)
    edge_in = from_behind(edge, "seq", -1)
    dw_conv, token_grad, ggrad = last(
        z, cig, edge_in, gate_grad, normed, w_conv, w_gate, tok, mid_grad, gpack, ggrad
    )
    gsmall = jnp.concatenate([gtop + gs[0:8], gs[8:], gx], axis=0)

    def reduce_rows(g):
        part = lax.psum_scatter(g, "exp", scatter_dimension=0, tiled=True)
        return lax.psum(part, "seq").astype(F32)

    dw_in = reduce_rows(jnp.concatenate([dw_conv, dw_gate], axis=1))
    dw_out = reduce_rows(dw_out)
    gsmall = lax.psum(gsmall, ("seq", "exp"))
    gsmall = lax.dynamic_slice_in_dim(gsmall, me_e * cw, cw, axis=1)
    ggrad = lax.psum(ggrad, ("seq", "exp"))
    dwid = norm_gain.shape[0]
    ggrad = lax.dynamic_slice_in_dim(ggrad, me_e * dwid, dwid, axis=1)
    return (
        from_chunks(output, J)[None],
        from_chunks(token_grad, J)[None],
        ggrad[0],
        dw_in,
        gsmall[CONV_W : CONV_W + 4],
        gsmall[CONV_B],
        gsmall[z.X0 :].T,
        gsmall[z.DT0 : z.X0],
        gsmall[DT_B],
        gsmall[A_LOG : A_LOG + N],
        gsmall[SKIP],
        dw_out,
        ggrad[1],
        ggrad[2 : 2 + E].T,
        up_part[None],
        down_part[None],
    )


def solution(mesh):
    row = P("exp", "seq", None)
    in_specs = (
        row, P("exp", "seq"), row, row, P("exp"), P("exp", None), P(None, "exp"), P("exp"), P("exp", None),
        P(None, "exp"), P("exp"), P(None, "exp"), P("exp"), P("exp", None), P("exp"), P("exp", None),
        P("exp", None, None), P("exp", None, None),
    )
    out_specs = (
        row, row, P("exp"), P("exp", None), P(None, "exp"), P("exp"), P("exp", None), P(None, "exp"), P("exp"),
        P(None, "exp"), P("exp"), P("exp", None), P("exp"), P("exp", None), row, row,
    )
    return jax.shard_map(on_device, mesh=mesh, in_specs=in_specs, out_specs=out_specs, check_vma=False)
```

time: 3950 us -> 1100 us (0.28)
  local copies, waits for them, and re-layouts: 2070 us -> 34.5 us
  other arithmetic: 825 us -> 24.3 us
  blocking collectives: 731 us -> 185 us
  waiting for transfers between devices: 158 us -> 696 us
  Pallas kernels: 0 us -> 121 us
  matrix products: 91 us -> 1.41 us
    pad x192 -> x0, local copies, waits for them, and re-layouts: 1030 us -> none  [the longest x64 348 us: retreat(): lax.associative_scan(compose, (decays, drives), axis=0)]
    unnamed x2 -> x0, blocking collectives: 573 us -> none
    add x207 -> x2, other arithmetic: 404 us -> 0.03 us  [the longest x1 0.02 us: on_device(): route * CAP + rank]
    slice x123 -> x14, local copies, waits for them, and re-layouts: 419 us -> 18.4 us  [the longest x1 8.94 us: on_device(): w_conv, w_gate = (w_in[:, :DI], w_in[:, DI:])]
    reduce_scatter x2 -> x4, waiting for transfers between devices: 0.01 us -> 339 us  [the longest x2 210 us: reduce_rows(): part = lax.psum_scatter(g, 'exp', scatter_dimension=0, tiled=True)]
    unnamed x220 -> x59, local copies, waits for them, and re-layouts: 299 us -> 5.25 us
    psum x0 -> x2, waiting for transfers between devices: none -> 174 us  [the longest x1 93.8 us: on_device(): gsmall = lax.psum(gsmall, ('seq', 'exp'))]
    reshape x22 -> x1, local copies, waits for them, and re-layouts: 156 us -> 0.09 us  [to_chunks(): return a.reshape((SUB, J) + a.shape[1:]).swapaxes(0, 1).reshape(a.shape)]
  transfers between devices with their start and end apart: 10 -> 13, of which waited for: 4 -> 10; matrix products, arithmetic and copies ran while one was open for 30% -> 4% of each run, Pallas kernels for 0% -> 8%
where the time goes in v1:
time: 1100 us; the launch traced here: 1090 us
  waiting for transfers between devices  696 us (63%)
  blocking collectives  185 us (17%)
  Pallas kernels  121 us (11%)
  local copies, waits for them, and re-layouts  34.5 us (3%)
  other arithmetic  24.3 us (2%)
  starting transfers between devices  15 us (1%)
  between operations  14.7 us (1%)
    reduce_scatter x2, waiting for transfers between devices, reduce_rows(): part = lax.psum_scatter(g, 'exp', scatter_dimension=0, tiled=True)  210 us
    pallas_call x8, Pallas kernels, call(): pl.pallas_call(body, name=name, grid=grid, in_specs=in_specs, out_specs=o...  121 us
    all_gather x1, waiting for transfers between devices, on_device(): w_in = lax.all_gather(in_proj, 'exp', axis=0, tiled=True)  119 us
    psum x1, waiting for transfers between devices, on_device(): gsmall = lax.psum(gsmall, ('seq', 'exp'))  93.8 us
    psum x1, waiting for transfers between devices, reduce_rows(): return lax.psum(part, 'seq').astype(F32)  80.2 us
    reduce_scatter x1, waiting for transfers between devices, on_device(): lax.psum_scatter(dwu, 'seq', scatter_dimension=0, tiled=True).astype(F32)  67 us
    reduce_scatter x1, waiting for transfers between devices, on_device(): lax.psum_scatter(dwd, 'seq', scatter_dimension=0, tiled=True).astype(F32)  62.3 us
    all_gather x1, waiting for transfers between devices, on_device(): w_out = lax.all_gather(out_proj, 'exp', axis=0, tiled=True)  49 us
  transfers between devices with their start and end apart: 13, of which 10 were waited for; matrix products, arithmetic and copies ran while one was open for 4% of the time, Pallas kernels for 8%

profile of v1, /device:TPU:23, one launch (start us, length us, event | category | flops | bytes accessed | tf_op | source)
XLA Modules:
  0.0 1092.1 jit_solution(16351797202305142260)
XLA Ops:
  8.9 1.3 collective-permute-start.1
  10.2 1.3 collective-permute-start
  13.1 1.3 convolution_convert_fusion
  14.4 4.6 all-to-all-start.1
  20.0 32.5 %all-gather.3 = bf16[4,288,8]{1,2,0:T(8,128)(2,1)S(1)} all-gather(bf16[1,288,8]{1,2,0:T(8,128)(2,1)S(1)} %maximum_bitcast_fusion), channel_id=1, replica_groups=mesh['seq'=8,'exp'=4] {'exp'}, dimensions={0}, use_global_device_ids=true | all-gather | bytes 23040 | tf_op jit(solution)/shard_map/all_gather | solution.py:1079
  54.6 40.9 %all-gather.4 = bf16[4,576,200]{1,2,0:T(8,128)(2,1)S(1)} all-gather(bf16[1,576,200]{1,2,0:T(8,128)(2,1)S(1)} %bitcast.100), channel_id=1, replica_groups=mesh['seq'=8,'exp'=4] {'exp'}, dimensions={0}, use_global_device_ids=true | all-gather | bytes 1152000 | tf_op jit(solution)/shard_map/all_gather | solution.py:1078
  95.9 2.5 reshape.201
  101.5 118.8 %all-gather.9.cloned.1.call-done = bf16[1152,4608]{1,0:T(8,128)(2,1)} async-done(((bf16[288,4608]{1,0:T(8,128)(2,1)}), bf16[1152,4608]{1,0:T(8,128)(2,1)}) %all-gather.9.cloned.1.call-update) | async-done | bytes 10616848 | tf_op jit(solution)/shard_map/all_gather | solution.py:1076
  220.3 8.9 fusion.5
  229.8 9.5 front.1
  239.3 10.9 summary.1
  250.2 12.5 %all-gather.5.sa = f32[8,1,2304]{2,1,0:T(1,128)} all-gather(f32[1,1,2304]{2,1,0:T(1,128)} %bitcast.111), channel_id=3, replica_groups=mesh['seq'=8,'exp'=4] {'seq'}, dimensions={0}, use_global_device_ids=true | all-gather | bytes 82944 | tf_op jit(solution)/shard_map/all_gather | solution.py:1106
  262.7 11.0 %all-gather = bf16[128,2304]{1,0:T(8,128)(2,1)} all-gather(bf16[16,2304]{1,0:T(8,128)(2,1)} %get-tuple-element.74), channel_id=2, replica_groups=mesh['seq'=8,'exp'=4] {'seq'}, dimensions={0}, use_global_device_ids=true | all-gather | bytes 663552 | tf_op jit(solution)/shard_map/all_gather | solution.py:1105
  273.7 49.0 %all-gather.11.cloned.1.call-done.wo = bf16[2304,1152]{1,0:T(8,128)(2,1)} async-done(((bf16[576,1152]{1,0:T(8,128)(2,1)}), bf16[2304,1152]{1,0:T(8,128)(2,1)}) %all-gather.11.cloned.1.call-update) | async-done | bytes 5308432 | tf_op jit(solution)/shard_map/all_gather | solution.py:1077
  322.7 18.2 %scan_forward.1 = (bf16[2176,2304]{1,0:T(8,128)(2,1)}, f32[128,2304]{1,0:T(8,128)}, f32[128,1152]{1,0:T(8,128)}, bf16[128,1152]{1,0:T(8,128)(2,1)}, f32[128,128]{1,0:T(8,128)}, /*index=5*/bf16[256,1152]{1,0:T(8,128)(2,1)}) custom-call(s32[2]{0:T(128)} %pad_add_fusion.1.wh, f32[128,104]{1,0:T(8,128)} %get-tuple-element.68.mix, ...), custom_call_target="tpu_custom_call" | custom-call | tf_op jit(solution)/shard_map/scan_forward/pallas_call | solution.py:70
  340.9 19.7 %all_to_all.20 = bf16[4,64,1152]{2,1,0:T(8,128)(2,1)} all-to-all(bf16[4,64,1152]{2,1,0:T(8,128)(2,1)} %bitcast.103), channel_id=1, replica_groups=mesh['seq'=8,'exp'=4] {'exp'}, dimensions={0} | all-to-all | bytes 1179648 | tf_op jit(solution)/shard_map/all_to_all | solution.py:1099
  360.5 19.7 %expert.1 = (bf16[2,256,1152]{2,1,0:T(8,128)(2,1)}, f32[256,128]{1,0:T(8,128)}, bf16[1152,3072]{1,0:T(8,128)(2,1)}, bf16[3072,1152]{1,0:T(8,128)(2,1)}) custom-call(s32[2]{0:T(128)} %pad_add_fusion.1.wh, bf16[256,1152]{1,0:T(8,128)(2,1)} %bitcast.92, bf16[256,1152]{1,0:T(8,128)(2,1)} %bitcast.90, bf16[128,1152]{1,0:T(8,128)(2,1)} %scatter.4.rt, ...), custom_call_target="tpu_custom_call" | custom-call | tf_op jit(solution)/shard_map/expert/pallas_call | solution.py:70
  380.2 2.2 fusion.6
  382.4 18.4 %all_to_all.21 = bf16[4,64,1152]{2,1,0:T(8,128)(2,1)} all-to-all(bf16[4,64,1152]{2,1,0:T(8,128)(2,1)S(1)} %bitcast.93), channel_id=1, replica_groups=mesh['seq'=8,'exp'=4] {'exp'}, dimensions={0} | all-to-all | bytes 1179648 | tf_op jit(solution)/shard_map/all_to_all | solution.py:1099
  400.7 5.5 all-to-all-start.3
  407.7 10.9 %all-to-all-done.3 = bf16[4,64,1152]{2,1,0:T(8,128)(2,1)S(1)} async-done(((bf16[4,64,1152]{2,1,0:T(8,128)(2,1)}), bf16[4,64,1152]{2,1,0:T(8,128)(2,1)S(1)}, u32[]{:S(2)}, u32[]{:S(2)}) %all-to-all-start.3) | async-done | bytes 589856 | tf_op jit(solution)/shard_map/all_to_all | solution.py:1099
  419.4 19.1 %middle.1 = (bf16[128,1152]{1,0:T(8,128)(2,1)}, f32[128,1152]{1,0:T(8,128)}, f32[8,1152]{1,0:T(8,128)}, f32[128,2304]{1,0:T(8,128)}, bf16[128,2304]{1,0:T(8,128)...) custom-call(bf16[256,1152]{1,0:T(8,128)(2,1)} %bitcast.94, ...), custom_call_target="tpu_custom_call" | custom-call | tf_op jit(solution)/shard_map/middle/pallas_call | solution.py:70
  439.4 11.4 %all-gather.2 = bf16[128,2304]{1,0:T(8,128)(2,1)} all-gather(bf16[16,2304]{1,0:T(8,128)(2,1)S(1)} %copy-done.12), channel_id=4, replica_groups=mesh['seq'=8,'exp'=4] {'seq'}, dimensions={0}, use_global_device_ids=true | all-gather | bytes 663552 | tf_op jit(solution)/shard_map/all_gather | solution.py:1120
  450.7 25.9 %scan_backward.1 = (f32[128,2304]{1,0:T(8,128)}, bf16[128,2304]{1,0:T(8,128)(2,1)}, bf16[128,104]{1,0:T(8,128)(2,1)}, f32[96,2304]{1,0:T(8,128)}) custom-call(s32[2]{0:T(128)} %pad_add_fusion.1.wh, f32[128,104]{1,0:T(8,128)} %get-tuple-element.68.mix, f32[128,2304]{1,0:T(8,128)} %get-tuple-element.70.dt_r, bf16[128,2304]{1,0:T(8,128)(2,1)} %get-tuple-element.69.sg, ...), custom_call_target="tpu_custom_call" | custom-call | tf_op jit(solution)/shard_map/scan_backward/pallas_call | solution.py:70
  476.6 6.5 conv_backward.1
  483.2 2.1 collective-permute-start.2
  485.2 1.1 collective-permute-done.2.eg
  487.0 11.7 %last.1 = (bf16[1152,2304]{1,0:T(8,128)(2,1)}, f32[128,1152]{1,0:T(8,128)}, f32[8,1152]{1,0:T(8,128)}) custom-call(f32[128,2304]{1,0:T(8,128)} %get-tuple-element.93.cg, f32[8,2304]{1,0:T(8,128)} %copy-done.13, bf16[128,2304]{1,0:T(8,128)(2,1)} %get-tuple-element.95.gg, bf16[128,1152]{1,0:T(8,128)(2,1)} %get-tuple-element.82.nm, ...), custom_call_target="tpu_custom_call" | custom-call | tf_op jit(solution)/shard_map/last/pallas_call | solution.py:70
  498.7 7.2 pad_maximum_fusion
  506.0 1.1 copy-done.5
  507.4 1.4 pad_maximum_fusion.1
  510.2 26.5 %reduce-scatter.7.cloned.1.call-done = bf16[576,1152]{1,0:T(8,128)(2,1)} async-done(((bf16[2304,1152]{1,0:T(8,128)(2,1)}), bf16[576,1152]{1,0:T(8,128)(2,1)}) %reduce-scatter.7.cloned.1.call-update) | async-done | bytes 1327120 | tf_op jit(solution)/shard_map/reduce_scatter | solution.py:1132
  536.7 183.5 %reduce-scatter.5.cloned.1.call-done = bf16[288,4608]{1,0:T(8,128)(2,1)} async-done(((bf16[1152,4608]{1,0:T(8,128)(2,1)}), bf16[288,4608]{1,0:T(8,128)(2,1)}) %reduce-scatter.5.cloned.1.call-update) | async-done | bytes 2654224 | tf_op jit(solution)/shard_map/reduce_scatter | solution.py:1132
  721.4 0.9 copy.57
  722.3 38.7 %psum.28 = f32[8,1152]{1,0:T(8,128)S(1)} all-reduce(f32[8,1152]{1,0:T(8,128)S(1)} %copy-done.15), channel_id=1, replica_groups=mesh['seq'=8,'exp'=4] {'seq','exp'}, use_global_device_ids=true, to_apply=%region_1.0 | all-reduce | flops 9216 | bytes 73728 | tf_op jit(solution)/shard_map/psum | solution.py:1139
  762.4 93.8 %all-reduce.5.cloned.1.call-done = f32[200,2304]{1,0:T(8,128)} async-done(((f32[200,2304]{1,0:T(8,128)}), f32[200,2304]{1,0:T(8,128)}) %all-reduce.5.cloned.1.call-update) | async-done | bytes 1843216 | tf_op jit(solution)/shard_map/psum | solution.py:1137
  856.2 1.5 dynamic-slice.13
  857.7 1.7 dynamic-slice.11
  859.4 1.6 dynamic-slice_reduce_fusion
  861.0 1.4 constant_dynamic-slice_fusion
  862.4 1.8 dynamic-slice_bitcast_fusion
  864.2 62.3 %reduce-scatter.11.cloned.1.call-done = bf16[384,1152]{1,0:T(8,128)(2,1)} async-done(((bf16[3072,1152]{1,0:T(8,128)(2,1)}), bf16[384,1152]{1,0:T(8,128)(2,1)}) %reduce-scatter.11.cloned.1.call-update) | async-done | bytes 884752 | tf_op jit(solution)/shard_map/reduce_scatter | solution.py:1113
  926.5 2.5 bitcast_convert_fusion
  928.9 67.0 %reduce-scatter.9.cloned.1.call-done = bf16[144,3072]{1,0:T(8,128)(2,1)} async-done(((bf16[1152,3072]{1,0:T(8,128)(2,1)}), bf16[144,3072]{1,0:T(8,128)(2,1)}) %reduce-scatter.9.cloned.1.call-update) | async-done | bytes 884752 | tf_op jit(solution)/shard_map/reduce_scatter | solution.py:1112
  995.9 2.6 bitcast_convert_fusion.1
  998.5 80.2 %all-reduce.7.cloned.1.call-done = (bf16[288,4608]{1,0:T(8,128)(2,1)}, bf16[576,1152]{1,0:T(8,128)(2,1)}) async-done(((bf16[288,4608]{1,0:T(8,128)(2,1)}, bf16[576,1152]{1,0:T(8,128)(2,1)}), (bf16[288,4608]{1,0:T(8,128)(2,1)}, bf16[576,1152]{1,0:T(8,128)(2,1)})) %all-reduce.7.cloned.1.call-update) | async-done | bytes 3981328 | tf_op jit(solution)/shard_map/psum | solution.py:1133
  1078.7 4.9 convert_element_type.81
  1083.5 1.7 convert_element_type.82
  (126 shorter events, 18.2 us)
Async XLA Ops:
  7.2 1.6 copy-start.24
  7.2 3.0 copy-start.7
  7.2 4.8 copy-start.25
  7.2 5.9 copy-start.3
  7.2 213.0 %all-gather.9.cloned.1.call-start = ((), (), s32[]{:S(2)}) async-start(), calls=%async_computation.8 | async-start | bytes 13271040 | tf_op jit(solution)/shard_map/all_gather | solution.py:1076
  8.0 11.7 %copy-start.22 = (bf16[288]{0:T(512)(128)(2,1)S(1)}, bf16[288]{0:T(512)(128)(2,1)}, u32[]{:S(2)}) copy-start(bf16[288]{0:T(512)(128)(2,1)} %param.24) | copy-start | bytes 1732
  8.0 11.7 %copy-start.23 = (bf16[288]{0:T(512)(128)(2,1)S(1)}, bf16[288]{0:T(512)(128)(2,1)}, u32[]{:S(2)}) copy-start(bf16[288]{0:T(512)(128)(2,1)} %param.34) | copy-start | bytes 1732
  8.0 11.8 %copy-start.19 = (bf16[576]{0:T(1024)(128)(2,1)S(1)}, bf16[576]{0:T(1024)(128)(2,1)}, u32[]{:S(2)}) copy-start(bf16[576]{0:T(1024)(128)(2,1)} %param.27) | copy-start | bytes 3460
  8.0 11.8 %copy-start.20 = (bf16[576]{0:T(1024)(128)(2,1)S(1)}, bf16[576]{0:T(1024)(128)(2,1)}, u32[]{:S(2)}) copy-start(bf16[576]{0:T(1024)(128)(2,1)} %param.30) | copy-start | bytes 3460
  8.0 11.8 %copy-start.21 = (bf16[576]{0:T(1024)(128)(2,1)S(1)}, bf16[576]{0:T(1024)(128)(2,1)}, u32[]{:S(2)}) copy-start(bf16[576]{0:T(1024)(128)(2,1)} %param.32) | copy-start | bytes 3460
  8.0 12.0 %copy-start.18 = (bf16[288,4]{0,1:T(4,128)(2,1)S(1)}, bf16[288,4]{0,1:T(4,128)(2,1)}, u32[]{:S(2)}) copy-start(bf16[288,4]{0,1:T(4,128)(2,1)} %param.35) | copy-start | bytes 6916
  8.0 46.2 %copy-start.9 = (bf16[576,104]{0,1:T(8,128)(2,1)S(1)}, bf16[576,104]{0,1:T(8,128)(2,1)}, u32[]{:S(2)}) copy-start(bf16[576,104]{0,1:T(8,128)(2,1)} %param.28) | copy-start | bytes 359428
  8.0 46.2 %copy-start.10 = (bf16[72,576]{1,0:T(8,128)(2,1)S(1)}, bf16[72,576]{1,0:T(8,128)(2,1)}, u32[]{:S(2)}) copy-start(bf16[72,576]{1,0:T(8,128)(2,1)} %param.29) | copy-start | bytes 248836
  8.0 46.2 %copy-start.16 = (bf16[16,576]{1,0:T(8,128)(2,1)S(1)}, bf16[16,576]{1,0:T(8,128)(2,1)}, u32[]{:S(2)}) copy-start(bf16[16,576]{1,0:T(8,128)(2,1)} %param.31) | copy-start | bytes 55300
  8.1 46.2 %copy-start.17 = (bf16[4,576]{1,0:T(4,128)(2,1)S(1)}, bf16[4,576]{1,0:T(4,128)(2,1)}, u32[]{:S(2)}) copy-start(bf16[4,576]{1,0:T(4,128)(2,1)} %param.26) | copy-start | bytes 13828
  8.1 314.6 %all-gather.11.cloned.1.call-start = ((), (), s32[]{:S(2)}) async-start(), calls=%async_computation.9 | async-start | bytes 6635520 | tf_op jit(solution)/shard_map/all_gather | solution.py:1077
  8.9 91.4 %collective-permute-start.1 = (s32[3]{0:T(128)S(1)}, s32[3]{0:T(128)S(1)}, u32[]{:S(2)}, u32[]{:S(2)}) collective-permute-start(s32[3]{0:T(128)S(1)} %slice_bitcast_fusion.1), channel_id=1, source_target_pairs={{0,4},{4,8},{8,12},{12,16},{16,20},{20,24},{24,28},{1,5},{5,9},{9,... | collective-permute-start | bytes 44 | tf_op jit(solution)/shard_map/ppermute | solution.py:1049
  10.2 219.0 %collective-permute-start = (bf16[16,1152]{1,0:T(8,128)(2,1)S(1)}, bf16[16,1152]{1,0:T(8,128)(2,1)S(1)}, u32[]{:S(2)}, u32[]{:S(2)}) collective-permute-start(bf16[16,1152]{1,0:T(8,128)(2,1)S(1)} %slice_bitcast_fusion), channel_id=1, source_target_pairs={{0,4},{4,8},{8,12},{12,16},{16,20},{20,24},{24,28},{1,5},{5,9},{9,... | collective-permute-start | bytes 110600 | tf_op jit(solution)/shard_map/ppermute | solution.py:1049
  14.4 326.5 %all-to-all-start.1 = ((bf16[4,64,1152]{2,1,0:T(8,128)(2,1)}), bf16[4,64,1152]{2,1,0:T(8,128)(2,1)S(1)}, u32[]{:S(2)}, u32[]{:S(2)}) async-start(bf16[4,64,1152]{2,1,0:T(8,128)(2,1)} %bitcast.26), calls=%async_computation.1 | async-start | bytes 1179648 | tf_op jit(solution)/shard_map/all_to_all | solution.py:1099
  229.2 0.6 copy-start.14
  340.9 19.7 %copy-start = (bf16[4,64,1152]{2,1,0:T(8,128)(2,1)}, bf16[4,64,1152]{2,1,0:T(8,128)(2,1)S(1)}, u32[]{:S(2)}) copy-start(bf16[4,64,1152]{2,1,0:T(8,128)(2,1)S(1)} %all-to-all-done.1) | copy-start | bytes 1769476
  400.7 17.9 %all-to-all-start.3 = ((bf16[4,64,1152]{2,1,0:T(8,128)(2,1)}), bf16[4,64,1152]{2,1,0:T(8,128)(2,1)S(1)}, u32[]{:S(2)}, u32[]{:S(2)}) async-start(bf16[4,64,1152]{2,1,0:T(8,128)(2,1)} %bitcast.32), calls=%async_computation.3 | async-start | bytes 1179648 | tf_op jit(solution)/shard_map/all_to_all | solution.py:1099
  406.2 130.5 %reduce-scatter.7.cloned.1.call-start = ((), (), s32[]{:S(2)}) async-start(), calls=%async_computation.12 | async-start | bytes 6635520 | tf_op jit(solution)/shard_map/reduce_scatter | solution.py:1132
  418.6 0.8 copy-start.1
  438.5 0.9 copy-start.12
  438.5 281.7 %reduce-scatter.5.cloned.1.call-start = ((), (), s32[]{:S(2)}) async-start(), calls=%async_computation.10 | async-start | bytes 13271040 | tf_op jit(solution)/shard_map/reduce_scatter | solution.py:1132
  483.2 3.2 collective-permute-start.2
  486.3 0.6 copy-start.13
  486.3 12.4 %slice-start = ((s8[5308416]{0:T(1024)(128)(4,1)}), s8[4194304]{0:T(1024)(128)(4,1)S(1)}, s32[]{:S(2)}) async-start(s8[5308416]{0:T(1024)(128)(4,1)} %bitcast.79), calls=%async_computation.16 | async-start | bytes 8388608
  487.0 11.7 %slice-start.1 = ((s8[5308416]{0:T(1024)(128)(4,1)}), s8[1114112]{0:T(1024)(128)(4,1)S(1)}, s32[]{:S(2)}) async-start(s8[5308416]{0:T(1024)(128)(4,1)} %bitcast.79), calls=%async_computation.17 | async-start | bytes 2228224
  505.9 1.2 copy-start.5
  505.9 1.2 copy-start.11
  505.9 1.5 copy-start.4
  506.0 350.2 %all-reduce.5.cloned.1.call-start = ((), (), s32[]{:S(2)}) async-start(), calls=%async_computation.11 | async-start | bytes 3686400 | tf_op jit(solution)/shard_map/psum | solution.py:1137
  508.8 417.7 %reduce-scatter.11.cloned.1.call-start = ((), (), s32[]{:S(2)}) async-start(), calls=%async_computation.14 | async-start | bytes 7962624 | tf_op jit(solution)/shard_map/reduce_scatter | solution.py:1113
  509.4 486.5 %reduce-scatter.9.cloned.1.call-start = ((), (), s32[]{:S(2)}) async-start(), calls=%async_computation.13 | async-start | bytes 7962624 | tf_op jit(solution)/shard_map/reduce_scatter | solution.py:1112
  510.1 210.1 %copy-start.8 = (bf16[128,1152]{1,0:T(8,128)(2,1)S(1)}, bf16[128,1152]{1,0:T(8,128)(2,1)}, u32[]{:S(2)}) copy-start(bf16[128,1152]{1,0:T(8,128)(2,1)} %get-tuple-element.83) | copy-start | bytes 884740
  510.1 568.5 %all-reduce.7.cloned.1.call-start = ((), (), s32[]{:S(2)}) async-start(), calls=%async_computation.15 | async-start | bytes 7962624 | tf_op jit(solution)/shard_map/psum | solution.py:1133
  720.2 1.2 copy-start.6
  720.2 2.1 copy-start.15
  1078.7 4.9 copy-start.2
Sparse Core Ops, SparseCore 0:
  9.6 210.5 all-gather.8
  221.8 100.8 all-gather.10
  438.6 97.9 reduce-scatter.6
  539.0 181.1 reduce-scatter.4
  726.0 130.1 all-reduce.4
  859.6 66.8 reduce-scatter.10
  930.4 65.4 reduce-scatter.8
  999.4 79.1 all-reduce.6

commit v2 on v1

--- a/solution.py
+++ b/solution.py
@@ -111,7 +111,470 @@
         self.SMALL = self.X0 + self.XW
 
 
-def front(z, tokens, halo, masks, gpack, w_conv, w_gate, small):
+MESH = pl.DeviceIdType.MESH
+ANY = pl.BlockSpec(memory_space=pl.ANY)
+
+
+def greet(peers):
+    barrier = pltpu.get_barrier_semaphore()
+    for peer in peers:
+        pl.semaphore_signal(barrier, inc=1, device_id=peer, device_id_type=MESH)
+    pl.semaphore_wait(barrier, len(peers))
+
+
+def exchange(axis, count, arrays, spread, cid):
+    n = len(arrays)
+    blocks = [a.shape[1:] if not s else a.shape for a, s in zip(arrays, spread)]
+
+    def body(*refs):
+        xs, os = refs[:n], refs[n : 2 * n]
+        send, recv, own = refs[2 * n :]
+        me = lax.axis_index(axis)
+        peers = [lax.rem(me + k, count) for k in range(1, count)]
+        greet([{axis: p} for p in peers])
+        copies = []
+        for a in range(n):
+            for k, p in enumerate(peers):
+                c = pltpu.make_async_remote_copy(
+                    xs[a] if spread[a] else xs[a].at[p],
+                    os[a].at[me],
+                    send.at[a, k],
+                    recv.at[a, k],
+                    device_id={axis: p},
+                    device_id_type=MESH,
+                )
+                c.start()
+                copies.append(c)
+        locals_ = []
+        for a in range(n):
+            c = pltpu.make_async_copy(xs[a] if spread[a] else xs[a].at[me], os[a].at[me], own.at[a])
+            c.start()
+            locals_.append(c)
+        for c in locals_ + copies:
+            c.wait()
+
+    outs = [sds((count,) + tuple(b), a.dtype) for a, b in zip(arrays, blocks)]
+    return pl.pallas_call(
+        body,
+        name="exchange_" + axis,
+        in_specs=[ANY] * n,
+        out_specs=[ANY] * n,
+        out_shape=outs,
+        scratch_shapes=[
+            pltpu.SemaphoreType.DMA((n, count - 1)),
+            pltpu.SemaphoreType.DMA((n, count - 1)),
+            pltpu.SemaphoreType.DMA((n,)),
+        ],
+        compiler_params=pltpu.CompilerParams(collective_id=cid, has_side_effects=True),
+    )(*arrays)
+
+
+def gather_weights(E, arrays, regions, cid):
+    n = len(arrays)
+    offsets = [d for k in range(1, E) for d in (-k, k)]
+
+    def slot(d):
+        return 2 * (abs(d) - 1) + (1 if d > 0 else 0)
+
+    def body(*refs):
+        xs, os = refs[:n], refs[n : 2 * n]
+        zs, zr, ps, pr, cs, cr, own = refs[2 * n :]
+        s, me = lax.axis_index("seq"), lax.axis_index("exp")
+        chip, core = s // 2, lax.rem(s, 2)
+        sib = chip * 2 + (1 - core)
+        chips = [
+            chip + 1 - 2 * lax.rem(chip, 2),
+            chip + 2 - 4 * (chip // 2),
+            3 - chip,
+        ]
+        right, left = lax.rem(me + 1, E), lax.rem(me + E - 1, E)
+        greet(
+            [{"seq": s, "exp": right}, {"seq": s, "exp": left}, {"seq": sib, "exp": me}]
+            + [{"seq": q * 2 + core, "exp": me} for q in chips]
+        )
+        owns = [pltpu.make_async_copy(xs[a], os[a].at[me], own.at[a]) for a in range(n)]
+        for c in owns:
+            c.start()
+
+        def part(a, region, q):
+            rows = arrays[a].shape[0] // 2
+            r = pl.ds(pl.multiple_of(core * rows, 16), rows)
+            whole_cols, each = regions[a]
+            if region == 0:
+                return (r, slice(None)) if whole_cols == arrays[a].shape[1] else (r, pl.ds(0, whole_cols))
+            return (r, pl.ds(pl.multiple_of(whole_cols + q * each, LANES), each))
+
+        def kinds(a):
+            return [1, 0] if regions[a][1] else [0]
+
+        def z_copy(a, region, d, to_right):
+            at = part(a, region, chip)
+            src = xs[a].at[at] if d == 0 else os[a].at[(me + d,) + at]
+            there = slot(d - 1 if to_right else d + 1)
+            return pltpu.make_async_remote_copy(
+                src, os[a].at[(me + d,) + at], zs.at[a, region, there], zr.at[a, region, there],
+                device_id={"seq": s, "exp": right if to_right else left}, device_id_type=MESH,
+            )
+
+        def z_arrival(a, region, d):
+            at = part(a, region, chip)
+            ref = os[a].at[(me + d,) + at]
+            return pltpu.make_async_remote_copy(
+                ref, ref, zs.at[a, region, slot(d)], zr.at[a, region, slot(d)],
+                device_id={"seq": s, "exp": right}, device_id_type=MESH,
+            )
+
+        def plane_copy(a, k, d):
+            ref = os[a].at[(me + d,) + part(a, 1, chip)]
+            return pltpu.make_async_remote_copy(
+                ref, ref, ps.at[a, k, slot(d)], pr.at[a, k, slot(d)],
+                device_id={"seq": chips[k] * 2 + core, "exp": me}, device_id_type=MESH,
+            )
+
+        def plane_arrival(a, k, d):
+            ref = os[a].at[(me + d,) + part(a, 1, chips[k])]
+            return pltpu.make_async_remote_copy(
+                ref, ref, ps.at[a, k, slot(d)], pr.at[a, k, slot(d)],
+                device_id={"seq": chips[k] * 2 + core, "exp": me}, device_id_type=MESH,
+            )
+
+        def sib_copy(a, which, d):
+            at = part(a, 0, chip) if which == 0 else part(a, 1, chip if which == 1 else chips[which - 2])
+            ref = os[a].at[(me + d,) + at]
+            return pltpu.make_async_remote_copy(
+                ref, ref, cs.at[a, which, slot(d)], cr.at[a, which, slot(d)],
+                device_id={"seq": sib, "exp": me}, device_id_type=MESH,
+            )
+
+        def sib_arrival(a, which, d):
+            rows = arrays[a].shape[0] // 2
+            at = part(a, 0, chip) if which == 0 else part(a, 1, chip if which == 1 else chips[which - 2])
+            ref = os[a].at[(me + d, pl.ds(pl.multiple_of((1 - core) * rows, 16), rows), at[1])]
+            return pltpu.make_async_remote_copy(
+                ref, ref, cs.at[a, which, slot(d)], cr.at[a, which, slot(d)],
+                device_id={"seq": sib, "exp": me}, device_id_type=MESH,
+            )
+
+        def exists(d):
+            return (me + d >= 0) & (me + d < E)
+
+        def z_starts(a, region, d):
+            if d <= 0:
+                @pl.when(exists(d) & (me < E - 1))
+                def _():
+                    z_copy(a, region, d, True).start()
+            if d >= 0:
+                @pl.when(exists(d) & (me > 0))
+                def _():
+                    z_copy(a, region, d, False).start()
+
+        order = [(a, r) for a in range(n) for r in kinds(a)]
+        for a, r in order:
+            z_starts(a, r, 0)
+
+        def arrivals(k):
+            for a, r in order:
+                for d in (-k, k):
+                    @pl.when(exists(d))
+                    def _():
+                        z_arrival(a, r, d).wait_recv()
+                    if k < E - 1:
+                        z_starts(a, r, d)
+
+                    @pl.when(exists(d))
+                    def _():
+                        if r == 1:
+                            for j in range(3):
+                                plane_copy(a, j, d).start()
+                        sib_copy(a, r, d).start()
+
+        def plane(k):
+            for a in range(n):
+                if regions[a][1]:
+                    for d in (-k, k):
+                        @pl.when(exists(d))
+                        def _():
+                            for j in range(3):
+                                plane_arrival(a, j, d).wait_recv()
+                                sib_copy(a, 2 + j, d).start()
+
+        for k in range(1, E):
+            arrivals(k)
+            if k > 1:
+                plane(k - 1)
+        plane(E - 1)
+        for a in range(n):
+            whiches = [0] + ([1, 2, 3, 4] if regions[a][1] else [])
+            for d in offsets:
+                @pl.when(exists(d))
+                def _():
+                    for w in whiches:
+                        sib_arrival(a, w, d).wait_recv()
+                        sib_copy(a, w, d).wait_send()
+                    if regions[a][1]:
+                        for j in range(3):
+                            plane_copy(a, j, d).wait_send()
+        for a, r in order:
+            for d in [0] + offsets:
+                if d <= 0 and abs(d) < E - 1:
+                    @pl.when(exists(d) & (me < E - 1))
+                    def _():
+                        z_copy(a, r, d, True).wait_send()
+                if d >= 0 and abs(d) < E - 1:
+                    @pl.when(exists(d) & (me > 0))
+                    def _():
+                        z_copy(a, r, d, False).wait_send()
+        for c in owns:
+            c.wait()
+
+    slots = 2 * (E - 1)
+    sem = lambda *dims: pltpu.SemaphoreType.DMA(dims)
+    return pl.pallas_call(
+        body,
+        name="gather_weights",
+        in_specs=[ANY] * n,
+        out_specs=[ANY] * n,
+        out_shape=[sds((E,) + a.shape, a.dtype) for a in arrays],
+        scratch_shapes=[
+            sem(n, 2, slots), sem(n, 2, slots), sem(n, 3, slots), sem(n, 3, slots),
+            sem(n, 5, slots), sem(n, 5, slots), sem(n),
+        ],
+        compiler_params=pltpu.CompilerParams(collective_id=cid, has_side_effects=True),
+    )(*arrays)
+
+
+def gather_chain(E, arrays, cid):
+    n = len(arrays)
+
+    def slot(d):
+        return 2 * (abs(d) - 1) + (1 if d > 0 else 0)
+
+    def body(*refs):
+        xs, os = refs[:n], refs[n : 2 * n]
+        zs, zr, own = refs[2 * n :]
+        me = lax.axis_index("exp")
+        right, left = lax.rem(me + 1, E), lax.rem(me + E - 1, E)
+        greet([{"exp": right}, {"exp": left}])
+
+        def exists(d):
+            return (me + d >= 0) & (me + d < E)
+
+        def copy(a, d, to_right):
+            there = slot(d - 1 if to_right else d + 1)
+            return pltpu.make_async_remote_copy(
+                xs[a] if d == 0 else os[a].at[me + d], os[a].at[me + d], zs.at[a, there], zr.at[a, there],
+                device_id={"exp": right if to_right else left}, device_id_type=MESH,
+            )
+
+        def arrival(a, d):
+            ref = os[a].at[me + d]
+            return pltpu.make_async_remote_copy(
+                ref, ref, zs.at[a, slot(d)], zr.at[a, slot(d)],
+                device_id={"exp": right}, device_id_type=MESH,
+            )
+
+        def each(a, d, act):
+            if d <= 0:
+                @pl.when(exists(d) & (me < E - 1))
+                def _():
+                    act(copy(a, d, True))
+            if d >= 0:
+                @pl.when(exists(d) & (me > 0))
+                def _():
+                    act(copy(a, d, False))
+
+        for a in range(n):
+            each(a, 0, lambda c: c.start())
+        owns = [pltpu.make_async_copy(xs[a], os[a].at[me], own.at[a]) for a in range(n)]
+        for c in owns:
+            c.start()
+        for k in range(1, E):
+            for a in range(n):
+                for d in (-k, k):
+                    @pl.when(exists(d))
+                    def _():
+                        arrival(a, d).wait_recv()
+                    if k < E - 1:
+                        each(a, d, lambda c: c.start())
+        for a in range(n):
+            for k in range(0, E - 1):
+                for d in (-k, k) if k else (0,):
+                    each(a, d, lambda c: c.wait_send())
+        for c in owns:
+            c.wait()
+
+    slots = 2 * (E - 1)
+    return pl.pallas_call(
+        body,
+        name="gather_chain",
+        in_specs=[ANY] * n,
+        out_specs=[ANY] * n,
+        out_shape=[sds((E,) + a.shape, a.dtype) for a in arrays],
+        scratch_shapes=[
+            pltpu.SemaphoreType.DMA((n, slots)),
+            pltpu.SemaphoreType.DMA((n, slots)),
+            pltpu.SemaphoreType.DMA((n,)),
+        ],
+        compiler_params=pltpu.CompilerParams(collective_id=cid, has_side_effects=True),
+    )(*arrays)
+
+
+def reduce_plane(E, p_in, p_out, p_small, cid):
+    RI, CI = p_in.shape
+    ri, ci = RI // 2, CI // 4
+    _, ro, co = p_out.shape
+    _, rs8, cs = p_small.shape
+    rs = rs8 // 8
+    p_small = p_small.reshape(E, 4, 2, rs, cs)
+    p_out = p_out.reshape(4, 2, ro, co)
+
+    def body(xi, xo, xs, oi, oo, os, a_i, b_i, a_o, b_o, a_s, b_s, t_i, t_o, t_s, z_s, r_i, r_o, r_s,
+             lsem, c_send, c_recv, q_send, q_recv, z_send, z_recv, g_send, g_recv, f_send, f_recv):
+        s, me = lax.axis_index("seq"), lax.axis_index("exp")
+        chip, core = s // 2, lax.rem(s, 2)
+        other = 1 - core
+        sib = {"seq": chip * 2 + other, "exp": me}
+        chips = [chip + 1 - 2 * lax.rem(chip, 2), chip + 2 - 4 * (chip // 2), 3 - chip]
+        there = [{"seq": q * 2 + core, "exp": me} for q in chips]
+        zs = [lax.rem(me + k, E) for k in range(1, E)]
+        greet([sib] + there + [{"seq": s, "exp": p} for p in zs])
+
+        def remote(src, dst, send, recv, to):
+            return pltpu.make_async_remote_copy(src, dst, send, recv, device_id=to, device_id_type=MESH)
+
+        half = lambda c: pl.ds(pl.multiple_of(c * ri, 16), ri)
+        first = [
+            remote(xi.at[half(other)], b_i, c_send.at[0], c_recv.at[0], sib),
+            remote(xo.at[:, other], b_o, c_send.at[1], c_recv.at[1], sib),
+            remote(xs.at[:, :, other], b_s, c_send.at[2], c_recv.at[2], sib),
+        ]
+        for c in first:
+            c.start()
+        mine = [
+            pltpu.make_async_copy(xi.at[half(core)], a_i, lsem.at[0]),
+            pltpu.make_async_copy(xo.at[:, core], a_o, lsem.at[1]),
+            pltpu.make_async_copy(xs.at[:, :, core], a_s, lsem.at[2]),
+        ]
+        for c in mine:
+            c.start()
+        adds = lambda a, b: (a.astype(F32) + b.astype(F32)).astype(BF16)
+        cols = lambda q: pl.ds(pl.multiple_of(q * ci, LANES), ci)
+        second = []
+        for w in (0, 1, 2):
+            mine[w].wait()
+            first[w].wait()
+            if w == 0:
+                a_i[...] = adds(a_i[...], b_i[...])
+            elif w == 1:
+                a_o[...] = adds(a_o[...], b_o[...])
+            else:
+                a_s[...] = adds(a_s[...], b_s[...])
+            for k in range(3):
+                src = [a_i.at[:, cols(chips[k])], a_o.at[chips[k]], a_s.at[:, chips[k]]][w]
+                dst = [t_i, t_o, t_s][w].at[k]
+                c = remote(src, dst, q_send.at[w, k], q_recv.at[w, k], there[k])
+                c.start()
+                second.append(c)
+
+        def total(own, parts):
+            out = own.astype(F32)
+            for k in range(3):
+                out = out + parts[k].astype(F32)
+            return out.astype(BF16)
+
+        for c in second[6:9]:
+            c.wait()
+        a_s[:, chip] = total(a_s[:, chip], t_s)
+        third = []
+        for k, p in enumerate(zs):
+            c = remote(a_s.at[p, chip], z_s.at[me], z_send.at[k], z_recv.at[k], {"seq": s, "exp": p})
+            c.start()
+            third.append(c)
+
+        gathers = []
+
+        def spread(w, ref):
+            for k in range(3):
+                c = remote(ref, ref, g_send.at[w, k], g_recv.at[w, k], there[k])
+                c.start()
+                gathers.append(c)
+            c = remote(ref, ref, f_send.at[w, 3], f_recv.at[w, 3], sib)
+            c.start()
+            gathers.append(c)
+
+        for c in second[0:3]:
+            c.wait()
+        r_i[core, chip] = total(a_i[:, cols(chip)], t_i)
+        spread(0, r_i.at[core, chip])
+        for c in second[3:6]:
+            c.wait()
+        r_o[core, chip] = total(a_o[chip], t_o)
+        spread(1, r_o.at[core, chip])
+        for c in third:
+            c.wait()
+        out = a_s[me, chip].astype(F32)
+        for k, p in enumerate(zs):
+            out = out + z_s[p].astype(F32)
+        r_s[core, chip] = out.astype(BF16)
+        spread(2, r_s.at[core, chip])
+
+        def landed(w, c, q):
+            return [r_i, r_o, r_s][w].at[c, q]
+
+        passed = []
+        for w in (0, 1, 2):
+            for k in range(3):
+                ref = landed(w, core, chips[k])
+                remote(ref, ref, g_send.at[w, k], g_recv.at[w, k], there[k]).wait_recv()
+                c = remote(ref, ref, f_send.at[w, k], f_recv.at[w, k], sib)
+                c.start()
+                passed.append(c)
+        for c in gathers:
+            c.wait_send()
+        for c in passed:
+            c.wait_send()
+        for w in (0, 1, 2):
+            for k in range(4):
+                ref = landed(w, other, chips[k] if k < 3 else chip)
+                remote(ref, ref, f_send.at[w, k], f_recv.at[w, k], sib).wait_recv()
+        writes = []
+        for c in range(2):
+            for q in range(4):
+                writes.append(
+                    pltpu.make_async_copy(
+                        r_i.at[c, q], oi.at[c * ri : (c + 1) * ri, q * ci : (q + 1) * ci], lsem.at[3 + c * 4 + q]
+                    )
+                )
+                writes.append(pltpu.make_async_copy(r_o.at[c, q], oo.at[q, c], lsem.at[11 + c * 4 + q]))
+                writes.append(pltpu.make_async_copy(r_s.at[c, q], os.at[q, c], lsem.at[19 + c * 4 + q]))
+        for c in writes:
+            c.start()
+        for c in writes:
+            c.wait()
+
+    v = lambda *dims: pltpu.VMEM(dims, BF16)
+    sem = lambda *dims: pltpu.SemaphoreType.DMA(dims)
+    oi, oo, os = pl.pallas_call(
+        body,
+        name="reduce_plane",
+        in_specs=[ANY] * 3,
+        out_specs=[ANY] * 3,
+        out_shape=[sds((RI, CI), BF16), sds((4, 2, ro, co), BF16), sds((4, 2, rs, cs), BF16)],
+        scratch_shapes=[
+            v(ri, CI), v(ri, CI), v(4, ro, co), v(4, ro, co), v(E, 4, rs, cs), v(E, 4, rs, cs),
+            v(3, ri, ci), v(3, ro, co), v(3, E, rs, cs), v(E, rs, cs),
+            v(2, 4, ri, ci), v(2, 4, ro, co), v(2, 4, rs, cs),
+            sem(27), sem(3), sem(3), sem(3, 3), sem(3, 3), sem(E - 1), sem(E - 1),
+            sem(3, 3), sem(3, 3), sem(3, 4), sem(3, 4),
+        ],
+        compiler_params=pltpu.CompilerParams(
+            collective_id=cid, has_side_effects=True, vmem_limit_bytes=VMEM_LIMIT
+        ),
+    )(p_in, p_out, p_small)
+    return oi, oo.reshape(8, ro, co), os.reshape(8 * rs, cs)
+
+
+def front(z, tokens, halo, masks, gpack, w_in, small):
     T, D, DI, J = z.T, z.D, z.DI, z.J
     H = halo.shape[0]
     cb = pick(DI, (384, 256, 128))
@@ -150,14 +613,14 @@
         body,
         "front",
         (steps,),
-        (tokens, halo, masks, gpack, w_conv, w_gate, small),
+        (tokens, halo, masks, gpack, w_in, w_in, small),
         [
             whole(tokens.shape),
             whole(halo.shape),
             whole(masks.shape),
             whole(gpack.shape),
             col(D),
-            col(D),
+            block((D, cb), lambda i: (0, i + steps)),
             col(z.SMALL),
         ],
         [
@@ -485,7 +948,7 @@
     fb = pick(FF, (512, 256, 128))
     steps = FF // fb
 
-    def body(wh, x_r, c_r, rt, up_r, dn_r, ret_o, gg_o, dwu_o, dwd_o, g_s, out_s, dx_s):
+    def body(wh, x_r, c_r, rt, up_r, dn_r, ret_o, rdx_o, dwu_o, dwd_o, g_s, out_s, dx_s):
         i = pl.program_id(0)
 
         @pl.when(i == 0)
@@ -512,11 +975,13 @@
         @pl.when(i == steps - 1)
         def _():
             out = out_s[...].astype(BF16)
-            ret_o[0] = out
-            ret_o[1] = dx_s[...].astype(BF16)
-            gg_o[...] = jnp.broadcast_to(
-                jnp.sum(out.astype(F32) * c_r[...].astype(F32), axis=-1, keepdims=True), gg_o.shape
-            )
+            ret_o[...] = out
+            rdx_o[:, 0:D] = dx_s[...].astype(BF16)
+            gg = jnp.sum(out.astype(F32) * c_r[...].astype(F32), axis=-1, keepdims=True)
+            hi, lo = split_hi_lo(gg)
+            lane = lax.broadcasted_iota(jnp.int32, (M, LANES), 1)
+            both = jnp.where(lane == 0, hi.astype(F32), jnp.where(lane == 1, lo.astype(F32), 0.0))
+            rdx_o[:, D : D + LANES] = both.astype(BF16)
 
     return call(
         body,
@@ -532,14 +997,14 @@
             block((fb, D), lambda i: (i, 0)),
         ],
         [
-            sds((2, M, D), BF16),
-            sds((M, LANES), F32),
+            sds((M, D), BF16),
+            sds((M, D + LANES), BF16),
             sds((D, FF), BF16),
             sds((FF, D), BF16),
         ],
         [
-            whole((2, M, D)),
-            whole((M, LANES)),
+            whole((M, D)),
+            whole((M, D + LANES)),
             block((D, fb), lambda i: (0, i)),
             block((fb, D), lambda i: (i, 0)),
         ],
@@ -547,8 +1012,8 @@
     )
 
 
-def middle(z, ret_out, ret_dx, table, choose, chances, mid, moe, cot, gpack, router, gate, y, sig,
-           small, w_out, mixed, dt, masks, normed):
+def middle(z, ret_dx, table, choose, chances, mid, moe, cot, gpack, router, gate, y, sig,
+           small, w_out, mixed, dt, masks):
     T, D, DI, N, J, E = z.T, z.D, z.DI, z.N, z.J, z.E
     cb = pick(DI, (384, 256, 128))
     tg = 1 if cb % 256 else 2
@@ -557,9 +1022,9 @@
     steps = DI // cb
     G = gpack.shape[0]
 
-    def body(ro, rd, tb, cho, chn, md, me_r, ct, gp, rt, gt, yr, sg, sm, wo, mix, dt_r, msk, nm,
-             out_o, mg_o, gg_o, yg_o, gi_o, dwo_o, dwg_o, fdev_o, suf_o, skip_o,
-             cx, cl, rates_s, br, fd):
+    def body(rd, tb, cho, chn, md, me_r, ct, gp, rt, gt, yr, sg, sm, wo, mix, dt_r, msk,
+             mg_o, br, gg_o, yg_o, gi_o, gd_o, fdev_o, suf_o, skip_o,
+             cx, cl, rates_s, fd):
         i = pl.program_id(0)
 
         @pl.when(i == 0)
@@ -567,17 +1032,16 @@
             expand_columns(z, mix, z.R + N, cx)
             expand_closed(z, msk, cl)
             tbv = tb[...]
-            eo = mm(tbv, ro[...])
+            back = mm(tbv, rd[...])
             grad = ct[...].astype(F32)
             ch = chn[...]
             pick_e = cho[...]
             gating = jnp.sum(ch * pick_e, axis=-1, keepdims=True)
-            out_o[...] = (md[...] + gating * eo).astype(BF16)
-            gate_grad = jnp.sum(grad * eo, axis=-1, keepdims=True)
+            gate_grad = back[:, D : D + 1] + back[:, D + 1 : D + 2]
             lg = ch * (gate_grad * pick_e - gate_grad * gating)
             hi, lo = split_hi_lo(lg)
             rtv = rt[...]
-            mig = mm(tbv, rd[...]) + mm(hi, rtv) + mm(lo, rtv)
+            mig = back[:, 0:D] + mm(hi, rtv) + mm(lo, rtv)
             mev = me_r[...]
             rg = mm_tn(hi, mev) + mm_tn(lo, mev)
             d, gain_g = rms_back(md[...], gp[1:2, :], mig)
@@ -597,9 +1061,7 @@
         yg_o[...] = yg
         gi = (gg * yv * (s * (1.0 + g_in * (1.0 - s)))).astype(BF16)
         gi_o[...] = gi
-        gated = (yv * act).astype(BF16)
-        dwo_o[...] = mm_tn(gated, br[...]).astype(BF16)
-        dwg_o[...] = mm_tn(nm[...], gi).astype(BF16)
+        gd_o[...] = (yv * act).astype(BF16)
         skip_o[...] = jnp.sum(yg * sg[...].astype(F32), axis=0, keepdims=True)
         rates_s[...] = -jnp.exp(sm[A_LOG : A_LOG + N, :]) * LOG2E
 
@@ -658,10 +1120,9 @@
         body,
         "middle",
         (steps,),
-        (ret_out, ret_dx, table, choose, chances, mid, moe, cot, gpack, router, gate, y, sig, small,
-         w_out, mixed, dt, masks, normed),
-        [
-            whole(ret_out.shape),
+        (ret_dx, table, choose, chances, mid, moe, cot, gpack, router, gate, y, sig, small,
+         w_out, mixed, dt, masks),
+        [
             whole(ret_dx.shape),
             whole(table.shape),
             whole(choose.shape),
@@ -679,16 +1140,14 @@
             whole(mixed.shape),
             col(T),
             whole(masks.shape),
-            whole(normed.shape),
-        ],
-        [
+        ],
+        [
+            sds((T, D), F32),
             sds((T, D), BF16),
-            sds((T, D), F32),
             sds((G, D), F32),
             sds((T, DI), F32),
             sds((T, DI), BF16),
-            sds((DI, D), BF16),
-            sds((D, DI), BF16),
+            sds((T, DI), BF16),
             sds((N, DI), BF16),
             sds(((N + 1) * SUB, DI), F32),
             sds((1, DI), F32),
@@ -699,8 +1158,7 @@
             whole((G, D)),
             col(T),
             col(T),
-            row(D),
-            col(D),
+            col(T),
             col(N),
             col((N + 1) * SUB),
             col(1),
@@ -709,7 +1167,6 @@
             pltpu.VMEM((J * N * SUB, LANES), F32),
             pltpu.VMEM((T, LANES), F32),
             pltpu.VMEM((N, cb), F32),
-            pltpu.VMEM((T, D), BF16),
             pltpu.VMEM((N, cb), F32),
         ],
     )
@@ -978,13 +1435,13 @@
     )
 
 
-def last(z, cig, edge, gate_grad, normed, w_conv, w_gate, tokens, mid_grad, gpack, ggrad):
+def last(z, cig, edge, gate_grad, w_in, tokens, mid_grad, gpack, ggrad):
     T, D, DI, J = z.T, z.D, z.DI, z.J
     cb = pick(DI, (384, 256, 128))
     steps = DI // cb
     G = gpack.shape[0]
 
-    def body(cg, eg, gg, nm, wc, wg, tok, mg, gp, gpre, dw_o, tg_o, gn_o, acc):
+    def body(cg, eg, gg, wc, wg, tok, mg, gp, gpre, pc_o, tg_o, gn_o, acc):
         i = pl.program_id(0)
 
         @pl.when(i == 0)
@@ -1001,7 +1458,7 @@
             ]
         )
         pc = jnp.concatenate([c3[: J - 3], fixed], axis=0).reshape(T, cb).astype(BF16)
-        dw_o[...] = mm_tn(nm[...], pc).astype(BF16)
+        pc_o[...] = pc
         acc[...] += mm_nt(pc, wc[...]) + mm_nt(gg[...], wg[...])
 
         @pl.when(i == steps - 1)
@@ -1016,21 +1473,20 @@
         body,
         "last",
         (steps,),
-        (cig, edge, gate_grad, normed, w_conv, w_gate, tokens, mid_grad, gpack, ggrad),
+        (cig, edge, gate_grad, w_in, w_in, tokens, mid_grad, gpack, ggrad),
         [
             col(T),
             col(SUB),
             col(T),
-            whole(normed.shape),
             col(D),
-            col(D),
+            block((D, cb), lambda i: (0, i + steps)),
             whole(tokens.shape),
             whole(mid_grad.shape),
             whole(gpack.shape),
             whole(ggrad.shape),
         ],
-        [sds((D, DI), BF16), sds((T, D), F32), sds((G, D), F32)],
-        [col(D), whole((T, D)), whole((G, D))],
+        [sds((T, DI), BF16), sds((T, D), F32), sds((G, D), F32)],
+        [col(T), whole((T, D)), whole((G, D))],
         [pltpu.VMEM((T, D), F32)],
     )
 
@@ -1063,23 +1519,34 @@
     seg = segment_ids[0]
     seg_tail = from_behind(seg[T - 3 :], "seq", 1)
 
-    own = in_proj.shape[1] // 2
     cw = dt_proj.shape[1]
-    zero = jnp.zeros((1, cw), BF16)
+    dw = norm_gain.shape[0]
+    plane = S == 8 and dw % 32 == 0
     small_own = jnp.concatenate(
-        [conv_weight, conv_bias[None], dt_bias[None], d_skip[None], zero, a_log, dt_proj, x_proj.T], axis=0
-    )
+        [conv_weight, conv_bias[None], dt_bias[None], d_skip[None], jnp.zeros((1, cw), BF16), a_log, dt_proj,
+         x_proj.T, jnp.zeros((-z.SMALL % 32, cw), BF16)], axis=0
+    )
+    g_own = jnp.concatenate(
+        [norm_gain[None], moe_gain[None], router.T, jnp.zeros((32 - 2 - E, dw), BF16)], axis=0
+    )
+    owned = [in_proj, out_proj, small_own, g_own]
+    if plane:
+        each = lambda cols, most: (cols - 4 * most * LANES, most * LANES)
+        tiles_in, tiles_out = 2 * DI // LANES, D // LANES
+        regions = [
+            each(2 * DI, max(1, tiles_in * 5 // 36)), each(D, max(1, tiles_out * 2 // 9)), (cw, 0), (dw, 0)
+        ]
+        w_in, w_out, small, gpack_low = gather_weights(E, owned, regions, 1)
+    else:
+        w_in, w_out, small, gpack_low = [lax.all_gather(a, "exp") for a in owned]
+    w_in = w_in.reshape(D, 2 * DI)
+    w_out = w_out.reshape(DI, D)
+    join = lambda a: a.swapaxes(0, 1).reshape(a.shape[1], -1)
+    small = join(small[:, : z.SMALL]).astype(F32)
+    gpack_low = join(gpack_low[:, : 2 + E])
     gr = 8 * -(-(2 + E) // 8)
-    g_own = jnp.concatenate(
-        [norm_gain[None], moe_gain[None], router.T, jnp.zeros((gr - 2 - E, router.shape[0]), BF16)], axis=0
-    )
-    w_in = lax.all_gather(in_proj, "exp", axis=0, tiled=True)
-    w_out = lax.all_gather(out_proj, "exp", axis=0, tiled=True)
-    small = lax.all_gather(small_own, "exp", axis=1, tiled=True).astype(F32)
-    gpack_low = lax.all_gather(g_own, "exp", axis=1, tiled=True)
-    gpack = gpack_low.astype(F32)
+    gpack = jnp.zeros((gr, D), F32).at[: 2 + E].set(gpack_low.astype(F32))
     router_t = jnp.zeros((LANES, D), BF16).at[0:E].set(gpack_low[2 : 2 + E])
-    w_conv, w_gate = w_in[:, :DI], w_in[:, DI:]
 
     padded_seg = jnp.concatenate([seg_tail, seg])
     masks = jnp.stack([(padded_seg[o : o + T] == seg).astype(F32) for o in range(4)] + [seg * 0.0] * 4, axis=1)
@@ -1096,67 +1563,108 @@
     cot_slots = lax.dot_general(table, cot, (((0,), (0,)), ((), ())), preferred_element_type=F32).astype(BF16)
 
     def trade(a):
-        return lax.all_to_all(a.reshape(E, CAP, -1), "exp", split_axis=0, concat_axis=0, tiled=True).reshape(a.shape)
-
-    cot_here = trade(cot_slots)
-
-    normed, conv_in, hconv, gate, sig, mixed = front(z, tok, halo, masks, gpack, w_conv, w_gate, small)
+        return lax.all_to_all(a, "exp", split_axis=0, concat_axis=0, tiled=True)
+
+    def columns(a):
+        return a.reshape(T, E, -1).swapaxes(0, 1)
+
+    cot_here = trade(cot_slots.reshape(E, CAP, D)).reshape(E * CAP, D)
+
+    normed, conv_in, hconv, gate, sig, mixed = front(z, tok, halo, masks, gpack, w_in, small)
+    normed_z = trade(columns(normed)).reshape(E * T, -1)
     dt, pre, hdev, stot, dwin = summary(z, mixed, sig, masks, small)
-    h_all = lax.all_gather(hdev, "seq")
-    s_all = lax.all_gather(stot, "seq")
+    h_all, s_all = exchange("seq", S, [hdev, stot], [True, True], 2)
     states, y, mid, moe, chances, outbound = scan_forward(
         z, where, mixed, dt, sig, gate, masks, small, pre, dwin, h_all, s_all, w_out, tok, gpack, router_t, table
     )
-    arrived = trade(outbound)
-    ret, _, dwu, dwd = expert(z, where, arrived, cot_here, router_t, up_proj[0], down_proj[0])
-    up_part = lax.psum_scatter(dwu, "seq", scatter_dimension=0, tiled=True).astype(F32)
-    down_part = lax.psum_scatter(dwd, "seq", scatter_dimension=0, tiled=True).astype(F32)
-    ret_dx = trade(ret[1])
-    ret_out = trade(ret[0])
-    output, mid_grad, ggrad, yg, gate_grad, dw_out, dw_gate, fdev, suf, skip = middle(
-        z, ret_out, ret_dx, table, choose_wide, chances, mid, moe, cot, gpack, router_t, gate, y, sig, small,
-        w_out, mixed, dt, masks, normed
-    )
-    f_all = lax.all_gather(fdev, "seq")
+    (arrived,) = exchange("exp", E, [outbound.reshape(E, CAP, D)], [False], 3)
+    ret_out, ret_dx, dwu, dwd = expert(
+        z, where, arrived.reshape(E * CAP, D), cot_here, router_t, up_proj[0], down_proj[0]
+    )
+    (back_dx,) = exchange("exp", E, [ret_dx.reshape(E, CAP, -1)], [False], 4)
+    up_part, down_part = scatter_plane(dwu, dwd, S)
+    back_out = trade(ret_out.reshape(E, CAP, D)).reshape(E * CAP, D)
+    mid_grad, branch, ggrad, yg, gate_grad, gated, fdev, suf, skip = middle(
+        z, back_dx.reshape(E * CAP, -1), table, choose_wide, chances, mid, moe, cot, gpack, router_t, gate, y, sig,
+        small, w_out, mixed, dt, masks
+    )
+    (f_all,) = exchange("seq", S, [fdev], [True], 5)
+    gated_z = trade(columns(gated)).reshape(E * T, -1)
+    branch_all = lax.all_gather(branch, "exp", tiled=True)
+    gate_all = lax.all_gather(gate_grad, "exp", tiled=True)
+    out_rows = contract(gated_z, branch_all).astype(BF16)
+    gate_cols = contract(normed_z, gate_all).astype(BF16)
+    gating = jnp.sum(chances * choose_wide, axis=-1, keepdims=True)
+    output = (mid + gating * jnp.dot(table, back_out, preferred_element_type=F32)).astype(BF16)
     ssg, dpl, mixed_grad, gs = scan_backward(
         z, where, mixed, dt, sig, yg, masks, small, suf, f_all, s_all, states
     )
     cig, edge, gtop, gx = conv_backward(z, mixed_grad, sig, ssg, conv_in, hconv, masks, small, skip)
     edge_in = from_behind(edge, "seq", -1)
-    dw_conv, token_grad, ggrad = last(
-        z, cig, edge_in, gate_grad, normed, w_conv, w_gate, tok, mid_grad, gpack, ggrad
-    )
+    conv_grad, token_grad, ggrad = last(z, cig, edge_in, gate_grad, w_in, tok, mid_grad, gpack, ggrad)
+    (conv_all,) = gather_chain(E, [conv_grad], 6)
+    conv_cols = contract(normed_z, conv_all.reshape(E * T, DI)).astype(BF16)
+
     gsmall = jnp.concatenate([gtop + gs[0:8], gs[8:], gx], axis=0)
-
-    def reduce_rows(g):
-        part = lax.psum_scatter(g, "exp", scatter_dimension=0, tiled=True)
-        return lax.psum(part, "seq").astype(F32)
-
-    dw_in = reduce_rows(jnp.concatenate([dw_conv, dw_gate], axis=1))
-    dw_out = reduce_rows(dw_out)
-    gsmall = lax.psum(gsmall, ("seq", "exp"))
-    gsmall = lax.dynamic_slice_in_dim(gsmall, me_e * cw, cw, axis=1)
-    ggrad = lax.psum(ggrad, ("seq", "exp"))
-    dwid = norm_gain.shape[0]
-    ggrad = lax.dynamic_slice_in_dim(ggrad, me_e * dwid, dwid, axis=1)
+    blocks = lambda a: a.reshape(a.shape[0], E, -1).swapaxes(0, 1)
+    gpart = jnp.pad(blocks(ggrad), ((0, 0), (0, 0), (0, cw - dw)))
+    rows = z.SMALL + gr
+    pad = -rows % 128
+    smalls = jnp.concatenate(
+        [blocks(gsmall), gpart, jnp.zeros((E, pad, cw), F32)], axis=1
+    ).astype(BF16)
+    cols = jnp.concatenate([conv_cols, gate_cols], axis=1)
+    if plane:
+        each = cw // 8
+        each_pad = 16 * -(-each // 16)
+        padded = jnp.pad(out_rows.reshape(8, each, D), ((0, 0), (0, each_pad - each), (0, 0)))
+        dw_in, dw_out, gsum = reduce_plane(E, cols, padded, smalls, 7)
+        dw_out = dw_out[:, :each].reshape(cw, D)
+    else:
+        dw_in, dw_out = lax.psum(cols, "seq"), lax.psum(out_rows, "seq")
+        gsum = lax.psum_scatter(lax.psum(smalls, "seq"), "exp", scatter_dimension=0, tiled=True)[0]
+    gsum = gsum.astype(F32)
     return (
         from_chunks(output, J)[None],
         from_chunks(token_grad, J)[None],
-        ggrad[0],
-        dw_in,
-        gsmall[CONV_W : CONV_W + 4],
-        gsmall[CONV_B],
-        gsmall[z.X0 :].T,
-        gsmall[z.DT0 : z.X0],
-        gsmall[DT_B],
-        gsmall[A_LOG : A_LOG + N],
-        gsmall[SKIP],
-        dw_out,
-        ggrad[1],
-        ggrad[2 : 2 + E].T,
+        gsum[z.SMALL, :dw],
+        dw_in.astype(F32),
+        gsum[CONV_W : CONV_W + 4],
+        gsum[CONV_B],
+        gsum[z.X0 : z.SMALL].T,
+        gsum[z.DT0 : z.X0],
+        gsum[DT_B],
+        gsum[A_LOG : A_LOG + N],
+        gsum[SKIP],
+        dw_out.astype(F32),
+        gsum[z.SMALL + 1, :dw],
+        gsum[z.SMALL + 2 : z.SMALL + 2 + E, :dw].T,
         up_part[None],
         down_part[None],
     )
+
+
+def contract(a, b):
+    return lax.dot_general(a, b, (((0,), (0,)), ((), ())), preferred_element_type=F32)
+
+
+def scatter_plane(a, b, S):
+    if S != 8:
+        return [lax.psum_scatter(v, "seq", scatter_dimension=0, tiled=True).astype(F32) for v in (a, b)]
+    s = lax.axis_index("seq")
+    place = {1: lax.rem(s, 2), 2: lax.rem(s // 2, 2), 4: s // 4}
+
+    def halve(v, axis, bit):
+        keep = lax.dynamic_index_in_dim(v, place[bit], axis, keepdims=False)
+        give = lax.dynamic_index_in_dim(v, 1 - place[bit], axis, keepdims=False)
+        got = lax.ppermute(give, "seq", [(i, i ^ bit) for i in range(8)])
+        return keep.astype(F32) + got.astype(F32)
+
+    split = lambda v: v.reshape((2, 2, 2, v.shape[0] // 8) + v.shape[1:])
+    a, b = split(a), split(b)
+    a, b = halve(a, 2, 1).astype(BF16), halve(b, 2, 1).astype(BF16)
+    a, b = halve(a, 1, 2).astype(BF16), halve(b, 0, 4).astype(BF16)
+    return halve(a, 0, 4), halve(b, 0, 2)
 
 
 def solution(mesh):

time: 1100 us -> 663 us (0.60)
  waiting for transfers between devices: 696 us -> 25.9 us
  Pallas kernels: 121 us -> 470 us
  blocking collectives: 185 us -> 0 us
  local copies, waits for them, and re-layouts: 34.5 us -> 56.6 us
  starting transfers between devices: 15 us -> 35 us
  other arithmetic: 24.3 us -> 39.2 us
    pallas_call x0 -> x7, Pallas kernels: none -> 355 us  [the longest x1 139 us: gather_weights(): pl.pallas_call(body, name='gather_weights', in_specs=[ANY] * n, out_specs...]
    reduce_scatter x4 -> x0, waiting for transfers between devices: 339 us -> none  [the longest x2 210 us: reduce_rows(): part = lax.psum_scatter(g, 'exp', scatter_dimension=0, tiled=True)]
    psum x2 -> x0, waiting for transfers between devices: 174 us -> none  [the longest x1 93.8 us: on_device(): gsmall = lax.psum(gsmall, ('seq', 'exp'))]
    all_gather x2, waiting for transfers between devices: 168 us -> 0.01 us  [the longest x1 0.01 us: on_device(): branch_all = lax.all_gather(branch, 'exp', tiled=True)]
    all_gather x5 -> x0, blocking collectives: 108 us -> none  [the longest x1 40.9 us: on_device(): small = lax.all_gather(small_own, 'exp', axis=1, tiled=True).astype(F32)]
    psum x1 -> x0, blocking collectives: 38.7 us -> none  [on_device(): ggrad = lax.psum(ggrad, ('seq', 'exp'))]
    all_to_all x2 -> x0, blocking collectives: 38 us -> none  [trade(): lax.all_to_all(a.reshape(E, CAP, -1), 'exp', split_axis=0, concat_axis=0,...]
    slice x7 -> x6, local copies, waits for them, and re-layouts: 18 us -> 3.23 us  [the longest x1 0.69 us: on_device(): gsum[z.DT0:z.X0]]
  transfers between devices with their start and end apart: 13 -> 15, of which waited for: 10 -> 3; matrix products, arithmetic and copies ran while one was open for 4% -> 16% of each run, Pallas kernels for 8% -> 64%
where the time goes in v2:
time: 663 us; the launch traced here: 653 us
  Pallas kernels  470 us (71%)
  local copies, waits for them, and re-layouts  56.6 us (9%)
  other arithmetic  39.2 us (6%)
  starting transfers between devices  35 us (5%)
  waiting for transfers between devices  25.9 us (4%)
  between operations  14.5 us (2%)
  matrix products  11.8 us (2%)
    pallas_call x1, Pallas kernels, gather_weights(): pl.pallas_call(body, name='gather_weights', in_specs=[ANY] * n, out_specs...  139 us
    pallas_call x8, Pallas kernels, call(): pl.pallas_call(body, name=name, grid=grid, in_specs=in_specs, out_specs=o...  115 us
    pallas_call x1, Pallas kernels, reduce_plane(): pl.pallas_call(body, name='reduce_plane', in_specs=[ANY] * 3, out_specs=[...  93.4 us
    pallas_call x1, Pallas kernels, gather_chain(): pl.pallas_call(body, name='gather_chain', in_specs=[ANY] * n, out_specs=[...  69.2 us
    pallas_call x4, Pallas kernels, exchange(): pl.pallas_call(body, name='exchange_' + axis, in_specs=[ANY] * n, out_spe...  54 us
    all_to_all x4, starting transfers between devices, trade(): return lax.all_to_all(a, 'exp', split_axis=0, concat_axis=0, tiled=True)  24 us
    all_to_all x4, waiting for transfers between devices, trade(): return lax.all_to_all(a, 'exp', split_axis=0, concat_axis=0, tiled=True)  13.6 us
  transfers between devices with their start and end apart: 15, of which 3 were waited for; matrix products, arithmetic and copies ran while one was open for 16% of the time, Pallas kernels for 64%

profile of v2, /device:TPU:23, one launch (start us, length us, event | category | flops | bytes accessed | tf_op | source)
XLA Modules:
  0.0 653.4 jit_solution(6180089095782992890)
XLA Ops:
  13.6 2.2 convolution_convert_fusion.2
  15.8 4.6 all-to-all-start
  26.6 5.5 concatenate.26.refs_2_
  32.2 138.7 %gather_weights.1 = (bf16[4,288,4608]{2,1,0:T(8,128)(2,1)}, bf16[4,576,1152]{2,1,0:T(8,128)(2,1)}, bf16[4,224,576]{2,1,0:T(8,128)(2,1)}, bf16[4,32,288]{2,1,0:T(8,128)(2,1)}) custom-call(bf16[288,4608]{1,0:T(8,128)(2,1)} %refs_0_.1, bf16[576,1152]{1,0:T(8,128)(2,1)} %refs_1_.1, bf16[224,576]{1,0:T(8,128)(2,1)} %concatenate.26.refs_2_, ...), custom_call_target="tpu_custom_call" | custom-call | tf_op jit(solution)/shard_map/gather_weights/pallas_call | solution.py:332
  177.3 2.4 reshape.307.sm
  183.1 8.9 %front.1 = (bf16[128,1152]{1,0:T(8,128)(2,1)}, f32[128,2304]{1,0:T(8,128)}, f32[16,2304]{1,0:T(8,128)}, f32[128,2304]{1,0:T(8,128)}, bf16[128,2304]{1,0:T(8,128)(2,1)}, /*index=5*/f32[128,104]{1,0:T(8,128)}) custom-call(bf16[128,1152]{1,0:T(8,128)(2,1)} %bitcast.156, bf16[16,1152]{1,0:T(8,128)(2,1)} %copy-done.12, f32[128,8]{1,0:T(8,128)} %bitcast.160, ...), custom_call_target="tpu_custom_call" | custom-call | tf_op jit(solution)/shard_map/front/pallas_call | solution.py:70
  191.9 10.9 %summary.1 = (f32[128,2304]{1,0:T(8,128)}, f32[128,2304]{1,0:T(8,128)}, bf16[16,2304]{1,0:T(8,128)(2,1)}, f32[1,2304]{1,0:T(1,128)}, f32[16,2304]{1,0:T(8,128)}) custom-call(f32[128,104]{1,0:T(8,128)} %get-tuple-element.92.mix, bf16[128,2304]{1,0:T(8,128)(2,1)} %get-tuple-element.93.sg, f32[128,8]{1,0:T(8,128)} %bitcast.161, f32[200,2304]{1,0:T(8,128)} %reshape.307.sm), custom_call_target="tpu_custom_call" | custom-call | tf_op jit(solution)/shard_map/summary/pallas_call | solution.py:70
  202.8 12.6 %exchange_seq.2 = (bf16[8,16,2304]{2,1,0:T(8,128)(2,1)}, f32[8,1,2304]{2,1,0:T(1,128)}) custom-call(bf16[16,2304]{1,0:T(8,128)(2,1)} %get-tuple-element.98.refs_0_, f32[1,2304]{1,0:T(1,128)} %get-tuple-element.99.refs_1_), custom_call_target="tpu_custom_call" | custom-call | tf_op jit(solution)/shard_map/exchange_seq/pallas_call | solution.py:157
  215.4 18.2 %scan_forward.1 = (bf16[2176,2304]{1,0:T(8,128)(2,1)}, f32[128,2304]{1,0:T(8,128)}, f32[128,1152]{1,0:T(8,128)}, bf16[128,1152]{1,0:T(8,128)(2,1)}, f32[128,128]{1,0:T(8,128)}, /*index=5*/bf16[256,1152]{1,0:T(8,128)(2,1)}) custom-call(s32[2]{0:T(128)} %pad_add_fusion.1.wh, f32[128,104]{1,0:T(8,128)} %get-tuple-element.92.mix, ...), custom_call_target="tpu_custom_call" | custom-call | tf_op jit(solution)/shard_map/scan_forward/pallas_call | solution.py:70
  233.6 14.8 %exchange_exp.2 = bf16[4,64,1152]{2,1,0:T(8,128)(2,1)} custom-call(bf16[4,64,1152]{2,1,0:T(8,128)(2,1)} %bitcast.180), custom_call_target="tpu_custom_call" | custom-call | tf_op jit(solution)/shard_map/exchange_exp/pallas_call | solution.py:157
  249.3 19.6 %expert.1 = (bf16[256,1152]{1,0:T(8,128)(2,1)}, bf16[256,1280]{1,0:T(8,128)(2,1)}, bf16[1152,3072]{1,0:T(8,128)(2,1)}, bf16[3072,1152]{1,0:T(8,128)(2,1)}) custom-call(s32[2]{0:T(128)} %pad_add_fusion.1.wh, bf16[256,1152]{1,0:T(8,128)(2,1)} %bitcast.168, bf16[256,1152]{1,0:T(8,128)(2,1)} %bitcast.167, bf16[128,1152]{1,0:T(8,128)(2,1)} %scatter.14.rt, ...), custom_call_target="tpu_custom_call" | custom-call | tf_op jit(solution)/shard_map/expert/pallas_call | solution.py:70
  268.9 16.1 %exchange_exp.3 = bf16[4,64,1280]{2,1,0:T(8,128)(2,1)} custom-call(bf16[4,64,1280]{2,1,0:T(8,128)(2,1)} %bitcast.176), custom_call_target="tpu_custom_call" | custom-call | tf_op jit(solution)/shard_map/exchange_exp/pallas_call | solution.py:157
  285.0 15.5 %middle.1 = (f32[128,1152]{1,0:T(8,128)}, bf16[128,1152]{1,0:T(8,128)(2,1)}, f32[8,1152]{1,0:T(8,128)}, f32[128,2304]{1,0:T(8,128)}, bf16[128,2304]{1,0:T(8,128)...) custom-call(bf16[256,1280]{1,0:T(8,128)(2,1)} %bitcast.166, ...), custom_call_target="tpu_custom_call" | custom-call | tf_op jit(solution)/shard_map/middle/pallas_call | solution.py:70
  300.5 3.6 constant_dynamic-slice_fusion.1
  304.2 2.0 copy.88
  307.7 1.9 copy.58
  309.6 6.3 all-to-all-start.2
  316.0 13.6 %all-to-all-done.2 = bf16[4,128,288]{1,2,0:T(8,128)(2,1)} async-done(((bf16[4,128,288]{1,2,0:T(8,128)(2,1)}), bf16[4,128,288]{1,2,0:T(8,128)(2,1)}, u32[]{:S(2)}, u32[]{:S(2)}) %all-to-all-start.2) | async-done | bytes 294944 | tf_op jit(solution)/shard_map/all_to_all | solution.py:1566
  329.5 8.5 %all-to-all-start.1 = ((bf16[4,64,1152]{2,1,0:T(8,128)(2,1)}), bf16[4,64,1152]{2,1,0:T(8,128)(2,1)}, u32[]{:S(2)}, u32[]{:S(2)}) async-start(bf16[4,64,1152]{2,1,0:T(8,128)(2,1)} %bitcast.177), calls=%async_computation.1 | async-start | bytes 1179648 | tf_op jit(solution)/shard_map/all_to_all | solution.py:1566
  338.0 4.1 dynamic-slice_bitcast_fusion
  343.3 10.4 %exchange_seq.3.fa = bf16[8,16,2304]{2,1,0:T(8,128)(2,1)} custom-call(bf16[16,2304]{1,0:T(8,128)(2,1)} %get-tuple-element.112.refs_0_), custom_call_target="tpu_custom_call" | custom-call | tf_op jit(solution)/shard_map/exchange_seq/pallas_call | solution.py:157
  353.8 25.9 %scan_backward.1 = (f32[128,2304]{1,0:T(8,128)}, bf16[128,2304]{1,0:T(8,128)(2,1)}, bf16[128,104]{1,0:T(8,128)(2,1)}, f32[96,2304]{1,0:T(8,128)}) custom-call(s32[2]{0:T(128)} %pad_add_fusion.1.wh, f32[128,104]{1,0:T(8,128)} %get-tuple-element.92.mix, f32[128,2304]{1,0:T(8,128)} %get-tuple-element.94.dt_r, bf16[128,2304]{1,0:T(8,128)(2,1)} %get-tuple-element.93.sg, ...), custom_call_target="tpu_custom_call" | custom-call | tf_op jit(solution)/shard_map/scan_backward/pallas_call | solution.py:70
  379.7 6.5 conv_backward.1
  386.2 2.1 collective-permute-start.2
  388.3 2.1 copy.60
  390.4 2.0 convert.37
  392.5 1.9 slice.157
  396.0 4.5 all-to-all-start.3
  400.5 2.1 pad_maximum_fusion.1
  402.6 3.5 reshape.302
  406.1 2.3 copy.89
  408.4 9.7 %last.1 = (bf16[128,2304]{1,0:T(8,128)(2,1)}, f32[128,1152]{1,0:T(8,128)}, f32[8,1152]{1,0:T(8,128)}) custom-call(f32[128,2304]{1,0:T(8,128)} %get-tuple-element.119.cg, f32[8,2304]{1,0:T(8,128)} %collective-permute-done.2.eg, bf16[128,2304]{1,0:T(8,128)(2,1)} %get-tuple-element.121.gg, bf16[1152,4608]{1,0:T(8,128)(2,1)} %bitcast.143, ...), custom_call_target="tpu_custom_call" | custom-call | tf_op jit(solution)/shard_map/last/pallas_call | solution.py:70
  418.1 2.0 copy.57
  420.1 69.2 %gather_chain.1 = bf16[4,128,2304]{2,1,0:T(8,128)(2,1)} custom-call(bf16[128,2304]{1,0:T(8,128)(2,1)} %get-tuple-element.126.refs_0_), custom_call_target="tpu_custom_call" | custom-call | tf_op jit(solution)/shard_map/gather_chain/pallas_call | solution.py:407
  493.0 2.6 fusion.13
  495.6 3.0 fusion.2
  500.7 2.4 convolution_convert_fusion.1
  504.4 3.5 fusion.1
  509.3 3.2 fusion
  513.9 2.4 collective-permute-start.7
  516.3 2.7 convolution_convert_fusion
  519.0 1.7 pad_maximum_fusion.xi
  520.7 93.4 %reduce_plane.1 = (bf16[288,4608]{1,0:T(8,128)(2,1)}, bf16[4,2,80,1152]{3,2,1,0:T(8,128)(2,1)}, bf16[4,2,32,576]{3,2,1,0:T(8,128)(2,1)}) custom-call(bf16[288,4608]{1,0:T(8,128)(2,1)} %pad_maximum_fusion.xi, bf16[4,2,80,1152]{3,2,1,0:T(8,128)(2,1)} %bitcast.154, bf16[4,4,2,32,576]{4,3,2,1,0:T(8,128)(2,1)} %bitcast.155), custom_call_target="tpu_custom_call" | custom-call | tf_op jit(solution)/shard_map/reduce_plane/pallas_call | solution.py:557
  616.7 1.8 bitcast_convert_fusion
  619.6 2.1 fusion.4
  622.2 2.0 fusion.3
  627.9 3.0 convert_element_type.189
  631.5 11.4 %collective-permute-done.5 = bf16[144,3072]{1,0:T(8,128)(2,1)S(1)} collective-permute-done((bf16[144,3072]{1,0:T(8,128)(2,1)S(1)}, bf16[144,3072]{1,0:T(8,128)(2,1)S(1)}, u32[]{:S(2)}, u32[]{:S(2)}) %collective-permute-start.5) | collective-permute-done | bytes 884768 | tf_op jit(solution)/shard_map/ppermute | solution.py:1660
  (132 shorter events, 49.2 us)
Async XLA Ops:
  7.2 19.5 %copy-start.11 = (bf16[576,104]{0,1:T(8,128)(2,1)S(1)}, bf16[576,104]{0,1:T(8,128)(2,1)}, u32[]{:S(2)}) copy-start(bf16[576,104]{0,1:T(8,128)(2,1)} %param.30) | copy-start | bytes 359428
  8.0 174.4 %collective-permute-start = (bf16[16,1152]{1,0:T(8,128)(2,1)S(1)}, bf16[16,1152]{1,0:T(8,128)(2,1)S(1)}, u32[]{:S(2)}, u32[]{:S(2)}) collective-permute-start(bf16[16,1152]{1,0:T(8,128)(2,1)S(1)} %slice_bitcast_fusion.1), channel_id=1, source_target_pairs={{0,4},{4,8},{8,12},{12,16},{16,20},{20,24},{24,28},{1,5},{5,9},{9,... | collective-permute-start | bytes 110600 | tf_op jit(solution)/shard_map/ppermute | solution.py:1505
  10.0 171.2 %collective-permute-start.1 = (s32[3]{0:T(128)S(1)}, s32[3]{0:T(128)S(1)}, u32[]{:S(2)}, u32[]{:S(2)}) collective-permute-start(s32[3]{0:T(128)S(1)} %slice_bitcast_fusion.4), channel_id=1, source_target_pairs={{0,4},{4,8},{8,12},{12,16},{16,20},{20,24},{24,28},{1,5},{5,9},{9,... | collective-permute-start | bytes 44 | tf_op jit(solution)/shard_map/ppermute | solution.py:1505
  15.8 232.7 %all-to-all-start = ((bf16[4,64,1152]{2,1,0:T(8,128)(2,1)}), bf16[4,64,1152]{2,1,0:T(8,128)(2,1)S(1)}, u32[]{:S(2)}, u32[]{:S(2)}) async-start(bf16[4,64,1152]{2,1,0:T(8,128)(2,1)} %bitcast.22), calls=%async_computation | async-start | bytes 1179648 | tf_op jit(solution)/shard_map/all_to_all | solution.py:1566
  20.4 480.3 %all-gather.5.cloned.1.call-start = ((), (), s32[]{:S(2)}) async-start(), calls=%async_computation.5 | async-start | bytes 1474560 | tf_op jit(solution)/shard_map/all_gather | solution.py:1593
  32.2 140.9 %copy-start.8 = (bf16[1,128,1152]{2,1,0:T(8,128)(2,1)S(1)}, bf16[1,128,1152]{2,1,0:T(8,128)(2,1)}, u32[]{:S(2)}) copy-start(bf16[1,128,1152]{2,1,0:T(8,128)(2,1)} %param.25) | copy-start | bytes 884740
  32.2 141.7 %copy-start.9 = (bf16[1,128,1152]{2,1,0:T(8,128)(2,1)S(1)}, bf16[1,128,1152]{2,1,0:T(8,128)(2,1)}, u32[]{:S(2)}) copy-start(bf16[1,128,1152]{2,1,0:T(8,128)(2,1)} %param.22) | copy-start | bytes 884740
  177.3 3.9 copy-start.13
  182.4 0.6 copy-start.12
  248.5 0.8 copy-start.4
  306.2 198.2 %collective-permute-start.3 = (bf16[2,2,144,3072]{3,2,0,1:T(8,128)(2,1)}, bf16[2,2,144,3072]{3,2,0,1:T(8,128)(2,1)}, u32[]{:S(2)}, u32[]{:S(2)}) collective-permute-start(bf16[2,2,144,3072]{3,2,0,1:T(8,128)(2,1)} %bitcast.136), channel_id=1, source_target_pairs={{0,4},{4,0},{8,12},{12,8},{16,20},{20,16},{24,28},{28,24},{1,5},{5... | collective-permute-start | bytes 10616840 | tf_op jit(solution)/shard_map/ppermute | solution.py:1660
  309.6 19.9 %all-to-all-start.2 = ((bf16[4,128,288]{1,2,0:T(8,128)(2,1)}), bf16[4,128,288]{1,2,0:T(8,128)(2,1)}, u32[]{:S(2)}, u32[]{:S(2)}) async-start(bf16[4,128,288]{1,2,0:T(8,128)(2,1)} %bitcast.175), calls=%async_computation.2 | async-start | bytes 589824 | tf_op jit(solution)/shard_map/all_to_all | solution.py:1566
  329.5 66.4 %all-to-all-start.1 = ((bf16[4,64,1152]{2,1,0:T(8,128)(2,1)}), bf16[4,64,1152]{2,1,0:T(8,128)(2,1)}, u32[]{:S(2)}, u32[]{:S(2)}) async-start(bf16[4,64,1152]{2,1,0:T(8,128)(2,1)} %bitcast.177), calls=%async_computation.1 | async-start | bytes 1179648 | tf_op jit(solution)/shard_map/all_to_all | solution.py:1566
  338.0 178.3 %all-gather.3.cloned.1.call-start = ((), (), s32[]{:S(2)}) async-start(), calls=%async_computation.4 | async-start | bytes 2949120 | tf_op jit(solution)/shard_map/all_gather | solution.py:1594
  338.0 5.1 copy-start.10
  342.1 167.2 %collective-permute-start.6 = (bf16[2,2,384,1152]{3,2,1,0:T(8,128)(2,1)}, bf16[2,2,384,1152]{3,2,1,0:T(8,128)(2,1)}, u32[]{:S(2)}, u32[]{:S(2)}) collective-permute-start(bf16[2,2,384,1152]{3,2,1,0:T(8,128)(2,1)} %dynamic-slice_bitcast_fusion), channel_id=1, source_target_pairs={{0,4},{4,0},{8,12},{12,8},{16,20},{20,16},{24,28},{28,24},{1,5},{5... | collective-permute-start | bytes 10616840 | tf_op jit(solution)/shard_map/ppermute | solution.py:1660
  386.2 22.2 %collective-permute-start.2 = (f32[8,2304]{1,0:T(8,128)}, f32[8,2304]{1,0:T(8,128)}, u32[]{:S(2)}, u32[]{:S(2)}) collective-permute-start(f32[8,2304]{1,0:T(8,128)} %get-tuple-element.120), channel_id=1, source_target_pairs={{4,0},{8,4},{12,8},{16,12},{20,16},{24,20},{28,24},{5,1},{9,5},{13... | collective-permute-start | bytes 221192 | tf_op jit(solution)/shard_map/ppermute | solution.py:1505
  396.0 104.7 %all-to-all-start.3 = ((bf16[4,128,576]{1,2,0:T(8,128)(2,1)}), bf16[4,128,576]{1,2,0:T(8,128)(2,1)}, u32[]{:S(2)}, u32[]{:S(2)}) async-start(bf16[4,128,576]{1,2,0:T(8,128)(2,1)} %bitcast.169), calls=%async_computation.3 | async-start | bytes 1179648 | tf_op jit(solution)/shard_map/all_to_all | solution.py:1566
  492.1 3.5 copy-start.5
  495.6 3.0 copy-start.3
  504.3 5.0 slice-start
  504.3 5.0 slice-start.1
  507.8 4.7 copy-start
  509.3 109.2 %collective-permute-start.4 = (bf16[2,144,3072]{2,1,0:T(8,128)(2,1)}, bf16[2,144,3072]{2,1,0:T(8,128)(2,1)}, u32[]{:S(2)}, u32[]{:S(2)}) collective-permute-start(bf16[2,144,3072]{2,1,0:T(8,128)(2,1)} %dynamic-slice_bitcast_fusion.2), channel_id=1, source_target_pairs={{0,8},{4,12},{8,0},{12,4},{16,24},{20,28},{24,16},{28,20},{1,9},{5... | collective-permute-start | bytes 5308424 | tf_op jit(solution)/shard_map/ppermute | solution.py:1660
  513.9 108.3 %collective-permute-start.7 = (bf16[2,384,1152]{2,1,0:T(8,128)(2,1)}, bf16[2,384,1152]{2,1,0:T(8,128)(2,1)}, u32[]{:S(2)}, u32[]{:S(2)}) collective-permute-start(bf16[2,384,1152]{2,1,0:T(8,128)(2,1)} %dynamic-slice_bitcast_fusion.1), channel_id=1, source_target_pairs={{0,16},{4,20},{8,24},{12,28},{16,0},{20,4},{24,8},{28,12},{1,17},{... | collective-permute-start | bytes 5308424 | tf_op jit(solution)/shard_map/ppermute | solution.py:1660
  516.3 2.7 copy-start.6
  614.1 2.5 copy-start.7
  616.6 3.0 copy-start.1
  621.8 21.2 %collective-permute-start.5 = (bf16[144,3072]{1,0:T(8,128)(2,1)S(1)}, bf16[144,3072]{1,0:T(8,128)(2,1)S(1)}, u32[]{:S(2)}, u32[]{:S(2)}) collective-permute-start(bf16[144,3072]{1,0:T(8,128)(2,1)S(1)} %dynamic-slice_bitcast_fusion.4), channel_id=1, source_target_pairs={{0,16},{4,20},{8,24},{12,28},{16,0},{20,4},{24,8},{28,12},{1,17},{... | collective-permute-start | bytes 2654216 | tf_op jit(solution)/shard_map/ppermute | solution.py:1660
  622.2 5.7 copy-start.2
  624.4 20.9 %collective-permute-start.8 = (bf16[384,1152]{1,0:T(8,128)(2,1)S(1)}, bf16[384,1152]{1,0:T(8,128)(2,1)S(1)}, u32[]{:S(2)}, u32[]{:S(2)}) collective-permute-start(bf16[384,1152]{1,0:T(8,128)(2,1)S(1)} %dynamic-slice_bitcast_fusion.3), channel_id=1, source_target_pairs={{0,8},{4,12},{8,0},{12,4},{16,24},{20,28},{24,16},{28,20},{1,9},{5... | collective-permute-start | bytes 2654216 | tf_op jit(solution)/shard_map/ppermute | solution.py:1660
Sparse Core Ops, SparseCore 0:
  300.6 37.8 all-gather.4
  394.5 70.9 all-gather.2

commit v3 on v2

--- a/solution.py
+++ b/solution.py
@@ -128,8 +128,14 @@
 
     def body(*refs):
         xs, os = refs[:n], refs[n : 2 * n]
-        send, recv, own = refs[2 * n :]
+        send, recv, own = refs[2 * n : 2 * n + 3]
+        held = refs[2 * n + 3 :]
         me = lax.axis_index(axis)
+        ins = [
+            pltpu.make_async_copy(xs[a] if spread[a] else xs[a].at[me], held[a], own.at[a]) for a in range(n)
+        ]
+        for c in ins:
+            c.start()
         peers = [lax.rem(me + k, count) for k in range(1, count)]
         greet([{axis: p} for p in peers])
         copies = []
@@ -147,7 +153,8 @@
                 copies.append(c)
         locals_ = []
         for a in range(n):
-            c = pltpu.make_async_copy(xs[a] if spread[a] else xs[a].at[me], os[a].at[me], own.at[a])
+            ins[a].wait()
+            c = pltpu.make_async_copy(held[a], os[a].at[me], own.at[a])
             c.start()
             locals_.append(c)
         for c in locals_ + copies:
@@ -164,7 +171,8 @@
             pltpu.SemaphoreType.DMA((n, count - 1)),
             pltpu.SemaphoreType.DMA((n, count - 1)),
             pltpu.SemaphoreType.DMA((n,)),
-        ],
+        ]
+        + [pltpu.VMEM(b, a.dtype) for a, b in zip(arrays, blocks)],
         compiler_params=pltpu.CompilerParams(collective_id=cid, has_side_effects=True),
     )(*arrays)
 
@@ -178,7 +186,8 @@
 
     def body(*refs):
         xs, os = refs[:n], refs[n : 2 * n]
-        zs, zr, ps, pr, cs, cr, own = refs[2 * n :]
+        zs, zr, ps, pr, cs, cr, own = refs[2 * n : 2 * n + 7]
+        held = refs[2 * n + 7 :]
         s, me = lax.axis_index("seq"), lax.axis_index("exp")
         chip, core = s // 2, lax.rem(s, 2)
         sib = chip * 2 + (1 - core)
@@ -192,8 +201,9 @@
             [{"seq": s, "exp": right}, {"seq": s, "exp": left}, {"seq": sib, "exp": me}]
             + [{"seq": q * 2 + core, "exp": me} for q in chips]
         )
-        owns = [pltpu.make_async_copy(xs[a], os[a].at[me], own.at[a]) for a in range(n)]
-        for c in owns:
+        ins = [pltpu.make_async_copy(xs[a], held[a], own.at[a]) for a in range(n)]
+        owns = [pltpu.make_async_copy(held[a], os[a].at[me], own.at[a]) for a in range(n)]
+        for c in ins:
             c.start()
 
         def part(a, region, q):
@@ -271,6 +281,10 @@
         order = [(a, r) for a in range(n) for r in kinds(a)]
         for a, r in order:
             z_starts(a, r, 0)
+
+        for a in range(n):
+            ins[a].wait()
+            owns[a].start()
 
         def arrivals(k):
             for a, r in order:
@@ -338,84 +352,11 @@
         scratch_shapes=[
             sem(n, 2, slots), sem(n, 2, slots), sem(n, 3, slots), sem(n, 3, slots),
             sem(n, 5, slots), sem(n, 5, slots), sem(n),
-        ],
-        compiler_params=pltpu.CompilerParams(collective_id=cid, has_side_effects=True),
-    )(*arrays)
-
-
-def gather_chain(E, arrays, cid):
-    n = len(arrays)
-
-    def slot(d):
-        return 2 * (abs(d) - 1) + (1 if d > 0 else 0)
-
-    def body(*refs):
-        xs, os = refs[:n], refs[n : 2 * n]
-        zs, zr, own = refs[2 * n :]
-        me = lax.axis_index("exp")
-        right, left = lax.rem(me + 1, E), lax.rem(me + E - 1, E)
-        greet([{"exp": right}, {"exp": left}])
-
-        def exists(d):
-            return (me + d >= 0) & (me + d < E)
-
-        def copy(a, d, to_right):
-            there = slot(d - 1 if to_right else d + 1)
-            return pltpu.make_async_remote_copy(
-                xs[a] if d == 0 else os[a].at[me + d], os[a].at[me + d], zs.at[a, there], zr.at[a, there],
-                device_id={"exp": right if to_right else left}, device_id_type=MESH,
-            )
-
-        def arrival(a, d):
-            ref = os[a].at[me + d]
-            return pltpu.make_async_remote_copy(
-                ref, ref, zs.at[a, slot(d)], zr.at[a, slot(d)],
-                device_id={"exp": right}, device_id_type=MESH,
-            )
-
-        def each(a, d, act):
-            if d <= 0:
-                @pl.when(exists(d) & (me < E - 1))
-                def _():
-                    act(copy(a, d, True))
-            if d >= 0:
-                @pl.when(exists(d) & (me > 0))
-                def _():
-                    act(copy(a, d, False))
-
-        for a in range(n):
-            each(a, 0, lambda c: c.start())
-        owns = [pltpu.make_async_copy(xs[a], os[a].at[me], own.at[a]) for a in range(n)]
-        for c in owns:
-            c.start()
-        for k in range(1, E):
-            for a in range(n):
-                for d in (-k, k):
-                    @pl.when(exists(d))
-                    def _():
-                        arrival(a, d).wait_recv()
-                    if k < E - 1:
-                        each(a, d, lambda c: c.start())
-        for a in range(n):
-            for k in range(0, E - 1):
-                for d in (-k, k) if k else (0,):
-                    each(a, d, lambda c: c.wait_send())
-        for c in owns:
-            c.wait()
-
-    slots = 2 * (E - 1)
-    return pl.pallas_call(
-        body,
-        name="gather_chain",
-        in_specs=[ANY] * n,
-        out_specs=[ANY] * n,
-        out_shape=[sds((E,) + a.shape, a.dtype) for a in arrays],
-        scratch_shapes=[
-            pltpu.SemaphoreType.DMA((n, slots)),
-            pltpu.SemaphoreType.DMA((n, slots)),
-            pltpu.SemaphoreType.DMA((n,)),
-        ],
-        compiler_params=pltpu.CompilerParams(collective_id=cid, has_side_effects=True),
+        ]
+        + [pltpu.VMEM(a.shape, a.dtype) for a in arrays],
+        compiler_params=pltpu.CompilerParams(
+            collective_id=cid, has_side_effects=True, vmem_limit_bytes=VMEM_LIMIT
+        ),
     )(*arrays)
 
 
@@ -945,8 +886,8 @@
 def expert(z, where, x, cot, router, up, down):
     D, FF, E = z.D, z.FF, z.E
     M = x.shape[0]
-    fb = pick(FF, (512, 256, 128))
-    steps = FF // fb
+    fb = FF // 8
+    steps = 4
 
     def body(wh, x_r, c_r, rt, up_r, dn_r, ret_o, rdx_o, dwu_o, dwd_o, g_s, out_s, dx_s):
         i = pl.program_id(0)
@@ -974,379 +915,45 @@
 
         @pl.when(i == steps - 1)
         def _():
-            out = out_s[...].astype(BF16)
-            ret_o[...] = out
+            out = out_s[...]
+            ret_o[...] = out.astype(BF16)
             rdx_o[:, 0:D] = dx_s[...].astype(BF16)
-            gg = jnp.sum(out.astype(F32) * c_r[...].astype(F32), axis=-1, keepdims=True)
+            gg = jnp.sum(out * c_r[...].astype(F32), axis=-1, keepdims=True)
             hi, lo = split_hi_lo(gg)
             lane = lax.broadcasted_iota(jnp.int32, (M, LANES), 1)
             both = jnp.where(lane == 0, hi.astype(F32), jnp.where(lane == 1, lo.astype(F32), 0.0))
             rdx_o[:, D : D + LANES] = both.astype(BF16)
 
-    return call(
+    whole_ = lambda shape: pl.BlockSpec(shape, lambda i, w: (0,) * len(shape))
+    return pl.pallas_call(
         body,
-        "expert",
-        (steps,),
-        (where, x, cot, router, up, down),
-        [
-            pl.BlockSpec(memory_space=pltpu.SMEM),
-            whole(x.shape),
-            whole(cot.shape),
-            whole(router.shape),
-            block((D, fb), lambda i: (0, i)),
-            block((fb, D), lambda i: (i, 0)),
-        ],
-        [
+        name="expert",
+        grid_spec=pltpu.PrefetchScalarGridSpec(
+            num_scalar_prefetch=1,
+            grid=(steps,),
+            in_specs=[
+                whole_(x.shape),
+                whole_(cot.shape),
+                whole_(router.shape),
+                pl.BlockSpec((D, fb), lambda i, w: (0, 2 * i + w[2])),
+                pl.BlockSpec((fb, D), lambda i, w: (2 * i + w[2], 0)),
+            ],
+            out_specs=[
+                whole_((M, D)),
+                whole_((M, D + LANES)),
+                pl.BlockSpec((D, fb), lambda i, w: (0, i)),
+                pl.BlockSpec((fb, D), lambda i, w: (i, 0)),
+            ],
+            scratch_shapes=[pltpu.VMEM((M, D), BF16), pltpu.VMEM((M, D), F32), pltpu.VMEM((M, D), F32)],
+        ),
+        out_shape=[
             sds((M, D), BF16),
             sds((M, D + LANES), BF16),
-            sds((D, FF), BF16),
-            sds((FF, D), BF16),
+            sds((D, steps * fb), BF16),
+            sds((steps * fb, D), BF16),
         ],
-        [
-            whole((M, D)),
-            whole((M, D + LANES)),
-            block((D, fb), lambda i: (0, i)),
-            block((fb, D), lambda i: (i, 0)),
-        ],
-        [pltpu.VMEM((M, D), BF16), pltpu.VMEM((M, D), F32), pltpu.VMEM((M, D), F32)],
-    )
-
-
-def middle(z, ret_dx, table, choose, chances, mid, moe, cot, gpack, router, gate, y, sig,
-           small, w_out, mixed, dt, masks):
-    T, D, DI, N, J, E = z.T, z.D, z.DI, z.N, z.J, z.E
-    cb = pick(DI, (384, 256, 128))
-    tg = 1 if cb % 256 else 2
-    tg = 3 if cb == 384 else tg
-    ng = 4
-    steps = DI // cb
-    G = gpack.shape[0]
-
-    def body(rd, tb, cho, chn, md, me_r, ct, gp, rt, gt, yr, sg, sm, wo, mix, dt_r, msk,
-             mg_o, br, gg_o, yg_o, gi_o, gd_o, fdev_o, suf_o, skip_o,
-             cx, cl, rates_s, fd):
-        i = pl.program_id(0)
-
-        @pl.when(i == 0)
-        def _():
-            expand_columns(z, mix, z.R + N, cx)
-            expand_closed(z, msk, cl)
-            tbv = tb[...]
-            back = mm(tbv, rd[...])
-            grad = ct[...].astype(F32)
-            ch = chn[...]
-            pick_e = cho[...]
-            gating = jnp.sum(ch * pick_e, axis=-1, keepdims=True)
-            gate_grad = back[:, D : D + 1] + back[:, D + 1 : D + 2]
-            lg = ch * (gate_grad * pick_e - gate_grad * gating)
-            hi, lo = split_hi_lo(lg)
-            rtv = rt[...]
-            mig = back[:, 0:D] + mm(hi, rtv) + mm(lo, rtv)
-            mev = me_r[...]
-            rg = mm_tn(hi, mev) + mm_tn(lo, mev)
-            d, gain_g = rms_back(md[...], gp[1:2, :], mig)
-            total = grad + d
-            mg_o[...] = total
-            br[...] = total.astype(BF16)
-            gg_o[...] = jnp.zeros_like(gg_o)
-            gg_o[1:2, :] = gain_g
-            gg_o[2 : 2 + E, :] = rg[0:E, :]
-
-        gg = mm_nt(br[...], wo[...])
-        g_in = gt[...]
-        s = sigmoid(g_in)
-        act = g_in * s
-        yv = yr[...]
-        yg = gg * act
-        yg_o[...] = yg
-        gi = (gg * yv * (s * (1.0 + g_in * (1.0 - s)))).astype(BF16)
-        gi_o[...] = gi
-        gd_o[...] = (yv * act).astype(BF16)
-        skip_o[...] = jnp.sum(yg * sg[...].astype(F32), axis=0, keepdims=True)
-        rates_s[...] = -jnp.exp(sm[A_LOG : A_LOG + N, :]) * LOG2E
-
-        lanes = [slice(k * LANES, (k + 1) * LANES) for k in range(tg)]
-        for p in range(cb // (tg * LANES)):
-            wins = []
-            for k in range(tg):
-                tot = jnp.zeros((SUB, LANES), F32)
-                for j in range(J):
-                    tot = tot + (dt_r[j * SUB : j * SUB + SUB, lanes[k]] + cl[j * SUB : j * SUB + SUB, :])
-                w1 = tot
-                w2 = w1 + shift_up(w1, 1)
-                w4 = w2 + shift_up(w2, 2)
-                w8 = w4 + shift_up(w4, 4)
-                wins.append((w1, w2, w4))
-                suf_o[N * SUB : (N + 1) * SUB, lanes[k]] = shift_up(w8, 1)
-            for g in range(0, N, ng):
-                rr = [
-                    [jnp.broadcast_to(rates_s[g + n : g + n + 1, lanes[k]], (SUB, LANES)) for k in range(tg)]
-                    for n in range(ng)
-                ]
-
-                def step_j(jj, fs):
-                    j = J - 1 - jj
-                    dts = [dt_r[row8(j), lanes[k]] + cl[row8(j), :] for k in range(tg)]
-                    ygs = [yg_o[row8(j), lanes[k]] for k in range(tg)]
-                    new = []
-                    for n in range(ng):
-                        c = cx[row8(j * N + g + n), :]
-                        for k in range(tg):
-                            new.append(
-                                jnp.exp2(dts[k] * rr[n][k]) * (fs[n * tg + k] + ygs[k] * c)
-                            )
-                    return tuple(new)
-
-                fs = lax.fori_loop(
-                    0, J, step_j, tuple(jnp.zeros((SUB, LANES), F32) for _ in range(ng * tg)), unroll=2
-                )
-                for n in range(ng):
-                    for k in range(tg):
-                        f = fs[n * tg + k]
-                        w1, w2, w4 = wins[k]
-                        r = rr[n][k]
-                        f = f + jnp.exp2(r * w1) * shift_up(f, 1)
-                        f = f + jnp.exp2(r * w2) * shift_up(f, 2)
-                        f = f + jnp.exp2(r * w4) * shift_up(f, 4)
-                        at = (g + n) * SUB
-                        suf_o[at : at + SUB, lanes[k]] = shift_up(f, 1)
-                        fd[g + n : g + n + 1, lanes[k]] = f[0:1, :]
-        fdev_o[...] = fd[...].astype(BF16)
-
-    assert cb == tg * LANES
-    col = lambda r: block((r, cb), lambda i: (0, i))
-    row = lambda c: block((cb, c), lambda i: (i, 0))
-    return call(
-        body,
-        "middle",
-        (steps,),
-        (ret_dx, table, choose, chances, mid, moe, cot, gpack, router, gate, y, sig, small,
-         w_out, mixed, dt, masks),
-        [
-            whole(ret_dx.shape),
-            whole(table.shape),
-            whole(choose.shape),
-            whole(chances.shape),
-            whole(mid.shape),
-            whole(moe.shape),
-            whole(cot.shape),
-            whole(gpack.shape),
-            whole(router.shape),
-            col(T),
-            col(T),
-            col(T),
-            col(z.SMALL),
-            row(D),
-            whole(mixed.shape),
-            col(T),
-            whole(masks.shape),
-        ],
-        [
-            sds((T, D), F32),
-            sds((T, D), BF16),
-            sds((G, D), F32),
-            sds((T, DI), F32),
-            sds((T, DI), BF16),
-            sds((T, DI), BF16),
-            sds((N, DI), BF16),
-            sds(((N + 1) * SUB, DI), F32),
-            sds((1, DI), F32),
-        ],
-        [
-            whole((T, D)),
-            whole((T, D)),
-            whole((G, D)),
-            col(T),
-            col(T),
-            col(T),
-            col(N),
-            col((N + 1) * SUB),
-            col(1),
-        ],
-        [
-            pltpu.VMEM((J * N * SUB, LANES), F32),
-            pltpu.VMEM((T, LANES), F32),
-            pltpu.VMEM((N, cb), F32),
-            pltpu.VMEM((N, cb), F32),
-        ],
-    )
-
-
-def scan_backward(z, where, mixed, dt, sig, yg, masks, small, suf, f_all, s_all, states):
-    T, DI, N, J = z.T, z.DI, z.N, z.J
-    cb = pick(DI, (768, 384, 256, 128))
-    tg = tile_groups(cb)
-    ng = 4
-    S = f_all.shape[0]
-    steps = DI // cb
-
-    def body(wh, mix, dt_r, sg, yr, msk, sm, sf, fa, sa, st, ssg_o, dpl_o, mg_o, gs_o,
-             bx, cx, cl, u_s, rates_s, fin, dg_s, rs_s, ia, oa, rt_s, low_s):
-        i = pl.program_id(0)
-
-        @pl.when(i == 0)
-        def _():
-            expand_columns(z, mix, z.R, bx)
-            expand_columns(z, mix, z.R + N, cx)
-            expand_closed(z, msk, cl)
-            ia[...] = jnp.zeros_like(ia)
-            oa[...] = jnp.zeros_like(oa)
-            low_s[...] = jnp.zeros_like(low_s)
-
-        me = wh[0]
-        rates2 = -jnp.exp(sm[A_LOG : A_LOG + N, :]) * LOG2E
-        rates_s[...] = rates2
-        fin[...] = chain_states(
-            S - 1, lambda k: k > me, lambda k: S - 1 - k, lambda k: sa[k], lambda k: fa[k], rates2
-        )
-        sigf = sg[...].astype(F32)
-        u_s[...] = dt_r[...] * sigf
-
-        def pair(p, carry):
-            lanes = [lane_at(p, tg, k) for k in range(tg)]
-            for g in range(0, N, ng):
-                rr = [
-                    [jnp.broadcast_to(rates_s[g + n : g + n + 1, lanes[k]], (SUB, LANES)) for k in range(tg)]
-                    for n in range(ng)
-                ]
-                flow = []
-                for n in range(ng):
-                    for k in range(tg):
-                        at = (g + n) * SUB
-                        flow.append(
-                            sf[at : at + SUB, lanes[k]]
-                            + jnp.exp2(rr[n][k] * sf[N * SUB : (N + 1) * SUB, lanes[k]])
-                            * jnp.broadcast_to(fin[g + n : g + n + 1, lanes[k]], (SUB, LANES))
-                        )
-
-                def load(j):
-                    got = [[None] * tg for _ in range(ng)]
-                    for n in range(0, ng, 2):
-                        for k in range(tg):
-                            at = pl.multiple_of(j * N * SUB + (g + n) * SUB, 2 * SUB)
-                            two = st[pl.ds(at, 2 * SUB), lanes[k]].astype(F32)
-                            got[n][k] = two[0:SUB]
-                            got[n + 1][k] = two[SUB : 2 * SUB]
-                    return [got[n][k] for n in range(ng) for k in range(tg)]
-
-                def step_j(jj, carry):
-                    fs, hs, rts = carry
-                    j = J - 1 - jj
-                    dtp = [dt_r[row8(j), lanes[k]] for k in range(tg)]
-                    dts = [dtp[k] + cl[row8(j), :] for k in range(tg)]
-                    us = [u_s[row8(j), lanes[k]] for k in range(tg)]
-                    ygs = [yr[row8(j), lanes[k]] for k in range(tg)]
-                    before = load(j)
-                    if g == 0:
-                        dgs = [jnp.zeros((SUB, LANES), F32) for k in range(tg)]
-                        rss = [jnp.zeros((SUB, LANES), F32) for k in range(tg)]
-                    else:
-                        dgs = [dg_s[row8(j), lanes[k]] for k in range(tg)]
-                        rss = [rs_s[row8(j), lanes[k]] for k in range(tg)]
-                    nf, nr = [], []
-                    for n in range(ng):
-                        at = row8(j * N + g + n)
-                        b = bx[at, :]
-                        c = cx[at, :]
-                        ig = jnp.zeros((SUB, LANES), F32)
-                        og = jnp.zeros((SUB, LANES), F32)
-                        for k in range(tg):
-                            q = n * tg + k
-                            grad = ygs[k] * c + fs[q]
-                            f = jnp.exp2(dts[k] * rr[n][k]) * grad
-                            rt = f * before[q]
-                            rss[k] = rss[k] + rt * rr[n][k]
-                            dgs[k] = dgs[k] + grad * b
-                            nr.append(rts[q] + rt * dtp[k])
-                            ig = ig + grad * us[k]
-                            og = og + hs[q] * ygs[k]
-                            nf.append(f)
-                        ia[at, :] += ig
-                        oa[at, :] += og
-                    for k in range(tg):
-                        dg_s[row8(j), lanes[k]] = dgs[k]
-                        rs_s[row8(j), lanes[k]] = rss[k]
-                    return tuple(nf), tuple(before), tuple(nr)
-
-                zero = tuple(jnp.zeros((SUB, LANES), F32) for _ in range(ng * tg))
-                _, _, rts = lax.fori_loop(
-                    0, J, step_j, (tuple(flow), tuple(load(J)), zero), unroll=2
-                )
-                for n in range(ng):
-                    for k in range(tg):
-                        rt_s[g + n : g + n + 1, lanes[k]] = jnp.sum(rts[n * tg + k], axis=0, keepdims=True)
-            return carry
-
-        lax.fori_loop(0, cb // (tg * LANES), pair, 0)
-        dg = dg_s[...]
-        ssg_o[...] = dg * dt_r[...] + yr[...] * sm[SKIP : SKIP + 1, :]
-        step_grad = rs_s[...] * LN2 + dg * sigf
-        low = mix[:, 0 : z.R].astype(BF16)
-        dtw = sm[z.DT0 : z.DT0 + z.R, :].astype(BF16)
-        pre = mm(low, dtw) + sm[DT_B : DT_B + 1, :]
-        dpg = step_grad * sigmoid(pre)
-        dpl = dpg.astype(BF16)
-        dpl_o[...] = dpl
-        gs_o[...] = jnp.zeros_like(gs_o)
-        gs_o[DT_B : DT_B + 1, :] = jnp.sum(dpg, axis=0, keepdims=True)
-        gs_o[A_LOG : A_LOG + N, :] = rt_s[...] * (rates2 * LN2)
-        gs_o[z.DT0 : z.DT0 + z.R, :] = mm_tn(low, dpl)
-        low_s[...] += mm_nt(dpl, dtw)
-
-        @pl.when(i == steps - 1)
-        def _():
-            mg_o[:, 0 : z.R] = low_s[...].astype(BF16)
-            lane = lax.broadcasted_iota(jnp.int32, (SUB, LANES), 1)
-
-            def gather(j, carry):
-                both = jnp.zeros((SUB, LANES), F32)
-                for n in range(N):
-                    at = row8(j * N + n)
-                    both = jnp.where(lane == n, jnp.sum(ia[at, :], axis=1, keepdims=True), both)
-                    both = jnp.where(lane == N + n, jnp.sum(oa[at, :], axis=1, keepdims=True), both)
-                cl[row8(j), :] = both
-                return carry
-
-            lax.fori_loop(0, J, gather, 0)
-            mg_o[:, z.R : z.R + 2 * N] = cl[:, 0 : 2 * N].astype(BF16)
-
-    col = lambda r: block((r, cb), lambda i: (0, i))
-    wide = lambda: pltpu.VMEM((J * N * SUB, LANES), F32)
-    return call(
-        body,
-        "scan_backward",
-        (steps,),
-        (where, mixed, dt, sig, yg, masks, small, suf, f_all, s_all, states),
-        [
-            pl.BlockSpec(memory_space=pltpu.SMEM),
-            whole(mixed.shape),
-            col(T),
-            col(T),
-            col(T),
-            whole(masks.shape),
-            col(z.SMALL),
-            col((N + 1) * SUB),
-            block((S, N, cb), lambda i: (0, 0, i)),
-            block((S, 1, cb), lambda i: (0, 0, i)),
-            col((J + 1) * N * SUB),
-        ],
-        [sds((T, DI), F32), sds((T, DI), BF16), sds((T, z.XW), BF16), sds((z.X0, DI), F32)],
-        [col(T), col(T), whole((T, z.XW)), col(z.X0)],
-        [
-            wide(),
-            wide(),
-            pltpu.VMEM((T, LANES), F32),
-            pltpu.VMEM((T, cb), F32),
-            pltpu.VMEM((N, cb), F32),
-            pltpu.VMEM((N, cb), F32),
-            pltpu.VMEM((T, cb), F32),
-            pltpu.VMEM((T, cb), F32),
-            wide(),
-            wide(),
-            pltpu.VMEM((N, cb), F32),
-            pltpu.VMEM((T, z.R), F32),
-        ],
-    )
+        compiler_params=pltpu.CompilerParams(vmem_limit_bytes=VMEM_LIMIT),
+    )(where, x, cot, router, up, down)
 
 
 def padded_rows(main, edge, J, cb):
@@ -1366,129 +973,666 @@
     return jnp.concatenate([tail, m3], axis=0)
 
 
-def conv_backward(z, mixed_grad, sig, ssg, conv_in, hconv, masks, small, skip):
-    T, DI, J = z.T, z.DI, z.J
+def at_cols(i, cb):
+    return pl.ds(pl.multiple_of(i * cb, LANES), cb)
+
+
+def lanes_of(i, cb, p, tg, k):
+    return pl.ds(pl.multiple_of(i * cb + p * tg * LANES, LANES) + k * LANES, LANES)
+
+
+class Chain:
+    def __init__(self, E, src, dst, send, recv, own):
+        self.E, self.src, self.dst, self.send, self.recv, self.own = E, src, dst, send, recv, own
+        self.me = lax.axis_index("exp")
+        self.right, self.left = lax.rem(self.me + 1, E), lax.rem(self.me + E - 1, E)
+
+    def slot(self, d):
+        return 2 * (abs(d) - 1) + (1 if d > 0 else 0)
+
+    def exists(self, d):
+        return (self.me + d >= 0) & (self.me + d < self.E)
+
+    def each(self, d, act):
+        for to_right in (True, False):
+            if (d <= 0) if to_right else (d >= 0):
+                edge = self.me < self.E - 1 if to_right else self.me > 0
+                there = self.slot(d - 1 if to_right else d + 1)
+
+                @pl.when(self.exists(d) & edge)
+                def _():
+                    act(
+                        pltpu.make_async_remote_copy(
+                            self.src if d == 0 else self.dst.at[self.me + d],
+                            self.dst.at[self.me + d],
+                            self.send.at[there],
+                            self.recv.at[there],
+                            device_id={"exp": self.right if to_right else self.left},
+                            device_id_type=MESH,
+                        )
+                    )
+
+    def local(self):
+        return pltpu.make_async_copy(self.src, self.dst.at[self.me], self.own)
+
+    def start(self):
+        self.each(0, lambda c: c.start())
+        self.local().start()
+
+    def hop(self, k):
+        for d in (-k, k):
+            ref = self.dst.at[self.me + d]
+
+            @pl.when(self.exists(d))
+            def _():
+                pltpu.make_async_remote_copy(
+                    ref, ref, self.send.at[self.slot(d)], self.recv.at[self.slot(d)],
+                    device_id={"exp": self.right}, device_id_type=MESH,
+                ).wait_recv()
+
+            if k < self.E - 1:
+                self.each(d, lambda c: c.start())
+
+    def finish(self):
+        for k in range(self.E - 1):
+            for d in (-k, k) if k else (0,):
+                self.each(d, lambda c: c.wait_send())
+        self.local().wait()
+
+
+def backward(z, S, plane, dxp, outp, dwu, dwd, states, w_out, w_in, table, choose, chances, mid, moe, cot, gpack,
+             router, gate, y, sig, small, mixed, dt, masks, conv_in, hconv, s_all, tok, cid):
+    T, D, DI, N, J, E, CAP = z.T, z.D, z.DI, z.N, z.J, z.E, z.CAP
+    M = E * CAP
+    G = gpack.shape[0]
     H = hconv.shape[0]
-    cb = pick(DI, (384, 256, 128))
-    steps = DI // cb
-
-    def body(mg, sg, ss, ci, hc, msk, sm, sk, cig_o, edge_o, gt_o, gx_o):
-        mgv = mg[...]
-        sgv = sg[...]
-        xw = sm[z.X0 : z.X0 + z.XW, :].astype(BF16)
-        gx_o[...] = mm_tn(mgv, sgv)
-        sgrad = ss[...] + mm(mgv, xw)
-        xpad = padded_rows(ci[...], hc[...], J, cb)
-        valid = [jnp.broadcast_to(msk[:, o : o + 1], (T, cb)) for o in range(4)]
-        out = jnp.broadcast_to(sm[CONV_B : CONV_B + 1, :], (T, cb))
-        for o in range(4):
-            out = out + sm[CONV_W + o : CONV_W + o + 1, :] * xpad[o : o + J].reshape(T, cb) * valid[o]
-        s = sigmoid(out)
-        cg = sgrad * (s * (1.0 + out * (1.0 - s)))
-        gt_o[CONV_B : CONV_B + 1, :] = jnp.sum(cg, axis=0, keepdims=True)
-        gt_o[DT_B : DT_B + 1, :] = jnp.zeros((1, cb), F32)
-        gt_o[SKIP : SKIP + 1, :] = sk[...]
-        gt_o[SKIP + 1 : SKIP + 2, :] = jnp.zeros((1, cb), F32)
-        total = jnp.zeros((J, SUB, cb), F32)
-        last = lax.broadcasted_iota(jnp.int32, (SUB, cb), 0) == SUB - 1
-        edges = [jnp.zeros((1, cb), F32) for _ in range(3)]
-        for o in range(4):
-            masked = cg * valid[o]
-            gt_o[CONV_W + o : CONV_W + o + 1, :] = jnp.sum(
-                masked * xpad[o : o + J].reshape(T, cb), axis=0, keepdims=True
+    DZ = DI // E
+    cb_m = pick(DI, (384, 256, 128))
+    cb_s = pick(DI, (768, 384, 256, 128))
+    steps_s = DI // cb_s
+    tg_s = tile_groups(cb_s)
+    ng_s = 4
+    uq, uc = dwu.shape[0] // 4, dwu.shape[1]
+    dq, dc = dwd.shape[0] // 4, dwd.shape[1]
+    ST = (J + 1) * N * SUB
+    rows_big = max(ST, 2 * D)
+    chain_slots = 2 * (E - 1)
+
+    def body(
+        dxp, outp, dwu, dwd, states, w_out, w_in, table, choose, chances, mid, moe, cot, gp, router, gate, y, sig,
+        small, mixed, dt, masks, conv_in, hconv, s_all, tok,
+        tg_o, gs_o, gg_o, back_o, gate_o, pc_o, br_o, gz_o, up_o, down_o,
+        big, wo_v, dx_a, dx_b, out_a, out_b, dx_z, yg, gi, gd, gz, br, mg, fdev, f_all, suf, ssg, dpl, cig, cg_edge,
+        edge_in, pc, bx, cx, ia, oa, cl, u_s, rates_s, fin, dg_s, rs_s, rt_s, low_s, mxg, acc, fd,
+        ua, ub, ub2, uf, da, db, db2,
+        ld, sw_s, sw_r, dz_s, dz_r, oz_s, oz_r, f_s, f_r, e_s, e_r, g_s, g_r, p_s, p_r, b_s, b_r, a_s, a_r, x_s, x_r,
+    ):
+        s, me = lax.axis_index("seq"), lax.axis_index("exp")
+        core = lax.rem(s, 2)
+        other = 1 - core
+        sib = {"seq": s + 1 - 2 * core}
+        seqs = [lax.rem(s + k, S) for k in range(1, S)]
+        zs = [lax.rem(me + k, E) for k in range(1, E)]
+        greet([{"seq": p} for p in seqs] + [{"exp": p} for p in zs])
+
+        def remote(src, dst, send, recv, to):
+            return pltpu.make_async_remote_copy(src, dst, send, recv, device_id=to, device_id_type=MESH)
+
+        swaps = [
+            remote(dxp.at[other], dx_b, sw_s.at[0], sw_r.at[0], sib),
+            remote(outp.at[other], out_b, sw_s.at[1], sw_r.at[1], sib),
+        ]
+        for c in swaps:
+            c.start()
+        loads = [
+            pltpu.make_async_copy(dxp.at[core], dx_a, ld.at[0]),
+            pltpu.make_async_copy(outp.at[core], out_a, ld.at[1]),
+            pltpu.make_async_copy(w_out, wo_v, ld.at[2]),
+        ]
+        for c in loads:
+            c.start()
+
+        def state_load(i):
+            half = pl.ds((i % 2) * cb_s, cb_s)
+            return pltpu.make_async_copy(
+                states.at[:, i * cb_s : (i + 1) * cb_s], big.at[0:ST, half], ld.at[3 + i % 2]
             )
-            c3 = (sm[CONV_W + o : CONV_W + o + 1, :] * masked).reshape(J, SUB, cb)
-            k = 3 - o
-            if k == 0:
-                total = total + c3
-            else:
-                wrap = jnp.stack(
-                    [jnp.where(last, 0.0, pltpu.roll(c3[t], SUB - 1, 0)) for t in range(k)]
+
+        state_load(0).start()
+        if plane:
+            chip = s // 2
+            xx, yy = lax.rem(chip, 2), chip // 2
+            to_x = {"seq": s + 2 - 4 * xx}
+            to_y = {"seq": s + 4 - 8 * yy}
+            u4 = lambda ref, v, w: ref.at[pl.ds(pl.multiple_of((2 * v + w) * uq, 16), uq)]
+            up1 = [
+                remote(u4(dwu, v, 1 - xx), ub.at[v], a_s.at[v], a_r.at[v], to_x) for v in range(2)
+            ]
+            d_half = lambda v: pl.ds(pl.multiple_of(v * 2 * dq, 16), 2 * dq)
+            down1 = remote(dwd.at[d_half(1 - yy)], db, a_s.at[2], a_r.at[2], to_y)
+            for c in up1 + [down1]:
+                c.start()
+            mine = [pltpu.make_async_copy(u4(dwu, v, xx), ua.at[v], ld.at[5 + v]) for v in range(2)]
+            mine.append(pltpu.make_async_copy(dwd.at[d_half(yy)], da, ld.at[7]))
+            for c in mine:
+                c.start()
+
+        adds = lambda a, b: (a.astype(F32) + b.astype(F32)).astype(BF16)
+        loads[0].wait()
+        swaps[0].wait()
+        dx_a[...] = adds(dx_a[...], dx_b[...])
+        block_of = lambda ref, p: ref.at[pl.ds(pl.multiple_of(p * CAP, 16), CAP)]
+        dx_moves = [
+            remote(block_of(dx_a, p), block_of(dx_z, me), dz_s.at[k], dz_r.at[k], {"exp": p})
+            for k, p in enumerate(zs)
+        ]
+        for c in dx_moves:
+            c.start()
+        here = pl.ds(pl.multiple_of(me * CAP, 16), CAP)
+        dx_z[here, :] = dx_a[here, :]
+        loads[1].wait()
+        swaps[1].wait()
+        out_a[...] = adds(out_a[...], out_b[...])
+        out_moves = [
+            remote(block_of(out_a, p), block_of(back_o, me), oz_s.at[k], oz_r.at[k], {"exp": p})
+            for k, p in enumerate(zs)
+        ]
+        for c in out_moves:
+            c.start()
+        back_own = pltpu.make_async_copy(block_of(out_a, me), block_of(back_o, me), ld.at[8])
+        back_own.start()
+        expand_columns(z, mixed, z.R, bx)
+        expand_columns(z, mixed, z.R + N, cx)
+        expand_closed(z, masks, cl)
+        for c in dx_moves:
+            c.wait()
+
+        back = mm(table[...], dx_z[...])
+        grad = cot[...].astype(F32)
+        ch = chances[...]
+        pick_e = choose[...]
+        gating = jnp.sum(ch * pick_e, axis=-1, keepdims=True)
+        gate_grad = back[:, D : D + 1] + back[:, D + 1 : D + 2]
+        lg = ch * (gate_grad * pick_e - gate_grad * gating)
+        hi, lo = split_hi_lo(lg)
+        rtv = router[...]
+        mig = back[:, 0:D] + mm(hi, rtv) + mm(lo, rtv)
+        mev = moe[...]
+        rg = mm_tn(hi, mev) + mm_tn(lo, mev)
+        d, gain_g = rms_back(mid[...], gp[1:2, :], mig)
+        mg[...] = grad + d
+        br[...] = mg[...].astype(BF16)
+        gg_o[...] = jnp.zeros_like(gg_o)
+        gg_o[1:2, :] = gain_g
+        gg_o[2 : 2 + E, :] = rg[0:E, :]
+        chain_b = Chain(E, br, br_o, b_s, b_r, ld.at[9])
+        loads[2].wait()
+
+        def middle_block(i, carry):
+            C = at_cols(i, cb_m)
+            gg = mm_nt(br[...], wo_v[C, :])
+            g_in = gate[:, C]
+            sg = sigmoid(g_in)
+            act = g_in * sg
+            yv = y[:, C]
+            ygv = gg * act
+            yg[:, C] = ygv
+            gi[:, C] = (gg * yv * (sg * (1.0 + g_in * (1.0 - sg)))).astype(BF16)
+            gd[:, C] = (yv * act).astype(BF16)
+            gs_o[SKIP : SKIP + 1, C] = jnp.sum(ygv * sig[:, C].astype(F32), axis=0, keepdims=True)
+            return carry
+
+        lax.fori_loop(0, DI // cb_m, middle_block, 0)
+        chain_g = Chain(E, gi, gate_o, g_s, g_r, ld.at[10])
+        chain_g.start()
+        chain_b.start()
+
+        tg, ng = 2 if DI % 256 == 0 else 1, 8
+        wide = tg * LANES
+
+        def flow_block(i, carry):
+            lanes = [pl.ds(pl.multiple_of(i * wide, LANES) + k * LANES, LANES) for k in range(tg)]
+            both = pl.ds(pl.multiple_of(i * wide, LANES), wide)
+            rates = -jnp.exp(small[A_LOG : A_LOG + N, both]) * LOG2E
+            wins = []
+            for k in range(tg):
+                w1 = jnp.zeros((SUB, LANES), F32)
+                for j in range(J):
+                    w1 = w1 + (dt[j * SUB : j * SUB + SUB, lanes[k]] + cl[j * SUB : j * SUB + SUB, :])
+                w2 = w1 + shift_up(w1, 1)
+                w4 = w2 + shift_up(w2, 2)
+                w8 = w4 + shift_up(w4, 4)
+                wins.append((w1, w2, w4))
+                suf[N * SUB : (N + 1) * SUB, lanes[k]] = shift_up(w8, 1)
+            for g in range(0, N, ng):
+                rr = [
+                    [
+                        jnp.broadcast_to(rates[g + n : g + n + 1, k * LANES : (k + 1) * LANES], (SUB, LANES))
+                        for k in range(tg)
+                    ]
+                    for n in range(ng)
+                ]
+
+                def step_j(jj, fs):
+                    j = J - 1 - jj
+                    dts = [dt[row8(j), lanes[k]] + cl[row8(j), :] for k in range(tg)]
+                    ygs = [yg[row8(j), lanes[k]] for k in range(tg)]
+                    new = []
+                    for n in range(ng):
+                        c = cx[row8(j * N + g + n), :]
+                        for k in range(tg):
+                            new.append(jnp.exp2(dts[k] * rr[n][k]) * (fs[n * tg + k] + ygs[k] * c))
+                    return tuple(new)
+
+                fs = lax.fori_loop(
+                    0, J, step_j, tuple(jnp.zeros((SUB, LANES), F32) for _ in range(ng * tg)), unroll=2
                 )
-                total = total + jnp.concatenate([c3[k:], wrap], axis=0)
-                for i in range(o, 3):
-                    edges[i] = edges[i] + c3[i - o, 0:1, :]
-        cig_o[...] = total.reshape(T, cb)
-        edge_o[...] = jnp.zeros_like(edge_o)
-        for i in range(3):
-            edge_o[i : i + 1, :] = edges[i]
-
-    col = lambda r: block((r, cb), lambda i: (0, i))
-    return call(
+                for n in range(ng):
+                    for k in range(tg):
+                        f = fs[n * tg + k]
+                        w1, w2, w4 = wins[k]
+                        r = rr[n][k]
+                        f = f + jnp.exp2(r * w1) * shift_up(f, 1)
+                        f = f + jnp.exp2(r * w2) * shift_up(f, 2)
+                        f = f + jnp.exp2(r * w4) * shift_up(f, 4)
+                        suf[(g + n) * SUB : (g + n + 1) * SUB, lanes[k]] = shift_up(f, 1)
+                        fd[g + n : g + n + 1, lanes[k]] = f[0:1, :]
+            return carry
+
+        lax.fori_loop(0, DI // wide, flow_block, 0)
+        fdev[...] = fd[...].astype(BF16)
+        f_moves = [
+            remote(fdev, f_all.at[s], f_s.at[k], f_r.at[k], {"seq": p}) for k, p in enumerate(seqs)
+        ]
+        for c in f_moves:
+            c.start()
+        f_all[s] = fdev[...]
+        for e in range(E):
+            gz[e] = gd[:, e * DZ : (e + 1) * DZ]
+        gz_moves = [remote(gz.at[p], gz_o.at[me], x_s.at[k], x_r.at[k], {"exp": p}) for k, p in enumerate(zs)]
+        for c in gz_moves:
+            c.start()
+        gz_own = pltpu.make_async_copy(gz.at[me], gz_o.at[me], ld.at[11])
+        gz_own.start()
+        chain_g.hop(1)
+        chain_b.hop(1)
+        if plane:
+            for c in mine + up1 + [down1]:
+                c.wait()
+            ua[...] = adds(ua[...], ub[...])
+            da[...] = adds(da[...], db[...])
+            up2 = remote(ua.at[1 - yy], ub2, a_s.at[3], a_r.at[3], to_y)
+            down2 = remote(
+                da.at[pl.ds(pl.multiple_of((1 - xx) * dq, 16), dq)], db2, a_s.at[4], a_r.at[4], to_x
+            )
+            up2.start()
+            down2.start()
+        for c in f_moves:
+            c.wait()
+
+        ia[...] = jnp.zeros_like(ia)
+        oa[...] = jnp.zeros_like(oa)
+        low_s[...] = jnp.zeros_like(low_s)
+        for i in range(steps_s):
+            state_load(i).wait()
+            if i + 1 < steps_s:
+                state_load(i + 1).start()
+            C = slice(i * cb_s, (i + 1) * cb_s)
+            base = (i % 2) * cb_s
+            rates2 = -jnp.exp(small[A_LOG : A_LOG + N, C]) * LOG2E
+            rates_s[...] = rates2
+            fin[...] = chain_states(
+                S - 1, lambda k: k > s, lambda k: S - 1 - k, lambda k: s_all[k, :, C], lambda k: f_all[k, :, C],
+                rates2,
+            )
+            sigf = sig[:, C].astype(F32)
+            u_s[...] = dt[:, C] * sigf
+
+            def pair(p, carry):
+                lanes = [lanes_of(i, cb_s, p, tg_s, k) for k in range(tg_s)]
+                near = [lane_at(p, tg_s, k) for k in range(tg_s)]
+                held = [
+                    pl.ds(base + pl.multiple_of(p * tg_s * LANES, LANES) + k * LANES, LANES) for k in range(tg_s)
+                ]
+                for g in range(0, N, ng_s):
+                    rr = [
+                        [
+                            jnp.broadcast_to(rates_s[g + n : g + n + 1, near[k]], (SUB, LANES))
+                            for k in range(tg_s)
+                        ]
+                        for n in range(ng_s)
+                    ]
+                    flow = []
+                    for n in range(ng_s):
+                        for k in range(tg_s):
+                            at = (g + n) * SUB
+                            flow.append(
+                                suf[at : at + SUB, lanes[k]]
+                                + jnp.exp2(rr[n][k] * suf[N * SUB : (N + 1) * SUB, lanes[k]])
+                                * jnp.broadcast_to(fin[g + n : g + n + 1, near[k]], (SUB, LANES))
+                            )
+
+                    def load(j):
+                        got = [[None] * tg_s for _ in range(ng_s)]
+                        for n in range(0, ng_s, 2):
+                            for k in range(tg_s):
+                                at = pl.multiple_of(j * N * SUB + (g + n) * SUB, 2 * SUB)
+                                two = big[pl.ds(at, 2 * SUB), held[k]].astype(F32)
+                                got[n][k] = two[0:SUB]
+                                got[n + 1][k] = two[SUB : 2 * SUB]
+                        return [got[n][k] for n in range(ng_s) for k in range(tg_s)]
+
+                    def step_j(jj, carry):
+                        fs, hs, rts = carry
+                        j = J - 1 - jj
+                        dtp = [dt[row8(j), lanes[k]] for k in range(tg_s)]
+                        dts = [dtp[k] + cl[row8(j), :] for k in range(tg_s)]
+                        us = [u_s[row8(j), near[k]] for k in range(tg_s)]
+                        ygs = [yg[row8(j), lanes[k]] for k in range(tg_s)]
+                        before = load(j)
+                        if g == 0:
+                            dgs = [jnp.zeros((SUB, LANES), F32) for k in range(tg_s)]
+                            rss = [jnp.zeros((SUB, LANES), F32) for k in range(tg_s)]
+                        else:
+                            dgs = [dg_s[row8(j), near[k]] for k in range(tg_s)]
+                            rss = [rs_s[row8(j), near[k]] for k in range(tg_s)]
+                        nf, nr = [], []
+                        for n in range(ng_s):
+                            at = row8(j * N + g + n)
+                            b = bx[at, :]
+                            c = cx[at, :]
+                            ig = jnp.zeros((SUB, LANES), F32)
+                            og = jnp.zeros((SUB, LANES), F32)
+                            for k in range(tg_s):
+                                q = n * tg_s + k
+                                gr = ygs[k] * c + fs[q]
+                                f = jnp.exp2(dts[k] * rr[n][k]) * gr
+                                rt = f * before[q]
+                                rss[k] = rss[k] + rt * rr[n][k]
+                                dgs[k] = dgs[k] + gr * b
+                                nr.append(rts[q] + rt * dtp[k])
+                                ig = ig + gr * us[k]
+                                og = og + hs[q] * ygs[k]
+                                nf.append(f)
+                            ia[at, :] += ig
+                            oa[at, :] += og
+                        for k in range(tg_s):
+                            dg_s[row8(j), near[k]] = dgs[k]
+                            rs_s[row8(j), near[k]] = rss[k]
+                        return tuple(nf), tuple(before), tuple(nr)
+
+                    zero = tuple(jnp.zeros((SUB, LANES), F32) for _ in range(ng_s * tg_s))
+                    _, _, rts = lax.fori_loop(
+                        0, J, step_j, (tuple(flow), tuple(load(J)), zero), unroll=2
+                    )
+                    for n in range(ng_s):
+                        for k in range(tg_s):
+                            rt_s[g + n : g + n + 1, near[k]] = jnp.sum(rts[n * tg_s + k], axis=0, keepdims=True)
+                return carry
+
+            lax.fori_loop(0, cb_s // (tg_s * LANES), pair, 0)
+            dg = dg_s[...]
+            ssg[:, C] = dg * dt[:, C] + yg[:, C] * small[SKIP : SKIP + 1, C]
+            step_grad = rs_s[...] * LN2 + dg * sigf
+            low = mixed[:, 0 : z.R].astype(BF16)
+            dtw = small[z.DT0 : z.DT0 + z.R, C].astype(BF16)
+            pre = mm(low, dtw) + small[DT_B : DT_B + 1, C]
+            dpg = step_grad * sigmoid(pre)
+            dpl = dpg.astype(BF16)
+            gs_o[DT_B : DT_B + 1, C] = jnp.sum(dpg, axis=0, keepdims=True)
+            gs_o[SKIP + 1 : SKIP + 2, C] = jnp.zeros((1, cb_s), F32)
+            gs_o[A_LOG : A_LOG + N, C] = rt_s[...] * (rates2 * LN2)
+            gs_o[z.DT0 : z.DT0 + z.R, C] = mm_tn(low, dpl)
+            low_s[...] += mm_nt(dpl, dtw)
+            if i + 2 <= E - 1:
+                chain_g.hop(i + 2)
+                chain_b.hop(i + 2)
+        for k in range(steps_s + 2, E):
+            chain_g.hop(k)
+            chain_b.hop(k)
+
+        mxg[:, 0 : z.R] = low_s[...].astype(BF16)
+        lane = lax.broadcasted_iota(jnp.int32, (SUB, LANES), 1)
+
+        def gather(j, carry):
+            both = jnp.zeros((SUB, LANES), F32)
+            for n in range(N):
+                at = row8(j * N + n)
+                both = jnp.where(lane == n, jnp.sum(ia[at, :], axis=1, keepdims=True), both)
+                both = jnp.where(lane == N + n, jnp.sum(oa[at, :], axis=1, keepdims=True), both)
+            cl[row8(j), :] = both
+            return carry
+
+        lax.fori_loop(0, J, gather, 0)
+        mxg[:, z.R : z.R + 2 * N] = cl[:, 0 : 2 * N].astype(BF16)
+
+        def weight_load(i):
+            half = pl.ds((i % 2) * cb_s, cb_s)
+            return [
+                pltpu.make_async_copy(
+                    w_in.at[:, h * DI + i * cb_s : h * DI + (i + 1) * cb_s], big.at[h * D : (h + 1) * D, half],
+                    ld.at[12 + 2 * (i % 2) + h],
+                )
+                for h in range(2)
+            ]
+
+        for c in weight_load(0):
+            c.start()
+
+        def conv_block(i, carry):
+            C = at_cols(i, cb_m)
+            mgv = mxg[...]
+            sgv = sig[:, C]
+            xw = small[z.X0 : z.X0 + z.XW, C].astype(BF16)
+            gs_o[z.X0 : z.X0 + z.XW, C] = mm_tn(mgv, sgv)
+            sgrad = ssg[:, C] + mm(mgv, xw)
+            xpad = padded_rows(conv_in[:, C], hconv[:, C], J, cb_m)
+            valid = [jnp.broadcast_to(masks[:, o : o + 1], (T, cb_m)) for o in range(4)]
+            out = jnp.broadcast_to(small[CONV_B : CONV_B + 1, C], (T, cb_m))
+            for o in range(4):
+                w = small[CONV_W + o : CONV_W + o + 1, C]
+                out = out + w * xpad[o : o + J].reshape(T, cb_m) * valid[o]
+            sv = sigmoid(out)
+            cg = sgrad * (sv * (1.0 + out * (1.0 - sv)))
+            gs_o[CONV_B : CONV_B + 1, C] = jnp.sum(cg, axis=0, keepdims=True)
+            total = jnp.zeros((J, SUB, cb_m), F32)
+            final = lax.broadcasted_iota(jnp.int32, (SUB, cb_m), 0) == SUB - 1
+            edges = [jnp.zeros((1, cb_m), F32) for _ in range(3)]
+            for o in range(4):
+                masked = cg * valid[o]
+                gs_o[CONV_W + o : CONV_W + o + 1, C] = jnp.sum(
+                    masked * xpad[o : o + J].reshape(T, cb_m), axis=0, keepdims=True
+                )
+                c3 = (small[CONV_W + o : CONV_W + o + 1, C] * masked).reshape(J, SUB, cb_m)
+                k = 3 - o
+                if k == 0:
+                    total = total + c3
+                else:
+                    wrap = jnp.stack(
+                        [jnp.where(final, 0.0, pltpu.roll(c3[t], SUB - 1, 0)) for t in range(k)]
+                    )
+                    total = total + jnp.concatenate([c3[k:], wrap], axis=0)
+                    for i2 in range(o, 3):
+                        edges[i2] = edges[i2] + c3[i2 - o, 0:1, :]
+            cig[:, C] = total.reshape(T, cb_m)
+            cg_edge[:, C] = jnp.concatenate(edges + [jnp.zeros((SUB - 3, cb_m), F32)], axis=0)
+            return carry
+
+        lax.fori_loop(0, DI // cb_m, conv_block, 0)
+        back_edge = remote(cg_edge, edge_in, e_s, e_r, {"seq": lax.rem(s + S - 1, S)})
+        back_edge.start()
+        if plane:
+            up2.wait()
+            down2.wait()
+            uf[...] = adds(ua[yy], ub2[...])
+            half_u = uq // 2
+            rows_u = lambda c: pl.ds(pl.multiple_of(c * half_u, 16), half_u)
+            up3 = remote(uf.at[rows_u(other)], up_o.at[core], a_s.at[5], a_r.at[5], sib)
+            up3.start()
+            up_own = pltpu.make_async_copy(uf.at[rows_u(core)], up_o.at[core], ld.at[16])
+            up_own.start()
+            down_o[...] = da[pl.ds(pl.multiple_of(xx * dq, 16), dq), :].astype(F32) + db2[...].astype(F32)
+        else:
+            down_o[...] = jnp.zeros_like(down_o)
+        back_edge.wait()
+        live = jnp.where(s < S - 1, 1.0, 0.0)
+
+        def fix_block(i, carry):
+            C = at_cols(i, cb_m)
+            c3 = cig[:, C].reshape(J, SUB, cb_m)
+            final = lax.broadcasted_iota(jnp.int32, (SUB, cb_m), 0) == SUB - 1
+            fixed = jnp.stack(
+                [
+                    c3[J - 3 + k]
+                    + jnp.where(final, jnp.broadcast_to(edge_in[k : k + 1, C] * live, (SUB, cb_m)), 0.0)
+                    for k in range(3)
+                ]
+            )
+            pc[:, C] = jnp.concatenate([c3[: J - 3], fixed], axis=0).reshape(T, cb_m).astype(BF16)
+            return carry
+
+        lax.fori_loop(0, DI // cb_m, fix_block, 0)
+        chain_p = Chain(E, pc, pc_o, p_s, p_r, ld.at[17])
+        chain_p.start()
+        acc[...] = jnp.zeros_like(acc)
+        for i in range(steps_s):
+            for c in weight_load(i):
+                c.wait()
+            if i + 1 < steps_s:
+                for c in weight_load(i + 1):
+                    c.start()
+            C = slice(i * cb_s, (i + 1) * cb_s)
+            half = slice((i % 2) * cb_s, (i % 2 + 1) * cb_s)
+            acc[...] += mm_nt(pc[:, C], big[0:D, half]) + mm_nt(gi[:, C], big[D : 2 * D, half])
+        d, gain_g = rms_back(tok[...].astype(F32), gp[0:1, :], acc[...])
+        tg_o[...] = mg[...] + d
+        gg_o[0:1, :] = gain_g
+        for k in range(1, E):
+            chain_p.hop(k)
+        for c in out_moves + gz_moves:
+            c.wait()
+        back_own.wait()
+        gz_own.wait()
+        if plane:
+            up3.wait()
+            up_own.wait()
+        for ch_ in (chain_g, chain_b, chain_p):
+            ch_.finish()
+
+    v = pltpu.VMEM
+    sem = lambda *dims: pltpu.SemaphoreType.DMA(dims)
+    vm = pl.BlockSpec(memory_space=pltpu.VMEM)
+    up_shape = (2, uq // 2, uc) if plane else (1, 16, LANES)
+    down_shape = (dq, dc) if plane else (16, LANES)
+    u_shape = (2, uq, uc) if plane else (2, 16, LANES)
+    d_shape = (2 * dq, dc) if plane else (32, LANES)
+    ins = (dxp, outp, dwu, dwd, states, w_out, w_in, table, choose, chances, mid, moe, cot, gpack, router, gate, y,
+           sig, small, mixed, dt, masks, conv_in, hconv, s_all, tok)
+    return pl.pallas_call(
         body,
-        "conv_backward",
-        (steps,),
-        (mixed_grad, sig, ssg, conv_in, hconv, masks, small, skip),
-        [
-            whole(mixed_grad.shape),
-            col(T),
-            col(T),
-            col(T),
-            col(H),
-            whole(masks.shape),
-            col(z.SMALL),
-            col(1),
+        name="backward",
+        in_specs=[ANY] * 7 + [vm] * (len(ins) - 7),
+        out_specs=[vm] * 3 + [ANY] * 5 + [ANY, vm],
+        out_shape=[
+            sds((T, D), F32),
+            sds((z.SMALL, DI), F32),
+            sds((G, D), F32),
+            sds((M, D), BF16),
+            sds((E, T, DI), BF16),
+            sds((E, T, DI), BF16),
+            sds((E, T, D), BF16),
+            sds((E, T, DZ), BF16),
+            sds(up_shape, BF16),
+            sds(down_shape, F32),
         ],
-        [sds((T, DI), F32), sds((SUB, DI), F32), sds((SUB, DI), F32), sds((z.XW, DI), F32)],
-        [col(T), col(SUB), col(SUB), col(z.XW)],
-        [],
-    )
-
-
-def last(z, cig, edge, gate_grad, w_in, tokens, mid_grad, gpack, ggrad):
-    T, D, DI, J = z.T, z.D, z.DI, z.J
-    cb = pick(DI, (384, 256, 128))
-    steps = DI // cb
-    G = gpack.shape[0]
-
-    def body(cg, eg, gg, wc, wg, tok, mg, gp, gpre, pc_o, tg_o, gn_o, acc):
-        i = pl.program_id(0)
-
-        @pl.when(i == 0)
-        def _():
-            acc[...] = jnp.zeros_like(acc)
-
-        c3 = cg[...].reshape(J, SUB, cb)
-        is_last = lax.broadcasted_iota(jnp.int32, (SUB, cb), 0) == SUB - 1
-        fixed = jnp.stack(
-            [
-                c3[J - 3 + k]
-                + jnp.where(is_last, jnp.broadcast_to(eg[k : k + 1, :], (SUB, cb)), 0.0)
-                for k in range(3)
-            ]
-        )
-        pc = jnp.concatenate([c3[: J - 3], fixed], axis=0).reshape(T, cb).astype(BF16)
-        pc_o[...] = pc
-        acc[...] += mm_nt(pc, wc[...]) + mm_nt(gg[...], wg[...])
-
-        @pl.when(i == steps - 1)
-        def _():
-            d, gain_g = rms_back(tok[...].astype(F32), gp[0:1, :], acc[...])
-            tg_o[...] = mg[...] + d
-            gn_o[...] = gpre[...]
-            gn_o[0:1, :] = gain_g
-
-    col = lambda r: block((r, cb), lambda i: (0, i))
-    return call(
+        scratch_shapes=[
+            v((rows_big, 2 * cb_s), BF16),
+            v((DI, D), BF16),
+            v((M, D + LANES), BF16), v((M, D + LANES), BF16), v((M, D), BF16), v((M, D), BF16),
+            v((M, D + LANES), BF16),
+            v((T, DI), F32), v((T, DI), BF16), v((T, DI), BF16), v((E, T, DZ), BF16),
+            v((T, D), BF16), v((T, D), F32),
+            v((N, DI), BF16), v((S, N, DI), BF16), v(((N + 1) * SUB, DI), F32),
+            v((T, DI), F32), v((SUB, LANES), F32), v((T, DI), F32), v((SUB, DI), F32), v((SUB, DI), F32),
+            v((T, DI), BF16),
+            v((J * N * SUB, LANES), F32), v((J * N * SUB, LANES), F32),
+            v((J * N * SUB, LANES), F32), v((J * N * SUB, LANES), F32),
+            v((T, LANES), F32), v((T, cb_s), F32), v((N, cb_s), F32), v((N, cb_s), F32),
+            v((T, cb_s), F32), v((T, cb_s), F32), v((N, cb_s), F32), v((T, z.R), F32), v((T, z.XW), BF16),
+            v((T, D), F32), v((N, DI), F32),
+            v(u_shape, BF16), v(u_shape, BF16), v(u_shape[1:], BF16), v(u_shape[1:], BF16),
+            v(d_shape, BF16), v(d_shape, BF16), v((d_shape[0] // 2, d_shape[1]), BF16),
+            sem(18), sem(2), sem(2), sem(E - 1), sem(E - 1), sem(E - 1), sem(E - 1), sem(S - 1), sem(S - 1),
+            pltpu.SemaphoreType.DMA, pltpu.SemaphoreType.DMA,
+            sem(chain_slots), sem(chain_slots), sem(chain_slots), sem(chain_slots), sem(chain_slots), sem(chain_slots),
+            sem(6), sem(6), sem(E - 1), sem(E - 1),
+        ],
+        compiler_params=pltpu.CompilerParams(
+            collective_id=cid, has_side_effects=True, vmem_limit_bytes=60 * 1024 * 1024
+        ),
+    )(*ins)
+
+
+def dispatch(E, S, outbound, cid):
+    CAP, D = outbound.shape[1:]
+
+    def body(x, o, zs_s, zs_r, c_s, c_r, own):
+        s, me = lax.axis_index("seq"), lax.axis_index("exp")
+        core = lax.rem(s, 2)
+        sib = {"seq": s + 1 - 2 * core}
+        zs = [lax.rem(me + k, E) for k in range(1, E)]
+        greet([sib] + [{"exp": p} for p in zs])
+        sends = [
+            pltpu.make_async_remote_copy(
+                x.at[p], o.at[core, me], zs_s.at[k], zs_r.at[k], device_id={"exp": p}, device_id_type=MESH
+            )
+            for k, p in enumerate(zs)
+        ]
+        for c in sends:
+            c.start()
+        local = pltpu.make_async_copy(x.at[me], o.at[core, me], own)
+        local.start()
+        passes = [
+            pltpu.make_async_remote_copy(
+                x.at[me], o.at[core, me], c_s.at[0], c_r.at[0], device_id=sib, device_id_type=MESH
+            )
+        ]
+        passes[0].start()
+        for k in range(1, E):
+            frm = lax.rem(me + E - k, E)
+            ref = o.at[core, frm]
+            pltpu.make_async_remote_copy(
+                ref, ref, zs_s.at[k - 1], zs_r.at[k - 1], device_id={"exp": frm}, device_id_type=MESH
+            ).wait_recv()
+            c = pltpu.make_async_remote_copy(
+                ref, ref, c_s.at[k], c_r.at[k], device_id=sib, device_id_type=MESH
+            )
+            c.start()
+            passes.append(c)
+        local.wait()
+        for c in sends:
+            c.wait_send()
+        for c in passes:
+            c.wait_send()
+        for k in range(E):
+            ref = o.at[1 - core, lax.rem(me + E - k, E)]
+            pltpu.make_async_remote_copy(
+                ref, ref, c_s.at[k], c_r.at[k], device_id=sib, device_id_type=MESH
+            ).wait_recv()
+
+    vm = pl.BlockSpec(memory_space=pltpu.VMEM)
+    return pl.pallas_call(
         body,
-        "last",
-        (steps,),
-        (cig, edge, gate_grad, w_in, w_in, tokens, mid_grad, gpack, ggrad),
-        [
-            col(T),
-            col(SUB),
-            col(T),
-            col(D),
-            block((D, cb), lambda i: (0, i + steps)),
-            whole(tokens.shape),
-            whole(mid_grad.shape),
-            whole(gpack.shape),
-            whole(ggrad.shape),
+        name="dispatch",
+        in_specs=[vm],
+        out_specs=vm,
+        out_shape=sds((2, E, CAP, D), outbound.dtype),
+        scratch_shapes=[
+            pltpu.SemaphoreType.DMA((E - 1,)), pltpu.SemaphoreType.DMA((E - 1,)),
+            pltpu.SemaphoreType.DMA((E,)), pltpu.SemaphoreType.DMA((E,)), pltpu.SemaphoreType.DMA,
         ],
-        [sds((T, DI), BF16), sds((T, D), F32), sds((G, D), F32)],
-        [col(T), whole((T, D)), whole((G, D))],
-        [pltpu.VMEM((T, D), F32)],
-    )
+        compiler_params=pltpu.CompilerParams(collective_id=cid, has_side_effects=True),
+    )(outbound)
 
 
 def to_chunks(a, J):
@@ -1514,7 +1658,8 @@
     z = Sizes(tokens, in_proj, dt_proj, x_proj, a_log, up_proj, E)
     T, D, DI, N, J, CAP = z.T, z.D, z.DI, z.N, z.J, z.CAP
     me_s, me_e = lax.axis_index("seq"), lax.axis_index("exp")
-    where = jnp.stack([me_s, me_e]).astype(jnp.int32)
+    core = lax.rem(me_s, 2)
+    where = jnp.stack([me_s, me_e, core]).astype(jnp.int32)
     halo = from_behind(tokens[0, T - J :], "seq", 1)
     seg = segment_ids[0]
     seg_tail = from_behind(seg[T - 3 :], "seq", 1)
@@ -1569,6 +1714,10 @@
         return a.reshape(T, E, -1).swapaxes(0, 1)
 
     cot_here = trade(cot_slots.reshape(E, CAP, D)).reshape(E * CAP, D)
+    cot_there = lax.ppermute(cot_here, "seq", [(i, i ^ 1) for i in range(S)])
+    cot_pair = jnp.where(
+        core == 0, jnp.concatenate([cot_here, cot_there]), jnp.concatenate([cot_there, cot_here])
+    )
 
     normed, conv_in, hconv, gate, sig, mixed = front(z, tok, halo, masks, gpack, w_in, small)
     normed_z = trade(columns(normed)).reshape(E * T, -1)
@@ -1577,35 +1726,33 @@
     states, y, mid, moe, chances, outbound = scan_forward(
         z, where, mixed, dt, sig, gate, masks, small, pre, dwin, h_all, s_all, w_out, tok, gpack, router_t, table
     )
-    (arrived,) = exchange("exp", E, [outbound.reshape(E, CAP, D)], [False], 3)
-    ret_out, ret_dx, dwu, dwd = expert(
-        z, where, arrived.reshape(E * CAP, D), cot_here, router_t, up_proj[0], down_proj[0]
+    arrived = dispatch(E, S, outbound.reshape(E, CAP, D), 3)
+    outp, dxp, dwu, dwd = expert(
+        z, where, arrived.reshape(2 * E * CAP, D), cot_pair, router_t, up_proj[0], down_proj[0]
     )
-    (back_dx,) = exchange("exp", E, [ret_dx.reshape(E, CAP, -1)], [False], 4)
-    up_part, down_part = scatter_plane(dwu, dwd, S)
-    back_out = trade(ret_out.reshape(E, CAP, D)).reshape(E * CAP, D)
-    mid_grad, branch, ggrad, yg, gate_grad, gated, fdev, suf, skip = middle(
-        z, back_dx.reshape(E * CAP, -1), table, choose_wide, chances, mid, moe, cot, gpack, router_t, gate, y, sig,
-        small, w_out, mixed, dt, masks
+    token_grad, gsmall, ggrad, back_out, gate_all, conv_all, branch_all, gated_z, up_sum, down_part = backward(
+        z, S, plane, dxp.reshape(2, E * CAP, -1), outp.reshape(2, E * CAP, D), dwu, dwd, states, w_out, w_in, table,
+        choose_wide, chances, mid, moe, cot, gpack, router_t, gate, y, sig, small, mixed, dt, masks, conv_in, hconv,
+        s_all, tok, 4
     )
-    (f_all,) = exchange("seq", S, [fdev], [True], 5)
-    gated_z = trade(columns(gated)).reshape(E * T, -1)
-    branch_all = lax.all_gather(branch, "exp", tiled=True)
-    gate_all = lax.all_gather(gate_grad, "exp", tiled=True)
-    out_rows = contract(gated_z, branch_all).astype(BF16)
-    gate_cols = contract(normed_z, gate_all).astype(BF16)
+    fb = z.FF // 8
+    if plane:
+        up_part = up_sum.reshape(2, D // 8, 4, fb).transpose(1, 2, 0, 3).reshape(D // 8, z.FF).astype(F32)
+    else:
+        up_full = jnp.zeros((D, 4, 2, fb), BF16)
+        up_full = lax.dynamic_update_slice_in_dim(up_full, dwu.reshape(D, 4, 1, fb), core, axis=2)
+        down_full = jnp.zeros((4, 2, fb, D), BF16)
+        down_full = lax.dynamic_update_slice_in_dim(down_full, dwd.reshape(4, 1, fb, D), core, axis=1)
+        up_part, down_part = [
+            lax.psum_scatter(v, "seq", scatter_dimension=0, tiled=True).astype(F32)
+            for v in (up_full.reshape(D, z.FF), down_full.reshape(z.FF, D))
+        ]
+    out_rows = contract(gated_z.reshape(E * T, -1), branch_all.reshape(E * T, D)).astype(BF16)
+    gate_cols = contract(normed_z, gate_all.reshape(E * T, DI)).astype(BF16)
+    conv_cols = contract(normed_z, conv_all.reshape(E * T, DI)).astype(BF16)
     gating = jnp.sum(chances * choose_wide, axis=-1, keepdims=True)
     output = (mid + gating * jnp.dot(table, back_out, preferred_element_type=F32)).astype(BF16)
-    ssg, dpl, mixed_grad, gs = scan_backward(
-        z, where, mixed, dt, sig, yg, masks, small, suf, f_all, s_all, states
-    )
-    cig, edge, gtop, gx = conv_backward(z, mixed_grad, sig, ssg, conv_in, hconv, masks, small, skip)
-    edge_in = from_behind(edge, "seq", -1)
-    conv_grad, token_grad, ggrad = last(z, cig, edge_in, gate_grad, w_in, tok, mid_grad, gpack, ggrad)
-    (conv_all,) = gather_chain(E, [conv_grad], 6)
-    conv_cols = contract(normed_z, conv_all.reshape(E * T, DI)).astype(BF16)
-
-    gsmall = jnp.concatenate([gtop + gs[0:8], gs[8:], gx], axis=0)
+
     blocks = lambda a: a.reshape(a.shape[0], E, -1).swapaxes(0, 1)
     gpart = jnp.pad(blocks(ggrad), ((0, 0), (0, 0), (0, cw - dw)))
     rows = z.SMALL + gr
@@ -1648,25 +1795,6 @@
     return lax.dot_general(a, b, (((0,), (0,)), ((), ())), preferred_element_type=F32)
 
 
-def scatter_plane(a, b, S):
-    if S != 8:
-        return [lax.psum_scatter(v, "seq", scatter_dimension=0, tiled=True).astype(F32) for v in (a, b)]
-    s = lax.axis_index("seq")
-    place = {1: lax.rem(s, 2), 2: lax.rem(s // 2, 2), 4: s // 4}
-
-    def halve(v, axis, bit):
-        keep = lax.dynamic_index_in_dim(v, place[bit], axis, keepdims=False)
-        give = lax.dynamic_index_in_dim(v, 1 - place[bit], axis, keepdims=False)
-        got = lax.ppermute(give, "seq", [(i, i ^ bit) for i in range(8)])
-        return keep.astype(F32) + got.astype(F32)
-
-    split = lambda v: v.reshape((2, 2, 2, v.shape[0] // 8) + v.shape[1:])
-    a, b = split(a), split(b)
-    a, b = halve(a, 2, 1).astype(BF16), halve(b, 2, 1).astype(BF16)
-    a, b = halve(a, 1, 2).astype(BF16), halve(b, 0, 4).astype(BF16)
-    return halve(a, 0, 4), halve(b, 0, 2)
-
-
 def solution(mesh):
     row = P("exp", "seq", None)
     in_specs = (

time: 663 us -> 491 us (0.74)
  Pallas kernels: 470 us -> 410 us
  local copies, waits for them, and re-layouts: 56.6 us -> 29.3 us
  waiting for transfers between devices: 25.9 us -> 0.01 us
  starting transfers between devices: 35 us -> 16.4 us
  other arithmetic: 39.2 us -> 20.7 us
  between operations: 14.5 us -> 1.2 us
    pallas_call x1 -> x3, Pallas kernels: 69.2 us -> 207 us  [the longest x1 162 us: backward(): pl.pallas_call(body, name='backward', in_specs=[ANY] * 7 + [vm] * (len(in...]
    pallas_call x8 -> x3, Pallas kernels: 115 us -> 38 us  [call(): pl.pallas_call(body, name=name, grid=grid, in_specs=in_specs, out_specs=o...]
    pallas_call x1, Pallas kernels: 139 us -> 83.7 us  [gather_weights(): pl.pallas_call(body, name='gather_weights', in_specs=[ANY] * n, out_specs...]
    pallas_call x4 -> x1, Pallas kernels: 54 us -> 11.7 us  [exchange(): pl.pallas_call(body, name='exchange_' + axis, in_specs=[ANY] * n, out_spe...]
    pallas_call x1, Pallas kernels: 93.4 us -> 70.2 us  [reduce_plane(): pl.pallas_call(body, name='reduce_plane', in_specs=[ANY] * 3, out_specs=[...]
    all_to_all x4 -> x2, waiting for transfers between devices: 13.6 us -> 0.01 us  [trade(): return lax.all_to_all(a, 'exp', split_axis=0, concat_axis=0, tiled=True)]
    ppermute x6 -> x1, waiting for transfers between devices: 12.3 us -> 0.01 us  [on_device(): cot_there = lax.ppermute(cot_here, 'seq', [(i, i ^ 1) for i in range(S)])]
    all_to_all x4 -> x2, starting transfers between devices: 24 us -> 12.4 us  [trade(): return lax.all_to_all(a, 'exp', split_axis=0, concat_axis=0, tiled=True)]
  transfers between devices with their start and end apart: 15 -> 5, of which waited for: 3 -> 0; matrix products, arithmetic and copies ran while one was open for 16% -> 6% of each run, Pallas kernels for 64% -> 70%
where the time goes in v3:
time: 491 us; the launch traced here: 487 us
  Pallas kernels  410 us (84%)
  local copies, waits for them, and re-layouts  29.3 us (6%)
  other arithmetic  20.7 us (4%)
  starting transfers between devices  16.4 us (3%)
  matrix products  8.63 us (2%)
    pallas_call x1, Pallas kernels, backward(): pl.pallas_call(body, name='backward', in_specs=[ANY] * 7 + [vm] * (len(in...  162 us
    pallas_call x1, Pallas kernels, gather_weights(): pl.pallas_call(body, name='gather_weights', in_specs=[ANY] * n, out_specs...  83.7 us
    pallas_call x1, Pallas kernels, reduce_plane(): pl.pallas_call(body, name='reduce_plane', in_specs=[ANY] * 3, out_specs=[...  70.2 us
    pallas_call x3, Pallas kernels, call(): pl.pallas_call(body, name=name, grid=grid, in_specs=in_specs, out_specs=o...  38 us
    pallas_call x1, Pallas kernels, dispatch(): pl.pallas_call(body, name='dispatch', in_specs=[vm], out_specs=vm, out_sh...  22.6 us
    pallas_call x1, Pallas kernels, expert(): pl.pallas_call(body, name='expert', grid_spec=pltpu.PrefetchScalarGridSpe...  22.5 us
    all_to_all x2, starting transfers between devices, trade(): return lax.all_to_all(a, 'exp', split_axis=0, concat_axis=0, tiled=True)  12.4 us
    pallas_call x1, Pallas kernels, exchange(): pl.pallas_call(body, name='exchange_' + axis, in_specs=[ANY] * n, out_spe...  11.7 us
  transfers between devices with their start and end apart: 5, of which 0 were waited for; matrix products, arithmetic and copies ran while one was open for 6% of the time, Pallas kernels for 70%

profile of v3, /device:TPU:23, one launch (start us, length us, event | category | flops | bytes accessed | tf_op | source)
XLA Modules:
  0.0 486.7 jit_solution(4501825679610142450)
XLA Ops:
  0.8 0.8 slice_bitcast_fusion.4
  1.6 1.3 collective-permute-start.1
  2.9 0.8 slice_bitcast_fusion.1
  3.7 1.3 collective-permute-start
  5.5 1.3 reduce.21
  7.2 2.2 convolution_convert_fusion
  9.4 4.6 all-to-all-start
  14.7 0.7 fusion.11.tb.table
  16.4 3.3 concatenate.28.refs_2_
  19.6 83.7 %gather_weights.1 = (bf16[4,288,4608]{2,1,0:T(8,128)(2,1)}, bf16[4,576,1152]{2,1,0:T(8,128)(2,1)}, bf16[4,224,576]{2,1,0:T(8,128)(2,1)}, bf16[4,32,288]{2,1,0:T(8,128)(2,1)}) custom-call(bf16[288,4608]{1,0:T(8,128)(2,1)} %refs_0_.1, bf16[576,1152]{1,0:T(8,128)(2,1)} %refs_1_.1, bf16[224,576]{1,0:T(8,128)(2,1)} %concatenate.28.refs_2_, ...), custom_call_target="tpu_custom_call" | custom-call | tf_op jit(solution)/shard_map/gather_weights/pallas_call | solution.py:346
  103.4 0.7 slice_bitcast_fusion.2
  104.1 0.7 fusion.12.choose
  104.8 0.8 copy.69
  105.7 1.4 convert_bitcast_fusion
  107.6 2.4 reshape.287.sm.small
  110.8 0.8 copy.70
  111.6 0.8 scatter.14.rt.router
  113.5 1.5 collective-permute-start.2
  115.0 0.7 copy.49
  116.4 8.9 %front.1 = (bf16[128,1152]{1,0:T(8,128)(2,1)}, f32[128,2304]{1,0:T(8,128)}, f32[16,2304]{1,0:T(8,128)}, f32[128,2304]{1,0:T(8,128)}, bf16[128,2304]{1,0:T(8,128)(2,1)}, /*index=5*/f32[128,104]{1,0:T(8,128)}) custom-call(bf16[128,1152]{1,0:T(8,128)(2,1)} %bitcast.105, bf16[16,1152]{1,0:T(8,128)(2,1)} %copy-done.12, f32[128,8]{1,0:T(8,128)} %bitcast.112, ...), custom_call_target="tpu_custom_call" | custom-call | tf_op jit(solution)/shard_map/front/pallas_call | solution.py:70
  125.2 10.9 %summary.1 = (f32[128,2304]{1,0:T(8,128)}, f32[128,2304]{1,0:T(8,128)}, bf16[16,2304]{1,0:T(8,128)(2,1)}, f32[1,2304]{1,0:T(1,128)}, f32[16,2304]{1,0:T(8,128)}) custom-call(f32[128,104]{1,0:T(8,128)} %get-tuple-element.83.mix.mixed, bf16[128,2304]{1,0:T(8,128)(2,1)} %get-tuple-element.84.sg.sig, f32[128,8]{1,0:T(8,128)} %bitcast.113, ...), custom_call_target="tpu_custom_call" | custom-call | tf_op jit(solution)/shard_map/summary/pallas_call | solution.py:70
  136.2 11.7 %exchange_seq.1 = (bf16[8,16,2304]{2,1,0:T(8,128)(2,1)}, f32[8,1,2304]{2,1,0:T(1,128)}) custom-call(bf16[16,2304]{1,0:T(8,128)(2,1)} %get-tuple-element.89.refs_0_, f32[1,2304]{1,0:T(1,128)} %get-tuple-element.90.refs_1_), custom_call_target="tpu_custom_call" | custom-call | tf_op jit(solution)/shard_map/exchange_seq/pallas_call | solution.py:164
  147.9 18.2 %scan_forward.1 = (bf16[2176,2304]{1,0:T(8,128)(2,1)}, f32[128,2304]{1,0:T(8,128)}, f32[128,1152]{1,0:T(8,128)}, bf16[128,1152]{1,0:T(8,128)(2,1)}, f32[128,128]{1,0:T(8,128)}, /*index=5*/bf16[256,1152]{1,0:T(8,128)(2,1)}) custom-call(s32[3]{0:T(128)} %pad_add_fusion.1.wh, f32[128,104]{1,0:T(8,128)} %get-tuple-element.83.mix.mixed, ...), custom_call_target="tpu_custom_call" | custom-call | tf_op jit(solution)/shard_map/scan_forward/pallas_call | solution.py:70
  166.1 22.6 %dispatch.1 = bf16[2,4,64,1152]{3,2,1,0:T(8,128)(2,1)} custom-call(bf16[4,64,1152]{2,1,0:T(8,128)(2,1)} %bitcast.123), custom_call_target="tpu_custom_call" | custom-call | tf_op jit(solution)/shard_map/dispatch/pallas_call | solution.py:1624
  188.7 0.9 copy.57
  189.6 7.7 %all-to-all-start.1 = ((bf16[4,128,288]{1,2,0:T(8,128)(2,1)}), bf16[4,128,288]{1,2,0:T(8,128)(2,1)S(1)}, u32[]{:S(2)}, u32[]{:S(2)}) async-start(bf16[4,128,288]{1,2,0:T(8,128)(2,1)} %bitcast.37), calls=%async_computation.1 | async-start | bytes 589824 | tf_op jit(solution)/shard_map/all_to_all | solution.py:1711
  197.5 1.5 maximum_select_fusion.c_r
  199.0 22.5 %expert.1 = (bf16[512,1152]{1,0:T(8,128)(2,1)}, bf16[512,1280]{1,0:T(8,128)(2,1)}, bf16[1152,1536]{1,0:T(8,128)(2,1)}, bf16[1536,1152]{1,0:T(8,128)(2,1)}) custom-call(s32[3]{0:T(128)} %pad_add_fusion.1.wh, bf16[512,1152]{1,0:T(8,128)(2,1)} %bitcast.104, bf16[512,1152]{1,0:T(8,128)(2,1)} %maximum_select_fusion.c_r, bf16[128,1152]{1,0:T(8,128)(2,1)} %scatter.14.rt.router, ...), custom_call_target="tpu_custom_call" | custom-call | tf_op jit(solution)/shard_map/expert/pallas_call | solution.py:928
  221.5 161.6 %backward.1 = (f32[128,1152]{1,0:T(8,128)}, f32[200,2304]{1,0:T(8,128)}, f32[8,1152]{1,0:T(8,128)}, bf16[256,1152]{1,0:T(8,128)(2,1)}, bf16[4,128,2304]{2,1,0:T(...) custom-call(bf16[2,256,1280]{2,1,0:T(8,128)(2,1)} %bitcast.117, ...), custom_call_target="tpu_custom_call" | custom-call | tf_op jit(solution)/shard_map/backward/pallas_call | solution.py:1531
  383.2 1.6 convert.24
  384.8 1.2 reshape.284
  386.2 2.4 fusion.2
  388.7 1.2 pad.16
  389.9 2.7 fusion
  392.6 0.9 fusion.1
  393.4 1.7 pad_maximum_fusion.xi
  395.1 1.3 fusion.9
  396.5 70.2 %reduce_plane.1 = (bf16[288,4608]{1,0:T(8,128)(2,1)}, bf16[4,2,80,1152]{3,2,1,0:T(8,128)(2,1)}, bf16[4,2,32,576]{3,2,1,0:T(8,128)(2,1)}) custom-call(bf16[288,4608]{1,0:T(8,128)(2,1)} %pad_maximum_fusion.xi, bf16[4,2,80,1152]{3,2,1,0:T(8,128)(2,1)} %bitcast.102, bf16[4,4,2,32,576]{4,3,2,1,0:T(8,128)(2,1)} %bitcast.103), custom_call_target="tpu_custom_call" | custom-call | tf_op jit(solution)/shard_map/reduce_plane/pallas_call | solution.py:498
  466.6 1.0 bitcast_convert_fusion.1
  467.6 0.7 slice_bitcast_fusion
  468.4 0.7 slice.127
  472.1 4.9 %convert_element_type.142 = f32[288,4608]{1,0:T(8,128)} convert(bf16[288,4608]{1,0:T(8,128)(2,1)} %get-tuple-element.116) | non-fusion elementwise | flops 1327104 | bytes 7962624 | tf_op jit(solution)/shard_map/convert_element_type | solution.py:1778
  477.1 1.8 bitcast_convert_fusion
  479.4 1.4 copy.61
  480.8 2.6 reshape.290
  483.8 0.7 copy.55
  484.5 0.9 copy.56
  485.4 1.2 copy.80
  (107 shorter events, 10.0 us)
Async XLA Ops:
  0.7 13.4 %copy-start.22 = (s32[1,128]{1,0:T(1,128)S(1)}, s32[1,128]{1,0:T(1,128)}, u32[]{:S(2)}) copy-start(s32[1,128]{1,0:T(1,128)} %param.23) | copy-start | bytes 1540
  0.7 14.8 %copy-start.17 = (bf16[576]{0:T(1024)(128)(2,1)S(1)}, bf16[576]{0:T(1024)(128)(2,1)}, u32[]{:S(2)}) copy-start(bf16[576]{0:T(1024)(128)(2,1)} %param.29) | copy-start | bytes 3460
  0.7 14.8 %copy-start.18 = (bf16[576]{0:T(1024)(128)(2,1)S(1)}, bf16[576]{0:T(1024)(128)(2,1)}, u32[]{:S(2)}) copy-start(bf16[576]{0:T(1024)(128)(2,1)} %param.32) | copy-start | bytes 3460
  0.7 14.8 %copy-start.19 = (bf16[576]{0:T(1024)(128)(2,1)S(1)}, bf16[576]{0:T(1024)(128)(2,1)}, u32[]{:S(2)}) copy-start(bf16[576]{0:T(1024)(128)(2,1)} %param.34) | copy-start | bytes 3460
  0.7 14.8 %copy-start.20 = (bf16[288]{0:T(512)(128)(2,1)S(1)}, bf16[288]{0:T(512)(128)(2,1)}, u32[]{:S(2)}) copy-start(bf16[288]{0:T(512)(128)(2,1)} %param.26) | copy-start | bytes 1732
  0.7 14.8 %copy-start.21 = (bf16[288]{0:T(512)(128)(2,1)S(1)}, bf16[288]{0:T(512)(128)(2,1)}, u32[]{:S(2)}) copy-start(bf16[288]{0:T(512)(128)(2,1)} %param.36) | copy-start | bytes 1732
  0.7 14.9 %copy-start.16 = (bf16[288,4]{0,1:T(4,128)(2,1)S(1)}, bf16[288,4]{0,1:T(4,128)(2,1)}, u32[]{:S(2)}) copy-start(bf16[288,4]{0,1:T(4,128)(2,1)} %param.37) | copy-start | bytes 6916
  0.7 15.6 %copy-start.10 = (bf16[576,104]{0,1:T(8,128)(2,1)S(1)}, bf16[576,104]{0,1:T(8,128)(2,1)}, u32[]{:S(2)}) copy-start(bf16[576,104]{0,1:T(8,128)(2,1)} %param.30) | copy-start | bytes 359428
  0.7 15.6 %copy-start.15 = (bf16[4,576]{1,0:T(4,128)(2,1)S(1)}, bf16[4,576]{1,0:T(4,128)(2,1)}, u32[]{:S(2)}) copy-start(bf16[4,576]{1,0:T(4,128)(2,1)} %param.28) | copy-start | bytes 13828
  0.7 15.6 %copy-start.11 = (bf16[72,576]{1,0:T(8,128)(2,1)S(1)}, bf16[72,576]{1,0:T(8,128)(2,1)}, u32[]{:S(2)}) copy-start(bf16[72,576]{1,0:T(8,128)(2,1)} %param.31) | copy-start | bytes 248836
  0.8 15.6 %copy-start.14 = (bf16[16,576]{1,0:T(8,128)(2,1)S(1)}, bf16[16,576]{1,0:T(8,128)(2,1)}, u32[]{:S(2)}) copy-start(bf16[16,576]{1,0:T(8,128)(2,1)} %param.33) | copy-start | bytes 55300
  1.6 111.5 %collective-permute-start.1 = (s32[3]{0:T(128)S(1)}, s32[3]{0:T(128)S(1)}, u32[]{:S(2)}, u32[]{:S(2)}) collective-permute-start(s32[3]{0:T(128)S(1)} %slice_bitcast_fusion.4), channel_id=1, source_target_pairs={{0,4},{4,8},{8,12},{12,16},{16,20},{20,24},{24,28},{1,5},{5,9},{9,... | collective-permute-start | bytes 44 | tf_op jit(solution)/shard_map/ppermute | solution.py:1649
  3.7 112.1 %collective-permute-start = (bf16[16,1152]{1,0:T(8,128)(2,1)S(1)}, bf16[16,1152]{1,0:T(8,128)(2,1)S(1)}, u32[]{:S(2)}, u32[]{:S(2)}) collective-permute-start(bf16[16,1152]{1,0:T(8,128)(2,1)S(1)} %slice_bitcast_fusion.1), channel_id=1, source_target_pairs={{0,4},{4,8},{8,12},{12,16},{16,20},{20,24},{24,28},{1,5},{5,9},{9,... | collective-permute-start | bytes 110600 | tf_op jit(solution)/shard_map/ppermute | solution.py:1649
  9.4 104.1 %all-to-all-start = ((bf16[4,64,1152]{2,1,0:T(8,128)(2,1)}), bf16[4,64,1152]{2,1,0:T(8,128)(2,1)S(1)}, u32[]{:S(2)}, u32[]{:S(2)}) async-start(bf16[4,64,1152]{2,1,0:T(8,128)(2,1)} %bitcast.23), calls=%async_computation | async-start | bytes 1179648 | tf_op jit(solution)/shard_map/all_to_all | solution.py:1711
  19.6 85.2 %copy-start.3 = (bf16[1,128,1152]{2,1,0:T(8,128)(2,1)S(1)}, bf16[1,128,1152]{2,1,0:T(8,128)(2,1)}, u32[]{:S(2)}) copy-start(bf16[1,128,1152]{2,1,0:T(8,128)(2,1)} %param.25) | copy-start | bytes 884740
  107.6 3.2 copy-start.7
  113.5 84.0 %collective-permute-start.2 = (bf16[256,1152]{1,0:T(8,128)(2,1)S(1)}, bf16[256,1152]{1,0:T(8,128)(2,1)S(1)}, u32[]{:S(2)}, u32[]{:S(2)}) collective-permute-start(bf16[256,1152]{1,0:T(8,128)(2,1)S(1)} %bitcast.109), channel_id=1, source_target_pairs={{0,4},{4,0},{8,12},{12,8},{16,20},{20,16},{24,28},{28,24},{1,5},{5... | collective-permute-start | bytes 1769480 | tf_op jit(solution)/shard_map/ppermute | solution.py:1717
  115.8 0.6 copy-start.12
  166.1 22.6 %copy-start.8 = (bf16[128,1152]{1,0:T(8,128)(2,1)S(1)}, bf16[128,1152]{1,0:T(8,128)(2,1)}, u32[]{:S(2)}) copy-start(bf16[128,1152]{1,0:T(8,128)(2,1)} %get-tuple-element.108) | copy-start | bytes 884740
  166.1 31.3 %copy-start.9 = (f32[128,128]{1,0:T(8,128)S(1)}, f32[128,128]{1,0:T(8,128)}, u32[]{:S(2)}) copy-start(f32[128,128]{1,0:T(8,128)} %get-tuple-element.95.chances) | copy-start | bytes 196612
  189.6 200.3 %all-to-all-start.1 = ((bf16[4,128,288]{1,2,0:T(8,128)(2,1)}), bf16[4,128,288]{1,2,0:T(8,128)(2,1)S(1)}, u32[]{:S(2)}, u32[]{:S(2)}) async-start(bf16[4,128,288]{1,2,0:T(8,128)(2,1)} %bitcast.37), calls=%async_computation.1 | async-start | bytes 589824 | tf_op jit(solution)/shard_map/all_to_all | solution.py:1711
  384.8 1.3 copy-start.13
  389.9 2.7 copy-start.23
  472.1 4.9 %copy-start.2 = (bf16[4,2,80,1152]{3,2,1,0:T(8,128)(2,1)S(1)}, bf16[4,2,80,1152]{3,2,1,0:T(8,128)(2,1)}, u32[]{:S(2)}) copy-start(bf16[4,2,80,1152]{3,2,1,0:T(8,128)(2,1)} %get-tuple-element.117) | copy-start | bytes 4423684
  477.1 1.8 copy-start.4
  480.8 2.7 copy-start
  480.8 2.6 copy-start.6
  480.8 3.7 copy-start.5
  483.5 2.0 copy-start.1

commit v4 on v3

--- a/solution.py
+++ b/solution.py
@@ -120,244 +120,6 @@
     for peer in peers:
         pl.semaphore_signal(barrier, inc=1, device_id=peer, device_id_type=MESH)
     pl.semaphore_wait(barrier, len(peers))
-
-
-def exchange(axis, count, arrays, spread, cid):
-    n = len(arrays)
-    blocks = [a.shape[1:] if not s else a.shape for a, s in zip(arrays, spread)]
-
-    def body(*refs):
-        xs, os = refs[:n], refs[n : 2 * n]
-        send, recv, own = refs[2 * n : 2 * n + 3]
-        held = refs[2 * n + 3 :]
-        me = lax.axis_index(axis)
-        ins = [
-            pltpu.make_async_copy(xs[a] if spread[a] else xs[a].at[me], held[a], own.at[a]) for a in range(n)
-        ]
-        for c in ins:
-            c.start()
-        peers = [lax.rem(me + k, count) for k in range(1, count)]
-        greet([{axis: p} for p in peers])
-        copies = []
-        for a in range(n):
-            for k, p in enumerate(peers):
-                c = pltpu.make_async_remote_copy(
-                    xs[a] if spread[a] else xs[a].at[p],
-                    os[a].at[me],
-                    send.at[a, k],
-                    recv.at[a, k],
-                    device_id={axis: p},
-                    device_id_type=MESH,
-                )
-                c.start()
-                copies.append(c)
-        locals_ = []
-        for a in range(n):
-            ins[a].wait()
-            c = pltpu.make_async_copy(held[a], os[a].at[me], own.at[a])
-            c.start()
-            locals_.append(c)
-        for c in locals_ + copies:
-            c.wait()
-
-    outs = [sds((count,) + tuple(b), a.dtype) for a, b in zip(arrays, blocks)]
-    return pl.pallas_call(
-        body,
-        name="exchange_" + axis,
-        in_specs=[ANY] * n,
-        out_specs=[ANY] * n,
-        out_shape=outs,
-        scratch_shapes=[
-            pltpu.SemaphoreType.DMA((n, count - 1)),
-            pltpu.SemaphoreType.DMA((n, count - 1)),
-            pltpu.SemaphoreType.DMA((n,)),
-        ]
-        + [pltpu.VMEM(b, a.dtype) for a, b in zip(arrays, blocks)],
-        compiler_params=pltpu.CompilerParams(collective_id=cid, has_side_effects=True),
-    )(*arrays)
-
-
-def gather_weights(E, arrays, regions, cid):
-    n = len(arrays)
-    offsets = [d for k in range(1, E) for d in (-k, k)]
-
-    def slot(d):
-        return 2 * (abs(d) - 1) + (1 if d > 0 else 0)
-
-    def body(*refs):
-        xs, os = refs[:n], refs[n : 2 * n]
-        zs, zr, ps, pr, cs, cr, own = refs[2 * n : 2 * n + 7]
-        held = refs[2 * n + 7 :]
-        s, me = lax.axis_index("seq"), lax.axis_index("exp")
-        chip, core = s // 2, lax.rem(s, 2)
-        sib = chip * 2 + (1 - core)
-        chips = [
-            chip + 1 - 2 * lax.rem(chip, 2),
-            chip + 2 - 4 * (chip // 2),
-            3 - chip,
-        ]
-        right, left = lax.rem(me + 1, E), lax.rem(me + E - 1, E)
-        greet(
-            [{"seq": s, "exp": right}, {"seq": s, "exp": left}, {"seq": sib, "exp": me}]
-            + [{"seq": q * 2 + core, "exp": me} for q in chips]
-        )
-        ins = [pltpu.make_async_copy(xs[a], held[a], own.at[a]) for a in range(n)]
-        owns = [pltpu.make_async_copy(held[a], os[a].at[me], own.at[a]) for a in range(n)]
-        for c in ins:
-            c.start()
-
-        def part(a, region, q):
-            rows = arrays[a].shape[0] // 2
-            r = pl.ds(pl.multiple_of(core * rows, 16), rows)
-            whole_cols, each = regions[a]
-            if region == 0:
-                return (r, slice(None)) if whole_cols == arrays[a].shape[1] else (r, pl.ds(0, whole_cols))
-            return (r, pl.ds(pl.multiple_of(whole_cols + q * each, LANES), each))
-
-        def kinds(a):
-            return [1, 0] if regions[a][1] else [0]
-
-        def z_copy(a, region, d, to_right):
-            at = part(a, region, chip)
-            src = xs[a].at[at] if d == 0 else os[a].at[(me + d,) + at]
-            there = slot(d - 1 if to_right else d + 1)
-            return pltpu.make_async_remote_copy(
-                src, os[a].at[(me + d,) + at], zs.at[a, region, there], zr.at[a, region, there],
-                device_id={"seq": s, "exp": right if to_right else left}, device_id_type=MESH,
-            )
-
-        def z_arrival(a, region, d):
-            at = part(a, region, chip)
-            ref = os[a].at[(me + d,) + at]
-            return pltpu.make_async_remote_copy(
-                ref, ref, zs.at[a, region, slot(d)], zr.at[a, region, slot(d)],
-                device_id={"seq": s, "exp": right}, device_id_type=MESH,
-            )
-
-        def plane_copy(a, k, d):
-            ref = os[a].at[(me + d,) + part(a, 1, chip)]
-            return pltpu.make_async_remote_copy(
-                ref, ref, ps.at[a, k, slot(d)], pr.at[a, k, slot(d)],
-                device_id={"seq": chips[k] * 2 + core, "exp": me}, device_id_type=MESH,
-            )
-
-        def plane_arrival(a, k, d):
-            ref = os[a].at[(me + d,) + part(a, 1, chips[k])]
-            return pltpu.make_async_remote_copy(
-                ref, ref, ps.at[a, k, slot(d)], pr.at[a, k, slot(d)],
-                device_id={"seq": chips[k] * 2 + core, "exp": me}, device_id_type=MESH,
-            )
-
-        def sib_copy(a, which, d):
-            at = part(a, 0, chip) if which == 0 else part(a, 1, chip if which == 1 else chips[which - 2])
-            ref = os[a].at[(me + d,) + at]
-            return pltpu.make_async_remote_copy(
-                ref, ref, cs.at[a, which, slot(d)], cr.at[a, which, slot(d)],
-                device_id={"seq": sib, "exp": me}, device_id_type=MESH,
-            )
-
-        def sib_arrival(a, which, d):
-            rows = arrays[a].shape[0] // 2
-            at = part(a, 0, chip) if which == 0 else part(a, 1, chip if which == 1 else chips[which - 2])
-            ref = os[a].at[(me + d, pl.ds(pl.multiple_of((1 - core) * rows, 16), rows), at[1])]
-            return pltpu.make_async_remote_copy(
-                ref, ref, cs.at[a, which, slot(d)], cr.at[a, which, slot(d)],
-                device_id={"seq": sib, "exp": me}, device_id_type=MESH,
-            )
-
-        def exists(d):
-            return (me + d >= 0) & (me + d < E)
-
-        def z_starts(a, region, d):
-            if d <= 0:
-                @pl.when(exists(d) & (me < E - 1))
-                def _():
-                    z_copy(a, region, d, True).start()
-            if d >= 0:
-                @pl.when(exists(d) & (me > 0))
-                def _():
-                    z_copy(a, region, d, False).start()
-
-        order = [(a, r) for a in range(n) for r in kinds(a)]
-        for a, r in order:
-            z_starts(a, r, 0)
-
-        for a in range(n):
-            ins[a].wait()
-            owns[a].start()
-
-        def arrivals(k):
-            for a, r in order:
-                for d in (-k, k):
-                    @pl.when(exists(d))
-                    def _():
-                        z_arrival(a, r, d).wait_recv()
-                    if k < E - 1:
-                        z_starts(a, r, d)
-
-                    @pl.when(exists(d))
-                    def _():
-                        if r == 1:
-                            for j in range(3):
-                                plane_copy(a, j, d).start()
-                        sib_copy(a, r, d).start()
-
-        def plane(k):
-            for a in range(n):
-                if regions[a][1]:
-                    for d in (-k, k):
-                        @pl.when(exists(d))
-                        def _():
-                            for j in range(3):
-                                plane_arrival(a, j, d).wait_recv()
-                                sib_copy(a, 2 + j, d).start()
-
-        for k in range(1, E):
-            arrivals(k)
-            if k > 1:
-                plane(k - 1)
-        plane(E - 1)
-        for a in range(n):
-            whiches = [0] + ([1, 2, 3, 4] if regions[a][1] else [])
-            for d in offsets:
-                @pl.when(exists(d))
-                def _():
-                    for w in whiches:
-                        sib_arrival(a, w, d).wait_recv()
-                        sib_copy(a, w, d).wait_send()
-                    if regions[a][1]:
-                        for j in range(3):
-                            plane_copy(a, j, d).wait_send()
-        for a, r in order:
-            for d in [0] + offsets:
-                if d <= 0 and abs(d) < E - 1:
-                    @pl.when(exists(d) & (me < E - 1))
-                    def _():
-                        z_copy(a, r, d, True).wait_send()
-                if d >= 0 and abs(d) < E - 1:
-                    @pl.when(exists(d) & (me > 0))
-                    def _():
-                        z_copy(a, r, d, False).wait_send()
-        for c in owns:
-            c.wait()
-
-    slots = 2 * (E - 1)
-    sem = lambda *dims: pltpu.SemaphoreType.DMA(dims)
-    return pl.pallas_call(
-        body,
-        name="gather_weights",
-        in_specs=[ANY] * n,
-        out_specs=[ANY] * n,
-        out_shape=[sds((E,) + a.shape, a.dtype) for a in arrays],
-        scratch_shapes=[
-            sem(n, 2, slots), sem(n, 2, slots), sem(n, 3, slots), sem(n, 3, slots),
-            sem(n, 5, slots), sem(n, 5, slots), sem(n),
-        ]
-        + [pltpu.VMEM(a.shape, a.dtype) for a in arrays],
-        compiler_params=pltpu.CompilerParams(
-            collective_id=cid, has_side_effects=True, vmem_limit_bytes=VMEM_LIMIT
-        ),
-    )(*arrays)
 
 
 def reduce_plane(E, p_in, p_out, p_small, cid):
@@ -515,68 +277,6 @@
     return oi, oo.reshape(8, ro, co), os.reshape(8 * rs, cs)
 
 
-def front(z, tokens, halo, masks, gpack, w_in, small):
-    T, D, DI, J = z.T, z.D, z.DI, z.J
-    H = halo.shape[0]
-    cb = pick(DI, (384, 256, 128))
-    steps = DI // cb
-
-    def body(tok, hal, msk, gp, wc, wg, sm, normed_o, conv_o, hconv_o, gate_o, sig_o, mixed_o, nrm):
-        i = pl.program_id(0)
-
-        @pl.when(i == 0)
-        def _():
-            gain = gp[0:1, :]
-            t = tok[...].astype(F32)
-            nt = (t * rms_scale(t) * gain).astype(BF16)
-            h = hal[...].astype(F32)
-            nrm[0:T, :] = nt
-            nrm[T : T + H, :] = (h * rms_scale(h) * gain).astype(BF16)
-            normed_o[...] = nt
-            mixed_o[...] = jnp.zeros_like(mixed_o)
-
-        conv = mm(nrm[...], wc[...])
-        gate_o[...] = mm(nrm[0:T, :], wg[...])
-        main, edge = conv[:T], conv[T:]
-        conv_o[...] = main
-        hconv_o[...] = edge
-        xpad = padded_rows(main, edge, J, cb)
-        out = jnp.broadcast_to(sm[CONV_B : CONV_B + 1, :], (T, cb))
-        for o in range(4):
-            m = jnp.broadcast_to(msk[:, o : o + 1], (T, cb))
-            out = out + sm[CONV_W + o : CONV_W + o + 1, :] * xpad[o : o + J].reshape(T, cb) * m
-        sig = (out * sigmoid(out)).astype(BF16)
-        sig_o[...] = sig
-        mixed_o[...] += mm_nt(sig, sm[z.X0 : z.X0 + z.XW, :].astype(BF16))
-
-    col = lambda r: block((r, cb), lambda i: (0, i))
-    return call(
-        body,
-        "front",
-        (steps,),
-        (tokens, halo, masks, gpack, w_in, w_in, small),
-        [
-            whole(tokens.shape),
-            whole(halo.shape),
-            whole(masks.shape),
-            whole(gpack.shape),
-            col(D),
-            block((D, cb), lambda i: (0, i + steps)),
-            col(z.SMALL),
-        ],
-        [
-            sds((T, D), BF16),
-            sds((T, DI), F32),
-            sds((H, DI), F32),
-            sds((T, DI), F32),
-            sds((T, DI), BF16),
-            sds((T, z.XW), F32),
-        ],
-        [whole((T, D)), col(T), col(H), col(T), col(T), whole((T, z.XW))],
-        [pltpu.VMEM((T + H, D), BF16)],
-    )
-
-
 def expand_columns(z, src, col0, dst):
     def one(j, carry):
         rows = src[pl.ds(pl.multiple_of(j * SUB, SUB), SUB), :]
@@ -616,109 +316,6 @@
     return jnp.where(rows < SUB - d, pltpu.roll(v, SUB - d, 0), 0.0)
 
 
-def summary(z, mixed, sig, masks, small):
-    T, DI, N, J = z.T, z.DI, z.N, z.J
-    cb = pick(DI, (768, 384, 256, 128))
-    tg = tile_groups(cb)
-    ng = 8
-
-    def body(mix, sg, msk, sm, dt_o, pre_o, hdev_o, stot_o, dwin_o, bx, cl, u_s, hd, rates_s):
-        i = pl.program_id(0)
-
-        @pl.when(i == 0)
-        def _():
-            expand_columns(z, mix, z.R, bx)
-            expand_closed(z, msk, cl)
-
-        low = mix[:, 0 : z.R].astype(BF16)
-        pre = mm(low, sm[z.DT0 : z.DT0 + z.R, :].astype(BF16)) + sm[DT_B : DT_B + 1, :]
-        step = softplus(pre)
-        dt_o[...] = step
-        u_s[...] = step * sg[...].astype(F32)
-        rates_s[...] = -jnp.exp(sm[A_LOG : A_LOG + N, :]) * LOG2E
-
-        def pair(p, carry):
-            totals = []
-            for k in range(tg):
-                tot = jnp.zeros((SUB, LANES), F32)
-                for j in range(J):
-                    tot = tot + (dt_o[j * SUB : j * SUB + SUB, lane_at(p, tg, k)] + cl[j * SUB : j * SUB + SUB, :])
-                totals.append(tot)
-            wins = []
-            for k in range(tg):
-                w1 = totals[k]
-                w2 = w1 + shift_down(w1, 1)
-                w4 = w2 + shift_down(w2, 2)
-                w8 = w4 + shift_down(w4, 4)
-                wins.append((w1, w2, w4))
-                dwin_o[0:SUB, lane_at(p, tg, k)] = w1
-                dwin_o[SUB : 2 * SUB, lane_at(p, tg, k)] = shift_down(w8, 1)
-                stot_o[:, lane_at(p, tg, k)] = w8[SUB - 1 : SUB, :]
-            for g in range(0, N, ng):
-                rr = [
-                    [
-                        jnp.broadcast_to(rates_s[g + n : g + n + 1, lane_at(p, tg, k)], (SUB, LANES))
-                        for k in range(tg)
-                    ]
-                    for n in range(ng)
-                ]
-
-                def step_j(j, hs):
-                    dts = [dt_o[row8(j), lane_at(p, tg, k)] + cl[row8(j), :] for k in range(tg)]
-                    us = [u_s[row8(j), lane_at(p, tg, k)] for k in range(tg)]
-                    new = []
-                    for n in range(ng):
-                        b = bx[row8(j * N + g + n), :]
-                        for k in range(tg):
-                            new.append(
-                                jnp.exp2(dts[k] * rr[n][k]) * hs[n * tg + k] + us[k] * b
-                            )
-                    return tuple(new)
-
-                hs = lax.fori_loop(
-                    0, J, step_j, tuple(jnp.zeros((SUB, LANES), F32) for _ in range(ng * tg)), unroll=2
-                )
-                for n in range(ng):
-                    for k in range(tg):
-                        h = hs[n * tg + k]
-                        w1, w2, w4 = wins[k]
-                        r = rr[n][k]
-                        h = h + jnp.exp2(r * w1) * shift_down(h, 1)
-                        h = h + jnp.exp2(r * w2) * shift_down(h, 2)
-                        h = h + jnp.exp2(r * w4) * shift_down(h, 4)
-                        at = (g + n) * SUB
-                        pre_o[at : at + SUB, lane_at(p, tg, k)] = shift_down(h, 1)
-                        hd[g + n : g + n + 1, lane_at(p, tg, k)] = h[SUB - 1 : SUB, :]
-            return carry
-
-        lax.fori_loop(0, cb // (tg * LANES), pair, 0)
-        hdev_o[...] = hd[...].astype(BF16)
-
-    col = lambda r: block((r, cb), lambda i: (0, i))
-    return call(
-        body,
-        "summary",
-        (DI // cb,),
-        (mixed, sig, masks, small),
-        [whole(mixed.shape), col(T), whole(masks.shape), col(z.SMALL)],
-        [
-            sds((T, DI), F32),
-            sds((N * SUB, DI), F32),
-            sds((N, DI), BF16),
-            sds((1, DI), F32),
-            sds((2 * SUB, DI), F32),
-        ],
-        [col(T), col(N * SUB), col(N), col(1), col(2 * SUB)],
-        [
-            pltpu.VMEM((J * N * SUB, LANES), F32),
-            pltpu.VMEM((T, LANES), F32),
-            pltpu.VMEM((T, cb), F32),
-            pltpu.VMEM((N, cb), F32),
-            pltpu.VMEM((N, cb), F32),
-        ],
-    )
-
-
 def chain_states(count, mine, order, sums, heads, rates2):
     state = jnp.zeros_like(rates2)
     for k in range(count):
@@ -726,153 +323,6 @@
         new = jnp.exp2(rates2 * sums(at)) * state + heads(at).astype(F32)
         state = jnp.where(mine(at), new, state)
     return state
-
-
-def scan_forward(z, where, mixed, dt, sig, gate, masks, small, pre, dwin, h_all, s_all, w_out,
-                 tokens, gpack, router, table):
-    T, D, DI, N, J, E = z.T, z.D, z.DI, z.N, z.J, z.E
-    cb = pick(DI, (768, 384, 256, 128))
-    tg = tile_groups(cb)
-    ng = 8
-    S = h_all.shape[0]
-    slots = table.shape[1]
-    steps = DI // cb
-
-    def body(wh, mix, dt_r, sg, gt, msk, sm, pr, dw, ha, sa, wo, tok, gp, rt, tb,
-             st_o, y_o, mid_o, moe_o, ch_o, out_o, bx, cx, cl, u_s, rates_s, hin, acc):
-        i = pl.program_id(0)
-
-        @pl.when(i == 0)
-        def _():
-            expand_columns(z, mix, z.R, bx)
-            expand_columns(z, mix, z.R + N, cx)
-            expand_closed(z, msk, cl)
-            acc[...] = jnp.zeros_like(acc)
-
-        me = wh[0]
-        rates2 = -jnp.exp(sm[A_LOG : A_LOG + N, :]) * LOG2E
-        rates_s[...] = rates2
-        hin[...] = chain_states(
-            S - 1, lambda k: k < me, lambda k: k, lambda k: sa[k], lambda k: ha[k], rates2
-        )
-        u_s[...] = dt_r[...] * sg[...].astype(F32)
-
-        def pair(p, carry):
-            lanes = [lane_at(p, tg, k) for k in range(tg)]
-            for g in range(0, N, ng):
-                rr = [
-                    [jnp.broadcast_to(rates_s[g + n : g + n + 1, lanes[k]], (SUB, LANES)) for k in range(tg)]
-                    for n in range(ng)
-                ]
-                init = []
-                for n in range(ng):
-                    for k in range(tg):
-                        at = (g + n) * SUB
-                        init.append(
-                            pr[at : at + SUB, lanes[k]]
-                            + jnp.exp2(rr[n][k] * dw[SUB : 2 * SUB, lanes[k]])
-                            * jnp.broadcast_to(hin[g + n : g + n + 1, lanes[k]], (SUB, LANES))
-                        )
-
-                def keep(j, hs):
-                    for n in range(0, ng, 2):
-                        for k in range(tg):
-                            two = jnp.concatenate([hs[n * tg + k], hs[(n + 1) * tg + k]], axis=0)
-                            at = pl.multiple_of(j * N * SUB + (g + n) * SUB, 2 * SUB)
-                            st_o[pl.ds(at, 2 * SUB), lanes[k]] = two.astype(BF16)
-
-                keep(0, init)
-
-                def step_j(j, hs):
-                    dts = [dt_r[row8(j), lanes[k]] + cl[row8(j), :] for k in range(tg)]
-                    us = [u_s[row8(j), lanes[k]] for k in range(tg)]
-                    if g == 0:
-                        ys = [jnp.zeros((SUB, LANES), F32) for k in range(tg)]
-                    else:
-                        ys = [y_o[row8(j), lanes[k]] for k in range(tg)]
-                    new = []
-                    for n in range(ng):
-                        b = bx[row8(j * N + g + n), :]
-                        c = cx[row8(j * N + g + n), :]
-                        for k in range(tg):
-                            h = jnp.exp2(dts[k] * rr[n][k]) * hs[n * tg + k] + us[k] * b
-                            ys[k] = ys[k] + h * c
-                            new.append(h)
-                    for k in range(tg):
-                        y_o[row8(j), lanes[k]] = ys[k]
-                    keep(j + 1, new)
-                    return tuple(new)
-
-                lax.fori_loop(0, J, step_j, tuple(init), unroll=2)
-            return carry
-
-        lax.fori_loop(0, cb // (tg * LANES), pair, 0)
-        y = y_o[...] + sm[SKIP : SKIP + 1, :] * sg[...].astype(F32)
-        y_o[...] = y
-        g_in = gt[...]
-        gated = (y * (g_in * sigmoid(g_in))).astype(BF16)
-        acc[...] += mm(gated, wo[...])
-
-        @pl.when(i == steps - 1)
-        def _():
-            mid = tok[...].astype(F32) + acc[...]
-            mid_o[...] = mid
-            moe = (mid * rms_scale(mid) * gp[1:2, :]).astype(BF16)
-            moe_o[...] = moe
-            logits = mm_nt(moe, rt[...])
-            ch_o[...] = router_softmax(logits, E)
-            out_o[...] = mm_tn(tb[...], moe).astype(BF16)
-
-    col = lambda r: block((r, cb), lambda i: (0, i))
-    return call(
-        body,
-        "scan_forward",
-        (steps,),
-        (where, mixed, dt, sig, gate, masks, small, pre, dwin, h_all, s_all, w_out, tokens, gpack, router, table),
-        [
-            pl.BlockSpec(memory_space=pltpu.SMEM),
-            whole(mixed.shape),
-            col(T),
-            col(T),
-            col(T),
-            whole(masks.shape),
-            col(z.SMALL),
-            col(N * SUB),
-            col(2 * SUB),
-            block((S, N, cb), lambda i: (0, 0, i)),
-            block((S, 1, cb), lambda i: (0, 0, i)),
-            block((cb, D), lambda i: (i, 0)),
-            whole(tokens.shape),
-            whole(gpack.shape),
-            whole(router.shape),
-            whole(table.shape),
-        ],
-        [
-            sds(((J + 1) * N * SUB, DI), BF16),
-            sds((T, DI), F32),
-            sds((T, D), F32),
-            sds((T, D), BF16),
-            sds((T, LANES), F32),
-            sds((slots, D), BF16),
-        ],
-        [
-            col((J + 1) * N * SUB),
-            col(T),
-            whole((T, D)),
-            whole((T, D)),
-            whole((T, LANES)),
-            whole((slots, D)),
-        ],
-        [
-            pltpu.VMEM((J * N * SUB, LANES), F32),
-            pltpu.VMEM((J * N * SUB, LANES), F32),
-            pltpu.VMEM((T, LANES), F32),
-            pltpu.VMEM((T, cb), F32),
-            pltpu.VMEM((N, cb), F32),
-            pltpu.VMEM((N, cb), F32),
-            pltpu.VMEM((T, D), F32),
-        ],
-    )
 
 
 def router_softmax(logits, experts):
@@ -1038,6 +488,541 @@
             for d in (-k, k) if k else (0,):
                 self.each(d, lambda c: c.wait_send())
         self.local().wait()
+
+
+class Spread:
+    def __init__(self, E, src, col0, dst, cols, whole_cols, each, sems):
+        self.E, self.src, self.col0, self.dst, self.cols = E, src, col0, dst, cols
+        self.whole_cols, self.each_cols = whole_cols, each
+        self.zs, self.zr, self.ps, self.pr, self.cs, self.cr = sems
+        self.rows = src.shape[0]
+        s, self.me = lax.axis_index("seq"), lax.axis_index("exp")
+        self.chip, self.core = s // 2, lax.rem(s, 2)
+        self.sib = {"seq": s + 1 - 2 * self.core}
+        self.chips = [self.chip + 1 - 2 * lax.rem(self.chip, 2), self.chip + 2 - 4 * (self.chip // 2), 3 - self.chip]
+        self.right, self.left = lax.rem(self.me + 1, E), lax.rem(self.me + E - 1, E)
+        self.regions = [1, 0] if each else [0]
+        self.offsets = [d for k in range(1, E) for d in (-k, k)]
+
+    def slot(self, d):
+        return 2 * (abs(d) - 1) + (1 if d > 0 else 0)
+
+    def exists(self, d):
+        return (self.me + d >= 0) & (self.me + d < self.E)
+
+    def span(self, region, q):
+        if region == 0:
+            return 0, self.whole_cols
+        return pl.multiple_of(self.whole_cols + q * self.each_cols, LANES), self.each_cols
+
+    def there(self, d, region, q, core):
+        half = self.rows // 2
+        start, width = self.span(region, q)
+        at = pl.ds(pl.multiple_of((self.me + d) * self.rows + core * half, 16), half)
+        return self.dst.at[at] if width == self.cols else self.dst.at[at, pl.ds(start, width)]
+
+    def own(self, region):
+        half = self.rows // 2
+        start, width = self.span(region, self.chip)
+        at = pl.ds(pl.multiple_of(self.core * half, 16), half)
+        if width == self.src.shape[1]:
+            return self.src.at[at]
+        return self.src.at[at, pl.ds(pl.multiple_of(self.col0 + start, LANES), width)]
+
+    def local(self, sem):
+        at = pl.ds(pl.multiple_of(self.me * self.rows, 16), self.rows)
+        src = self.src if self.cols == self.src.shape[1] else self.src.at[:, self.col0 : self.col0 + self.cols]
+        return pltpu.make_async_copy(src, self.dst.at[at], sem)
+
+    def z_each(self, region, d, act):
+        for to_right in (True, False):
+            if (d <= 0) if to_right else (d >= 0):
+                edge = self.me < self.E - 1 if to_right else self.me > 0
+                slot = self.slot(d - 1 if to_right else d + 1)
+
+                @pl.when(self.exists(d) & edge)
+                def _():
+                    act(
+                        pltpu.make_async_remote_copy(
+                            self.own(region) if d == 0 else self.there(d, region, self.chip, self.core),
+                            self.there(d, region, self.chip, self.core),
+                            self.zs.at[region, slot],
+                            self.zr.at[region, slot],
+                            device_id={"exp": self.right if to_right else self.left},
+                            device_id_type=MESH,
+                        )
+                    )
+
+    def start(self):
+        for r in self.regions:
+            self.z_each(r, 0, lambda c: c.start())
+
+    def plane_copy(self, k, d):
+        ref = self.there(d, 1, self.chip, self.core)
+        return pltpu.make_async_remote_copy(
+            ref, ref, self.ps.at[k, self.slot(d)], self.pr.at[k, self.slot(d)],
+            device_id={"seq": self.chips[k] * 2 + self.core}, device_id_type=MESH,
+        )
+
+    def piece(self, which, d, core):
+        if which == 0:
+            return self.there(d, 0, self.chip, core)
+        return self.there(d, 1, self.chip if which == 1 else self.chips[which - 2], core)
+
+    def sib_copy(self, which, d, core):
+        ref = self.piece(which, d, core)
+        return pltpu.make_async_remote_copy(
+            ref, ref, self.cs.at[which, self.slot(d)], self.cr.at[which, self.slot(d)],
+            device_id=self.sib, device_id_type=MESH,
+        )
+
+    def hop(self, k):
+        for r in self.regions:
+            for d in (-k, k):
+                @pl.when(self.exists(d))
+                def _():
+                    ref = self.there(d, r, self.chip, self.core)
+                    pltpu.make_async_remote_copy(
+                        ref, ref, self.zs.at[r, self.slot(d)], self.zr.at[r, self.slot(d)],
+                        device_id={"exp": self.right}, device_id_type=MESH,
+                    ).wait_recv()
+
+                if k < self.E - 1:
+                    self.z_each(r, d, lambda c: c.start())
+
+                @pl.when(self.exists(d))
+                def _():
+                    if r == 1:
+                        for j in range(3):
+                            self.plane_copy(j, d).start()
+                    self.sib_copy(r, d, self.core).start()
+
+    def plane(self, k):
+        if not self.each_cols:
+            return
+        for d in (-k, k):
+            @pl.when(self.exists(d))
+            def _():
+                for j in range(3):
+                    ref = self.there(d, 1, self.chips[j], self.core)
+                    pltpu.make_async_remote_copy(
+                        ref, ref, self.ps.at[j, self.slot(d)], self.pr.at[j, self.slot(d)],
+                        device_id=self.sib, device_id_type=MESH,
+                    ).wait_recv()
+                    self.sib_copy(2 + j, d, self.core).start()
+
+    def landed(self):
+        for d in self.offsets:
+            @pl.when(self.exists(d))
+            def _():
+                for w in range(5 if self.each_cols else 1):
+                    self.sib_copy(w, d, 1 - self.core).wait_recv()
+
+    def finish(self):
+        for d in self.offsets:
+            @pl.when(self.exists(d))
+            def _():
+                for w in range(5 if self.each_cols else 1):
+                    self.sib_copy(w, d, self.core).wait_send()
+                if self.each_cols:
+                    for j in range(3):
+                        self.plane_copy(j, d).wait_send()
+        for r in self.regions:
+            for k in range(self.E - 1):
+                for d in (-k, k) if k else (0,):
+                    self.z_each(r, d, lambda c: c.wait_send())
+
+
+def forward(z, S, plane, tok, tail, seg_tail, seg_head, cot, route, masks, in_proj, out_proj, small_own, g_own, gr, cid):
+    T, D, DI, N, J, E, CAP = z.T, z.D, z.DI, z.N, z.J, z.E, z.CAP
+    H = tail.shape[0]
+    M = E * CAP
+    DZ, NZ = DI // E, D // E
+    rs, rg = small_own.shape[0], g_own.shape[0]
+    if not plane:
+        rs, rg = rs // E, rg // E
+    cb = pick(DI, (384, 256, 128))
+    cs = pick(DI, (768, 384, 256, 128))
+    tg = tile_groups(cs)
+    wide = tg * LANES
+    ng = 8
+    steps = DI // cs
+    ST = (J + 1) * N * SUB
+    tiles, tiles_o = DI // LANES, D // LANES
+    split = (tiles // 4 - (0 if tiles % 4 else 1)) * LANES
+    split_o = max(1, tiles_o * 2 // 9) * LANES
+
+    def body(
+        tok, tail, seg_t, seg_h, cot, route, msk_in, in_p, out_p, sm_p, g_p,
+        sm, gp, rt, table, choose, masks, conv_in, hconv, gate, sig, mixed, dt, y, mid, moe, ch_o, s_all,
+        st_o, win_o, wout_o, arr_o, cot_o, nz_o,
+        wc, wg, wo, smb, gb, nrm, halo, seg_in, bx, cx, cl, u_s, rates_s, hd, hdev, stot, h_all, pre_s, dwin, hin,
+        st_v, acc, outb, cotb, nz,
+        ld, zs, zr, ps, pr, c_s, c_r, t_s, t_r, h_s, h_r, d_s, d_r, q_s, q_r, k_s, k_r, n_s, n_r, x_s, x_r,
+    ):
+        s, me = lax.axis_index("seq"), lax.axis_index("exp")
+        core = lax.rem(s, 2)
+        sib = {"seq": s + 1 - 2 * core}
+        seqs = [lax.rem(s + k, S) for k in range(1, S)]
+        zz = [lax.rem(me + k, E) for k in range(1, E)]
+        greet([{"seq": p} for p in seqs] + [{"exp": p} for p in zz])
+
+        def remote(src, dst, send, recv, to):
+            return pltpu.make_async_remote_copy(src, dst, send, recv, device_id=to, device_id_type=MESH)
+
+        ahead = {"seq": lax.rem(s + 1, S)}
+        edges = [remote(tail, halo, t_s.at[0], t_r.at[0], ahead), remote(seg_t, seg_in, t_s.at[1], t_r.at[1], ahead)]
+        for c in edges:
+            c.start()
+        sems = lambda a: (zs.at[a], zr.at[a], ps.at[a], pr.at[a], c_s.at[a], c_r.at[a])
+        if plane:
+            parts = [
+                Spread(E, sm_p, 0, smb, sm_p.shape[1], sm_p.shape[1], 0, sems(0)),
+                Spread(E, g_p, 0, gb, g_p.shape[1], g_p.shape[1], 0, sems(1)),
+                Spread(E, in_p, 0, wc, DI, DI - 4 * split, split, sems(2)),
+                Spread(E, in_p, DI, wg, DI, DI - 4 * split, split, sems(3)),
+                Spread(E, out_p, 0, wo, D, D - 4 * split_o, split_o, sems(4)),
+            ]
+            for p in parts[:4]:
+                p.start()
+            loads = [p.local(ld.at[a]) for a, p in enumerate(parts)]
+        else:
+            loads = [
+                pltpu.make_async_copy(sm_p, smb, ld.at[0]),
+                pltpu.make_async_copy(g_p, gb, ld.at[1]),
+                pltpu.make_async_copy(in_p.at[:, 0:DI], wc, ld.at[2]),
+                pltpu.make_async_copy(in_p.at[:, DI : 2 * DI], wg, ld.at[3]),
+                pltpu.make_async_copy(out_p, wo, ld.at[4]),
+            ]
+        for c in loads:
+            c.start()
+
+        lane = lax.broadcasted_iota(jnp.int32, (T, LANES), 1)
+        chosen = (lane == route[...]).astype(F32)
+        choose[...] = chosen
+        upto = lax.broadcasted_iota(jnp.int32, (T, T), 1) <= lax.broadcasted_iota(jnp.int32, (T, T), 0)
+        counts = mm(upto.astype(F32).astype(BF16), chosen.astype(BF16))
+        rank = jnp.sum(counts * chosen, axis=-1, keepdims=True).astype(jnp.int32) - 1
+        slots = lax.broadcasted_iota(jnp.int32, (T, M), 1)
+        table[...] = (slots == route[...] * CAP + rank).astype(F32).astype(BF16)
+        cotb[...] = mm_tn(table[...], cot[...]).astype(BF16)
+
+        if plane:
+            for k in range(1, E):
+                for p in parts[:4]:
+                    p.hop(k)
+                if k == 1:
+                    parts[4].start()
+                if k == 2:
+                    parts[2].plane(1)
+            for k in range(2, E):
+                parts[2].plane(k)
+        block_of = lambda ref, p: ref.at[pl.ds(pl.multiple_of(p * CAP, 16), CAP)]
+        cot_moves = [remote(block_of(cotb, p), cot_o.at[core, me], k_s.at[k], k_r.at[k], {"exp": p}) for k, p in enumerate(zz)]
+        if plane:
+            for p in parts[:3]:
+                p.landed()
+        for c in loads:
+            c.wait()
+        for e in range(E):
+            sm[:, e * DZ : (e + 1) * DZ] = smb[e * rs : (e + 1) * rs, :].astype(F32)[0 : z.SMALL]
+        gp[...] = jnp.zeros_like(gp)
+        rt[...] = jnp.zeros_like(rt)
+        for e in range(E):
+            cols = slice(e * NZ, (e + 1) * NZ)
+            gp[:, cols] = gb[e * rg : e * rg + 16, :].astype(F32)[0:gr]
+        rt[0:16, :] = jnp.concatenate([gp[2 : 2 + E, :], jnp.zeros((16 - E, D), F32)], axis=0).astype(BF16)
+
+        for c in edges:
+            c.wait()
+        live = jnp.where(s > 0, 1.0, 0.0)
+        masks[...] = msk_in[...]
+        col8 = lax.broadcasted_iota(jnp.int32, (1, SUB), 1)
+        for t in range(3):
+            row = masks[SUB * t : SUB * t + 1, :]
+            for o in range(3 - t):
+                before = seg_in[t + o : t + o + 1, 0:SUB] * live
+                same = (before == seg_h[t : t + 1, 0:SUB]).astype(F32)
+                row = jnp.where(col8 == o, same, row)
+            masks[SUB * t : SUB * t + 1, :] = row
+        t32 = tok[...].astype(F32)
+        nrm[0:T, :] = (t32 * rms_scale(t32) * gp[0:1, :]).astype(BF16)
+        h32 = halo[...].astype(F32) * live
+        nrm[T : T + H, :] = (h32 * rms_scale(h32) * gp[0:1, :]).astype(BF16)
+        mixed[...] = jnp.zeros_like(mixed)
+
+        def conv_block(i, carry):
+            C = at_cols(i, cb)
+            both = mm(nrm[...], wc[:, C])
+            main, edge = both[:T], both[T:]
+            conv_in[:, C] = main
+            hconv[:, C] = edge
+            xpad = padded_rows(main, edge, J, cb)
+            out = jnp.broadcast_to(sm[CONV_B : CONV_B + 1, C], (T, cb))
+            for o in range(4):
+                m = jnp.broadcast_to(masks[:, o : o + 1], (T, cb))
+                out = out + sm[CONV_W + o : CONV_W + o + 1, C] * xpad[o : o + J].reshape(T, cb) * m
+            sv = (out * sigmoid(out)).astype(BF16)
+            sig[:, C] = sv
+            mixed[...] += mm_nt(sv, sm[z.X0 : z.X0 + z.XW, C].astype(BF16))
+            return carry
+
+        lax.fori_loop(0, DI // cb, conv_block, 0)
+        for e in range(E):
+            nz[e] = nrm[0:T, e * NZ : (e + 1) * NZ]
+        nz_moves = [remote(nz.at[p], nz_o.at[me], n_s.at[k], n_r.at[k], {"exp": p}) for k, p in enumerate(zz)]
+        nz_own = pltpu.make_async_copy(nz.at[me], nz_o.at[me], ld.at[5])
+        nz_own.start()
+        if plane:
+            for k in range(1, E):
+                parts[4].hop(k)
+                parts[3].plane(k)
+        for c in cot_moves + nz_moves:
+            c.start()
+        cot_own = pltpu.make_async_copy(block_of(cotb, me), cot_o.at[core, me], ld.at[6])
+        cot_own.start()
+
+        expand_columns(z, mixed, z.R, bx)
+        expand_columns(z, mixed, z.R + N, cx)
+        expand_closed(z, masks, cl)
+        low = mixed[:, 0 : z.R].astype(BF16)
+
+        def step_block(i, carry):
+            C = at_cols(i, cs)
+            pre = mm(low, sm[z.DT0 : z.DT0 + z.R, C].astype(BF16)) + sm[DT_B : DT_B + 1, C]
+            step = softplus(pre)
+            dt[:, C] = step
+            u_s[:, C] = step * sig[:, C].astype(F32)
+            rates_s[:, C] = -jnp.exp(sm[A_LOG : A_LOG + N, C]) * LOG2E
+            return carry
+
+        lax.fori_loop(0, DI // cs, step_block, 0)
+
+        def chunk_block(p, carry):
+            lanes = [lane_at(p, tg, k) for k in range(tg)]
+            wins = []
+            for k in range(tg):
+                w1 = jnp.zeros((SUB, LANES), F32)
+                for j in range(J):
+                    w1 = w1 + (dt[j * SUB : j * SUB + SUB, lanes[k]] + cl[j * SUB : j * SUB + SUB, :])
+                w2 = w1 + shift_down(w1, 1)
+                w4 = w2 + shift_down(w2, 2)
+                w8 = w4 + shift_down(w4, 4)
+                wins.append((w1, w2, w4))
+                dwin[:, lanes[k]] = shift_down(w8, 1)
+                stot[:, lanes[k]] = w8[SUB - 1 : SUB, :]
+            for g in range(0, N, ng):
+                rr = [
+                    [jnp.broadcast_to(rates_s[g + n : g + n + 1, lanes[k]], (SUB, LANES)) for k in range(tg)]
+                    for n in range(ng)
+                ]
+
+                def step_j(j, hs):
+                    dts = [dt[row8(j), lanes[k]] + cl[row8(j), :] for k in range(tg)]
+                    us = [u_s[row8(j), lanes[k]] for k in range(tg)]
+                    new = []
+                    for n in range(ng):
+                        b = bx[row8(j * N + g + n), :]
+                        for k in range(tg):
+                            new.append(jnp.exp2(dts[k] * rr[n][k]) * hs[n * tg + k] + us[k] * b)
+                    return tuple(new)
+
+                hs = lax.fori_loop(
+                    0, J, step_j, tuple(jnp.zeros((SUB, LANES), F32) for _ in range(ng * tg)), unroll=2
+                )
+                for n in range(ng):
+                    for k in range(tg):
+                        h = hs[n * tg + k]
+                        w1, w2, w4 = wins[k]
+                        r = rr[n][k]
+                        h = h + jnp.exp2(r * w1) * shift_down(h, 1)
+                        h = h + jnp.exp2(r * w2) * shift_down(h, 2)
+                        h = h + jnp.exp2(r * w4) * shift_down(h, 4)
+                        pre_s[(g + n) * SUB : (g + n + 1) * SUB, lanes[k]] = shift_down(h, 1)
+                        hd[g + n : g + n + 1, lanes[k]] = h[SUB - 1 : SUB, :]
+            return carry
+
+        lax.fori_loop(0, DI // wide, chunk_block, 0)
+        hdev[...] = hd[...].astype(BF16)
+        h_moves = [remote(hdev, h_all.at[s], h_s.at[0, k], h_r.at[0, k], {"seq": p}) for k, p in enumerate(seqs)]
+        h_moves += [remote(stot, s_all.at[s], h_s.at[1, k], h_r.at[1, k], {"seq": p}) for k, p in enumerate(seqs)]
+        for c in h_moves:
+            c.start()
+        h_all[s] = hdev[...]
+        s_all[s] = stot[...]
+        if plane:
+            parts[3].landed()
+
+        def gate_block(i, carry):
+            C = at_cols(i, cb)
+            gate[:, C] = mm(nrm[0:T, :], wg[:, C])
+            return carry
+
+        lax.fori_loop(0, DI // cb, gate_block, 0)
+        if plane:
+            for k in range(1, E):
+                parts[4].plane(k)
+            parts[4].landed()
+        outs = [
+            pltpu.make_async_copy(wc, win_o.at[:, 0:DI], ld.at[7]),
+            pltpu.make_async_copy(wg, win_o.at[:, DI : 2 * DI], ld.at[8]),
+            pltpu.make_async_copy(wo, wout_o, ld.at[9]),
+        ]
+        for c in outs:
+            c.start()
+        for c in h_moves:
+            c.wait()
+        acc[...] = jnp.zeros_like(acc)
+
+        def save(i):
+            return pltpu.make_async_copy(
+                st_v.at[i % 2], st_o.at[:, i * cs : (i + 1) * cs], ld.at[10 + i % 2]
+            )
+
+        for i in range(steps):
+            if i >= 2:
+                save(i - 2).wait()
+            C = slice(i * cs, (i + 1) * cs)
+            hin[...] = chain_states(
+                S - 1, lambda k: k < s, lambda k: k, lambda k: s_all[k, :, C], lambda k: h_all[k, :, C],
+                rates_s[:, C],
+            )
+
+            def pair(p, carry):
+                lanes = [lanes_of(i, cs, p, tg, k) for k in range(tg)]
+                near = [lane_at(p, tg, k) for k in range(tg)]
+                for g in range(0, N, ng):
+                    rr = [
+                        [jnp.broadcast_to(rates_s[g + n : g + n + 1, lanes[k]], (SUB, LANES)) for k in range(tg)]
+                        for n in range(ng)
+                    ]
+                    init = []
+                    for n in range(ng):
+                        for k in range(tg):
+                            at = (g + n) * SUB
+                            init.append(
+                                pre_s[at : at + SUB, lanes[k]]
+                                + jnp.exp2(rr[n][k] * dwin[:, lanes[k]])
+                                * jnp.broadcast_to(hin[g + n : g + n + 1, near[k]], (SUB, LANES))
+                            )
+
+                    def keep(j, hs):
+                        for n in range(0, ng, 2):
+                            for k in range(tg):
+                                two = jnp.concatenate([hs[n * tg + k], hs[(n + 1) * tg + k]], axis=0)
+                                at = pl.multiple_of(j * N * SUB + (g + n) * SUB, 2 * SUB)
+                                st_v[i % 2, pl.ds(at, 2 * SUB), near[k]] = two.astype(BF16)
+
+                    keep(0, init)
+
+                    def step_j(j, hs):
+                        dts = [dt[row8(j), lanes[k]] + cl[row8(j), :] for k in range(tg)]
+                        us = [u_s[row8(j), lanes[k]] for k in range(tg)]
+                        if g == 0:
+                            ys = [jnp.zeros((SUB, LANES), F32) for k in range(tg)]
+                        else:
+                            ys = [y[row8(j), lanes[k]] for k in range(tg)]
+                        new = []
+                        for n in range(ng):
+                            b = bx[row8(j * N + g + n), :]
+                            c = cx[row8(j * N + g + n), :]
+                            for k in range(tg):
+                                h = jnp.exp2(dts[k] * rr[n][k]) * hs[n * tg + k] + us[k] * b
+                                ys[k] = ys[k] + h * c
+                                new.append(h)
+                        for k in range(tg):
+                            y[row8(j), lanes[k]] = ys[k]
+                        keep(j + 1, new)
+                        return tuple(new)
+
+                    lax.fori_loop(0, J, step_j, tuple(init), unroll=2)
+                return carry
+
+            lax.fori_loop(0, cs // wide, pair, 0)
+            save(i).start()
+            yv = y[:, C] + sm[SKIP : SKIP + 1, C] * sig[:, C].astype(F32)
+            y[:, C] = yv
+            g_in = gate[:, C]
+            gated = (yv * (g_in * sigmoid(g_in))).astype(BF16)
+            acc[...] += mm(gated, wo[C, :])
+
+        m32 = tok[...].astype(F32) + acc[...]
+        mid[...] = m32
+        moe[...] = (m32 * rms_scale(m32) * gp[1:2, :]).astype(BF16)
+        ch_o[...] = router_softmax(mm_nt(moe[...], rt[...]), E)
+        outb[...] = mm_tn(table[...], moe[...]).astype(BF16)
+        out_moves = [remote(block_of(outb, p), arr_o.at[core, me], d_s.at[k], d_r.at[k], {"exp": p}) for k, p in enumerate(zz)]
+        for c in out_moves:
+            c.start()
+        arr_own = pltpu.make_async_copy(block_of(outb, me), arr_o.at[core, me], ld.at[12])
+        arr_own.start()
+        passes = [
+            remote(block_of(cotb, me), cot_o.at[core, me], x_s.at[0, 0], x_r.at[0, 0], sib),
+            remote(block_of(outb, me), arr_o.at[core, me], x_s.at[1, 0], x_r.at[1, 0], sib),
+        ]
+        for c in passes:
+            c.start()
+        for w, ref, send, recv in ((0, cot_o, k_s, k_r), (1, arr_o, d_s, d_r)):
+            for k in range(1, E):
+                frm = lax.rem(me + E - k, E)
+                at = ref.at[core, frm]
+                remote(at, at, send.at[k - 1], recv.at[k - 1], {"exp": frm}).wait_recv()
+                c = remote(at, at, x_s.at[w, k], x_r.at[w, k], sib)
+                c.start()
+                passes.append(c)
+        if plane:
+            for p in parts:
+                p.finish()
+        for c in outs + [nz_own, cot_own, arr_own]:
+            c.wait()
+        for i in range(max(0, steps - 2), steps):
+            save(i).wait()
+        for c in nz_moves:
+            c.wait()
+        for c in cot_moves + out_moves + passes:
+            c.wait_send()
+        for w, ref in ((0, cot_o), (1, arr_o)):
+            for k in range(E):
+                at = ref.at[1 - core, lax.rem(me + E - k, E)]
+                remote(at, at, x_s.at[w, k], x_r.at[w, k], sib).wait_recv()
+
+    v = pltpu.VMEM
+    sem = lambda *dims: pltpu.SemaphoreType.DMA(dims)
+    vm = pl.BlockSpec(memory_space=pltpu.VMEM)
+    zslots = 2 * (E - 1)
+    ins = (tok, tail, seg_tail, seg_head, cot, route, masks, in_proj, out_proj, small_own, g_own)
+    vm_outs = [
+        sds((z.SMALL, DI), F32), sds((gr, D), F32), sds((LANES, D), BF16), sds((T, M), BF16), sds((T, LANES), F32),
+        sds((T, SUB), F32), sds((T, DI), F32), sds((H, DI), F32), sds((T, DI), F32), sds((T, DI), BF16),
+        sds((T, z.XW), F32), sds((T, DI), F32), sds((T, DI), F32), sds((T, D), F32), sds((T, D), BF16),
+        sds((T, LANES), F32), sds((S, 1, DI), F32),
+    ]
+    any_outs = [
+        sds((ST, DI), BF16), sds((D, 2 * DI), BF16), sds((DI, D), BF16), sds((2, E, CAP, D), BF16),
+        sds((2, E, CAP, D), BF16), sds((E, T, NZ), BF16),
+    ]
+    return pl.pallas_call(
+        body,
+        name="forward",
+        in_specs=[vm] * 7 + [ANY] * 4,
+        out_specs=[vm] * len(vm_outs) + [ANY] * len(any_outs),
+        out_shape=vm_outs + any_outs,
+        scratch_shapes=[
+            v((D, DI), BF16), v((D, DI), BF16), v((DI, D), BF16), v((E * rs, DZ), BF16), v((E * rg, NZ), BF16),
+            v((T + H, D), BF16), v((H, D), BF16), v((SUB, LANES), F32),
+            v((J * N * SUB, LANES), F32), v((J * N * SUB, LANES), F32), v((T, LANES), F32), v((T, DI), F32),
+            v((N, DI), F32), v((N, DI), F32), v((N, DI), BF16), v((1, DI), F32), v((S, N, DI), BF16),
+            v((N * SUB, DI), F32), v((SUB, DI), F32), v((N, cs), F32),
+            v((2, ST, cs), BF16), v((T, D), F32), v((M, D), BF16), v((M, D), BF16), v((E, T, NZ), BF16),
+            sem(13), sem(5, 2, zslots), sem(5, 2, zslots), sem(5, 3, zslots), sem(5, 3, zslots),
+            sem(5, 5, zslots), sem(5, 5, zslots), sem(2), sem(2), sem(2, S - 1), sem(2, S - 1),
+            sem(E - 1), sem(E - 1), sem(1), sem(1), sem(E - 1), sem(E - 1), sem(E - 1), sem(E - 1),
+            sem(2, E), sem(2, E),
+        ],
+        compiler_params=pltpu.CompilerParams(
+            collective_id=cid, has_side_effects=True, vmem_limit_bytes=60 * 1024 * 1024
+        ),
+    )(*ins)
 
 
 def backward(z, S, plane, dxp, outp, dwu, dwd, states, w_out, w_in, table, choose, chances, mid, moe, cot, gpack,
@@ -1573,80 +1558,12 @@
     )(*ins)
 
 
-def dispatch(E, S, outbound, cid):
-    CAP, D = outbound.shape[1:]
-
-    def body(x, o, zs_s, zs_r, c_s, c_r, own):
-        s, me = lax.axis_index("seq"), lax.axis_index("exp")
-        core = lax.rem(s, 2)
-        sib = {"seq": s + 1 - 2 * core}
-        zs = [lax.rem(me + k, E) for k in range(1, E)]
-        greet([sib] + [{"exp": p} for p in zs])
-        sends = [
-            pltpu.make_async_remote_copy(
-                x.at[p], o.at[core, me], zs_s.at[k], zs_r.at[k], device_id={"exp": p}, device_id_type=MESH
-            )
-            for k, p in enumerate(zs)
-        ]
-        for c in sends:
-            c.start()
-        local = pltpu.make_async_copy(x.at[me], o.at[core, me], own)
-        local.start()
-        passes = [
-            pltpu.make_async_remote_copy(
-                x.at[me], o.at[core, me], c_s.at[0], c_r.at[0], device_id=sib, device_id_type=MESH
-            )
-        ]
-        passes[0].start()
-        for k in range(1, E):
-            frm = lax.rem(me + E - k, E)
-            ref = o.at[core, frm]
-            pltpu.make_async_remote_copy(
-                ref, ref, zs_s.at[k - 1], zs_r.at[k - 1], device_id={"exp": frm}, device_id_type=MESH
-            ).wait_recv()
-            c = pltpu.make_async_remote_copy(
-                ref, ref, c_s.at[k], c_r.at[k], device_id=sib, device_id_type=MESH
-            )
-            c.start()
-            passes.append(c)
-        local.wait()
-        for c in sends:
-            c.wait_send()
-        for c in passes:
-            c.wait_send()
-        for k in range(E):
-            ref = o.at[1 - core, lax.rem(me + E - k, E)]
-            pltpu.make_async_remote_copy(
-                ref, ref, c_s.at[k], c_r.at[k], device_id=sib, device_id_type=MESH
-            ).wait_recv()
-
-    vm = pl.BlockSpec(memory_space=pltpu.VMEM)
-    return pl.pallas_call(
-        body,
-        name="dispatch",
-        in_specs=[vm],
-        out_specs=vm,
-        out_shape=sds((2, E, CAP, D), outbound.dtype),
-        scratch_shapes=[
-            pltpu.SemaphoreType.DMA((E - 1,)), pltpu.SemaphoreType.DMA((E - 1,)),
-            pltpu.SemaphoreType.DMA((E,)), pltpu.SemaphoreType.DMA((E,)), pltpu.SemaphoreType.DMA,
-        ],
-        compiler_params=pltpu.CompilerParams(collective_id=cid, has_side_effects=True),
-    )(outbound)
-
-
 def to_chunks(a, J):
     return a.reshape((SUB, J) + a.shape[1:]).swapaxes(0, 1).reshape(a.shape)
 
 
 def from_chunks(a, J):
     return a.reshape((J, SUB) + a.shape[1:]).swapaxes(0, 1).reshape(a.shape)
-
-
-def from_behind(block_in, axis, distance):
-    devices = range(lax.axis_size(axis))
-    route = [(i - distance, i) for i in devices if i - distance in devices]
-    return lax.ppermute(block_in, axis, route)
 
 
 def on_device(
@@ -1660,10 +1577,10 @@
     me_s, me_e = lax.axis_index("seq"), lax.axis_index("exp")
     core = lax.rem(me_s, 2)
     where = jnp.stack([me_s, me_e, core]).astype(jnp.int32)
-    halo = from_behind(tokens[0, T - J :], "seq", 1)
     seg = segment_ids[0]
-    seg_tail = from_behind(seg[T - 3 :], "seq", 1)
-
+    wide_rows = lambda v: jnp.pad(
+        jnp.broadcast_to(v.astype(F32)[:, None], (3, LANES)), ((0, SUB - 3), (0, 0))
+    )
     cw = dt_proj.shape[1]
     dw = norm_gain.shape[0]
     plane = S == 8 and dw % 32 == 0
@@ -1675,60 +1592,24 @@
         [norm_gain[None], moe_gain[None], router.T, jnp.zeros((32 - 2 - E, dw), BF16)], axis=0
     )
     owned = [in_proj, out_proj, small_own, g_own]
-    if plane:
-        each = lambda cols, most: (cols - 4 * most * LANES, most * LANES)
-        tiles_in, tiles_out = 2 * DI // LANES, D // LANES
-        regions = [
-            each(2 * DI, max(1, tiles_in * 5 // 36)), each(D, max(1, tiles_out * 2 // 9)), (cw, 0), (dw, 0)
-        ]
-        w_in, w_out, small, gpack_low = gather_weights(E, owned, regions, 1)
-    else:
-        w_in, w_out, small, gpack_low = [lax.all_gather(a, "exp") for a in owned]
-    w_in = w_in.reshape(D, 2 * DI)
-    w_out = w_out.reshape(DI, D)
-    join = lambda a: a.swapaxes(0, 1).reshape(a.shape[1], -1)
-    small = join(small[:, : z.SMALL]).astype(F32)
-    gpack_low = join(gpack_low[:, : 2 + E])
+    if not plane:
+        owned = [lax.all_gather(a, "exp", tiled=True) for a in owned]
     gr = 8 * -(-(2 + E) // 8)
-    gpack = jnp.zeros((gr, D), F32).at[: 2 + E].set(gpack_low.astype(F32))
-    router_t = jnp.zeros((LANES, D), BF16).at[0:E].set(gpack_low[2 : 2 + E])
-
-    padded_seg = jnp.concatenate([seg_tail, seg])
+    padded_seg = jnp.concatenate([jnp.zeros((3,), seg.dtype), seg])
     masks = jnp.stack([(padded_seg[o : o + T] == seg).astype(F32) for o in range(4)] + [seg * 0.0] * 4, axis=1)
-    masks = to_chunks(masks, J)
     tok = to_chunks(tokens[0], J)
     cot = to_chunks(cotangent[0], J)
-    route = to_chunks(routes[0, :, 0], J)
-    choose = route[:, None] == jnp.arange(E)[None, :]
-    upto = (jnp.arange(T)[None, :] <= jnp.arange(T)[:, None]).astype(BF16)
-    counts = jnp.dot(upto, choose.astype(BF16), preferred_element_type=F32)
-    rank = jnp.sum(counts * choose, axis=-1).astype(jnp.int32) - 1
-    table = ((route * CAP + rank)[:, None] == jnp.arange(E * CAP)[None, :]).astype(BF16)
-    choose_wide = (route[:, None] == jnp.arange(LANES)[None, :]).astype(F32)
-    cot_slots = lax.dot_general(table, cot, (((0,), (0,)), ((), ())), preferred_element_type=F32).astype(BF16)
-
-    def trade(a):
-        return lax.all_to_all(a, "exp", split_axis=0, concat_axis=0, tiled=True)
-
-    def columns(a):
-        return a.reshape(T, E, -1).swapaxes(0, 1)
-
-    cot_here = trade(cot_slots.reshape(E, CAP, D)).reshape(E * CAP, D)
-    cot_there = lax.ppermute(cot_here, "seq", [(i, i ^ 1) for i in range(S)])
-    cot_pair = jnp.where(
-        core == 0, jnp.concatenate([cot_here, cot_there]), jnp.concatenate([cot_there, cot_here])
+    route = to_chunks(routes[0], J)
+    (
+        small, gpack, router_t, table, choose_wide, masks, conv_in, hconv, gate, sig, mixed, dt, y, mid, moe, chances,
+        s_all, states, w_in, w_out, arrived, cot_pair, normed_z,
+    ) = forward(
+        z, S, plane, tok, tokens[0, T - J :], wide_rows(seg[T - 3 :]), wide_rows(seg[:3]), cot, route,
+        to_chunks(masks, J), *owned, gr, 1
     )
-
-    normed, conv_in, hconv, gate, sig, mixed = front(z, tok, halo, masks, gpack, w_in, small)
-    normed_z = trade(columns(normed)).reshape(E * T, -1)
-    dt, pre, hdev, stot, dwin = summary(z, mixed, sig, masks, small)
-    h_all, s_all = exchange("seq", S, [hdev, stot], [True, True], 2)
-    states, y, mid, moe, chances, outbound = scan_forward(
-        z, where, mixed, dt, sig, gate, masks, small, pre, dwin, h_all, s_all, w_out, tok, gpack, router_t, table
-    )
-    arrived = dispatch(E, S, outbound.reshape(E, CAP, D), 3)
+    normed_z = normed_z.reshape(E * T, -1)
     outp, dxp, dwu, dwd = expert(
-        z, where, arrived.reshape(2 * E * CAP, D), cot_pair, router_t, up_proj[0], down_proj[0]
+        z, where, arrived.reshape(2 * E * CAP, D), cot_pair.reshape(2 * E * CAP, D), router_t, up_proj[0], down_proj[0]
     )
     token_grad, gsmall, ggrad, back_out, gate_all, conv_all, branch_all, gated_z, up_sum, down_part = backward(
         z, S, plane, dxp.reshape(2, E * CAP, -1), outp.reshape(2, E * CAP, D), dwu, dwd, states, w_out, w_in, table,

time: 491 us -> 434 us (0.88)
  Pallas kernels: 410 us -> 374 us
  starting transfers between devices: 16.4 us -> 0 us
    pallas_call x6 -> x1, Pallas kernels: 156 us -> 117 us  [forward(): pl.pallas_call(body, name='forward', in_specs=[vm] * 7 + [ANY] * 4, out_s...]
    all_to_all x2 -> x0, starting transfers between devices: 12.4 us -> none  [trade(): return lax.all_to_all(a, 'exp', split_axis=0, concat_axis=0, tiled=True)]
  transfers between devices with their start and end apart: 5 -> 0, of which waited for: 0 -> 0; matrix products, arithmetic and copies ran while one was open for 6% -> 0% of each run, Pallas kernels for 70% -> 0%
where the time goes in v4:
time: 434 us; the launch traced here: 430 us
  Pallas kernels  374 us (86%)
  local copies, waits for them, and re-layouts  33.6 us (8%)
  other arithmetic  17.9 us (4%)
    pallas_call x1, Pallas kernels, backward(): pl.pallas_call(body, name='backward', in_specs=[ANY] * 7 + [vm] * (len(in...  162 us
    pallas_call x1, Pallas kernels, forward(): pl.pallas_call(body, name='forward', in_specs=[vm] * 7 + [ANY] * 4, out_s...  117 us
    pallas_call x1, Pallas kernels, reduce_plane(): pl.pallas_call(body, name='reduce_plane', in_specs=[ANY] * 3, out_specs=[...  71.5 us
    pallas_call x1, Pallas kernels, expert(): pl.pallas_call(body, name='expert', grid_spec=pltpu.PrefetchScalarGridSpe...  22.7 us

profile of v4, /device:TPU:23, one launch (start us, length us, event | category | flops | bytes accessed | tf_op | source)
XLA Modules:
  0.0 429.8 jit_solution(4852329223206333097)
XLA Ops:
  1.2 1.3 reduce.17
  2.6 0.8 pad_slice_fusion
  3.7 0.7 copy.50
  4.4 2.0 copy_bitcast_fusion.1
  6.4 1.3 reduce.16
  7.9 0.7 reshape.217.route
  8.6 0.8 convert_bitcast_fusion
  9.4 0.7 pad.22.seg_t
  10.1 0.7 pad.24.seg_h
  10.7 0.7 broadcast_in_dim.40
  11.4 0.7 broadcast_in_dim.41
  12.1 0.7 broadcast_in_dim.42
  12.8 6.3 %concatenate.18.sm_p = bf16[224,576]{1,0:T(8,128)(2,1)} concatenate(bf16[4,576]{1,0:T(4,128)(2,1)} %param.24, bf16[1,576]{1,0:T(2,128)(2,1)S(1)} %broadcast_in_dim.40, bf16[1,576]{1,0:T(2,128)(2,1)S(1)} %broadcast_in_dim.41, bf16[1,576]{1,0:T(2,128)(2,1)S(1)} %broadcast_in_dim.42, bf16[1,576]{1,0:T(2,128)(2,1)S(1)} %broadcast_in_dim.43, bf16[16,576]{1,0:T(8,128)(2,1)} %param.29, ...), dimensions={0} | concatenate | bytes 516096 | tf_op jit(solution)/shard_map/concatenate | solution.py:1587
  19.2 1.4 slice_bitcast_fusion.1.tail
  20.6 0.7 broadcast_in_dim.45
  21.2 0.7 broadcast_in_dim.46
  22.0 1.4 maximum_maximum_fusion.g_p
  23.4 117.4 %forward.1 = (f32[200,2304]{1,0:T(8,128)}, f32[8,1152]{1,0:T(8,128)}, bf16[128,1152]{1,0:T(8,128)(2,1)}, bf16[128,256]{1,0:T(8,128)(2,1)}, f32[128,128]{1,0:T(8,...) custom-call(bf16[128,1152]{1,0:T(8,128)(2,1)} %get-tuple-element.107, ...), custom_call_target="tpu_custom_call" | custom-call | tf_op jit(solution)/shard_map/forward/pallas_call | solution.py:1004
  140.7 0.6 pad_add_fusion.wh
  141.3 22.7 %expert.1 = (bf16[512,1152]{1,0:T(8,128)(2,1)}, bf16[512,1280]{1,0:T(8,128)(2,1)}, bf16[1152,1536]{1,0:T(8,128)(2,1)}, bf16[1536,1152]{1,0:T(8,128)(2,1)}) custom-call(s32[3]{0:T(128)} %pad_add_fusion.wh, bf16[512,1152]{1,0:T(8,128)(2,1)} %bitcast.95, bf16[512,1152]{1,0:T(8,128)(2,1)} %bitcast.96, bf16[128,1152]{1,0:T(8,128)(2,1)} %get-tuple-element.62.rt.router, ...), custom_call_target="tpu_custom_call" | custom-call | tf_op jit(solution)/shard_map/expert/pallas_call | solution.py:378
  164.1 161.9 %backward.1 = (f32[128,1152]{1,0:T(8,128)}, f32[200,2304]{1,0:T(8,128)}, f32[8,1152]{1,0:T(8,128)}, bf16[256,1152]{1,0:T(8,128)(2,1)}, bf16[4,128,2304]{2,1,0:T(...) custom-call(bf16[2,256,1280]{2,1,0:T(8,128)(2,1)} %bitcast.93, ...), custom_call_target="tpu_custom_call" | custom-call | tf_op jit(solution)/shard_map/backward/pallas_call | solution.py:1516
  326.0 1.6 convert.19
  327.6 1.2 reshape.207
  329.2 1.3 fusion.9
  330.5 1.0 fusion.2
  331.5 1.2 pad.25
  332.7 1.0 copy-done.1
  333.7 0.9 fusion
  334.7 0.9 fusion.1
  335.6 1.7 pad_maximum_fusion.xi
  337.3 71.5 %reduce_plane.1 = (bf16[288,4608]{1,0:T(8,128)(2,1)}, bf16[4,2,80,1152]{3,2,1,0:T(8,128)(2,1)}, bf16[4,2,32,576]{3,2,1,0:T(8,128)(2,1)}) custom-call(bf16[288,4608]{1,0:T(8,128)(2,1)} %pad_maximum_fusion.xi, bf16[4,2,80,1152]{3,2,1,0:T(8,128)(2,1)} %bitcast.88, bf16[4,4,2,32,576]{4,3,2,1,0:T(8,128)(2,1)} %bitcast.89), custom_call_target="tpu_custom_call" | custom-call | tf_op jit(solution)/shard_map/reduce_plane/pallas_call | solution.py:260
  408.7 4.9 %convert_element_type.131 = f32[288,4608]{1,0:T(8,128)} convert(bf16[288,4608]{1,0:T(8,128)(2,1)} %get-tuple-element.92) | non-fusion elementwise | flops 1327104 | bytes 7962624 | tf_op jit(solution)/shard_map/convert_element_type | solution.py:1659
  413.7 1.8 bitcast_convert_fusion
  415.6 0.7 slice_bitcast_fusion
  416.3 0.7 slice.83
  417.0 0.6 slice.85
  417.6 0.6 slice_reduce_fusion
  418.3 0.6 slice.80
  418.9 0.6 slice_bitcast_fusion.2
  419.5 0.6 slice_reduce_fusion.3
  420.1 0.6 reshape.213
  420.6 1.4 copy.59
  422.0 2.6 reshape.212
  424.6 1.1 multiply_reduce_fusion
  425.8 1.1 fusion.7
  426.9 0.7 copy.52
  427.6 0.9 copy.53
  428.5 1.2 copy.77
  (54 shorter events, 1.8 us)
Async XLA Ops:
  327.6 1.3 copy-start.10
  328.8 1.7 copy-start.11
  328.9 1.6 copy-start.12
  331.5 2.2 copy-start.1
  331.5 2.2 copy-start.4
  332.7 2.0 copy-start
  408.7 4.9 %copy-start.5 = (bf16[4,2,80,1152]{3,2,1,0:T(8,128)(2,1)S(1)}, bf16[4,2,80,1152]{3,2,1,0:T(8,128)(2,1)}, u32[]{:S(2)}) copy-start(bf16[4,2,80,1152]{3,2,1,0:T(8,128)(2,1)} %get-tuple-element.93) | copy-start | bytes 4423684
  413.7 1.8 copy-start.9
  413.7 6.3 %copy-start.6 = (bf16[2,144,1536]{2,1,0:T(8,128)(2,1)S(1)}, bf16[2,144,1536]{2,1,0:T(8,128)(2,1)}, u32[]{:S(2)}) copy-start(bf16[2,144,1536]{2,1,0:T(8,128)(2,1)} %get-tuple-element.94) | copy-start | bytes 2654212
  422.0 3.8 copy-start.2
  422.0 3.8 copy-start.8
  422.0 5.6 %copy-start.7 = (f32[128,1152]{1,0:T(8,128)S(1)}, f32[128,1152]{1,0:T(8,128)}, u32[]{:S(2)}) copy-start(f32[128,1152]{1,0:T(8,128)} %get-tuple-element.83) | copy-start | bytes 1769476
  424.6 3.9 copy-start.3

commit v5 on v4

--- a/solution.py
+++ b/solution.py
@@ -122,159 +122,103 @@
     pl.semaphore_wait(barrier, len(peers))
 
 
-def reduce_plane(E, p_in, p_out, p_small, cid):
-    RI, CI = p_in.shape
-    ri, ci = RI // 2, CI // 4
-    _, ro, co = p_out.shape
-    _, rs8, cs = p_small.shape
-    rs = rs8 // 8
-    p_small = p_small.reshape(E, 4, 2, rs, cs)
-    p_out = p_out.reshape(4, 2, ro, co)
-
-    def body(xi, xo, xs, oi, oo, os, a_i, b_i, a_o, b_o, a_s, b_s, t_i, t_o, t_s, z_s, r_i, r_o, r_s,
-             lsem, c_send, c_recv, q_send, q_recv, z_send, z_recv, g_send, g_recv, f_send, f_recv):
-        s, me = lax.axis_index("seq"), lax.axis_index("exp")
-        chip, core = s // 2, lax.rem(s, 2)
-        other = 1 - core
-        sib = {"seq": chip * 2 + other, "exp": me}
-        chips = [chip + 1 - 2 * lax.rem(chip, 2), chip + 2 - 4 * (chip // 2), 3 - chip]
-        there = [{"seq": q * 2 + core, "exp": me} for q in chips]
-        zs = [lax.rem(me + k, E) for k in range(1, E)]
-        greet([sib] + there + [{"seq": s, "exp": p} for p in zs])
-
-        def remote(src, dst, send, recv, to):
-            return pltpu.make_async_remote_copy(src, dst, send, recv, device_id=to, device_id_type=MESH)
-
-        half = lambda c: pl.ds(pl.multiple_of(c * ri, 16), ri)
-        first = [
-            remote(xi.at[half(other)], b_i, c_send.at[0], c_recv.at[0], sib),
-            remote(xo.at[:, other], b_o, c_send.at[1], c_recv.at[1], sib),
-            remote(xs.at[:, :, other], b_s, c_send.at[2], c_recv.at[2], sib),
+def group_place(groups, g):
+    main = groups // 8
+    if g < 8 * main:
+        return g // main, 16 * (g % main)
+    return g - 8 * main, 16 * main
+
+
+def chunk_rows(rows):
+    groups = rows // 16
+    return 16 * (groups // 8 + (1 if groups % 8 else 0))
+
+
+class PlaneSum:
+    def __init__(self, E, p, b, t, zb, out, add, sems):
+        self.E, self.p, self.b, self.t, self.zb, self.out, self.add = E, p, b, t, zb, out, add
+        self.cs, self.cr, self.qs, self.qr, self.zs, self.zr, self.gs, self.gr, self.fs, self.fr, self.own = sems
+        s, self.me = lax.axis_index("seq"), lax.axis_index("exp")
+        self.chip, self.core = s // 2, lax.rem(s, 2)
+        self.sib = {"seq": s + 1 - 2 * self.core}
+        self.chips = [self.chip + 1 - 2 * lax.rem(self.chip, 2), self.chip + 2 - 4 * (self.chip // 2), 3 - self.chip]
+        self.far = [{"seq": q * 2 + self.core} for q in self.chips]
+        self.zz = [lax.rem(self.me + k, E) for k in range(1, E)]
+
+    def remote(self, src, dst, send, recv, to):
+        return pltpu.make_async_remote_copy(src, dst, send, recv, device_id=to, device_id_type=MESH)
+
+    def swap_start(self):
+        self.swap = self.remote(self.p.at[:, :, 1 - self.core], self.b, self.cs, self.cr, self.sib)
+        self.swap.start()
+
+    def swap_finish(self):
+        self.swap.wait()
+        for l in range(self.p.shape[0]):
+            self.p[l, :, self.core] = (self.p[l, :, self.core].astype(F32) + self.b[l].astype(F32)).astype(BF16)
+        self.crossing = [
+            self.remote(self.p.at[:, self.chips[k], self.core], self.t.at[k], self.qs.at[k], self.qr.at[k], self.far[k])
+            for k in range(3)
         ]
-        for c in first:
-            c.start()
-        mine = [
-            pltpu.make_async_copy(xi.at[half(core)], a_i, lsem.at[0]),
-            pltpu.make_async_copy(xo.at[:, core], a_o, lsem.at[1]),
-            pltpu.make_async_copy(xs.at[:, :, core], a_s, lsem.at[2]),
+        for c in self.crossing:
+            c.start()
+
+    def chips_finish(self):
+        for c in self.crossing:
+            c.wait()
+        for l in range(self.p.shape[0]):
+            v = self.p[l, self.chip, self.core].astype(F32)
+            for k in range(3):
+                v = v + self.t[k, l].astype(F32)
+            self.p[l, self.chip, self.core] = v.astype(BF16)
+        if self.zb is None:
+            self.spread(self.p.at[:, self.chip, self.core])
+            return
+        self.along = [
+            self.remote(self.p.at[d, self.chip, self.core], self.zb.at[self.me], self.zs.at[k], self.zr.at[k], {"exp": d})
+            for k, d in enumerate(self.zz)
         ]
-        for c in mine:
-            c.start()
-        adds = lambda a, b: (a.astype(F32) + b.astype(F32)).astype(BF16)
-        cols = lambda q: pl.ds(pl.multiple_of(q * ci, LANES), ci)
-        second = []
-        for w in (0, 1, 2):
-            mine[w].wait()
-            first[w].wait()
-            if w == 0:
-                a_i[...] = adds(a_i[...], b_i[...])
-            elif w == 1:
-                a_o[...] = adds(a_o[...], b_o[...])
-            else:
-                a_s[...] = adds(a_s[...], b_s[...])
-            for k in range(3):
-                src = [a_i.at[:, cols(chips[k])], a_o.at[chips[k]], a_s.at[:, chips[k]]][w]
-                dst = [t_i, t_o, t_s][w].at[k]
-                c = remote(src, dst, q_send.at[w, k], q_recv.at[w, k], there[k])
-                c.start()
-                second.append(c)
-
-        def total(own, parts):
-            out = own.astype(F32)
-            for k in range(3):
-                out = out + parts[k].astype(F32)
-            return out.astype(BF16)
-
-        for c in second[6:9]:
+        for c in self.along:
+            c.start()
+
+    def z_finish(self):
+        for c in self.along:
             c.wait()
-        a_s[:, chip] = total(a_s[:, chip], t_s)
-        third = []
-        for k, p in enumerate(zs):
-            c = remote(a_s.at[p, chip], z_s.at[me], z_send.at[k], z_recv.at[k], {"seq": s, "exp": p})
-            c.start()
-            third.append(c)
-
-        gathers = []
-
-        def spread(w, ref):
-            for k in range(3):
-                c = remote(ref, ref, g_send.at[w, k], g_recv.at[w, k], there[k])
-                c.start()
-                gathers.append(c)
-            c = remote(ref, ref, f_send.at[w, 3], f_recv.at[w, 3], sib)
-            c.start()
-            gathers.append(c)
-
-        for c in second[0:3]:
-            c.wait()
-        r_i[core, chip] = total(a_i[:, cols(chip)], t_i)
-        spread(0, r_i.at[core, chip])
-        for c in second[3:6]:
-            c.wait()
-        r_o[core, chip] = total(a_o[chip], t_o)
-        spread(1, r_o.at[core, chip])
-        for c in third:
-            c.wait()
-        out = a_s[me, chip].astype(F32)
-        for k, p in enumerate(zs):
-            out = out + z_s[p].astype(F32)
-        r_s[core, chip] = out.astype(BF16)
-        spread(2, r_s.at[core, chip])
-
-        def landed(w, c, q):
-            return [r_i, r_o, r_s][w].at[c, q]
-
-        passed = []
-        for w in (0, 1, 2):
-            for k in range(3):
-                ref = landed(w, core, chips[k])
-                remote(ref, ref, g_send.at[w, k], g_recv.at[w, k], there[k]).wait_recv()
-                c = remote(ref, ref, f_send.at[w, k], f_recv.at[w, k], sib)
-                c.start()
-                passed.append(c)
-        for c in gathers:
+        v = self.p[self.me, self.chip, self.core]
+        if self.add:
+            v = v.astype(F32)
+            for d in self.zz:
+                v = v + self.zb[d].astype(F32)
+            self.zb[self.me] = v.astype(BF16)
+            self.spread(self.zb.at[self.me])
+        else:
+            self.zb[self.me] = v
+            self.spread(self.zb)
+
+    def spread(self, ref):
+        dst = self.out.at[self.chip, self.core]
+        self.sends = [self.remote(ref, dst, self.gs.at[k], self.gr.at[k], self.far[k]) for k in range(3)]
+        self.sends.append(self.remote(ref, dst, self.fs.at[3], self.fr.at[3], self.sib))
+        for c in self.sends:
+            c.start()
+        self.local = pltpu.make_async_copy(ref, dst, self.own)
+        self.local.start()
+
+    def forward(self):
+        for k in range(3):
+            ref = self.out.at[self.chips[k], self.core]
+            self.remote(ref, ref, self.gs.at[k], self.gr.at[k], self.far[k]).wait_recv()
+            c = self.remote(ref, ref, self.fs.at[k], self.fr.at[k], self.sib)
+            c.start()
+            self.sends.append(c)
+
+    def finish(self):
+        for c in self.sends:
             c.wait_send()
-        for c in passed:
-            c.wait_send()
-        for w in (0, 1, 2):
-            for k in range(4):
-                ref = landed(w, other, chips[k] if k < 3 else chip)
-                remote(ref, ref, f_send.at[w, k], f_recv.at[w, k], sib).wait_recv()
-        writes = []
-        for c in range(2):
-            for q in range(4):
-                writes.append(
-                    pltpu.make_async_copy(
-                        r_i.at[c, q], oi.at[c * ri : (c + 1) * ri, q * ci : (q + 1) * ci], lsem.at[3 + c * 4 + q]
-                    )
-                )
-                writes.append(pltpu.make_async_copy(r_o.at[c, q], oo.at[q, c], lsem.at[11 + c * 4 + q]))
-                writes.append(pltpu.make_async_copy(r_s.at[c, q], os.at[q, c], lsem.at[19 + c * 4 + q]))
-        for c in writes:
-            c.start()
-        for c in writes:
-            c.wait()
-
-    v = lambda *dims: pltpu.VMEM(dims, BF16)
-    sem = lambda *dims: pltpu.SemaphoreType.DMA(dims)
-    oi, oo, os = pl.pallas_call(
-        body,
-        name="reduce_plane",
-        in_specs=[ANY] * 3,
-        out_specs=[ANY] * 3,
-        out_shape=[sds((RI, CI), BF16), sds((4, 2, ro, co), BF16), sds((4, 2, rs, cs), BF16)],
-        scratch_shapes=[
-            v(ri, CI), v(ri, CI), v(4, ro, co), v(4, ro, co), v(E, 4, rs, cs), v(E, 4, rs, cs),
-            v(3, ri, ci), v(3, ro, co), v(3, E, rs, cs), v(E, rs, cs),
-            v(2, 4, ri, ci), v(2, 4, ro, co), v(2, 4, rs, cs),
-            sem(27), sem(3), sem(3), sem(3, 3), sem(3, 3), sem(E - 1), sem(E - 1),
-            sem(3, 3), sem(3, 3), sem(3, 4), sem(3, 4),
-        ],
-        compiler_params=pltpu.CompilerParams(
-            collective_id=cid, has_side_effects=True, vmem_limit_bytes=VMEM_LIMIT
-        ),
-    )(p_in, p_out, p_small)
-    return oi, oo.reshape(8, ro, co), os.reshape(8 * rs, cs)
+        self.local.wait()
+        for k in range(4):
+            ref = self.out.at[self.chips[k] if k < 3 else self.chip, 1 - self.core]
+            self.remote(ref, ref, self.fs.at[k], self.fr.at[k], self.sib).wait_recv()
 
 
 def expand_columns(z, src, col0, dst):
@@ -633,14 +577,30 @@
                     self.z_each(r, d, lambda c: c.wait_send())
 
 
-def forward(z, S, plane, tok, tail, seg_tail, seg_head, cot, route, masks, in_proj, out_proj, small_own, g_own, gr, cid):
+def small_rows(z):
+    return z.SMALL + -z.SMALL % 32
+
+
+def pack_small(z, par, own_sm, own_g):
+    conv_w, conv_b, dt_b, skip, a_log, dt_w, x_w, gain_a, gain_b, router = par
+    cw, dw = own_sm.shape[1], own_g.shape[1]
+    eye = lambda r, c: (
+        lax.broadcasted_iota(jnp.int32, (r, c), 0) == lax.broadcasted_iota(jnp.int32, (r, c), 1)
+    ).astype(F32).astype(BF16)
+    wide = lambda ref: ref[...].astype(F32)
+    rows = [wide(conv_w), wide(conv_b), wide(dt_b), wide(skip), jnp.zeros((1, cw), F32), wide(a_log), wide(dt_w)]
+    rows += [mm_nt(eye(z.XW, z.XW), x_w[...]), jnp.zeros((-z.SMALL % 32, cw), F32)]
+    own_sm[...] = jnp.concatenate(rows, axis=0).astype(BF16)
+    rows = [wide(gain_a), wide(gain_b), mm_nt(eye(16, z.E), router[...]), jnp.zeros((14, dw), F32)]
+    own_g[...] = jnp.concatenate(rows, axis=0).astype(BF16)
+
+
+def forward(z, S, plane, tokens, cotangent, seg, route, params, in_proj, out_proj, gr, cid):
     T, D, DI, N, J, E, CAP = z.T, z.D, z.DI, z.N, z.J, z.E, z.CAP
-    H = tail.shape[0]
+    H = J
     M = E * CAP
     DZ, NZ = DI // E, D // E
-    rs, rg = small_own.shape[0], g_own.shape[0]
-    if not plane:
-        rs, rg = rs // E, rg // E
+    rs, rg = small_rows(z), 32
     cb = pick(DI, (384, 256, 128))
     cs = pick(DI, (768, 384, 256, 128))
     tg = tile_groups(cs)
@@ -652,71 +612,112 @@
     split = (tiles // 4 - (0 if tiles % 4 else 1)) * LANES
     split_o = max(1, tiles_o * 2 // 9) * LANES
 
-    def body(
-        tok, tail, seg_t, seg_h, cot, route, msk_in, in_p, out_p, sm_p, g_p,
-        sm, gp, rt, table, choose, masks, conv_in, hconv, gate, sig, mixed, dt, y, mid, moe, ch_o, s_all,
-        st_o, win_o, wout_o, arr_o, cot_o, nz_o,
-        wc, wg, wo, smb, gb, nrm, halo, seg_in, bx, cx, cl, u_s, rates_s, hd, hdev, stot, h_all, pre_s, dwin, hin,
-        st_v, acc, outb, cotb, nz,
-        ld, zs, zr, ps, pr, c_s, c_r, t_s, t_r, h_s, h_r, d_s, d_r, q_s, q_r, k_s, k_r, n_s, n_r, x_s, x_r,
-    ):
+    def body(*refs):
+        tokn, cotn, seg_r, route_r = refs[:4]
+        np_ = len(params)
+        par = refs[4 : 4 + np_]
+        (
+            in_p, out_p,
+            sm, gp, rt, table, choose, masks, conv_in, hconv, gate, sig, mixed, dt, y, mid, moe, ch_o, s_all, tok, cot,
+            st_o, win_o, wout_o, arr_o, cot_o, nz_o,
+            wc, wg, wo, smb, gb, nrm, halo, seg_in, bx, cx, cl, u_s, rates_s, hd, hdev, stot, h_all, pre_s, dwin, hin,
+            st_v, acc, outb, cotb, own_sm, own_g, own_seg,
+            ld, zs, zr, ps, pr, c_s, c_r, t_s, t_r, h_s, h_r, d_s, d_r, q_s, q_r, k_s, k_r, n_s, n_r, x_s, x_r,
+        ) = refs[4 + np_ :]
         s, me = lax.axis_index("seq"), lax.axis_index("exp")
         core = lax.rem(s, 2)
         sib = {"seq": s + 1 - 2 * core}
         seqs = [lax.rem(s + k, S) for k in range(1, S)]
         zz = [lax.rem(me + k, E) for k in range(1, E)]
-        greet([{"seq": p} for p in seqs] + [{"exp": p} for p in zz])
+        barrier = pltpu.get_barrier_semaphore()
+        peers = [{"seq": p} for p in seqs] + [{"exp": p} for p in zz]
+        for peer in peers:
+            pl.semaphore_signal(barrier, inc=1, device_id=peer, device_id_type=MESH)
 
         def remote(src, dst, send, recv, to):
             return pltpu.make_async_remote_copy(src, dst, send, recv, device_id=to, device_id_type=MESH)
 
-        ahead = {"seq": lax.rem(s + 1, S)}
-        edges = [remote(tail, halo, t_s.at[0], t_r.at[0], ahead), remote(seg_t, seg_in, t_s.at[1], t_r.at[1], ahead)]
-        for c in edges:
-            c.start()
+        if plane:
+            pack_small(z, par, own_sm, own_g)
+        segrow = seg_r[...].astype(F32)
+        own_seg[...] = jnp.broadcast_to(segrow, (SUB, T))
+        pl.semaphore_wait(barrier, len(peers))
         sems = lambda a: (zs.at[a], zr.at[a], ps.at[a], pr.at[a], c_s.at[a], c_r.at[a])
         if plane:
             parts = [
-                Spread(E, sm_p, 0, smb, sm_p.shape[1], sm_p.shape[1], 0, sems(0)),
-                Spread(E, g_p, 0, gb, g_p.shape[1], g_p.shape[1], 0, sems(1)),
+                Spread(E, own_sm, 0, smb, DZ, DZ, 0, sems(0)),
+                Spread(E, own_g, 0, gb, NZ, NZ, 0, sems(1)),
                 Spread(E, in_p, 0, wc, DI, DI - 4 * split, split, sems(2)),
                 Spread(E, in_p, DI, wg, DI, DI - 4 * split, split, sems(3)),
                 Spread(E, out_p, 0, wo, D, D - 4 * split_o, split_o, sems(4)),
             ]
-            for p in parts[:4]:
+            for p in parts[:3]:
                 p.start()
             loads = [p.local(ld.at[a]) for a, p in enumerate(parts)]
         else:
             loads = [
-                pltpu.make_async_copy(sm_p, smb, ld.at[0]),
-                pltpu.make_async_copy(g_p, gb, ld.at[1]),
+                pltpu.make_async_copy(par[0], smb, ld.at[0]),
+                pltpu.make_async_copy(par[1], gb, ld.at[1]),
                 pltpu.make_async_copy(in_p.at[:, 0:DI], wc, ld.at[2]),
                 pltpu.make_async_copy(in_p.at[:, DI : 2 * DI], wg, ld.at[3]),
                 pltpu.make_async_copy(out_p, wo, ld.at[4]),
             ]
+        ahead = {"seq": lax.rem(s + 1, S)}
+        edges = [
+            remote(tokn.at[pl.ds(T - H, H)], halo, t_s.at[0], t_r.at[0], ahead),
+            remote(own_seg, seg_in, t_s.at[1], t_r.at[1], ahead),
+        ]
+        for c in edges:
+            c.start()
         for c in loads:
             c.start()
-
-        lane = lax.broadcasted_iota(jnp.int32, (T, LANES), 1)
-        chosen = (lane == route[...]).astype(F32)
+        queue = []
+        if plane:
+            wg_p, wo_p = parts[3], parts[4]
+            queue = [wg_p.start] + [functools.partial(wg_p.hop, k) for k in range(1, E - 1)]
+            queue += [wo_p.start, functools.partial(wg_p.hop, E - 1)]
+            for k in range(1, E):
+                queue += [functools.partial(wo_p.hop, k), functools.partial(wg_p.plane, k)]
+            queue += [functools.partial(wo_p.plane, k) for k in range(1, E)]
+
+        def progress(count):
+            for _ in range(count):
+                if queue:
+                    queue.pop(0)()
+
+        lane = lax.broadcasted_iota(jnp.int32, (T, T), 1)
+        prow = lax.broadcasted_iota(jnp.int32, (T, T), 0)
+        place = (prow % SUB) * J + prow // SUB
+        order = (lane == place).astype(F32).astype(BF16)
+        tok[...] = mm(order, tokn[...]).astype(BF16)
+        cot[...] = mm(order, cotn[...]).astype(BF16)
+        my_route = jnp.sum(
+            jnp.where(lane == place, route_r[...].astype(F32), 0.0), axis=1, keepdims=True
+        ).astype(jnp.int32)
+        chosen = (lane == my_route).astype(F32)
         choose[...] = chosen
-        upto = lax.broadcasted_iota(jnp.int32, (T, T), 1) <= lax.broadcasted_iota(jnp.int32, (T, T), 0)
-        counts = mm(upto.astype(F32).astype(BF16), chosen.astype(BF16))
+        counts = mm((lane <= prow).astype(F32).astype(BF16), chosen.astype(BF16))
         rank = jnp.sum(counts * chosen, axis=-1, keepdims=True).astype(jnp.int32) - 1
         slots = lax.broadcasted_iota(jnp.int32, (T, M), 1)
-        table[...] = (slots == route[...] * CAP + rank).astype(F32).astype(BF16)
+        table[...] = (slots == my_route * CAP + rank).astype(F32).astype(BF16)
         cotb[...] = mm_tn(table[...], cot[...]).astype(BF16)
+        t32 = tok[...].astype(F32)
+        scaled = t32 * rms_scale(t32)
 
         if plane:
             for k in range(1, E):
-                for p in parts[:4]:
+                for p in parts[:3]:
                     p.hop(k)
                 if k == 1:
-                    parts[4].start()
-                if k == 2:
+                    progress(1)
+                elif k == 2:
+                    progress(1)
                     parts[2].plane(1)
+                else:
+                    progress(1)
             for k in range(2, E):
                 parts[2].plane(k)
+            progress(1)
         block_of = lambda ref, p: ref.at[pl.ds(pl.multiple_of(p * CAP, 16), CAP)]
         cot_moves = [remote(block_of(cotb, p), cot_o.at[core, me], k_s.at[k], k_r.at[k], {"exp": p}) for k, p in enumerate(zz)]
         if plane:
@@ -736,17 +737,19 @@
         for c in edges:
             c.wait()
         live = jnp.where(s > 0, 1.0, 0.0)
-        masks[...] = msk_in[...]
-        col8 = lax.broadcasted_iota(jnp.int32, (1, SUB), 1)
-        for t in range(3):
-            row = masks[SUB * t : SUB * t + 1, :]
-            for o in range(3 - t):
-                before = seg_in[t + o : t + o + 1, 0:SUB] * live
-                same = (before == seg_h[t : t + 1, 0:SUB]).astype(F32)
-                row = jnp.where(col8 == o, same, row)
-            masks[SUB * t : SUB * t + 1, :] = row
-        t32 = tok[...].astype(F32)
-        nrm[0:T, :] = (t32 * rms_scale(t32) * gp[0:1, :]).astype(BF16)
+        col8 = lax.broadcasted_iota(jnp.int32, (T, SUB), 1)
+        prev = seg_in[0:1, :] * live
+
+        def seg_at(k):
+            own = jnp.where(lane == place - k, segrow, 0.0)
+            return jnp.sum(own + jnp.where(lane == place - k + T, prev, 0.0), axis=1, keepdims=True)
+
+        now = seg_at(0)
+        same = jnp.zeros((T, SUB), F32)
+        for o in range(4):
+            same = jnp.where(col8 == o, (seg_at(3 - o) == now).astype(F32), same)
+        masks[...] = same
+        nrm[0:T, :] = (scaled * gp[0:1, :]).astype(BF16)
         h32 = halo[...].astype(F32) * live
         nrm[T : T + H, :] = (h32 * rms_scale(h32) * gp[0:1, :]).astype(BF16)
         mixed[...] = jnp.zeros_like(mixed)
@@ -768,17 +771,8 @@
             return carry
 
         lax.fori_loop(0, DI // cb, conv_block, 0)
-        for e in range(E):
-            nz[e] = nrm[0:T, e * NZ : (e + 1) * NZ]
-        nz_moves = [remote(nz.at[p], nz_o.at[me], n_s.at[k], n_r.at[k], {"exp": p}) for k, p in enumerate(zz)]
-        nz_own = pltpu.make_async_copy(nz.at[me], nz_o.at[me], ld.at[5])
-        nz_own.start()
-        if plane:
-            for k in range(1, E):
-                parts[4].hop(k)
-                parts[3].plane(k)
-        for c in cot_moves + nz_moves:
-            c.start()
+        chain_n = Chain(E, nrm.at[0:T], nz_o, n_s, n_r, ld.at[5])
+        progress(2)
         cot_own = pltpu.make_async_copy(block_of(cotb, me), cot_o.at[core, me], ld.at[6])
         cot_own.start()
 
@@ -797,6 +791,7 @@
             return carry
 
         lax.fori_loop(0, DI // cs, step_block, 0)
+        progress(2)
 
         def chunk_block(p, carry):
             lanes = [lane_at(p, tg, k) for k in range(tg)]
@@ -842,7 +837,12 @@
                         hd[g + n : g + n + 1, lanes[k]] = h[SUB - 1 : SUB, :]
             return carry
 
-        lax.fori_loop(0, DI // wide, chunk_block, 0)
+        third = DI // wide // 3
+        lax.fori_loop(0, third, chunk_block, 0)
+        progress(2)
+        lax.fori_loop(third, 2 * third, chunk_block, 0)
+        progress(2)
+        lax.fori_loop(2 * third, DI // wide, chunk_block, 0)
         hdev[...] = hd[...].astype(BF16)
         h_moves = [remote(hdev, h_all.at[s], h_s.at[0, k], h_r.at[0, k], {"seq": p}) for k, p in enumerate(seqs)]
         h_moves += [remote(stot, s_all.at[s], h_s.at[1, k], h_r.at[1, k], {"seq": p}) for k, p in enumerate(seqs)]
@@ -850,6 +850,10 @@
             c.start()
         h_all[s] = hdev[...]
         s_all[s] = stot[...]
+        for c in cot_moves:
+            c.start()
+        chain_n.start()
+        progress(len(queue))
         if plane:
             parts[3].landed()
 
@@ -860,8 +864,6 @@
 
         lax.fori_loop(0, DI // cb, gate_block, 0)
         if plane:
-            for k in range(1, E):
-                parts[4].plane(k)
             parts[4].landed()
         outs = [
             pltpu.make_async_copy(wc, win_o.at[:, 0:DI], ld.at[7]),
@@ -940,12 +942,16 @@
 
             lax.fori_loop(0, cs // wide, pair, 0)
             save(i).start()
+            if i + 1 < E:
+                chain_n.hop(i + 1)
             yv = y[:, C] + sm[SKIP : SKIP + 1, C] * sig[:, C].astype(F32)
             y[:, C] = yv
             g_in = gate[:, C]
             gated = (yv * (g_in * sigmoid(g_in))).astype(BF16)
             acc[...] += mm(gated, wo[C, :])
 
+        for k in range(steps + 1, E):
+            chain_n.hop(k)
         m32 = tok[...].astype(F32) + acc[...]
         mid[...] = m32
         moe[...] = (m32 * rms_scale(m32) * gp[1:2, :]).astype(BF16)
@@ -973,12 +979,11 @@
         if plane:
             for p in parts:
                 p.finish()
-        for c in outs + [nz_own, cot_own, arr_own]:
+        for c in outs + [cot_own, arr_own]:
             c.wait()
+        chain_n.finish()
         for i in range(max(0, steps - 2), steps):
             save(i).wait()
-        for c in nz_moves:
-            c.wait()
         for c in cot_moves + out_moves + passes:
             c.wait_send()
         for w, ref in ((0, cot_o), (1, arr_o)):
@@ -990,21 +995,21 @@
     sem = lambda *dims: pltpu.SemaphoreType.DMA(dims)
     vm = pl.BlockSpec(memory_space=pltpu.VMEM)
     zslots = 2 * (E - 1)
-    ins = (tok, tail, seg_tail, seg_head, cot, route, masks, in_proj, out_proj, small_own, g_own)
+    ins = (tokens, cotangent, seg, route) + tuple(params) + (in_proj, out_proj)
     vm_outs = [
         sds((z.SMALL, DI), F32), sds((gr, D), F32), sds((LANES, D), BF16), sds((T, M), BF16), sds((T, LANES), F32),
         sds((T, SUB), F32), sds((T, DI), F32), sds((H, DI), F32), sds((T, DI), F32), sds((T, DI), BF16),
         sds((T, z.XW), F32), sds((T, DI), F32), sds((T, DI), F32), sds((T, D), F32), sds((T, D), BF16),
-        sds((T, LANES), F32), sds((S, 1, DI), F32),
+        sds((T, LANES), F32), sds((S, 1, DI), F32), sds((T, D), BF16), sds((T, D), BF16),
     ]
     any_outs = [
         sds((ST, DI), BF16), sds((D, 2 * DI), BF16), sds((DI, D), BF16), sds((2, E, CAP, D), BF16),
-        sds((2, E, CAP, D), BF16), sds((E, T, NZ), BF16),
+        sds((2, E, CAP, D), BF16), sds((E, T, D), BF16),
     ]
     return pl.pallas_call(
         body,
         name="forward",
-        in_specs=[vm] * 7 + [ANY] * 4,
+        in_specs=[vm] * 4 + [vm if plane else ANY] * len(params) + [ANY] * 2,
         out_specs=[vm] * len(vm_outs) + [ANY] * len(any_outs),
         out_shape=vm_outs + any_outs,
         scratch_shapes=[
@@ -1013,10 +1018,11 @@
             v((J * N * SUB, LANES), F32), v((J * N * SUB, LANES), F32), v((T, LANES), F32), v((T, DI), F32),
             v((N, DI), F32), v((N, DI), F32), v((N, DI), BF16), v((1, DI), F32), v((S, N, DI), BF16),
             v((N * SUB, DI), F32), v((SUB, DI), F32), v((N, cs), F32),
-            v((2, ST, cs), BF16), v((T, D), F32), v((M, D), BF16), v((M, D), BF16), v((E, T, NZ), BF16),
+            v((2, ST, cs), BF16), v((T, D), F32), v((M, D), BF16), v((M, D), BF16),
+            v((rs, DZ), BF16), v((rg, NZ), BF16), v((SUB, T), F32),
             sem(13), sem(5, 2, zslots), sem(5, 2, zslots), sem(5, 3, zslots), sem(5, 3, zslots),
             sem(5, 5, zslots), sem(5, 5, zslots), sem(2), sem(2), sem(2, S - 1), sem(2, S - 1),
-            sem(E - 1), sem(E - 1), sem(1), sem(1), sem(E - 1), sem(E - 1), sem(E - 1), sem(E - 1),
+            sem(E - 1), sem(E - 1), sem(1), sem(1), sem(E - 1), sem(E - 1), sem(zslots), sem(zslots),
             sem(2, E), sem(2, E),
         ],
         compiler_params=pltpu.CompilerParams(
@@ -1026,14 +1032,14 @@
 
 
 def backward(z, S, plane, dxp, outp, dwu, dwd, states, w_out, w_in, table, choose, chances, mid, moe, cot, gpack,
-             router, gate, y, sig, small, mixed, dt, masks, conv_in, hconv, s_all, tok, cid):
+             router, gate, y, sig, small, mixed, dt, masks, conv_in, hconv, s_all, tok, normed_all, cid):
     T, D, DI, N, J, E, CAP = z.T, z.D, z.DI, z.N, z.J, z.E, z.CAP
     M = E * CAP
     G = gpack.shape[0]
     H = hconv.shape[0]
-    DZ = DI // E
+    DZ, NZ = DI // E, D // E
     cb_m = pick(DI, (384, 256, 128))
-    cb_s = pick(DI, (768, 384, 256, 128))
+    cb_s = pick(DI, (256, 128))
     steps_s = DI // cb_s
     tg_s = tile_groups(cb_s)
     ng_s = 4
@@ -1045,13 +1051,24 @@
 
     def body(
         dxp, outp, dwu, dwd, states, w_out, w_in, table, choose, chances, mid, moe, cot, gp, router, gate, y, sig,
-        small, mixed, dt, masks, conv_in, hconv, s_all, tok,
-        tg_o, gs_o, gg_o, back_o, gate_o, pc_o, br_o, gz_o, up_o, down_o,
-        big, wo_v, dx_a, dx_b, out_a, out_b, dx_z, yg, gi, gd, gz, br, mg, fdev, f_all, suf, ssg, dpl, cig, cg_edge,
-        edge_in, pc, bx, cx, ia, oa, cl, u_s, rates_s, fin, dg_s, rs_s, rt_s, low_s, mxg, acc, fd,
-        ua, ub, ub2, uf, da, db, db2,
+        small, mixed, dt, masks, conv_in, hconv, s_all, tok, nall,
+        tg_o, gs_o, gg_o, back_o, pg_o, pc_o, pm_o, po_o, up_o, down_o,
+        big, wo_v, n_v, dx_a, dx_b, out_a, out_b, dx_z, yg, gi, gz, br, mg, fdev, f_all, suf, cg_edge,
+        edge_in, pc, bx, cx, ia, oa, cl, u_s, rates_s, fin, dg_s, rs_s, rt_s, low_s, mxg, fd,
+        ua, ub, ub2, da, db, db2, gi_all, pc_all, br_all, gz_all, gi_b,
+        p_g, p_c, p_m, p_o, bg, bc, bm, bo, tg_, tc_, tm_, to_, zg, zc, zm,
+        pcs, pcr, pqs, pqr, pzs, pzr, pgs, pgr, pfs, pfr, pown,
         ld, sw_s, sw_r, dz_s, dz_r, oz_s, oz_r, f_s, f_r, e_s, e_r, g_s, g_r, p_s, p_r, b_s, b_r, a_s, a_r, x_s, x_r,
     ):
+        psems = lambda a: (
+            pcs.at[a], pcr.at[a], pqs.at[a], pqr.at[a], pzs.at[a], pzr.at[a], pgs.at[a], pgr.at[a], pfs.at[a],
+            pfr.at[a], pown.at[a],
+        )
+        sum_g = PlaneSum(E, p_g, bg, tg_, zg, pg_o, False, psems(0))
+        sum_c = PlaneSum(E, p_c, bc, tc_, zc, pc_o, False, psems(1))
+        sum_m = PlaneSum(E, p_m, bm, tm_, zm, pm_o, True, psems(2))
+        sum_o = PlaneSum(E, p_o, bo, to_, None, po_o, False, psems(3))
+        stage = (lambda f: f()) if plane else (lambda f: None)
         s, me = lax.axis_index("seq"), lax.axis_index("exp")
         core = lax.rem(s, 2)
         other = 1 - core
@@ -1072,15 +1089,22 @@
         loads = [
             pltpu.make_async_copy(dxp.at[core], dx_a, ld.at[0]),
             pltpu.make_async_copy(outp.at[core], out_a, ld.at[1]),
-            pltpu.make_async_copy(w_out, wo_v, ld.at[2]),
         ]
         for c in loads:
             c.start()
 
+        def out_load(i):
+            slot = lax.rem(i, 2)
+            rows = pl.ds(pl.multiple_of(i * cb_m, LANES), cb_m)
+            return pltpu.make_async_copy(w_out.at[rows], wo_v.at[slot], ld.at[2 + 15 * slot])
+
+        out_load(0).start()
+        normed_load = pltpu.make_async_copy(nall, n_v, ld.at[10])
+        normed_load.start()
+
         def state_load(i):
-            half = pl.ds((i % 2) * cb_s, cb_s)
             return pltpu.make_async_copy(
-                states.at[:, i * cb_s : (i + 1) * cb_s], big.at[0:ST, half], ld.at[3 + i % 2]
+                states.at[:, at_cols(i, cb_s)], big.at[lax.rem(i, 2), 0:ST], ld.at[3 + lax.rem(i, 2)]
             )
 
         state_load(0).start()
@@ -1150,12 +1174,17 @@
         gg_o[...] = jnp.zeros_like(gg_o)
         gg_o[1:2, :] = gain_g
         gg_o[2 : 2 + E, :] = rg[0:E, :]
-        chain_b = Chain(E, br, br_o, b_s, b_r, ld.at[9])
-        loads[2].wait()
+        chain_b = Chain(E, br, br_all, b_s, b_r, ld.at[9])
 
         def middle_block(i, carry):
             C = at_cols(i, cb_m)
-            gg = mm_nt(br[...], wo_v[C, :])
+            out_load(i).wait()
+
+            @pl.when(i + 1 < DI // cb_m)
+            def _():
+                out_load(i + 1).start()
+
+            gg = mm_nt(br[...], wo_v[lax.rem(i, 2)])
             g_in = gate[:, C]
             sg = sigmoid(g_in)
             act = g_in * sg
@@ -1163,13 +1192,21 @@
             ygv = gg * act
             yg[:, C] = ygv
             gi[:, C] = (gg * yv * (sg * (1.0 + g_in * (1.0 - sg)))).astype(BF16)
-            gd[:, C] = (yv * act).astype(BF16)
+            pc[:, C] = (yv * act).astype(BF16)
             gs_o[SKIP : SKIP + 1, C] = jnp.sum(ygv * sig[:, C].astype(F32), axis=0, keepdims=True)
             return carry
 
         lax.fori_loop(0, DI // cb_m, middle_block, 0)
-        chain_g = Chain(E, gi, gate_o, g_s, g_r, ld.at[10])
-        chain_g.start()
+        for e in range(E):
+            gi_b[e] = gi[:, e * DZ : (e + 1) * DZ]
+
+        def trade(src, dst, send, recv):
+            return [remote(src.at[p], dst.at[me], send.at[k], recv.at[k], {"exp": p}) for k, p in enumerate(zs)]
+
+        gi_moves = trade(gi_b, gi_all, g_s, g_r)
+        for c in gi_moves:
+            c.start()
+        gi_all[me] = gi_b[me]
         chain_b.start()
 
         tg, ng = 2 if DI % 256 == 0 else 1, 8
@@ -1233,14 +1270,27 @@
             c.start()
         f_all[s] = fdev[...]
         for e in range(E):
-            gz[e] = gd[:, e * DZ : (e + 1) * DZ]
-        gz_moves = [remote(gz.at[p], gz_o.at[me], x_s.at[k], x_r.at[k], {"exp": p}) for k, p in enumerate(zs)]
+            gz[e] = pc[:, e * DZ : (e + 1) * DZ]
+        gz_moves = trade(gz, gz_all, x_s, x_r)
         for c in gz_moves:
             c.start()
-        gz_own = pltpu.make_async_copy(gz.at[me], gz_o.at[me], ld.at[11])
-        gz_own.start()
-        chain_g.hop(1)
-        chain_b.hop(1)
+        gz_all[me] = gz[me]
+        p_g[...] = jnp.zeros_like(p_g)
+        p_c[...] = jnp.zeros_like(p_c)
+        p_o[...] = jnp.zeros_like(p_o)
+
+        def place_in(dst, rhs):
+            blk = pick(D, (384, 256, 128))
+            for i in range(D // blk):
+                val = mm_tn(n_v[:, i * blk : (i + 1) * blk], rhs)
+                for g in range(blk // 16):
+                    row = i * blk + 16 * g
+                    chunk, off = group_place(D // E // 16, row % (D // E) // 16)
+                    dst[row // (D // E), chunk // 2, chunk % 2, off : off + 16, :] = val[16 * g : 16 * g + 16].astype(
+                        BF16
+                    )
+
+        flat = lambda ref: ref[...].reshape(E * T, ref.shape[-1])
         if plane:
             for c in mine + up1 + [down1]:
                 c.wait()
@@ -1258,12 +1308,17 @@
         ia[...] = jnp.zeros_like(ia)
         oa[...] = jnp.zeros_like(oa)
         low_s[...] = jnp.zeros_like(low_s)
-        for i in range(steps_s):
+        low = mixed[:, 0 : z.R].astype(BF16)
+
+        def scan_block(i, carry_):
             state_load(i).wait()
-            if i + 1 < steps_s:
+
+            @pl.when(i + 1 < steps_s)
+            def _():
                 state_load(i + 1).start()
-            C = slice(i * cb_s, (i + 1) * cb_s)
-            base = (i % 2) * cb_s
+
+            slot = lax.rem(i, 2)
+            C = at_cols(i, cb_s)
             rates2 = -jnp.exp(small[A_LOG : A_LOG + N, C]) * LOG2E
             rates_s[...] = rates2
             fin[...] = chain_states(
@@ -1275,10 +1330,7 @@
 
             def pair(p, carry):
                 lanes = [lanes_of(i, cb_s, p, tg_s, k) for k in range(tg_s)]
-                near = [lane_at(p, tg_s, k) for k in range(tg_s)]
-                held = [
-                    pl.ds(base + pl.multiple_of(p * tg_s * LANES, LANES) + k * LANES, LANES) for k in range(tg_s)
-                ]
+                near = [slice(k * LANES, (k + 1) * LANES) for k in range(tg_s)]
                 for g in range(0, N, ng_s):
                     rr = [
                         [
@@ -1302,7 +1354,7 @@
                         for n in range(0, ng_s, 2):
                             for k in range(tg_s):
                                 at = pl.multiple_of(j * N * SUB + (g + n) * SUB, 2 * SUB)
-                                two = big[pl.ds(at, 2 * SUB), held[k]].astype(F32)
+                                two = big[slot, pl.ds(at, 2 * SUB), near[k]].astype(F32)
                                 got[n][k] = two[0:SUB]
                                 got[n + 1][k] = two[SUB : 2 * SUB]
                         return [got[n][k] for n in range(ng_s) for k in range(tg_s)]
@@ -1355,11 +1407,10 @@
                             rt_s[g + n : g + n + 1, near[k]] = jnp.sum(rts[n * tg_s + k], axis=0, keepdims=True)
                 return carry
 
-            lax.fori_loop(0, cb_s // (tg_s * LANES), pair, 0)
+            pair(0, 0)
             dg = dg_s[...]
-            ssg[:, C] = dg * dt[:, C] + yg[:, C] * small[SKIP : SKIP + 1, C]
+            yg[:, C] = dg * dt[:, C] + yg[:, C] * small[SKIP : SKIP + 1, C]
             step_grad = rs_s[...] * LN2 + dg * sigf
-            low = mixed[:, 0 : z.R].astype(BF16)
             dtw = small[z.DT0 : z.DT0 + z.R, C].astype(BF16)
             pre = mm(low, dtw) + small[DT_B : DT_B + 1, C]
             dpg = step_grad * sigmoid(pre)
@@ -1369,12 +1420,23 @@
             gs_o[A_LOG : A_LOG + N, C] = rt_s[...] * (rates2 * LN2)
             gs_o[z.DT0 : z.DT0 + z.R, C] = mm_tn(low, dpl)
             low_s[...] += mm_nt(dpl, dtw)
-            if i + 2 <= E - 1:
-                chain_g.hop(i + 2)
-                chain_b.hop(i + 2)
-        for k in range(steps_s + 2, E):
-            chain_g.hop(k)
+            return carry_
+
+        third = steps_s // 3
+        lax.fori_loop(0, third, scan_block, 0)
+        chain_b.hop(1)
+        for c in gi_moves:
+            c.wait()
+        normed_load.wait()
+        place_in(p_g, flat(gi_all))
+        stage(sum_g.swap_start)
+        lax.fori_loop(third, 2 * third, scan_block, 0)
+        stage(sum_g.swap_finish)
+        chain_b.hop(2)
+        lax.fori_loop(2 * third, steps_s, scan_block, 0)
+        for k in range(3, E):
             chain_b.hop(k)
+        stage(sum_g.chips_finish)
 
         mxg[:, 0 : z.R] = low_s[...].astype(BF16)
         lane = lax.broadcasted_iota(jnp.int32, (SUB, LANES), 1)
@@ -1392,11 +1454,11 @@
         mxg[:, z.R : z.R + 2 * N] = cl[:, 0 : 2 * N].astype(BF16)
 
         def weight_load(i):
-            half = pl.ds((i % 2) * cb_s, cb_s)
             return [
                 pltpu.make_async_copy(
-                    w_in.at[:, h * DI + i * cb_s : h * DI + (i + 1) * cb_s], big.at[h * D : (h + 1) * D, half],
-                    ld.at[12 + 2 * (i % 2) + h],
+                    w_in.at[:, pl.ds(pl.multiple_of(h * DI + i * cb_s, LANES), cb_s)],
+                    big.at[lax.rem(i, 2), h * D : (h + 1) * D],
+                    ld.at[12 + 2 * lax.rem(i, 2) + h],
                 )
                 for h in range(2)
             ]
@@ -1410,7 +1472,7 @@
             sgv = sig[:, C]
             xw = small[z.X0 : z.X0 + z.XW, C].astype(BF16)
             gs_o[z.X0 : z.X0 + z.XW, C] = mm_tn(mgv, sgv)
-            sgrad = ssg[:, C] + mm(mgv, xw)
+            sgrad = yg[:, C] + mm(mgv, xw)
             xpad = padded_rows(conv_in[:, C], hconv[:, C], J, cb_m)
             valid = [jnp.broadcast_to(masks[:, o : o + 1], (T, cb_m)) for o in range(4)]
             out = jnp.broadcast_to(small[CONV_B : CONV_B + 1, C], (T, cb_m))
@@ -1439,7 +1501,7 @@
                     total = total + jnp.concatenate([c3[k:], wrap], axis=0)
                     for i2 in range(o, 3):
                         edges[i2] = edges[i2] + c3[i2 - o, 0:1, :]
-            cig[:, C] = total.reshape(T, cb_m)
+            yg[:, C] = total.reshape(T, cb_m)
             cg_edge[:, C] = jnp.concatenate(edges + [jnp.zeros((SUB - 3, cb_m), F32)], axis=0)
             return carry
 
@@ -1449,22 +1511,35 @@
         if plane:
             up2.wait()
             down2.wait()
-            uf[...] = adds(ua[yy], ub2[...])
+            ub2[...] = adds(ua[yy], ub2[...])
             half_u = uq // 2
             rows_u = lambda c: pl.ds(pl.multiple_of(c * half_u, 16), half_u)
-            up3 = remote(uf.at[rows_u(other)], up_o.at[core], a_s.at[5], a_r.at[5], sib)
+            up3 = remote(ub2.at[rows_u(other)], up_o.at[core], a_s.at[5], a_r.at[5], sib)
             up3.start()
-            up_own = pltpu.make_async_copy(uf.at[rows_u(core)], up_o.at[core], ld.at[16])
+            up_own = pltpu.make_async_copy(ub2.at[rows_u(core)], up_o.at[core], ld.at[16])
             up_own.start()
-            down_o[...] = da[pl.ds(pl.multiple_of(xx * dq, 16), dq), :].astype(F32) + db2[...].astype(F32)
-        else:
-            down_o[...] = jnp.zeros_like(down_o)
+            db2[...] = adds(da[pl.ds(pl.multiple_of(xx * dq, 16), dq), :], db2[...])
+            down_own = pltpu.make_async_copy(db2, down_o, ld.at[11])
+            down_own.start()
+        for c in gz_moves:
+            c.wait()
+        chain_b.local().wait()
+        groups_o = DZ // 16
+        bra = flat(br_all)
+        for i in range(2):
+            half_o = slice(i * (DZ // 2), (i + 1) * (DZ // 2))
+            val = mm_tn(flat(gz_all)[:, half_o], bra)
+            for g in range(DZ // 32):
+                chunk, off = group_place(groups_o, i * (DZ // 32) + g)
+                p_o[0, chunk // 2, chunk % 2, off : off + 16, :] = val[16 * g : 16 * g + 16].astype(BF16)
+        stage(sum_o.swap_start)
+        stage(sum_g.z_finish)
         back_edge.wait()
         live = jnp.where(s < S - 1, 1.0, 0.0)
 
         def fix_block(i, carry):
             C = at_cols(i, cb_m)
-            c3 = cig[:, C].reshape(J, SUB, cb_m)
+            c3 = yg[:, C].reshape(J, SUB, cb_m)
             final = lax.broadcasted_iota(jnp.int32, (SUB, cb_m), 0) == SUB - 1
             fixed = jnp.stack(
                 [
@@ -1477,32 +1552,75 @@
             return carry
 
         lax.fori_loop(0, DI // cb_m, fix_block, 0)
-        chain_p = Chain(E, pc, pc_o, p_s, p_r, ld.at[17])
-        chain_p.start()
-        acc[...] = jnp.zeros_like(acc)
-        for i in range(steps_s):
+        for e in range(E):
+            gi_b[e] = pc[:, e * DZ : (e + 1) * DZ]
+        pc_moves = trade(gi_b, pc_all, p_s, p_r)
+        for c in pc_moves:
+            c.start()
+        pc_all[me] = gi_b[me]
+        stage(sum_o.swap_finish)
+        tg_o[...] = jnp.zeros_like(tg_o)
+
+        def token_block(i, carry):
             for c in weight_load(i):
                 c.wait()
-            if i + 1 < steps_s:
+
+            @pl.when(i + 1 < steps_s)
+            def _():
                 for c in weight_load(i + 1):
                     c.start()
-            C = slice(i * cb_s, (i + 1) * cb_s)
-            half = slice((i % 2) * cb_s, (i % 2 + 1) * cb_s)
-            acc[...] += mm_nt(pc[:, C], big[0:D, half]) + mm_nt(gi[:, C], big[D : 2 * D, half])
-        d, gain_g = rms_back(tok[...].astype(F32), gp[0:1, :], acc[...])
+
+            slot = lax.rem(i, 2)
+            C = at_cols(i, cb_s)
+            tg_o[...] += mm_nt(pc[:, C], big[slot, 0:D, :]) + mm_nt(gi[:, C], big[slot, D : 2 * D, :])
+            return carry
+
+        lax.fori_loop(0, steps_s, token_block, 0)
+        d, gain_g = rms_back(tok[...].astype(F32), gp[0:1, :], tg_o[...])
         tg_o[...] = mg[...] + d
         gg_o[0:1, :] = gain_g
-        for k in range(1, E):
-            chain_p.hop(k)
-        for c in out_moves + gz_moves:
+        cr = p_m.shape[3]
+        for e in range(E):
+            side = jnp.concatenate([gg_o[:, e * NZ : (e + 1) * NZ], jnp.zeros((G, DZ - NZ), F32)], axis=1)
+            rows = [gs_o[:, e * DZ : (e + 1) * DZ], side, jnp.zeros((8 * cr - z.SMALL - G, DZ), F32)]
+            p_m[e] = jnp.concatenate(rows, axis=0).astype(BF16).reshape(4, 2, cr, DZ)
+        stage(sum_m.swap_start)
+        for c in pc_moves:
+            c.wait()
+        place_in(p_c, flat(pc_all))
+        stage(sum_c.swap_start)
+        stage(sum_m.swap_finish)
+        stage(sum_o.chips_finish)
+        stage(sum_c.swap_finish)
+        stage(sum_m.chips_finish)
+        stage(sum_g.forward)
+        stage(sum_c.chips_finish)
+        stage(sum_m.z_finish)
+        stage(sum_o.forward)
+        stage(sum_c.z_finish)
+        for c in out_moves:
             c.wait()
         back_own.wait()
-        gz_own.wait()
         if plane:
             up3.wait()
             up_own.wait()
-        for ch_ in (chain_g, chain_b, chain_p):
-            ch_.finish()
+            down_own.wait()
+            sum_m.forward()
+            sum_c.forward()
+            for sm_ in (sum_g, sum_o, sum_m, sum_c):
+                sm_.finish()
+        else:
+            copies = [
+                pltpu.make_async_copy(p, o, pown.at[a])
+                for a, (p, o) in enumerate(((p_g, pg_o), (p_c, pc_o), (p_m, pm_o), (p_o, po_o)))
+            ]
+            for c in copies:
+                c.start()
+            for c in copies:
+                c.wait()
+        for k in range(E - 1):
+            for d in (-k, k) if k else (0,):
+                chain_b.each(d, lambda c: c.wait_send())
 
     v = pltpu.VMEM
     sem = lambda *dims: pltpu.SemaphoreType.DMA(dims)
@@ -1512,44 +1630,56 @@
     u_shape = (2, uq, uc) if plane else (2, 16, LANES)
     d_shape = (2 * dq, dc) if plane else (32, LANES)
     ins = (dxp, outp, dwu, dwd, states, w_out, w_in, table, choose, chances, mid, moe, cot, gpack, router, gate, y,
-           sig, small, mixed, dt, masks, conv_in, hconv, s_all, tok)
+           sig, small, mixed, dt, masks, conv_in, hconv, s_all, tok, normed_all)
+    rg, ro, rm = chunk_rows(NZ), chunk_rows(DZ), 16 * -(-(z.SMALL + G) // 128)
+    p_shapes = [(E, 4, 2, rg, DZ), (E, 4, 2, rg, DZ), (E, 4, 2, rm, DZ), (1, 4, 2, ro, D)]
+    o_shapes = [(4, 2, E, rg, DZ)] * 2 + [(4, 2, rm, DZ), (4, 2, 1, ro, D)] if plane else p_shapes
     return pl.pallas_call(
         body,
         name="backward",
-        in_specs=[ANY] * 7 + [vm] * (len(ins) - 7),
-        out_specs=[vm] * 3 + [ANY] * 5 + [ANY, vm],
+        in_specs=[ANY] * 7 + [vm] * (len(ins) - 8) + [ANY],
+        out_specs=[vm] * 3 + [ANY] * 7,
         out_shape=[
             sds((T, D), F32),
             sds((z.SMALL, DI), F32),
             sds((G, D), F32),
             sds((M, D), BF16),
-            sds((E, T, DI), BF16),
-            sds((E, T, DI), BF16),
-            sds((E, T, D), BF16),
-            sds((E, T, DZ), BF16),
+        ]
+        + [sds(o, BF16) for o in o_shapes]
+        + [
             sds(up_shape, BF16),
-            sds(down_shape, F32),
+            sds(down_shape, BF16),
         ],
         scratch_shapes=[
-            v((rows_big, 2 * cb_s), BF16),
-            v((DI, D), BF16),
+            v((2, rows_big, cb_s), BF16),
+            v((2, cb_m, D), BF16), v((E * T, D), BF16),
             v((M, D + LANES), BF16), v((M, D + LANES), BF16), v((M, D), BF16), v((M, D), BF16),
             v((M, D + LANES), BF16),
-            v((T, DI), F32), v((T, DI), BF16), v((T, DI), BF16), v((E, T, DZ), BF16),
+            v((T, DI), F32), v((T, DI), BF16), v((E, T, DZ), BF16),
             v((T, D), BF16), v((T, D), F32),
             v((N, DI), BF16), v((S, N, DI), BF16), v(((N + 1) * SUB, DI), F32),
-            v((T, DI), F32), v((SUB, LANES), F32), v((T, DI), F32), v((SUB, DI), F32), v((SUB, DI), F32),
+            v((SUB, DI), F32), v((SUB, DI), F32),
             v((T, DI), BF16),
             v((J * N * SUB, LANES), F32), v((J * N * SUB, LANES), F32),
             v((J * N * SUB, LANES), F32), v((J * N * SUB, LANES), F32),
             v((T, LANES), F32), v((T, cb_s), F32), v((N, cb_s), F32), v((N, cb_s), F32),
             v((T, cb_s), F32), v((T, cb_s), F32), v((N, cb_s), F32), v((T, z.R), F32), v((T, z.XW), BF16),
-            v((T, D), F32), v((N, DI), F32),
-            v(u_shape, BF16), v(u_shape, BF16), v(u_shape[1:], BF16), v(u_shape[1:], BF16),
+            v((N, DI), F32),
+            v(u_shape, BF16), v(u_shape, BF16), v(u_shape[1:], BF16),
             v(d_shape, BF16), v(d_shape, BF16), v((d_shape[0] // 2, d_shape[1]), BF16),
+            v((E, T, DZ), BF16), v((E, T, DZ), BF16), v((E, T, D), BF16), v((E, T, DZ), BF16),
+            v((E, T, DZ), BF16),
+        ]
+        + [v(p, BF16) for p in p_shapes]
+        + [v((p[0], 4) + p[3:], BF16) for p in p_shapes]
+        + [v((3, p[0]) + p[3:], BF16) for p in p_shapes]
+        + [v((E,) + p[3:], BF16) for p in p_shapes[:3]]
+        + [
+            sem(4), sem(4), sem(4, 3), sem(4, 3), sem(4, E - 1), sem(4, E - 1), sem(4, 3), sem(4, 3), sem(4, 4),
+            sem(4, 4), sem(4),
             sem(18), sem(2), sem(2), sem(E - 1), sem(E - 1), sem(E - 1), sem(E - 1), sem(S - 1), sem(S - 1),
             pltpu.SemaphoreType.DMA, pltpu.SemaphoreType.DMA,
-            sem(chain_slots), sem(chain_slots), sem(chain_slots), sem(chain_slots), sem(chain_slots), sem(chain_slots),
+            sem(E - 1), sem(E - 1), sem(E - 1), sem(E - 1), sem(chain_slots), sem(chain_slots),
             sem(6), sem(6), sem(E - 1), sem(E - 1),
         ],
         compiler_params=pltpu.CompilerParams(
@@ -1558,12 +1688,68 @@
     )(*ins)
 
 
-def to_chunks(a, J):
-    return a.reshape((SUB, J) + a.shape[1:]).swapaxes(0, 1).reshape(a.shape)
-
-
-def from_chunks(a, J):
-    return a.reshape((J, SUB) + a.shape[1:]).swapaxes(0, 1).reshape(a.shape)
+def finish(z, gr, plane, pg, pc, pm, po, tg, mid, chances, choose, table, back, up, down):
+    T, D, DI, N, J, E = z.T, z.D, z.DI, z.N, z.J, z.E
+    DZ, NZ, FB = DI // E, D // E, z.FF // 8
+    U = up.shape[1]
+
+    def body(pg, pc, pm, po, tg, mid, ch, cho, tb, bk, up, dn, *outs):
+        dwi, dwo, out, tgo, cw, cb, xw, dw, db, al, sk, na, nb, ro = outs[:14]
+        for g in range(NZ // 16):
+            chunk, off = group_place(NZ // 16, g)
+            for h, src in enumerate((pc, pg)):
+                for e in range(E):
+                    dwi[16 * g : 16 * g + 16, h * DI + e * DZ : h * DI + (e + 1) * DZ] = src[
+                        chunk, e, off : off + 16, :
+                    ].astype(F32)
+        for g in range(DZ // 16):
+            chunk, off = group_place(DZ // 16, g)
+            dwo[16 * g : 16 * g + 16, :] = po[chunk, off : off + 16, :].astype(F32)
+        sm = pm[...].astype(F32)
+        cw[...] = sm[CONV_W : CONV_W + 4]
+        cb[...] = sm[CONV_B : CONV_B + 1]
+        db[...] = sm[DT_B : DT_B + 1]
+        sk[...] = sm[SKIP : SKIP + 1]
+        al[...] = sm[A_LOG : A_LOG + N]
+        dw[...] = sm[z.DT0 : z.X0]
+        xw[...] = sm[z.X0 : z.SMALL]
+        na[...] = sm[z.SMALL : z.SMALL + 1, 0:NZ]
+        nb[...] = sm[z.SMALL + 1 : z.SMALL + 2, 0:NZ]
+        ro[...] = sm[z.SMALL + 2 : z.SMALL + 2 + E, 0:NZ]
+        lane = lax.broadcasted_iota(jnp.int32, (T, T), 1)
+        prow = lax.broadcasted_iota(jnp.int32, (T, T), 0)
+        order = (lane == (prow % SUB) * J + prow // SUB).astype(F32).astype(BF16)
+        gating = jnp.sum(ch[...] * cho[...], axis=-1, keepdims=True)
+        low = (mid[...] + gating * mm(tb[...], bk[...])).astype(BF16)
+        out[...] = mm_tn(order, low).astype(BF16)
+        v = tg[...]
+        hi, rest = v.astype(BF16), v - v.astype(BF16).astype(F32)
+        lo, end = split_hi_lo(rest)
+        tgo[...] = mm_tn(order, hi) + (mm_tn(order, lo) + mm_tn(order, end))
+        if plane:
+            upo, dno = outs[14:]
+            for c in range(2):
+                for i in range(4):
+                    at = (2 * i + c) * FB
+                    upo[:, at : at + FB] = up[c, :, i * FB : (i + 1) * FB].astype(F32)
+            dno[...] = dn[...].astype(F32)
+
+    vm = pl.BlockSpec(memory_space=pltpu.VMEM)
+    shapes = [
+        sds((NZ, 2 * DI), F32), sds((DZ, D), F32), sds((T, D), BF16), sds((T, D), F32), sds((4, DZ), F32),
+        sds((1, DZ), F32), sds((z.XW, DZ), F32), sds((z.R, DZ), F32), sds((1, DZ), F32), sds((N, DZ), F32),
+        sds((1, DZ), F32), sds((1, NZ), F32), sds((1, NZ), F32), sds((E, NZ), F32),
+    ]
+    if plane:
+        shapes += [sds((U, z.FF), F32), sds(down.shape, F32)]
+    return pl.pallas_call(
+        body,
+        name="finish",
+        in_specs=[vm] * 12,
+        out_specs=[vm] * len(shapes),
+        out_shape=shapes,
+        compiler_params=pltpu.CompilerParams(vmem_limit_bytes=VMEM_LIMIT),
+    )(pg, pc, pm, po, tg, mid, chances, choose, table, back, up, down)
 
 
 def on_device(
@@ -1577,49 +1763,56 @@
     me_s, me_e = lax.axis_index("seq"), lax.axis_index("exp")
     core = lax.rem(me_s, 2)
     where = jnp.stack([me_s, me_e, core]).astype(jnp.int32)
-    seg = segment_ids[0]
-    wide_rows = lambda v: jnp.pad(
-        jnp.broadcast_to(v.astype(F32)[:, None], (3, LANES)), ((0, SUB - 3), (0, 0))
-    )
     cw = dt_proj.shape[1]
     dw = norm_gain.shape[0]
     plane = S == 8 and dw % 32 == 0
-    small_own = jnp.concatenate(
-        [conv_weight, conv_bias[None], dt_bias[None], d_skip[None], jnp.zeros((1, cw), BF16), a_log, dt_proj,
-         x_proj.T, jnp.zeros((-z.SMALL % 32, cw), BF16)], axis=0
-    )
-    g_own = jnp.concatenate(
-        [norm_gain[None], moe_gain[None], router.T, jnp.zeros((32 - 2 - E, dw), BF16)], axis=0
-    )
-    owned = [in_proj, out_proj, small_own, g_own]
-    if not plane:
-        owned = [lax.all_gather(a, "exp", tiled=True) for a in owned]
+    line = lambda v: v.reshape(1, -1)
+    if plane:
+        params = [conv_weight, line(conv_bias), line(dt_bias), line(d_skip), a_log, dt_proj, x_proj,
+                  line(norm_gain), line(moe_gain), router]
+        w_in, w_out = in_proj, out_proj
+    else:
+        small_own = jnp.concatenate(
+            [conv_weight, line(conv_bias), line(dt_bias), line(d_skip), jnp.zeros((1, cw), BF16), a_log, dt_proj,
+             x_proj.T, jnp.zeros((-z.SMALL % 32, cw), BF16)], axis=0
+        )
+        g_own = jnp.concatenate(
+            [line(norm_gain), line(moe_gain), router.T, jnp.zeros((32 - 2 - E, dw), BF16)], axis=0
+        )
+        gathered = [lax.all_gather(a, "exp", tiled=True) for a in (in_proj, out_proj, small_own, g_own)]
+        w_in, w_out, params = gathered[0], gathered[1], gathered[2:]
     gr = 8 * -(-(2 + E) // 8)
-    padded_seg = jnp.concatenate([jnp.zeros((3,), seg.dtype), seg])
-    masks = jnp.stack([(padded_seg[o : o + T] == seg).astype(F32) for o in range(4)] + [seg * 0.0] * 4, axis=1)
-    tok = to_chunks(tokens[0], J)
-    cot = to_chunks(cotangent[0], J)
-    route = to_chunks(routes[0], J)
     (
         small, gpack, router_t, table, choose_wide, masks, conv_in, hconv, gate, sig, mixed, dt, y, mid, moe, chances,
-        s_all, states, w_in, w_out, arrived, cot_pair, normed_z,
+        s_all, tok, cot, states, w_in, w_out, arrived, cot_pair, normed_all,
     ) = forward(
-        z, S, plane, tok, tokens[0, T - J :], wide_rows(seg[T - 3 :]), wide_rows(seg[:3]), cot, route,
-        to_chunks(masks, J), *owned, gr, 1
+        z, S, plane, tokens[0], cotangent[0], segment_ids, routes.reshape(1, T), params, w_in, w_out, gr, 1
     )
-    normed_z = normed_z.reshape(E * T, -1)
     outp, dxp, dwu, dwd = expert(
         z, where, arrived.reshape(2 * E * CAP, D), cot_pair.reshape(2 * E * CAP, D), router_t, up_proj[0], down_proj[0]
     )
-    token_grad, gsmall, ggrad, back_out, gate_all, conv_all, branch_all, gated_z, up_sum, down_part = backward(
+    token_grad, _, _, back_out, pg, pc, pm, po, up_sum, down_sum = backward(
         z, S, plane, dxp.reshape(2, E * CAP, -1), outp.reshape(2, E * CAP, D), dwu, dwd, states, w_out, w_in, table,
         choose_wide, chances, mid, moe, cot, gpack, router_t, gate, y, sig, small, mixed, dt, masks, conv_in, hconv,
-        s_all, tok, 4
+        s_all, tok, normed_all.reshape(E * T, D), 4
     )
-    fb = z.FF // 8
+    if not plane:
+        pg, pc, pm, po = [lax.psum(a, "seq") for a in (pg, pc, pm, po)]
+        pg, pc = [
+            lax.all_to_all(a, "exp", split_axis=0, concat_axis=0, tiled=True).transpose(1, 2, 0, 3, 4)
+            for a in (pg, pc)
+        ]
+        pm = lax.psum_scatter(pm, "exp", scatter_dimension=0, tiled=True)[0]
+        po = po[0]
+    eight = lambda a: a.reshape((8,) + a.shape[2:])
+    dw_in, dw_out, output, token_grad, g_cw, g_cb, g_xw, g_dw, g_db, g_al, g_sk, g_na, g_nb, g_ro, *rest = finish(
+        z, gr, plane, eight(pg), eight(pc), pm.reshape(-1, pm.shape[-1]), po.reshape(8, -1, D), token_grad, mid,
+        chances, choose_wide, table, back_out, up_sum, down_sum
+    )
     if plane:
-        up_part = up_sum.reshape(2, D // 8, 4, fb).transpose(1, 2, 0, 3).reshape(D // 8, z.FF).astype(F32)
+        up_part, down_part = rest
     else:
+        fb = z.FF // 8
         up_full = jnp.zeros((D, 4, 2, fb), BF16)
         up_full = lax.dynamic_update_slice_in_dim(up_full, dwu.reshape(D, 4, 1, fb), core, axis=2)
         down_full = jnp.zeros((4, 2, fb, D), BF16)
@@ -1628,52 +1821,10 @@
             lax.psum_scatter(v, "seq", scatter_dimension=0, tiled=True).astype(F32)
             for v in (up_full.reshape(D, z.FF), down_full.reshape(z.FF, D))
         ]
-    out_rows = contract(gated_z.reshape(E * T, -1), branch_all.reshape(E * T, D)).astype(BF16)
-    gate_cols = contract(normed_z, gate_all.reshape(E * T, DI)).astype(BF16)
-    conv_cols = contract(normed_z, conv_all.reshape(E * T, DI)).astype(BF16)
-    gating = jnp.sum(chances * choose_wide, axis=-1, keepdims=True)
-    output = (mid + gating * jnp.dot(table, back_out, preferred_element_type=F32)).astype(BF16)
-
-    blocks = lambda a: a.reshape(a.shape[0], E, -1).swapaxes(0, 1)
-    gpart = jnp.pad(blocks(ggrad), ((0, 0), (0, 0), (0, cw - dw)))
-    rows = z.SMALL + gr
-    pad = -rows % 128
-    smalls = jnp.concatenate(
-        [blocks(gsmall), gpart, jnp.zeros((E, pad, cw), F32)], axis=1
-    ).astype(BF16)
-    cols = jnp.concatenate([conv_cols, gate_cols], axis=1)
-    if plane:
-        each = cw // 8
-        each_pad = 16 * -(-each // 16)
-        padded = jnp.pad(out_rows.reshape(8, each, D), ((0, 0), (0, each_pad - each), (0, 0)))
-        dw_in, dw_out, gsum = reduce_plane(E, cols, padded, smalls, 7)
-        dw_out = dw_out[:, :each].reshape(cw, D)
-    else:
-        dw_in, dw_out = lax.psum(cols, "seq"), lax.psum(out_rows, "seq")
-        gsum = lax.psum_scatter(lax.psum(smalls, "seq"), "exp", scatter_dimension=0, tiled=True)[0]
-    gsum = gsum.astype(F32)
     return (
-        from_chunks(output, J)[None],
-        from_chunks(token_grad, J)[None],
-        gsum[z.SMALL, :dw],
-        dw_in.astype(F32),
-        gsum[CONV_W : CONV_W + 4],
-        gsum[CONV_B],
-        gsum[z.X0 : z.SMALL].T,
-        gsum[z.DT0 : z.X0],
-        gsum[DT_B],
-        gsum[A_LOG : A_LOG + N],
-        gsum[SKIP],
-        dw_out.astype(F32),
-        gsum[z.SMALL + 1, :dw],
-        gsum[z.SMALL + 2 : z.SMALL + 2 + E, :dw].T,
-        up_part[None],
-        down_part[None],
+        output[None], token_grad[None], g_na[0], dw_in, g_cw, g_cb[0], g_xw.T, g_dw, g_db[0], g_al, g_sk[0], dw_out,
+        g_nb[0], g_ro.T, up_part[None], down_part[None],
     )
-
-
-def contract(a, b):
-    return lax.dot_general(a, b, (((0,), (0,)), ((), ())), preferred_element_type=F32)
 
 
 def solution(mesh):

time: 434 us -> 338 us (0.78)
  Pallas kernels: 374 us -> 316 us
  local copies, waits for them, and re-layouts: 33.6 us -> 9.4 us
  other arithmetic: 17.9 us -> 6.97 us
    pallas_call x2, Pallas kernels: 189 us -> 133 us  [the longest x1 124 us: forward(): pl.pallas_call(body, name='forward', in_specs=[vm] * 4 + [vm if plane els...]
    convert_element_type x4 -> x0, other arithmetic: 7.54 us -> none  [the longest x1 4.88 us: on_device(): dw_in.astype(F32)]
    concatenate x3 -> x0, local copies, waits for them, and re-layouts: 6.5 us -> none  [the longest x1 6.35 us: on_device(): jnp.concatenate([conv_weight, conv_bias[None], dt_bias[None], d_skip[None...]
    pallas_call x0 -> x5, other arithmetic: none -> 6.38 us  [finish(): pl.pallas_call(body, name='finish', in_specs=[vm] * 12, out_specs=[vm] *...]
    convert_element_type x3 -> x0, local copies, waits for them, and re-layouts: 4.54 us -> none  [on_device(): up_sum.reshape(2, D // 8, 4, fb).transpose(1, 2, 0, 3).reshape(D // 8, z.FF)]
    concatenate x3 -> x0, other arithmetic: 4.37 us -> none  [the longest x1 1.69 us: on_device(): cols = jnp.concatenate([conv_cols, gate_cols], axis=1)]
where the time goes in v5:
time: 338 us; the launch traced here: 333 us
  Pallas kernels  316 us (93%)
  local copies, waits for them, and re-layouts  9.4 us (3%)
  other arithmetic  6.97 us (2%)
    pallas_call x1, Pallas kernels, backward(): pl.pallas_call(body, name='backward', in_specs=[ANY] * 7 + [vm] * (len(in...  160 us
    pallas_call x1, Pallas kernels, forward(): pl.pallas_call(body, name='forward', in_specs=[vm] * 4 + [vm if plane els...  124 us
    pallas_call x1, Pallas kernels, expert(): pl.pallas_call(body, name='expert', grid_spec=pltpu.PrefetchScalarGridSpe...  22.7 us
    pallas_call x1, Pallas kernels, finish(): pl.pallas_call(body, name='finish', in_specs=[vm] * 12, out_specs=[vm] *...  9.37 us

profile of v5, /device:TPU:23, one launch (start us, length us, event | category | flops | bytes accessed | tf_op | source)
XLA Modules:
  0.0 333.3 jit_solution(7188510403401526091)
XLA Ops:
  0.7 0.6 pad_add_fusion.wh
  1.2 1.2 reshape.81.refs_11_
  2.5 1.2 reshape.82.refs_12_
  3.7 1.3 reshape.78.refs_5_
  5.0 1.3 reshape.79.refs_6_
  6.2 1.3 reshape.80.refs_7_
  7.5 1.4 copy.35.refs_13_
  9.0 1.7 copy.34.refs_10_
  10.6 123.9 %forward.1 = (f32[200,2304]{1,0:T(8,128)}, f32[8,1152]{1,0:T(8,128)}, bf16[128,1152]{1,0:T(8,128)(2,1)}, bf16[128,256]{1,0:T(8,128)(2,1)}, f32[128,128]{1,0:T(8,...) custom-call(bf16[128,1152]{1,0:T(8,128)(2,1)} %bitcast.34, ...), custom_call_target="tpu_custom_call" | custom-call | tf_op jit(solution)/shard_map/forward/pallas_call | solution.py:1009
  134.5 22.7 %expert.1 = (bf16[512,1152]{1,0:T(8,128)(2,1)}, bf16[512,1280]{1,0:T(8,128)(2,1)}, bf16[1152,1536]{1,0:T(8,128)(2,1)}, bf16[1536,1152]{1,0:T(8,128)(2,1)}) custom-call(s32[3]{0:T(128)} %pad_add_fusion.wh, bf16[512,1152]{1,0:T(8,128)(2,1)} %bitcast.30, bf16[512,1152]{1,0:T(8,128)(2,1)} %bitcast.31, bf16[128,1152]{1,0:T(8,128)(2,1)} %get-tuple-element.71.rt.router, ...), custom_call_target="tpu_custom_call" | custom-call | tf_op jit(solution)/shard_map/expert/pallas_call | solution.py:322
  157.3 160.2 %backward.1 = (f32[128,1152]{1,0:T(8,128)}, f32[200,2304]{1,0:T(8,128)}, f32[8,1152]{1,0:T(8,128)}, bf16[256,1152]{1,0:T(8,128)(2,1)}, bf16[4,2,4,48,576]{4,3,2,...) custom-call(bf16[2,256,1280]{2,1,0:T(8,128)(2,1)} %bitcast.28, ...), custom_call_target="tpu_custom_call" | custom-call | tf_op jit(solution)/shard_map/backward/pallas_call | solution.py:1637
  317.5 9.4 %finish.1 = (f32[288,4608]{1,0:T(8,128)}, f32[576,1152]{1,0:T(8,128)}, bf16[128,1152]{1,0:T(8,128)(2,1)}, f32[128,1152]{1,0:T(8,128)}, f32[4,576]{1,0:T(4,128)},...) custom-call(bf16[8,4,48,576]{3,2,1,0:T(8,128)(2,1)} %bitcast.25, ...), custom_call_target="tpu_custom_call" | custom-call | tf_op jit(solution)/shard_map/finish/pallas_call | solution.py:1745
  326.9 1.3 reduce
  328.2 1.3 reduce.4
  329.4 1.3 reduce.1
  330.7 1.3 reduce.2
  332.0 1.3 reduce.3

commit v6 on v5

--- a/solution.py
+++ b/solution.py
@@ -135,8 +135,10 @@
 
 
 class PlaneSum:
-    def __init__(self, E, p, b, t, zb, out, add, sems):
+    def __init__(self, E, p, b, t, zb, out, add, base, full, sems):
         self.E, self.p, self.b, self.t, self.zb, self.out, self.add = E, p, b, t, zb, out, add
+        self.rows, self.full = p.shape[3], full
+        self.base = base if full < 4 else self.rows
         self.cs, self.cr, self.qs, self.qr, self.zs, self.zr, self.gs, self.gr, self.fs, self.fr, self.own = sems
         s, self.me = lax.axis_index("seq"), lax.axis_index("exp")
         self.chip, self.core = s // 2, lax.rem(s, 2)
@@ -145,45 +147,81 @@
         self.far = [{"seq": q * 2 + self.core} for q in self.chips]
         self.zz = [lax.rem(self.me + k, E) for k in range(1, E)]
 
-    def remote(self, src, dst, send, recv, to):
-        return pltpu.make_async_remote_copy(src, dst, send, recv, device_id=to, device_id_type=MESH)
+    def pair(self, src, dst, send, recv, to):
+        cut = lambda ref, a, n: ref.at[(slice(None),) * (len(ref.shape) - 2) + (pl.ds(a, n),)]
+        make = lambda a, n, i: pltpu.make_async_remote_copy(
+            cut(src, a, n), cut(dst, a, n), send.at[i], recv.at[i], device_id=to, device_id_type=MESH
+        )
+        if self.base == self.rows:
+            return [make(0, self.rows, 0)]
+        return [make(0, self.base, 0), make(self.base, self.rows - self.base, 1)]
+
+    def run(self, copies, chip, act):
+        act(copies[0])
+        if len(copies) > 1:
+            @pl.when(chip < self.full)
+            def _():
+                act(copies[1])
 
     def swap_start(self):
-        self.swap = self.remote(self.p.at[:, :, 1 - self.core], self.b, self.cs, self.cr, self.sib)
-        self.swap.start()
+        self.swap = self.pair(self.p.at[:, :, 1 - self.core], self.b, self.cs, self.cr, self.sib)
+        if len(self.swap) > 1:
+            src, dst = self.p.at[:, 0 : self.full, 1 - self.core], self.b.at[:, 0 : self.full]
+            self.swap[1] = self.pair(src, dst, self.cs, self.cr, self.sib)[1]
+        for c in self.swap:
+            c.start()
 
     def swap_finish(self):
-        self.swap.wait()
+        for c in self.swap:
+            c.wait()
+        B = self.base
         for l in range(self.p.shape[0]):
-            self.p[l, :, self.core] = (self.p[l, :, self.core].astype(F32) + self.b[l].astype(F32)).astype(BF16)
+            self.p[l, :, self.core, 0:B] = (
+                self.p[l, :, self.core, 0:B].astype(F32) + self.b[l, :, 0:B].astype(F32)
+            ).astype(BF16)
+            if B < self.rows:
+                F = self.full
+                self.p[l, 0:F, self.core, B:] = (
+                    self.p[l, 0:F, self.core, B:].astype(F32) + self.b[l, 0:F, B:].astype(F32)
+                ).astype(BF16)
         self.crossing = [
-            self.remote(self.p.at[:, self.chips[k], self.core], self.t.at[k], self.qs.at[k], self.qr.at[k], self.far[k])
+            self.pair(self.p.at[:, self.chips[k], self.core], self.t.at[k], self.qs.at[k], self.qr.at[k], self.far[k])
             for k in range(3)
         ]
-        for c in self.crossing:
-            c.start()
+        for k in range(3):
+            self.run(self.crossing[k], self.chips[k], lambda c: c.start())
 
     def chips_finish(self):
-        for c in self.crossing:
-            c.wait()
-        for l in range(self.p.shape[0]):
-            v = self.p[l, self.chip, self.core].astype(F32)
-            for k in range(3):
-                v = v + self.t[k, l].astype(F32)
-            self.p[l, self.chip, self.core] = v.astype(BF16)
+        for k in range(3):
+            self.run(self.crossing[k], self.chips[k], lambda c: c.wait_send())
+            self.run(self.crossing[k], self.chip, lambda c: c.wait_recv())
+
+        def total(rows):
+            for l in range(self.p.shape[0]):
+                v = self.p[l, self.chip, self.core, rows].astype(F32)
+                for k in range(3):
+                    v = v + self.t[k, l, rows].astype(F32)
+                self.p[l, self.chip, self.core, rows] = v.astype(BF16)
+
+        total(slice(0, self.base))
+        if self.base < self.rows:
+            @pl.when(self.chip < self.full)
+            def _():
+                total(slice(self.base, self.rows))
+
         if self.zb is None:
             self.spread(self.p.at[:, self.chip, self.core])
             return
         self.along = [
-            self.remote(self.p.at[d, self.chip, self.core], self.zb.at[self.me], self.zs.at[k], self.zr.at[k], {"exp": d})
+            self.pair(self.p.at[d, self.chip, self.core], self.zb.at[self.me], self.zs.at[k], self.zr.at[k], {"exp": d})
             for k, d in enumerate(self.zz)
         ]
         for c in self.along:
-            c.start()
+            self.run(c, self.chip, lambda c: c.start())
 
     def z_finish(self):
         for c in self.along:
-            c.wait()
+            self.run(c, self.chip, lambda c: c.wait())
         v = self.p[self.me, self.chip, self.core]
         if self.add:
             v = v.astype(F32)
@@ -197,28 +235,32 @@
 
     def spread(self, ref):
         dst = self.out.at[self.chip, self.core]
-        self.sends = [self.remote(ref, dst, self.gs.at[k], self.gr.at[k], self.far[k]) for k in range(3)]
-        self.sends.append(self.remote(ref, dst, self.fs.at[3], self.fr.at[3], self.sib))
+        self.sends = [self.pair(ref, dst, self.gs.at[k], self.gr.at[k], self.far[k]) for k in range(3)]
+        self.sends.append(self.pair(ref, dst, self.fs.at[3], self.fr.at[3], self.sib))
         for c in self.sends:
-            c.start()
+            self.run(c, self.chip, lambda c: c.start())
         self.local = pltpu.make_async_copy(ref, dst, self.own)
         self.local.start()
 
     def forward(self):
+        self.passed = []
         for k in range(3):
             ref = self.out.at[self.chips[k], self.core]
-            self.remote(ref, ref, self.gs.at[k], self.gr.at[k], self.far[k]).wait_recv()
-            c = self.remote(ref, ref, self.fs.at[k], self.fr.at[k], self.sib)
-            c.start()
-            self.sends.append(c)
+            self.run(self.pair(ref, ref, self.gs.at[k], self.gr.at[k], self.far[k]), self.chips[k], lambda c: c.wait_recv())
+            c = self.pair(ref, ref, self.fs.at[k], self.fr.at[k], self.sib)
+            self.run(c, self.chips[k], lambda c: c.start())
+            self.passed.append(c)
 
     def finish(self):
         for c in self.sends:
-            c.wait_send()
+            self.run(c, self.chip, lambda c: c.wait_send())
+        for k in range(3):
+            self.run(self.passed[k], self.chips[k], lambda c: c.wait_send())
         self.local.wait()
         for k in range(4):
-            ref = self.out.at[self.chips[k] if k < 3 else self.chip, 1 - self.core]
-            self.remote(ref, ref, self.fs.at[k], self.fr.at[k], self.sib).wait_recv()
+            q = self.chips[k] if k < 3 else self.chip
+            ref = self.out.at[q, 1 - self.core]
+            self.run(self.pair(ref, ref, self.fs.at[k], self.fr.at[k], self.sib), q, lambda c: c.wait_recv())
 
 
 def expand_columns(z, src, col0, dst):
@@ -277,77 +319,137 @@
     return e / jnp.sum(e, axis=-1, keepdims=True)
 
 
-def expert(z, where, x, cot, router, up, down):
-    D, FF, E = z.D, z.FF, z.E
-    M = x.shape[0]
+def expert(z, x, cot, router, normed, up, down, cid):
+    T, D, FF, E = z.T, z.D, z.FF, z.E
+    M = x.shape[0] // 2
+    CAP = z.CAP
     fb = FF // 8
-    steps = 4
-
-    def body(wh, x_r, c_r, rt, up_r, dn_r, ret_o, rdx_o, dwu_o, dwd_o, g_s, out_s, dx_s):
-        i = pl.program_id(0)
-
-        @pl.when(i == 0)
-        def _():
-            ch = router_softmax(mm_nt(x_r[...], rt[...]), E)
-            lane = lax.broadcasted_iota(jnp.int32, ch.shape, 1)
-            gating = jnp.sum(jnp.where(lane == wh[1], ch, 0.0), axis=-1, keepdims=True)
-            g_s[...] = (gating * c_r[...].astype(F32)).astype(BF16)
-            out_s[...] = jnp.zeros_like(out_s)
-            dx_s[...] = jnp.zeros_like(dx_s)
-
-        xv, gv = x_r[...], g_s[...]
-        upv, dnv = up_r[...], dn_r[...]
-        pre = mm(xv, upv)
-        cdf = 0.5 * (1.0 + lax.erf(pre * (2.0 ** -0.5)))
-        hidden = (pre * cdf).astype(BF16)
-        slope = cdf + pre * jnp.exp(-0.5 * pre * pre) * (1.0 / math.sqrt(2.0 * math.pi))
-        out_s[...] += mm(hidden, dnv)
-        pg = (mm_nt(gv, dnv) * slope).astype(BF16)
-        dx_s[...] += mm_nt(pg, upv)
-        dwd_o[...] = mm_tn(hidden, gv).astype(BF16)
-        dwu_o[...] = mm_tn(xv, pg).astype(BF16)
-
-        @pl.when(i == steps - 1)
-        def _():
-            out = out_s[...]
-            ret_o[...] = out.astype(BF16)
-            rdx_o[:, 0:D] = dx_s[...].astype(BF16)
-            gg = jnp.sum(out * c_r[...].astype(F32), axis=-1, keepdims=True)
-            hi, lo = split_hi_lo(gg)
-            lane = lax.broadcasted_iota(jnp.int32, (M, LANES), 1)
-            both = jnp.where(lane == 0, hi.astype(F32), jnp.where(lane == 1, lo.astype(F32), 0.0))
-            rdx_o[:, D : D + LANES] = both.astype(BF16)
-
-    whole_ = lambda shape: pl.BlockSpec(shape, lambda i, w: (0,) * len(shape))
+    wb = 2 * fb
+
+    def body(
+        x_r, c_r, rt, nrm, up_r, dn_r, dxz, back_o, dwu_o, dwd_o, nz_o,
+        up_v, dn_v, hid, pg_s, g_s, out_s, dx_s, dxb, outb, dx_r, out_r, dwu_v, dwd_v,
+        ld, c_s, c_q, sw_s, sw_r, dz_s, dz_r,
+    ):
+        s, me = lax.axis_index("seq"), lax.axis_index("exp")
+        core = lax.rem(s, 2)
+        other = 1 - core
+        sib = {"seq": s + 1 - 2 * core}
+        zs = [lax.rem(me + k, E) for k in range(1, E)]
+        loads = []
+        for i in range(4):
+            at = pl.multiple_of((2 * i + core) * fb, LANES)
+            t, off = i // 2, i % 2 * fb
+            loads.append(
+                [
+                    pltpu.make_async_copy(up_r.at[:, pl.ds(at, fb)], up_v.at[t, :, off : off + fb], ld.at[i]),
+                    pltpu.make_async_copy(dn_r.at[pl.ds(at, fb)], dn_v.at[t, off : off + fb], ld.at[4 + i]),
+                ]
+            )
+        for pair in loads:
+            for c in pair:
+                c.start()
+        greet([sib] + [{"exp": p} for p in zs])
+
+        def remote(src, dst, send, recv, to):
+            return pltpu.make_async_remote_copy(src, dst, send, recv, device_id=to, device_id_type=MESH)
+
+        chain = Chain(E, nrm, nz_o, c_s, c_q, ld.at[8])
+        chain.start()
+        ch = router_softmax(mm_nt(x_r[...], rt[...]), E)
+        lane = lax.broadcasted_iota(jnp.int32, ch.shape, 1)
+        gating = jnp.sum(jnp.where(lane == me, ch, 0.0), axis=-1, keepdims=True)
+        g_s[...] = (gating * c_r[...].astype(F32)).astype(BF16)
+        for t in range(2):
+            W = slice(t * wb, (t + 1) * wb)
+            for pair in loads[2 * t : 2 * t + 2]:
+                for c in pair:
+                    c.wait()
+            pre = mm(x_r[...], up_v[t])
+            cdf = 0.5 * (1.0 + lax.erf(pre * (2.0 ** -0.5)))
+            hid[:, W] = (pre * cdf).astype(BF16)
+            slope = cdf + pre * jnp.exp(-0.5 * pre * pre) * (1.0 / math.sqrt(2.0 * math.pi))
+            pg_s[:, W] = (mm_nt(g_s[...], dn_v[t]) * slope).astype(BF16)
+            if t == 0:
+                dx_s[...] = mm_nt(pg_s[:, W], up_v[t])
+                out_s[...] = mm(hid[:, W], dn_v[t])
+                chain.hop(1)
+            else:
+                dxb[:, 0:D] = (dx_s[...] + mm_nt(pg_s[:, W], up_v[t])).astype(BF16)
+                out = out_s[...] + mm(hid[:, W], dn_v[t])
+                outb[...] = out.astype(BF16)
+                gg = jnp.sum(out * c_r[...].astype(F32), axis=-1, keepdims=True)
+                hi, lo = split_hi_lo(gg)
+                lane = lax.broadcasted_iota(jnp.int32, (2 * M, LANES), 1)
+                both = jnp.where(lane == 0, hi.astype(F32), jnp.where(lane == 1, lo.astype(F32), 0.0))
+                dxb[:, D : D + LANES] = both.astype(BF16)
+        half = lambda c: pl.ds(pl.multiple_of(c * M, 16), M)
+        swaps = [
+            remote(dxb.at[half(other)], dx_r, sw_s.at[0], sw_r.at[0], sib),
+            remote(outb.at[half(other)], out_r, sw_s.at[1], sw_r.at[1], sib),
+        ]
+        for c in swaps:
+            c.start()
+        if E > 2:
+            chain.hop(2)
+
+        def grads(t):
+            W = slice(t * wb, (t + 1) * wb)
+            dwd_v[W, :] = mm_tn(hid[:, W], g_s[...]).astype(BF16)
+            dwu_v[:, W] = mm_tn(x_r[...], pg_s[:, W]).astype(BF16)
+            moves = [
+                pltpu.make_async_copy(dwd_v.at[W], dwd_o.at[W], ld.at[9 + t]),
+                pltpu.make_async_copy(dwu_v.at[:, W], dwu_o.at[:, W], ld.at[11 + t]),
+            ]
+            for c in moves:
+                c.start()
+            return moves
+
+        block_of = lambda ref, p: ref.at[pl.ds(pl.multiple_of(p * CAP, 16), CAP)]
+        here = pl.ds(pl.multiple_of(me * CAP, 16), CAP)
+        swaps[0].wait()
+        dx_r[...] = (dxb[half(core), :].astype(F32) + dx_r[...].astype(F32)).astype(BF16)
+        moves = [
+            remote(block_of(dx_r, p), block_of(dxz, me), dz_s.at[k], dz_r.at[k], {"exp": p}) for k, p in enumerate(zs)
+        ]
+        for c in moves:
+            c.start()
+        dxz[here, :] = dx_r[here, :]
+        kept = grads(0)
+        swaps[1].wait()
+        out_r[...] = (outb[half(core), :].astype(F32) + out_r[...].astype(F32)).astype(BF16)
+        kept.append(pltpu.make_async_copy(out_r, back_o, ld.at[13]))
+        kept[-1].start()
+        kept += grads(1)
+        for k in range(3, E):
+            chain.hop(k)
+        for c in moves + kept:
+            c.wait()
+        chain.finish()
+
+    v = pltpu.VMEM
+    sem = lambda *dims: pltpu.SemaphoreType.DMA(dims)
+    vm = pl.BlockSpec(memory_space=pltpu.VMEM)
+    slots = 2 * (E - 1)
     return pl.pallas_call(
         body,
         name="expert",
-        grid_spec=pltpu.PrefetchScalarGridSpec(
-            num_scalar_prefetch=1,
-            grid=(steps,),
-            in_specs=[
-                whole_(x.shape),
-                whole_(cot.shape),
-                whole_(router.shape),
-                pl.BlockSpec((D, fb), lambda i, w: (0, 2 * i + w[2])),
-                pl.BlockSpec((fb, D), lambda i, w: (2 * i + w[2], 0)),
-            ],
-            out_specs=[
-                whole_((M, D)),
-                whole_((M, D + LANES)),
-                pl.BlockSpec((D, fb), lambda i, w: (0, i)),
-                pl.BlockSpec((fb, D), lambda i, w: (i, 0)),
-            ],
-            scratch_shapes=[pltpu.VMEM((M, D), BF16), pltpu.VMEM((M, D), F32), pltpu.VMEM((M, D), F32)],
+        in_specs=[vm] * 4 + [ANY] * 2,
+        out_specs=[vm] + [ANY] * 4,
+        out_shape=[
+            sds((M, D + LANES), BF16), sds((M, D), BF16), sds((D, 2 * wb), BF16), sds((2 * wb, D), BF16),
+            sds((E, T, D), BF16),
+        ],
+        scratch_shapes=[
+            v((2, D, wb), BF16), v((2, wb, D), BF16), v((2 * M, 2 * wb), BF16), v((2 * M, 2 * wb), BF16),
+            v((2 * M, D), BF16), v((2 * M, D), F32), v((2 * M, D), F32), v((2 * M, D + LANES), BF16),
+            v((2 * M, D), BF16), v((M, D + LANES), BF16), v((M, D), BF16), v((D, 2 * wb), BF16), v((2 * wb, D), BF16),
+            sem(14), sem(slots), sem(slots), sem(2), sem(2), sem(E - 1), sem(E - 1),
+        ],
+        compiler_params=pltpu.CompilerParams(
+            collective_id=cid, has_side_effects=True, vmem_limit_bytes=VMEM_LIMIT
         ),
-        out_shape=[
-            sds((M, D), BF16),
-            sds((M, D + LANES), BF16),
-            sds((D, steps * fb), BF16),
-            sds((steps * fb, D), BF16),
-        ],
-        compiler_params=pltpu.CompilerParams(vmem_limit_bytes=VMEM_LIMIT),
-    )(where, x, cot, router, up, down)
+    )(x, cot, router, normed, up, down)
 
 
 def padded_rows(main, edge, J, cb):
@@ -435,17 +537,21 @@
 
 
 class Spread:
-    def __init__(self, E, src, col0, dst, cols, whole_cols, each, sems):
-        self.E, self.src, self.col0, self.dst, self.cols = E, src, col0, dst, cols
-        self.whole_cols, self.each_cols = whole_cols, each
+    def __init__(self, E, src, col0, dst, cols, each, by_rows, sems):
+        self.E, self.src, self.col0, self.dst, self.cols, self.each_cols = E, src, col0, dst, cols, each
+        self.by_rows = by_rows
         self.zs, self.zr, self.ps, self.pr, self.cs, self.cr = sems
         self.rows = src.shape[0]
         s, self.me = lax.axis_index("seq"), lax.axis_index("exp")
         self.chip, self.core = s // 2, lax.rem(s, 2)
         self.sib = {"seq": s + 1 - 2 * self.core}
         self.chips = [self.chip + 1 - 2 * lax.rem(self.chip, 2), self.chip + 2 - 4 * (self.chip // 2), 3 - self.chip]
+        self.far = [{"seq": q * 2 + self.core} for q in self.chips]
         self.right, self.left = lax.rem(self.me + 1, E), lax.rem(self.me + E - 1, E)
-        self.regions = [1, 0] if each else [0]
+        self.split = by_rows or each > 0
+        self.rest = 0 if by_rows else cols - 4 * each
+        self.regions = ([1] if self.split else []) + ([0] if self.rest else [])
+        self.pieces = ([0] if self.rest else []) + ([1, 2, 3, 4] if self.split else [])
         self.offsets = [d for k in range(1, E) for d in (-k, k)]
 
     def slot(self, d):
@@ -454,29 +560,41 @@
     def exists(self, d):
         return (self.me + d >= 0) & (self.me + d < self.E)
 
-    def span(self, region, q):
+    def view(self, ref, row0, col0, region, q, core, half):
+        rows = self.rows // 2
+        row = row0 + core * rows
+        if self.by_rows:
+            rows = rows // 4
+            row = row + q * rows
+            if half is not None:
+                rows = rows // 2
+                row = row + half * rows
+            return ref.at[pl.ds(pl.multiple_of(row, 16), rows)]
+        at = pl.ds(pl.multiple_of(row, 16), rows)
         if region == 0:
-            return 0, self.whole_cols
-        return pl.multiple_of(self.whole_cols + q * self.each_cols, LANES), self.each_cols
-
-    def there(self, d, region, q, core):
-        half = self.rows // 2
-        start, width = self.span(region, q)
-        at = pl.ds(pl.multiple_of((self.me + d) * self.rows + core * half, 16), half)
-        return self.dst.at[at] if width == self.cols else self.dst.at[at, pl.ds(start, width)]
+            start, width = col0, self.rest
+        else:
+            start, width = col0 + self.rest + q * self.each_cols, self.each_cols
+            if half is not None:
+                width = width // 2
+                start = start + half * width
+        if width == ref.shape[1]:
+            return ref.at[at]
+        return ref.at[at, pl.ds(pl.multiple_of(start, LANES), width)]
+
+    def there(self, d, region, q, core, half=None):
+        return self.view(self.dst, (self.me + d) * self.rows, 0, region, q, core, half)
 
     def own(self, region):
-        half = self.rows // 2
-        start, width = self.span(region, self.chip)
-        at = pl.ds(pl.multiple_of(self.core * half, 16), half)
-        if width == self.src.shape[1]:
-            return self.src.at[at]
-        return self.src.at[at, pl.ds(pl.multiple_of(self.col0 + start, LANES), width)]
+        return self.view(self.src, 0, self.col0, region, self.chip, self.core, None)
 
     def local(self, sem):
         at = pl.ds(pl.multiple_of(self.me * self.rows, 16), self.rows)
         src = self.src if self.cols == self.src.shape[1] else self.src.at[:, self.col0 : self.col0 + self.cols]
         return pltpu.make_async_copy(src, self.dst.at[at], sem)
+
+    def remote(self, src, dst, send, recv, to):
+        return pltpu.make_async_remote_copy(src, dst, send, recv, device_id=to, device_id_type=MESH)
 
     def z_each(self, region, d, act):
         for to_right in (True, False):
@@ -487,13 +605,12 @@
                 @pl.when(self.exists(d) & edge)
                 def _():
                     act(
-                        pltpu.make_async_remote_copy(
+                        self.remote(
                             self.own(region) if d == 0 else self.there(d, region, self.chip, self.core),
                             self.there(d, region, self.chip, self.core),
                             self.zs.at[region, slot],
                             self.zr.at[region, slot],
-                            device_id={"exp": self.right if to_right else self.left},
-                            device_id_type=MESH,
+                            {"exp": self.right if to_right else self.left},
                         )
                     )
 
@@ -501,24 +618,24 @@
         for r in self.regions:
             self.z_each(r, 0, lambda c: c.start())
 
-    def plane_copy(self, k, d):
-        ref = self.there(d, 1, self.chip, self.core)
-        return pltpu.make_async_remote_copy(
-            ref, ref, self.ps.at[k, self.slot(d)], self.pr.at[k, self.slot(d)],
-            device_id={"seq": self.chips[k] * 2 + self.core}, device_id_type=MESH,
-        )
-
-    def piece(self, which, d, core):
+    def cross(self, j, d):
+        if j < 2:
+            ref = self.there(d, 1, self.chip, self.core)
+        else:
+            ref = self.there(d, 1, self.chips[j - 2], self.core, j - 2)
+        to = self.far[(0, 1, 1, 0)[j]]
+        return self.remote(ref, ref, self.ps.at[j, self.slot(d)], self.pr.at[j, self.slot(d)], to)
+
+    def crossed(self, j, d):
+        ref = self.there(d, 1, self.chips[j], self.core) if j < 2 else self.there(d, 1, self.chips[2], self.core, j - 2)
+        self.remote(ref, ref, self.ps.at[j, self.slot(d)], self.pr.at[j, self.slot(d)], self.sib).wait_recv()
+
+    def sib_copy(self, which, d, core):
         if which == 0:
-            return self.there(d, 0, self.chip, core)
-        return self.there(d, 1, self.chip if which == 1 else self.chips[which - 2], core)
-
-    def sib_copy(self, which, d, core):
-        ref = self.piece(which, d, core)
-        return pltpu.make_async_remote_copy(
-            ref, ref, self.cs.at[which, self.slot(d)], self.cr.at[which, self.slot(d)],
-            device_id=self.sib, device_id_type=MESH,
-        )
+            ref = self.there(d, 0, self.chip, core)
+        else:
+            ref = self.there(d, 1, self.chip if which == 1 else self.chips[which - 2], core)
+        return self.remote(ref, ref, self.cs.at[which, self.slot(d)], self.cr.at[which, self.slot(d)], self.sib)
 
     def hop(self, k):
         for r in self.regions:
@@ -526,9 +643,8 @@
                 @pl.when(self.exists(d))
                 def _():
                     ref = self.there(d, r, self.chip, self.core)
-                    pltpu.make_async_remote_copy(
-                        ref, ref, self.zs.at[r, self.slot(d)], self.zr.at[r, self.slot(d)],
-                        device_id={"exp": self.right}, device_id_type=MESH,
+                    self.remote(
+                        ref, ref, self.zs.at[r, self.slot(d)], self.zr.at[r, self.slot(d)], self.sib
                     ).wait_recv()
 
                 if k < self.E - 1:
@@ -537,40 +653,43 @@
                 @pl.when(self.exists(d))
                 def _():
                     if r == 1:
-                        for j in range(3):
-                            self.plane_copy(j, d).start()
+                        for j in range(2):
+                            self.cross(j, d).start()
                     self.sib_copy(r, d, self.core).start()
 
     def plane(self, k):
-        if not self.each_cols:
-            return
-        for d in (-k, k):
+        for d in (-k, k) if self.split else ():
             @pl.when(self.exists(d))
             def _():
-                for j in range(3):
-                    ref = self.there(d, 1, self.chips[j], self.core)
-                    pltpu.make_async_remote_copy(
-                        ref, ref, self.ps.at[j, self.slot(d)], self.pr.at[j, self.slot(d)],
-                        device_id=self.sib, device_id_type=MESH,
-                    ).wait_recv()
+                for j in range(2):
+                    self.crossed(j, d)
+                    self.cross(2 + j, d).start()
                     self.sib_copy(2 + j, d, self.core).start()
+
+    def fourth(self, k):
+        for d in (-k, k) if self.split else ():
+            @pl.when(self.exists(d))
+            def _():
+                self.crossed(2, d)
+                self.crossed(3, d)
+                self.sib_copy(4, d, self.core).start()
 
     def landed(self):
         for d in self.offsets:
             @pl.when(self.exists(d))
             def _():
-                for w in range(5 if self.each_cols else 1):
+                for w in self.pieces:
                     self.sib_copy(w, d, 1 - self.core).wait_recv()
 
     def finish(self):
         for d in self.offsets:
             @pl.when(self.exists(d))
             def _():
-                for w in range(5 if self.each_cols else 1):
+                for w in self.pieces:
                     self.sib_copy(w, d, self.core).wait_send()
-                if self.each_cols:
-                    for j in range(3):
-                        self.plane_copy(j, d).wait_send()
+                if self.split:
+                    for j in range(4):
+                        self.cross(j, d).wait_send()
         for r in self.regions:
             for k in range(self.E - 1):
                 for d in (-k, k) if k else (0,):
@@ -578,20 +697,18 @@
 
 
 def small_rows(z):
-    return z.SMALL + -z.SMALL % 32
+    return 128 * -(-z.SMALL // 128)
 
 
 def pack_small(z, par, own_sm, own_g):
     conv_w, conv_b, dt_b, skip, a_log, dt_w, x_w, gain_a, gain_b, router = par
-    cw, dw = own_sm.shape[1], own_g.shape[1]
-    eye = lambda r, c: (
-        lax.broadcasted_iota(jnp.int32, (r, c), 0) == lax.broadcasted_iota(jnp.int32, (r, c), 1)
-    ).astype(F32).astype(BF16)
+    (rs, cw), (rg, dw) = own_sm.shape, own_g.shape
     wide = lambda ref: ref[...].astype(F32)
-    rows = [wide(conv_w), wide(conv_b), wide(dt_b), wide(skip), jnp.zeros((1, cw), F32), wide(a_log), wide(dt_w)]
-    rows += [mm_nt(eye(z.XW, z.XW), x_w[...]), jnp.zeros((-z.SMALL % 32, cw), F32)]
+    line = lambda ref: ref[...].astype(F32).reshape(1, ref.shape[0])
+    rows = [wide(conv_w), line(conv_b), line(dt_b), line(skip), jnp.zeros((1, cw), F32), wide(a_log), wide(dt_w)]
+    rows += [wide(x_w), jnp.zeros((rs - z.SMALL, cw), F32)]
     own_sm[...] = jnp.concatenate(rows, axis=0).astype(BF16)
-    rows = [wide(gain_a), wide(gain_b), mm_nt(eye(16, z.E), router[...]), jnp.zeros((14, dw), F32)]
+    rows = [line(gain_a), line(gain_b), wide(router), jnp.zeros((rg - 2 - z.E, dw), F32)]
     own_g[...] = jnp.concatenate(rows, axis=0).astype(BF16)
 
 
@@ -618,11 +735,11 @@
         par = refs[4 : 4 + np_]
         (
             in_p, out_p,
-            sm, gp, rt, table, choose, masks, conv_in, hconv, gate, sig, mixed, dt, y, mid, moe, ch_o, s_all, tok, cot,
-            st_o, win_o, wout_o, arr_o, cot_o, nz_o,
+            sm, gp, rt, table, choose, masks, conv_in, hconv, gate, sig, mixed, dt, y, mid, moe, ch_o, s_all, tok, cot, normed_o,
+            st_o, win_o, wout_o, arr_o, cot_o,
             wc, wg, wo, smb, gb, nrm, halo, seg_in, bx, cx, cl, u_s, rates_s, hd, hdev, stot, h_all, pre_s, dwin, hin,
             st_v, acc, outb, cotb, own_sm, own_g, own_seg,
-            ld, zs, zr, ps, pr, c_s, c_r, t_s, t_r, h_s, h_r, d_s, d_r, q_s, q_r, k_s, k_r, n_s, n_r, x_s, x_r,
+            ld, zs, zr, ps, pr, c_s, c_r, t_s, t_r, h_s, h_r, d_s, d_r, q_s, q_r, k_s, k_r, x_s, x_r,
         ) = refs[4 + np_ :]
         s, me = lax.axis_index("seq"), lax.axis_index("exp")
         core = lax.rem(s, 2)
@@ -645,11 +762,11 @@
         sems = lambda a: (zs.at[a], zr.at[a], ps.at[a], pr.at[a], c_s.at[a], c_r.at[a])
         if plane:
             parts = [
-                Spread(E, own_sm, 0, smb, DZ, DZ, 0, sems(0)),
-                Spread(E, own_g, 0, gb, NZ, NZ, 0, sems(1)),
-                Spread(E, in_p, 0, wc, DI, DI - 4 * split, split, sems(2)),
-                Spread(E, in_p, DI, wg, DI, DI - 4 * split, split, sems(3)),
-                Spread(E, out_p, 0, wo, D, D - 4 * split_o, split_o, sems(4)),
+                Spread(E, own_sm, 0, smb, DZ, 0, True, sems(0)),
+                Spread(E, own_g, 0, gb, NZ, 0, False, sems(1)),
+                Spread(E, in_p, 0, wc, DI, split, False, sems(2)),
+                Spread(E, in_p, DI, wg, DI, split, False, sems(3)),
+                Spread(E, out_p, 0, wo, D, split_o, False, sems(4)),
             ]
             for p in parts[:3]:
                 p.start()
@@ -677,8 +794,12 @@
             queue = [wg_p.start] + [functools.partial(wg_p.hop, k) for k in range(1, E - 1)]
             queue += [wo_p.start, functools.partial(wg_p.hop, E - 1)]
             for k in range(1, E):
-                queue += [functools.partial(wo_p.hop, k), functools.partial(wg_p.plane, k)]
-            queue += [functools.partial(wo_p.plane, k) for k in range(1, E)]
+                queue += [functools.partial(wg_p.plane, k), functools.partial(wo_p.hop, k)]
+                queue += [functools.partial(wg_p.fourth, k)]
+            for k in range(1, E):
+                queue += [functools.partial(wo_p.plane, k)]
+            for k in range(1, E):
+                queue += [functools.partial(wo_p.fourth, k)]
 
         def progress(count):
             for _ in range(count):
@@ -705,19 +826,18 @@
         scaled = t32 * rms_scale(t32)
 
         if plane:
-            for k in range(1, E):
-                for p in parts[:3]:
-                    p.hop(k)
-                if k == 1:
+            for k in range(1, E + 2):
+                if k < E:
+                    for p in parts[:3]:
+                        p.hop(k)
                     progress(1)
-                elif k == 2:
+                if 1 <= k - 1 < E:
+                    parts[0].plane(k - 1)
+                    parts[2].plane(k - 1)
                     progress(1)
-                    parts[2].plane(1)
-                else:
-                    progress(1)
-            for k in range(2, E):
-                parts[2].plane(k)
-            progress(1)
+                if 1 <= k - 2 < E:
+                    parts[0].fourth(k - 2)
+                    parts[2].fourth(k - 2)
         block_of = lambda ref, p: ref.at[pl.ds(pl.multiple_of(p * CAP, 16), CAP)]
         cot_moves = [remote(block_of(cotb, p), cot_o.at[core, me], k_s.at[k], k_r.at[k], {"exp": p}) for k, p in enumerate(zz)]
         if plane:
@@ -771,8 +891,8 @@
             return carry
 
         lax.fori_loop(0, DI // cb, conv_block, 0)
-        chain_n = Chain(E, nrm.at[0:T], nz_o, n_s, n_r, ld.at[5])
-        progress(2)
+        normed_o[...] = nrm[0:T, :]
+        progress(3)
         cot_own = pltpu.make_async_copy(block_of(cotb, me), cot_o.at[core, me], ld.at[6])
         cot_own.start()
 
@@ -791,7 +911,7 @@
             return carry
 
         lax.fori_loop(0, DI // cs, step_block, 0)
-        progress(2)
+        progress(3)
 
         def chunk_block(p, carry):
             lanes = [lane_at(p, tg, k) for k in range(tg)]
@@ -839,9 +959,9 @@
 
         third = DI // wide // 3
         lax.fori_loop(0, third, chunk_block, 0)
-        progress(2)
+        progress(3)
         lax.fori_loop(third, 2 * third, chunk_block, 0)
-        progress(2)
+        progress(3)
         lax.fori_loop(2 * third, DI // wide, chunk_block, 0)
         hdev[...] = hd[...].astype(BF16)
         h_moves = [remote(hdev, h_all.at[s], h_s.at[0, k], h_r.at[0, k], {"seq": p}) for k, p in enumerate(seqs)]
@@ -852,7 +972,6 @@
         s_all[s] = stot[...]
         for c in cot_moves:
             c.start()
-        chain_n.start()
         progress(len(queue))
         if plane:
             parts[3].landed()
@@ -942,16 +1061,12 @@
 
             lax.fori_loop(0, cs // wide, pair, 0)
             save(i).start()
-            if i + 1 < E:
-                chain_n.hop(i + 1)
             yv = y[:, C] + sm[SKIP : SKIP + 1, C] * sig[:, C].astype(F32)
             y[:, C] = yv
             g_in = gate[:, C]
             gated = (yv * (g_in * sigmoid(g_in))).astype(BF16)
             acc[...] += mm(gated, wo[C, :])
 
-        for k in range(steps + 1, E):
-            chain_n.hop(k)
         m32 = tok[...].astype(F32) + acc[...]
         mid[...] = m32
         moe[...] = (m32 * rms_scale(m32) * gp[1:2, :]).astype(BF16)
@@ -981,7 +1096,6 @@
                 p.finish()
         for c in outs + [cot_own, arr_own]:
             c.wait()
-        chain_n.finish()
         for i in range(max(0, steps - 2), steps):
             save(i).wait()
         for c in cot_moves + out_moves + passes:
@@ -1000,11 +1114,11 @@
         sds((z.SMALL, DI), F32), sds((gr, D), F32), sds((LANES, D), BF16), sds((T, M), BF16), sds((T, LANES), F32),
         sds((T, SUB), F32), sds((T, DI), F32), sds((H, DI), F32), sds((T, DI), F32), sds((T, DI), BF16),
         sds((T, z.XW), F32), sds((T, DI), F32), sds((T, DI), F32), sds((T, D), F32), sds((T, D), BF16),
-        sds((T, LANES), F32), sds((S, 1, DI), F32), sds((T, D), BF16), sds((T, D), BF16),
+        sds((T, LANES), F32), sds((S, 1, DI), F32), sds((T, D), BF16), sds((T, D), BF16), sds((T, D), BF16),
     ]
     any_outs = [
         sds((ST, DI), BF16), sds((D, 2 * DI), BF16), sds((DI, D), BF16), sds((2, E, CAP, D), BF16),
-        sds((2, E, CAP, D), BF16), sds((E, T, D), BF16),
+        sds((2, E, CAP, D), BF16),
     ]
     return pl.pallas_call(
         body,
@@ -1020,9 +1134,9 @@
             v((N * SUB, DI), F32), v((SUB, DI), F32), v((N, cs), F32),
             v((2, ST, cs), BF16), v((T, D), F32), v((M, D), BF16), v((M, D), BF16),
             v((rs, DZ), BF16), v((rg, NZ), BF16), v((SUB, T), F32),
-            sem(13), sem(5, 2, zslots), sem(5, 2, zslots), sem(5, 3, zslots), sem(5, 3, zslots),
+            sem(13), sem(5, 2, zslots), sem(5, 2, zslots), sem(5, 4, zslots), sem(5, 4, zslots),
             sem(5, 5, zslots), sem(5, 5, zslots), sem(2), sem(2), sem(2, S - 1), sem(2, S - 1),
-            sem(E - 1), sem(E - 1), sem(1), sem(1), sem(E - 1), sem(E - 1), sem(zslots), sem(zslots),
+            sem(E - 1), sem(E - 1), sem(1), sem(1), sem(E - 1), sem(E - 1),
             sem(2, E), sem(2, E),
         ],
         compiler_params=pltpu.CompilerParams(
@@ -1031,7 +1145,7 @@
     )(*ins)
 
 
-def backward(z, S, plane, dxp, outp, dwu, dwd, states, w_out, w_in, table, choose, chances, mid, moe, cot, gpack,
+def backward(z, S, plane, expert_out, dx_z, dwu, dwd, states, w_out, w_in, table, choose, chances, mid, moe, cot, gpack,
              router, gate, y, sig, small, mixed, dt, masks, conv_in, hconv, s_all, tok, normed_all, cid):
     T, D, DI, N, J, E, CAP = z.T, z.D, z.DI, z.N, z.J, z.E, z.CAP
     M = E * CAP
@@ -1050,24 +1164,25 @@
     chain_slots = 2 * (E - 1)
 
     def body(
-        dxp, outp, dwu, dwd, states, w_out, w_in, table, choose, chances, mid, moe, cot, gp, router, gate, y, sig,
+        eo, dwu, dwd, states, w_out, w_in, dx_z, table, choose, chances, mid, moe, cot, gp, router, gate, y, sig,
         small, mixed, dt, masks, conv_in, hconv, s_all, tok, nall,
         tg_o, gs_o, gg_o, back_o, pg_o, pc_o, pm_o, po_o, up_o, down_o,
-        big, wo_v, n_v, dx_a, dx_b, out_a, out_b, dx_z, yg, gi, gz, br, mg, fdev, f_all, suf, cg_edge,
+        own_v, big, wo_v, n_v, yg, gi, gz, br, mg, fdev, f_all, suf, cg_edge,
         edge_in, pc, bx, cx, ia, oa, cl, u_s, rates_s, fin, dg_s, rs_s, rt_s, low_s, mxg, fd,
         ua, ub, ub2, da, db, db2, gi_all, pc_all, br_all, gz_all, gi_b,
         p_g, p_c, p_m, p_o, bg, bc, bm, bo, tg_, tc_, tm_, to_, zg, zc, zm,
         pcs, pcr, pqs, pqr, pzs, pzr, pgs, pgr, pfs, pfr, pown,
-        ld, sw_s, sw_r, dz_s, dz_r, oz_s, oz_r, f_s, f_r, e_s, e_r, g_s, g_r, p_s, p_r, b_s, b_r, a_s, a_r, x_s, x_r,
+        ld, oz_s, oz_r, f_s, f_r, e_s, e_r, g_s, g_r, p_s, p_r, b_s, b_r, a_s, a_r, x_s, x_r,
     ):
         psems = lambda a: (
             pcs.at[a], pcr.at[a], pqs.at[a], pqr.at[a], pzs.at[a], pzr.at[a], pgs.at[a], pgr.at[a], pfs.at[a],
             pfr.at[a], pown.at[a],
         )
-        sum_g = PlaneSum(E, p_g, bg, tg_, zg, pg_o, False, psems(0))
-        sum_c = PlaneSum(E, p_c, bc, tc_, zc, pc_o, False, psems(1))
-        sum_m = PlaneSum(E, p_m, bm, tm_, zm, pm_o, True, psems(2))
-        sum_o = PlaneSum(E, p_o, bo, to_, None, po_o, False, psems(3))
+        extra = lambda rows: (16 * (rows // 128), -(-(rows // 16 % 8) // 2) if rows // 16 % 8 else 4)
+        sum_g = PlaneSum(E, p_g, bg, tg_, zg, pg_o, False, *extra(NZ), psems(0))
+        sum_c = PlaneSum(E, p_c, bc, tc_, zc, pc_o, False, *extra(NZ), psems(1))
+        sum_m = PlaneSum(E, p_m, bm, tm_, zm, pm_o, True, 0, 4, psems(2))
+        sum_o = PlaneSum(E, p_o, bo, to_, None, po_o, False, *extra(DZ), psems(3))
         stage = (lambda f: f()) if plane else (lambda f: None)
         s, me = lax.axis_index("seq"), lax.axis_index("exp")
         core = lax.rem(s, 2)
@@ -1079,19 +1194,6 @@
 
         def remote(src, dst, send, recv, to):
             return pltpu.make_async_remote_copy(src, dst, send, recv, device_id=to, device_id_type=MESH)
-
-        swaps = [
-            remote(dxp.at[other], dx_b, sw_s.at[0], sw_r.at[0], sib),
-            remote(outp.at[other], out_b, sw_s.at[1], sw_r.at[1], sib),
-        ]
-        for c in swaps:
-            c.start()
-        loads = [
-            pltpu.make_async_copy(dxp.at[core], dx_a, ld.at[0]),
-            pltpu.make_async_copy(outp.at[core], out_a, ld.at[1]),
-        ]
-        for c in loads:
-            c.start()
 
         def out_load(i):
             slot = lax.rem(i, 2)
@@ -1127,34 +1229,18 @@
                 c.start()
 
         adds = lambda a, b: (a.astype(F32) + b.astype(F32)).astype(BF16)
-        loads[0].wait()
-        swaps[0].wait()
-        dx_a[...] = adds(dx_a[...], dx_b[...])
         block_of = lambda ref, p: ref.at[pl.ds(pl.multiple_of(p * CAP, 16), CAP)]
-        dx_moves = [
-            remote(block_of(dx_a, p), block_of(dx_z, me), dz_s.at[k], dz_r.at[k], {"exp": p})
-            for k, p in enumerate(zs)
-        ]
-        for c in dx_moves:
-            c.start()
-        here = pl.ds(pl.multiple_of(me * CAP, 16), CAP)
-        dx_z[here, :] = dx_a[here, :]
-        loads[1].wait()
-        swaps[1].wait()
-        out_a[...] = adds(out_a[...], out_b[...])
         out_moves = [
-            remote(block_of(out_a, p), block_of(back_o, me), oz_s.at[k], oz_r.at[k], {"exp": p})
-            for k, p in enumerate(zs)
+            remote(block_of(eo, p), block_of(back_o, me), oz_s.at[k], oz_r.at[k], {"exp": p}) for k, p in enumerate(zs)
         ]
         for c in out_moves:
             c.start()
-        back_own = pltpu.make_async_copy(block_of(out_a, me), block_of(back_o, me), ld.at[8])
-        back_own.start()
+        back_load = pltpu.make_async_copy(block_of(eo, me), own_v, ld.at[8])
+        back_own = pltpu.make_async_copy(own_v, block_of(back_o, me), ld.at[8])
+        back_load.start()
         expand_columns(z, mixed, z.R, bx)
         expand_columns(z, mixed, z.R + N, cx)
         expand_closed(z, masks, cl)
-        for c in dx_moves:
-            c.wait()
 
         back = mm(table[...], dx_z[...])
         grad = cot[...].astype(F32)
@@ -1208,6 +1294,8 @@
             c.start()
         gi_all[me] = gi_b[me]
         chain_b.start()
+        back_load.wait()
+        back_own.start()
 
         tg, ng = 2 if DI % 256 == 0 else 1, 8
         wide = tg * LANES
@@ -1629,7 +1717,7 @@
     down_shape = (dq, dc) if plane else (16, LANES)
     u_shape = (2, uq, uc) if plane else (2, 16, LANES)
     d_shape = (2 * dq, dc) if plane else (32, LANES)
-    ins = (dxp, outp, dwu, dwd, states, w_out, w_in, table, choose, chances, mid, moe, cot, gpack, router, gate, y,
+    ins = (expert_out, dwu, dwd, states, w_out, w_in, dx_z, table, choose, chances, mid, moe, cot, gpack, router, gate, y,
            sig, small, mixed, dt, masks, conv_in, hconv, s_all, tok, normed_all)
     rg, ro, rm = chunk_rows(NZ), chunk_rows(DZ), 16 * -(-(z.SMALL + G) // 128)
     p_shapes = [(E, 4, 2, rg, DZ), (E, 4, 2, rg, DZ), (E, 4, 2, rm, DZ), (1, 4, 2, ro, D)]
@@ -1637,7 +1725,7 @@
     return pl.pallas_call(
         body,
         name="backward",
-        in_specs=[ANY] * 7 + [vm] * (len(ins) - 8) + [ANY],
+        in_specs=[ANY] * 6 + [vm] * (len(ins) - 7) + [ANY],
         out_specs=[vm] * 3 + [ANY] * 7,
         out_shape=[
             sds((T, D), F32),
@@ -1651,10 +1739,9 @@
             sds(down_shape, BF16),
         ],
         scratch_shapes=[
+            v((CAP, D), BF16),
             v((2, rows_big, cb_s), BF16),
             v((2, cb_m, D), BF16), v((E * T, D), BF16),
-            v((M, D + LANES), BF16), v((M, D + LANES), BF16), v((M, D), BF16), v((M, D), BF16),
-            v((M, D + LANES), BF16),
             v((T, DI), F32), v((T, DI), BF16), v((E, T, DZ), BF16),
             v((T, D), BF16), v((T, D), F32),
             v((N, DI), BF16), v((S, N, DI), BF16), v(((N + 1) * SUB, DI), F32),
@@ -1675,9 +1762,9 @@
         + [v((3, p[0]) + p[3:], BF16) for p in p_shapes]
         + [v((E,) + p[3:], BF16) for p in p_shapes[:3]]
         + [
-            sem(4), sem(4), sem(4, 3), sem(4, 3), sem(4, E - 1), sem(4, E - 1), sem(4, 3), sem(4, 3), sem(4, 4),
-            sem(4, 4), sem(4),
-            sem(18), sem(2), sem(2), sem(E - 1), sem(E - 1), sem(E - 1), sem(E - 1), sem(S - 1), sem(S - 1),
+            sem(4, 2), sem(4, 2), sem(4, 3, 2), sem(4, 3, 2), sem(4, E - 1, 2), sem(4, E - 1, 2), sem(4, 3, 2),
+            sem(4, 3, 2), sem(4, 4, 2), sem(4, 4, 2), sem(4),
+            sem(18), sem(E - 1), sem(E - 1), sem(S - 1), sem(S - 1),
             pltpu.SemaphoreType.DMA, pltpu.SemaphoreType.DMA,
             sem(E - 1), sem(E - 1), sem(E - 1), sem(E - 1), sem(chain_slots), sem(chain_slots),
             sem(6), sem(6), sem(E - 1), sem(E - 1),
@@ -1707,14 +1794,13 @@
             dwo[16 * g : 16 * g + 16, :] = po[chunk, off : off + 16, :].astype(F32)
         sm = pm[...].astype(F32)
         cw[...] = sm[CONV_W : CONV_W + 4]
-        cb[...] = sm[CONV_B : CONV_B + 1]
-        db[...] = sm[DT_B : DT_B + 1]
-        sk[...] = sm[SKIP : SKIP + 1]
+        for ref, row in ((cb, CONV_B), (db, DT_B), (sk, SKIP)):
+            ref[...] = sm[row : row + 1].reshape(DZ)
         al[...] = sm[A_LOG : A_LOG + N]
         dw[...] = sm[z.DT0 : z.X0]
         xw[...] = sm[z.X0 : z.SMALL]
-        na[...] = sm[z.SMALL : z.SMALL + 1, 0:NZ]
-        nb[...] = sm[z.SMALL + 1 : z.SMALL + 2, 0:NZ]
+        na[...] = sm[z.SMALL : z.SMALL + 1, 0:NZ].reshape(NZ)
+        nb[...] = sm[z.SMALL + 1 : z.SMALL + 2, 0:NZ].reshape(NZ)
         ro[...] = sm[z.SMALL + 2 : z.SMALL + 2 + E, 0:NZ]
         lane = lax.broadcasted_iota(jnp.int32, (T, T), 1)
         prow = lax.broadcasted_iota(jnp.int32, (T, T), 0)
@@ -1737,8 +1823,8 @@
     vm = pl.BlockSpec(memory_space=pltpu.VMEM)
     shapes = [
         sds((NZ, 2 * DI), F32), sds((DZ, D), F32), sds((T, D), BF16), sds((T, D), F32), sds((4, DZ), F32),
-        sds((1, DZ), F32), sds((z.XW, DZ), F32), sds((z.R, DZ), F32), sds((1, DZ), F32), sds((N, DZ), F32),
-        sds((1, DZ), F32), sds((1, NZ), F32), sds((1, NZ), F32), sds((E, NZ), F32),
+        sds((DZ,), F32), sds((z.XW, DZ), F32), sds((z.R, DZ), F32), sds((DZ,), F32), sds((N, DZ), F32),
+        sds((DZ,), F32), sds((NZ,), F32), sds((NZ,), F32), sds((E, NZ), F32),
     ]
     if plane:
         shapes += [sds((U, z.FF), F32), sds(down.shape, F32)]
@@ -1762,19 +1848,17 @@
     T, D, DI, N, J, CAP = z.T, z.D, z.DI, z.N, z.J, z.CAP
     me_s, me_e = lax.axis_index("seq"), lax.axis_index("exp")
     core = lax.rem(me_s, 2)
-    where = jnp.stack([me_s, me_e, core]).astype(jnp.int32)
     cw = dt_proj.shape[1]
     dw = norm_gain.shape[0]
     plane = S == 8 and dw % 32 == 0
     line = lambda v: v.reshape(1, -1)
     if plane:
-        params = [conv_weight, line(conv_bias), line(dt_bias), line(d_skip), a_log, dt_proj, x_proj,
-                  line(norm_gain), line(moe_gain), router]
+        params = [conv_weight, conv_bias, dt_bias, d_skip, a_log, dt_proj, x_proj.T, norm_gain, moe_gain, router.T]
         w_in, w_out = in_proj, out_proj
     else:
         small_own = jnp.concatenate(
             [conv_weight, line(conv_bias), line(dt_bias), line(d_skip), jnp.zeros((1, cw), BF16), a_log, dt_proj,
-             x_proj.T, jnp.zeros((-z.SMALL % 32, cw), BF16)], axis=0
+             x_proj.T, jnp.zeros((small_rows(z) - z.SMALL, cw), BF16)], axis=0
         )
         g_own = jnp.concatenate(
             [line(norm_gain), line(moe_gain), router.T, jnp.zeros((32 - 2 - E, dw), BF16)], axis=0
@@ -1784,17 +1868,17 @@
     gr = 8 * -(-(2 + E) // 8)
     (
         small, gpack, router_t, table, choose_wide, masks, conv_in, hconv, gate, sig, mixed, dt, y, mid, moe, chances,
-        s_all, tok, cot, states, w_in, w_out, arrived, cot_pair, normed_all,
+        s_all, tok, cot, normed, states, w_in, w_out, arrived, cot_pair,
     ) = forward(
         z, S, plane, tokens[0], cotangent[0], segment_ids, routes.reshape(1, T), params, w_in, w_out, gr, 1
     )
-    outp, dxp, dwu, dwd = expert(
-        z, where, arrived.reshape(2 * E * CAP, D), cot_pair.reshape(2 * E * CAP, D), router_t, up_proj[0], down_proj[0]
+    dx_z, expert_out, dwu, dwd, normed_all = expert(
+        z, arrived.reshape(2 * E * CAP, D), cot_pair.reshape(2 * E * CAP, D), router_t, normed, up_proj[0],
+        down_proj[0], 3
     )
     token_grad, _, _, back_out, pg, pc, pm, po, up_sum, down_sum = backward(
-        z, S, plane, dxp.reshape(2, E * CAP, -1), outp.reshape(2, E * CAP, D), dwu, dwd, states, w_out, w_in, table,
-        choose_wide, chances, mid, moe, cot, gpack, router_t, gate, y, sig, small, mixed, dt, masks, conv_in, hconv,
-        s_all, tok, normed_all.reshape(E * T, D), 4
+        z, S, plane, expert_out, dx_z, dwu, dwd, states, w_out, w_in, table, choose_wide, chances, mid, moe, cot, gpack, router_t,
+        gate, y, sig, small, mixed, dt, masks, conv_in, hconv, s_all, tok, normed_all.reshape(E * T, D), 4
     )
     if not plane:
         pg, pc, pm, po = [lax.psum(a, "seq") for a in (pg, pc, pm, po)]
@@ -1822,8 +1906,8 @@
             for v in (up_full.reshape(D, z.FF), down_full.reshape(z.FF, D))
         ]
     return (
-        output[None], token_grad[None], g_na[0], dw_in, g_cw, g_cb[0], g_xw.T, g_dw, g_db[0], g_al, g_sk[0], dw_out,
-        g_nb[0], g_ro.T, up_part[None], down_part[None],
+        output[None], token_grad[None], g_na, dw_in, g_cw, g_cb, g_xw.T, g_dw, g_db, g_al, g_sk, dw_out,
+        g_nb, g_ro.T, up_part[None], down_part[None],
     )
 
 

time: 338 us -> 321 us (0.950)
  local copies, waits for them, and re-layouts: 9.4 us -> 0 us
  other arithmetic: 6.97 us -> 0 us
    pallas_call x1, Pallas kernels: 124 us -> 113 us  [forward(): pl.pallas_call(body, name='forward', in_specs=[vm] * 4 + [vm if plane els...]
    pallas_call x2, Pallas kernels: 183 us -> 191 us  [the longest x1 156 us: backward(): pl.pallas_call(body, name='backward', in_specs=[ANY] * 6 + [vm] * (len(in...]
    pallas_call x5 -> x0, other arithmetic: 6.38 us -> none  [finish(): pl.pallas_call(body, name='finish', in_specs=[vm] * 12, out_specs=[vm] *...]
    reshape x5 -> x0, local copies, waits for them, and re-layouts: 6.27 us -> none  [on_device(): line = lambda v: v.reshape(1, -1)]
where the time goes in v6:
time: 321 us; the launch traced here: 315 us
  Pallas kernels  314 us (98%)
    pallas_call x1, Pallas kernels, backward(): pl.pallas_call(body, name='backward', in_specs=[ANY] * 6 + [vm] * (len(in...  156 us
    pallas_call x1, Pallas kernels, forward(): pl.pallas_call(body, name='forward', in_specs=[vm] * 4 + [vm if plane els...  113 us
    pallas_call x1, Pallas kernels, expert(): pl.pallas_call(body, name='expert', in_specs=[vm] * 4 + [ANY] * 2, out_sp...  35.6 us
    pallas_call x1, Pallas kernels, finish(): pl.pallas_call(body, name='finish', in_specs=[vm] * 12, out_specs=[vm] *...  9.37 us

profile of v6, /device:TPU:23, one launch (start us, length us, event | category | flops | bytes accessed | tf_op | source)
XLA Modules:
  0.0 315.1 jit_solution(17113214010533134673)
XLA Ops:
  0.7 113.2 %forward.1 = (f32[200,2304]{1,0:T(8,128)}, f32[8,1152]{1,0:T(8,128)}, bf16[128,1152]{1,0:T(8,128)(2,1)}, bf16[128,256]{1,0:T(8,128)(2,1)}, f32[128,128]{1,0:T(8,...) custom-call(bf16[128,1152]{1,0:T(8,128)(2,1)} %bitcast.29, ...), custom_call_target="tpu_custom_call" | custom-call | tf_op jit(solution)/shard_map/forward/pallas_call | solution.py:1123
  113.8 35.6 %expert.1 = (bf16[256,1280]{1,0:T(8,128)(2,1)}, bf16[256,1152]{1,0:T(8,128)(2,1)}, bf16[1152,1536]{1,0:T(8,128)(2,1)}, bf16[1536,1152]{1,0:T(8,128)(2,1)}, bf16[4,128,1152]{2,1,0:T(8,128)(2,1)}) custom-call(bf16[512,1152]{1,0:T(8,128)(2,1)} %bitcast.26, bf16[512,1152]{1,0:T(8,128)(2,1)} %bitcast.27, bf16[128,1152]{1,0:T(8,128)(2,1)} %get-tuple-element.72.rt.router, ...), custom_call_target="tpu_custom_call" | custom-call | tf_op jit(solution)/shard_map/expert/pallas_call | solution.py:434
  149.4 155.8 %backward.1 = (f32[128,1152]{1,0:T(8,128)}, f32[200,2304]{1,0:T(8,128)}, f32[8,1152]{1,0:T(8,128)}, bf16[256,1152]{1,0:T(8,128)(2,1)}, bf16[4,2,4,48,576]{4,3,2,...) custom-call(bf16[256,1152]{1,0:T(8,128)(2,1)} %get-tuple-element.74., ...), custom_call_target="tpu_custom_call" | custom-call | tf_op jit(solution)/shard_map/backward/pallas_call | solution.py:1725
  305.3 9.4 %finish.1 = (f32[288,4608]{1,0:T(8,128)}, f32[576,1152]{1,0:T(8,128)}, bf16[128,1152]{1,0:T(8,128)(2,1)}, f32[128,1152]{1,0:T(8,128)}, f32[4,576]{1,0:T(4,128)},...) custom-call(bf16[8,4,48,576]{3,2,1,0:T(8,128)(2,1)} %bitcast.22, ...), custom_call_target="tpu_custom_call" | custom-call | tf_op jit(solution)/shard_map/finish/pallas_call | solution.py:1831

commit v7 on v6

--- a/solution.py
+++ b/solution.py
@@ -735,8 +735,9 @@
         par = refs[4 : 4 + np_]
         (
             in_p, out_p,
-            sm, gp, rt, table, choose, masks, conv_in, hconv, gate, sig, mixed, dt, y, mid, moe, ch_o, s_all, tok, cot, normed_o,
-            st_o, win_o, wout_o, arr_o, cot_o,
+            sm, gp, rt, table, choose, masks, hconv, mixed, mid, moe, ch_o, s_all, tok, cot, normed_o,
+            st_o, win_o, wout_o, arr_o, cot_o, conv_o, gate_o, sig_o, dt_o, y_o,
+            conv_in, gate, sig, dt, y,
             wc, wg, wo, smb, gb, nrm, halo, seg_in, bx, cx, cl, u_s, rates_s, hd, hdev, stot, h_all, pre_s, dwin, hin,
             st_v, acc, outb, cotb, own_sm, own_g, own_seg,
             ld, zs, zr, ps, pr, c_s, c_r, t_s, t_r, h_s, h_r, d_s, d_r, q_s, q_r, k_s, k_r, x_s, x_r,
@@ -892,6 +893,12 @@
 
         lax.fori_loop(0, DI // cb, conv_block, 0)
         normed_o[...] = nrm[0:T, :]
+        keeps = [
+            pltpu.make_async_copy(a, b, ld.at[13 + n])
+            for n, (a, b) in enumerate(((conv_in, conv_o), (sig, sig_o), (dt, dt_o), (gate, gate_o), (y, y_o)))
+        ]
+        keeps[0].start()
+        keeps[1].start()
         progress(3)
         cot_own = pltpu.make_async_copy(block_of(cotb, me), cot_o.at[core, me], ld.at[6])
         cot_own.start()
@@ -957,6 +964,7 @@
                         hd[g + n : g + n + 1, lanes[k]] = h[SUB - 1 : SUB, :]
             return carry
 
+        keeps[2].start()
         third = DI // wide // 3
         lax.fori_loop(0, third, chunk_block, 0)
         progress(3)
@@ -982,6 +990,7 @@
             return carry
 
         lax.fori_loop(0, DI // cb, gate_block, 0)
+        keeps[3].start()
         if plane:
             parts[4].landed()
         outs = [
@@ -1067,6 +1076,7 @@
             gated = (yv * (g_in * sigmoid(g_in))).astype(BF16)
             acc[...] += mm(gated, wo[C, :])
 
+        keeps[4].start()
         m32 = tok[...].astype(F32) + acc[...]
         mid[...] = m32
         moe[...] = (m32 * rms_scale(m32) * gp[1:2, :]).astype(BF16)
@@ -1094,7 +1104,7 @@
         if plane:
             for p in parts:
                 p.finish()
-        for c in outs + [cot_own, arr_own]:
+        for c in outs + keeps + [cot_own, arr_own]:
             c.wait()
         for i in range(max(0, steps - 2), steps):
             save(i).wait()
@@ -1112,13 +1122,13 @@
     ins = (tokens, cotangent, seg, route) + tuple(params) + (in_proj, out_proj)
     vm_outs = [
         sds((z.SMALL, DI), F32), sds((gr, D), F32), sds((LANES, D), BF16), sds((T, M), BF16), sds((T, LANES), F32),
-        sds((T, SUB), F32), sds((T, DI), F32), sds((H, DI), F32), sds((T, DI), F32), sds((T, DI), BF16),
-        sds((T, z.XW), F32), sds((T, DI), F32), sds((T, DI), F32), sds((T, D), F32), sds((T, D), BF16),
+        sds((T, SUB), F32), sds((H, DI), F32), sds((T, z.XW), F32), sds((T, D), F32), sds((T, D), BF16),
         sds((T, LANES), F32), sds((S, 1, DI), F32), sds((T, D), BF16), sds((T, D), BF16), sds((T, D), BF16),
     ]
     any_outs = [
         sds((ST, DI), BF16), sds((D, 2 * DI), BF16), sds((DI, D), BF16), sds((2, E, CAP, D), BF16),
-        sds((2, E, CAP, D), BF16),
+        sds((2, E, CAP, D), BF16), sds((T, DI), F32), sds((T, DI), F32), sds((T, DI), BF16), sds((T, DI), F32),
+        sds((T, DI), F32),
     ]
     return pl.pallas_call(
         body,
@@ -1127,6 +1137,7 @@
         out_specs=[vm] * len(vm_outs) + [ANY] * len(any_outs),
         out_shape=vm_outs + any_outs,
         scratch_shapes=[
+            v((T, DI), F32), v((T, DI), F32), v((T, DI), BF16), v((T, DI), F32), v((T, DI), F32),
             v((D, DI), BF16), v((D, DI), BF16), v((DI, D), BF16), v((E * rs, DZ), BF16), v((E * rg, NZ), BF16),
             v((T + H, D), BF16), v((H, D), BF16), v((SUB, LANES), F32),
             v((J * N * SUB, LANES), F32), v((J * N * SUB, LANES), F32), v((T, LANES), F32), v((T, DI), F32),
@@ -1134,7 +1145,7 @@
             v((N * SUB, DI), F32), v((SUB, DI), F32), v((N, cs), F32),
             v((2, ST, cs), BF16), v((T, D), F32), v((M, D), BF16), v((M, D), BF16),
             v((rs, DZ), BF16), v((rg, NZ), BF16), v((SUB, T), F32),
-            sem(13), sem(5, 2, zslots), sem(5, 2, zslots), sem(5, 4, zslots), sem(5, 4, zslots),
+            sem(18), sem(5, 2, zslots), sem(5, 2, zslots), sem(5, 4, zslots), sem(5, 4, zslots),
             sem(5, 5, zslots), sem(5, 5, zslots), sem(2), sem(2), sem(2, S - 1), sem(2, S - 1),
             sem(E - 1), sem(E - 1), sem(1), sem(1), sem(E - 1), sem(E - 1),
             sem(2, E), sem(2, E),
@@ -1164,16 +1175,24 @@
     chain_slots = 2 * (E - 1)
 
     def body(
-        eo, dwu, dwd, states, w_out, w_in, dx_z, table, choose, chances, mid, moe, cot, gp, router, gate, y, sig,
-        small, mixed, dt, masks, conv_in, hconv, s_all, tok, nall,
+        eo, dwu, dwd, states, w_out, w_in, dx_z, table, choose, chances, mid, moe, cot, gp, router, gate_h, y_h, sig_h,
+        small_h, mixed, dt_h, masks, conv_h, hconv, s_all, tok, nall,
         tg_o, gs_o, gg_o, back_o, pg_o, pc_o, pm_o, po_o, up_o, down_o,
-        own_v, big, wo_v, n_v, yg, gi, gz, br, mg, fdev, f_all, suf, cg_edge,
+        gate, y, sig, small, dt, conv_in, own_v, big, wo_v, n_v, yg, gi, gz, br, mg, fdev, f_all, suf, cg_edge,
         edge_in, pc, bx, cx, ia, oa, cl, u_s, rates_s, fin, dg_s, rs_s, rt_s, low_s, mxg, fd,
         ua, ub, ub2, da, db, db2, gi_all, pc_all, br_all, gz_all, gi_b,
         p_g, p_c, p_m, p_o, bg, bc, bm, bo, tg_, tc_, tm_, to_, zg, zc, zm,
         pcs, pcr, pqs, pqr, pzs, pzr, pgs, pgr, pfs, pfr, pown,
         ld, oz_s, oz_r, f_s, f_r, e_s, e_r, g_s, g_r, p_s, p_r, b_s, b_r, a_s, a_r, x_s, x_r,
     ):
+        wide_loads = [
+            pltpu.make_async_copy(a, b, ld.at[18 + n])
+            for n, (a, b) in enumerate(
+                ((gate_h, gate), (y_h, y), (sig_h, sig), (small_h, small), (dt_h, dt), (conv_h, conv_in))
+            )
+        ]
+        for c in wide_loads:
+            c.start()
         psems = lambda a: (
             pcs.at[a], pcr.at[a], pqs.at[a], pqr.at[a], pzs.at[a], pzr.at[a], pgs.at[a], pgr.at[a], pfs.at[a],
             pfr.at[a], pown.at[a],
@@ -1261,6 +1280,8 @@
         gg_o[1:2, :] = gain_g
         gg_o[2 : 2 + E, :] = rg[0:E, :]
         chain_b = Chain(E, br, br_all, b_s, b_r, ld.at[9])
+        for c in wide_loads:
+            c.wait()
 
         def middle_block(i, carry):
             C = at_cols(i, cb_m)
@@ -1725,7 +1746,7 @@
     return pl.pallas_call(
         body,
         name="backward",
-        in_specs=[ANY] * 6 + [vm] * (len(ins) - 7) + [ANY],
+        in_specs=[ANY if a in (0, 1, 2, 3, 4, 5, 15, 16, 17, 18, 20, 22, 26) else vm for a in range(len(ins))],
         out_specs=[vm] * 3 + [ANY] * 7,
         out_shape=[
             sds((T, D), F32),
@@ -1739,6 +1760,7 @@
             sds(down_shape, BF16),
         ],
         scratch_shapes=[
+            v((T, DI), F32), v((T, DI), F32), v((T, DI), BF16), v((z.SMALL, DI), F32), v((T, DI), F32), v((T, DI), F32),
             v((CAP, D), BF16),
             v((2, rows_big, cb_s), BF16),
             v((2, cb_m, D), BF16), v((E * T, D), BF16),
@@ -1764,7 +1786,7 @@
         + [
             sem(4, 2), sem(4, 2), sem(4, 3, 2), sem(4, 3, 2), sem(4, E - 1, 2), sem(4, E - 1, 2), sem(4, 3, 2),
             sem(4, 3, 2), sem(4, 4, 2), sem(4, 4, 2), sem(4),
-            sem(18), sem(E - 1), sem(E - 1), sem(S - 1), sem(S - 1),
+            sem(24), sem(E - 1), sem(E - 1), sem(S - 1), sem(S - 1),
             pltpu.SemaphoreType.DMA, pltpu.SemaphoreType.DMA,
             sem(E - 1), sem(E - 1), sem(E - 1), sem(E - 1), sem(chain_slots), sem(chain_slots),
             sem(6), sem(6), sem(E - 1), sem(E - 1),
@@ -1867,8 +1889,8 @@
         w_in, w_out, params = gathered[0], gathered[1], gathered[2:]
     gr = 8 * -(-(2 + E) // 8)
     (
-        small, gpack, router_t, table, choose_wide, masks, conv_in, hconv, gate, sig, mixed, dt, y, mid, moe, chances,
-        s_all, tok, cot, normed, states, w_in, w_out, arrived, cot_pair,
+        small, gpack, router_t, table, choose_wide, masks, hconv, mixed, mid, moe, chances, s_all, tok, cot, normed,
+        states, w_in, w_out, arrived, cot_pair, conv_in, gate, sig, dt, y,
     ) = forward(
         z, S, plane, tokens[0], cotangent[0], segment_ids, routes.reshape(1, T), params, w_in, w_out, gr, 1
     )

time: 321 us -> 317 us (0.988)
  Pallas kernels: 314 us -> 310 us
where the time goes in v7:
time: 317 us; the launch traced here: 311 us
  Pallas kernels  310 us (98%)
    pallas_call x1, Pallas kernels, backward(): pl.pallas_call(body, name='backward', in_specs=[ANY if a in (0, 1, 2, 3,...  154 us
    pallas_call x1, Pallas kernels, forward(): pl.pallas_call(body, name='forward', in_specs=[vm] * 4 + [vm if plane els...  112 us
    pallas_call x1, Pallas kernels, expert(): pl.pallas_call(body, name='expert', in_specs=[vm] * 4 + [ANY] * 2, out_sp...  35.5 us
    pallas_call x1, Pallas kernels, finish(): pl.pallas_call(body, name='finish', in_specs=[vm] * 12, out_specs=[vm] *...  9.37 us

profile of v7, /device:TPU:23, one launch (start us, length us, event | category | flops | bytes accessed | tf_op | source)
XLA Modules:
  0.0 311.5 jit_solution(15464219008720675781)
XLA Ops:
  0.7 111.6 %forward.1 = (f32[200,2304]{1,0:T(8,128)}, f32[8,1152]{1,0:T(8,128)}, bf16[128,1152]{1,0:T(8,128)(2,1)}, bf16[128,256]{1,0:T(8,128)(2,1)}, f32[128,128]{1,0:T(8,...) custom-call(bf16[128,1152]{1,0:T(8,128)(2,1)} %bitcast.29, ...), custom_call_target="tpu_custom_call" | custom-call | tf_op jit(solution)/shard_map/forward/pallas_call | solution.py:1133
  112.3 35.5 %expert.1 = (bf16[256,1280]{1,0:T(8,128)(2,1)}, bf16[256,1152]{1,0:T(8,128)(2,1)}, bf16[1152,1536]{1,0:T(8,128)(2,1)}, bf16[1536,1152]{1,0:T(8,128)(2,1)}, bf16[4,128,1152]{2,1,0:T(8,128)(2,1)}) custom-call(bf16[512,1152]{1,0:T(8,128)(2,1)} %bitcast.26, bf16[512,1152]{1,0:T(8,128)(2,1)} %bitcast.27, bf16[128,1152]{1,0:T(8,128)(2,1)} %get-tuple-element.72.rt.router, ...), custom_call_target="tpu_custom_call" | custom-call | tf_op jit(solution)/shard_map/expert/pallas_call | solution.py:434
  147.8 153.8 %backward.1 = (f32[128,1152]{1,0:T(8,128)}, f32[200,2304]{1,0:T(8,128)}, f32[8,1152]{1,0:T(8,128)}, bf16[256,1152]{1,0:T(8,128)(2,1)}, bf16[4,2,4,48,576]{4,3,2,...) custom-call(bf16[256,1152]{1,0:T(8,128)(2,1)} %get-tuple-element.74., ...), custom_call_target="tpu_custom_call" | custom-call | tf_op jit(solution)/shard_map/backward/pallas_call | solution.py:1746
  301.7 9.4 %finish.1 = (f32[288,4608]{1,0:T(8,128)}, f32[576,1152]{1,0:T(8,128)}, bf16[128,1152]{1,0:T(8,128)(2,1)}, f32[128,1152]{1,0:T(8,128)}, f32[4,576]{1,0:T(4,128)},...) custom-call(bf16[8,4,48,576]{3,2,1,0:T(8,128)(2,1)} %bitcast.22, ...), custom_call_target="tpu_custom_call" | custom-call | tf_op jit(solution)/shard_map/finish/pallas_call | solution.py:1853

commit v8 on v7

--- a/solution.py
+++ b/solution.py
@@ -1252,8 +1252,6 @@
         out_moves = [
             remote(block_of(eo, p), block_of(back_o, me), oz_s.at[k], oz_r.at[k], {"exp": p}) for k, p in enumerate(zs)
         ]
-        for c in out_moves:
-            c.start()
         back_load = pltpu.make_async_copy(block_of(eo, me), own_v, ld.at[8])
         back_own = pltpu.make_async_copy(own_v, block_of(back_o, me), ld.at[8])
         back_load.start()
@@ -1696,6 +1694,8 @@
         stage(sum_m.swap_start)
         for c in pc_moves:
             c.wait()
+        for c in out_moves:
+            c.start()
         place_in(p_c, flat(pc_all))
         stage(sum_c.swap_start)
         stage(sum_m.swap_finish)

time: 317 us -> 317 us (level)
  no operation moved by 1% of the time
where the time goes in v8:
time: 317 us; the launch traced here: 311 us
  Pallas kernels  310 us (98%)
    pallas_call x1, Pallas kernels, backward(): pl.pallas_call(body, name='backward', in_specs=[ANY if a in (0, 1, 2, 3,...  154 us
    pallas_call x1, Pallas kernels, forward(): pl.pallas_call(body, name='forward', in_specs=[vm] * 4 + [vm if plane els...  112 us
    pallas_call x1, Pallas kernels, expert(): pl.pallas_call(body, name='expert', in_specs=[vm] * 4 + [ANY] * 2, out_sp...  35.5 us
    pallas_call x1, Pallas kernels, finish(): pl.pallas_call(body, name='finish', in_specs=[vm] * 12, out_specs=[vm] *...  9.37 us

profile of v8, /device:TPU:23, one launch (start us, length us, event | category | flops | bytes accessed | tf_op | source)
XLA Modules:
  0.0 311.5 jit_solution(15465872698709194040)
XLA Ops:
  0.7 111.6 %forward.1 = (f32[200,2304]{1,0:T(8,128)}, f32[8,1152]{1,0:T(8,128)}, bf16[128,1152]{1,0:T(8,128)(2,1)}, bf16[128,256]{1,0:T(8,128)(2,1)}, f32[128,128]{1,0:T(8,...) custom-call(bf16[128,1152]{1,0:T(8,128)(2,1)} %bitcast.29, ...), custom_call_target="tpu_custom_call" | custom-call | tf_op jit(solution)/shard_map/forward/pallas_call | solution.py:1133
  112.3 35.5 %expert.1 = (bf16[256,1280]{1,0:T(8,128)(2,1)}, bf16[256,1152]{1,0:T(8,128)(2,1)}, bf16[1152,1536]{1,0:T(8,128)(2,1)}, bf16[1536,1152]{1,0:T(8,128)(2,1)}, bf16[4,128,1152]{2,1,0:T(8,128)(2,1)}) custom-call(bf16[512,1152]{1,0:T(8,128)(2,1)} %bitcast.26, bf16[512,1152]{1,0:T(8,128)(2,1)} %bitcast.27, bf16[128,1152]{1,0:T(8,128)(2,1)} %get-tuple-element.72.rt.router, ...), custom_call_target="tpu_custom_call" | custom-call | tf_op jit(solution)/shard_map/expert/pallas_call | solution.py:434
  147.8 153.8 %backward.1 = (f32[128,1152]{1,0:T(8,128)}, f32[200,2304]{1,0:T(8,128)}, f32[8,1152]{1,0:T(8,128)}, bf16[256,1152]{1,0:T(8,128)(2,1)}, bf16[4,2,4,48,576]{4,3,2,...) custom-call(bf16[256,1152]{1,0:T(8,128)(2,1)} %get-tuple-element.74., ...), custom_call_target="tpu_custom_call" | custom-call | tf_op jit(solution)/shard_map/backward/pallas_call | solution.py:1746
  301.7 9.4 %finish.1 = (f32[288,4608]{1,0:T(8,128)}, f32[576,1152]{1,0:T(8,128)}, bf16[128,1152]{1,0:T(8,128)(2,1)}, f32[128,1152]{1,0:T(8,128)}, f32[4,576]{1,0:T(4,128)},...) custom-call(bf16[8,4,48,576]{3,2,1,0:T(8,128)(2,1)} %bitcast.22, ...), custom_call_target="tpu_custom_call" | custom-call | tf_op jit(solution)/shard_map/finish/pallas_call | solution.py:1853
